TPU v7x, 32 devices: a whole 2x2x4 slice. The times are simulated.
32 devices in a mesh: fsdp: 2 (over x), context: 4 (over z), tensor: 4 (over y, core).
Axes of the slice: x: 2, y: 2, z: 4, core: 2. Of those that a mesh axis runs over, the one named last changes fastest.
Arguments:
- tokens: bfloat16 [2, 640, 1024], P('fsdp', 'context'), may hold values from -6 to 6
- cotangent: bfloat16 [2, 640, 1024], P('fsdp', 'context'), may hold values from -6 to 6
- valid_count: int32 [2], P('fsdp'), may hold values from 481 to 640, as said below
- gain_first: bfloat16 [1024], P('fsdp'), may hold values from 0.5 to 1.5
- shift_first: bfloat16 [1024], P('fsdp'), may hold values from -1.75 to 1.75
- query_weight: bfloat16 [1024, 1024], P('fsdp', 'tensor'), may hold values from -0.25 to 0.25
- query_bias: bfloat16 [64, 16], P('fsdp', 'tensor'), may hold values from -1.75 to 1.75
- key_weight: bfloat16 [1024, 1024], P('fsdp', 'tensor'), may hold values from -0.25 to 0.25
- value_weight: bfloat16 [1024, 1024], P('fsdp', 'tensor'), may hold values from -0.1875 to 0.1875
- value_bias: bfloat16 [64, 16], P('fsdp', 'tensor'), may hold values from -1.75 to 1.75
- output_weight: bfloat16 [1024, 1024], P('tensor', 'fsdp'), may hold values from -0.5 to 0.5
- output_bias: bfloat16 [1024], P('fsdp'), may hold values from -1.75 to 1.75
- gain_second: bfloat16 [1024], P('fsdp'), may hold values from 0.5 to 1.5
- shift_second: bfloat16 [1024], P('fsdp'), may hold values from -1.75 to 1.75
- expand_weight: bfloat16 [1024, 4096], P('fsdp', 'tensor'), may hold values from -0.1875 to 0.1875
- expand_bias: bfloat16 [128, 32], P('fsdp', 'tensor'), may hold values from -1.75 to 1.75
- reduce_weight: bfloat16 [4096, 1024], P('tensor', 'fsdp'), may hold values from -0.09375 to 0.09375
- reduce_bias: bfloat16 [1024], P('fsdp'), may hold values from -1.75 to 1.75
Outputs:
- output: bfloat16 [2, 640, 1024], P('fsdp', 'context')
- grad_tokens: float32 [2, 640, 1024], P('fsdp', 'context')
- grad_gain_first: float32 [1024], P('fsdp')
- grad_shift_first: float32 [1024], P('fsdp')
- grad_query_weight: float32 [1024, 1024], P('fsdp', 'tensor')
- grad_query_bias: float32 [64, 16], P('fsdp', 'tensor')
- grad_key_weight: float32 [1024, 1024], P('fsdp', 'tensor')
- grad_value_weight: float32 [1024, 1024], P('fsdp', 'tensor')
- grad_value_bias: float32 [64, 16], P('fsdp', 'tensor')
- grad_output_weight: float32 [1024, 1024], P('tensor', 'fsdp')
- grad_output_bias: float32 [1024], P('fsdp')
- grad_gain_second: float32 [1024], P('fsdp')
- grad_shift_second: float32 [1024], P('fsdp')
- grad_expand_weight: float32 [1024, 4096], P('fsdp', 'tensor')
- grad_expand_bias: float32 [128, 32], P('fsdp', 'tensor')
- grad_reduce_weight: float32 [4096, 1024], P('tensor', 'fsdp')
- grad_reduce_bias: float32 [1024], P('fsdp')
Inputs may be any that keep to these rules, and one draw needn't show every extreme that they name: `valid_count`: some image, drawn from the seed, has all 640 positions valid; every image has more than three quarters of 640 valid.
All inputs are finite; a program needn't handle non-finite values.
Results may differ from a plain program's by a relative error of at most 0.025.
Values may be sent and summed in bfloat16 or wider, within the bound.
No kernel may reach another device: no remote copies, remote signals or barrier semaphores. Data moves between devices by JAX's collectives and lax.ppermute only.
A program may use at most 128 MiB of HBM per device.

v0:
```python
from functools import partial

import jax
import jax.numpy as jnp
from jax import lax
from jax.sharding import PartitionSpec as P

EPS = 1e-06


def from_behind(block, axis, distance):
    devices = range(lax.axis_size(axis))
    route = [((i - distance) % len(devices), i) for i in devices]
    return lax.ppermute(block, axis, route)


def product(left, right):
    return jnp.dot(left, right, preferred_element_type=jnp.float32)


def contract(form, left, right):
    return jnp.einsum(form, left, right, preferred_element_type=jnp.float32)


def layer_norm(values, gain, shift):
    center = values - jnp.mean(values, -1, keepdims=True)
    spread = jnp.mean(center * center, -1, keepdims=True)
    return center * lax.rsqrt(spread + EPS) * gain + shift


def norm_back(values, gain, shift, upstream):
    _, pull = jax.vjp(layer_norm, values, gain, shift)
    return pull(upstream)


def on_device(
    tokens,
    cotangent,
    valid_count,
    gain_first,
    shift_first,
    query_weight,
    query_bias,
    key_weight,
    value_weight,
    value_bias,
    output_weight,
    output_bias,
    gain_second,
    shift_second,
    expand_weight,
    expand_bias,
    reduce_weight,
    reduce_bias,
):
    (
        gain_one,
        shift_one,
        query_full,
        qbias_full,
        key_full,
        value_full,
        vbias_full,
        outb_full,
        gain_two,
        shift_two,
        expand_full,
        ebias_full,
        rbias_full,
        output_full,
        reduce_full,
    ) = (
        lax.all_gather(gain_first, "fsdp", axis=0, tiled=True),
        lax.all_gather(shift_first, "fsdp", axis=0, tiled=True),
        lax.all_gather(query_weight, "fsdp", axis=0, tiled=True),
        lax.all_gather(query_bias, "fsdp", axis=0, tiled=True),
        lax.all_gather(key_weight, "fsdp", axis=0, tiled=True),
        lax.all_gather(value_weight, "fsdp", axis=0, tiled=True),
        lax.all_gather(value_bias, "fsdp", axis=0, tiled=True),
        lax.all_gather(output_bias, "fsdp", axis=0, tiled=True),
        lax.all_gather(gain_second, "fsdp", axis=0, tiled=True),
        lax.all_gather(shift_second, "fsdp", axis=0, tiled=True),
        lax.all_gather(expand_weight, "fsdp", axis=0, tiled=True),
        lax.all_gather(expand_bias, "fsdp", axis=0, tiled=True),
        lax.all_gather(reduce_bias, "fsdp", axis=0, tiled=True),
        lax.all_gather(output_weight, "fsdp", axis=1, tiled=True),
        lax.all_gather(reduce_weight, "fsdp", axis=1, tiled=True),
    )
    images, seq, width = tokens.shape
    head_dim, heads_here = qbias_full.shape
    features = head_dim * heads_here
    scale = head_dim ** (-0.5)
    cycle = lax.axis_size("context")
    place = lax.axis_index("context")
    positions = jnp.arange(seq, dtype=jnp.int32)

    def key_valid(turn):
        anchor = (place - turn) % cycle
        valid = (anchor * seq + positions)[None, :] < valid_count[:, None]
        return valid[:, None, None, :]

    inputs = tokens.astype(jnp.float32).reshape(-1, width)
    normed_one = layer_norm(inputs, gain_one, shift_one).astype(jnp.bfloat16)
    queries = (product(normed_one, query_full) + qbias_full.T.reshape(-1)).astype(jnp.bfloat16)
    keys = product(normed_one, key_full).astype(jnp.bfloat16)
    values = (product(normed_one, value_full) + vbias_full.T.reshape(-1)).astype(jnp.bfloat16)
    shape_four = (images, seq, heads_here, head_dim)
    query_four = queries.reshape(shape_four)
    key_four = keys.reshape(shape_four)
    value_four = values.reshape(shape_four)
    top = jnp.full((images, heads_here, seq), -1e30, jnp.float32)
    total = jnp.zeros((images, heads_here, seq), jnp.float32)
    accum = jnp.zeros(shape_four, jnp.float32)
    moving = (key_four, value_four)
    for turn in range(cycle):
        if turn > 0:
            moving = from_behind((moving[0], moving[1]), "context", 1)
        key_block, value_block = moving
        valid = key_valid(turn)
        scores = jnp.where(valid, contract("isne,ijne->insj", query_four, key_block) * scale, -1e30)
        new_top = jnp.maximum(top, jnp.max(scores, -1))
        factor = jnp.exp(top - new_top)
        weights = jnp.where(valid, jnp.exp(scores - new_top[..., None]), 0.0)
        total = total * factor + jnp.sum(weights, -1)
        accum = accum * factor.transpose(0, 2, 1)[..., None] + contract(
            "insj,ijne->isne", weights.astype(jnp.bfloat16), value_block
        )
        top = new_top
    attended = accum / total.transpose(0, 2, 1)[..., None]
    log_total = top + jnp.log(total)
    context = attended.reshape(-1, features).astype(jnp.bfloat16)
    branch = (
        lax.psum(product(context, output_full).astype(jnp.bfloat16), "tensor").astype(jnp.float32)
        + outb_full
    )
    hidden = inputs + branch
    normed_two = layer_norm(hidden, gain_two, shift_two).astype(jnp.bfloat16)
    expanded = product(normed_two, expand_full) + ebias_full.T.reshape(-1)
    activated = jax.nn.gelu(expanded, approximate=False).astype(jnp.bfloat16)
    reduced = (
        lax.psum(product(activated, reduce_full).astype(jnp.bfloat16), "tensor").astype(jnp.float32)
        + rbias_full
    )
    output = (hidden + reduced).astype(jnp.bfloat16).reshape(tokens.shape)
    upstream_low = cotangent.reshape(-1, width)
    upstream = upstream_low.astype(jnp.float32)
    grad_rbias = jnp.sum(upstream, 0)
    grad_reduce = contract("rf,rd->fd", activated, upstream_low)
    grad_active = contract("rd,fd->rf", upstream_low, reduce_full)
    _, gelu_pull = jax.vjp(partial(jax.nn.gelu, approximate=False), expanded)
    grad_expanded = gelu_pull(grad_active)[0].astype(jnp.bfloat16)
    grad_ebias = jnp.sum(grad_expanded.astype(jnp.float32), 0).reshape(-1, 128).T
    grad_expand = contract("rd,rf->df", normed_two, grad_expanded)
    grad_normed_two = lax.psum(
        contract("rf,df->rd", grad_expanded, expand_full).astype(jnp.bfloat16), "tensor"
    ).astype(jnp.float32)
    grad_hidden, grad_gain_two, grad_shift_two = norm_back(
        hidden, gain_two, shift_two, grad_normed_two
    )
    grad_hidden = grad_hidden + upstream
    grad_branch = grad_hidden.astype(jnp.bfloat16)
    grad_outb = jnp.sum(grad_branch.astype(jnp.float32), 0)
    grad_output = contract("re,rd->ed", context, grad_branch)
    grad_context = contract("rd,ed->re", grad_branch, output_full).astype(jnp.bfloat16)
    grad_four = grad_context.reshape(shape_four)
    delta = jnp.sum(grad_four.astype(jnp.float32) * attended, -1).transpose(0, 2, 1)
    grad_query_four = jnp.zeros(shape_four, jnp.float32)
    moving = (key_four, value_four)
    carried = (jnp.zeros(shape_four, jnp.float32), jnp.zeros(shape_four, jnp.float32))
    for turn in range(cycle):
        if turn > 0:
            moving = from_behind((moving[0], moving[1]), "context", 1)
        key_block, value_block = moving
        valid = key_valid(turn)
        scores = jnp.where(valid, contract("isne,ijne->insj", query_four, key_block) * scale, -1e30)
        probs = jnp.where(valid, jnp.exp(scores - log_total[..., None]), 0.0)
        grad_probs = contract("isne,ijne->insj", grad_four, value_block)
        grad_scores = (probs * (grad_probs - delta[..., None])).astype(jnp.bfloat16)
        grad_query_four = (
            grad_query_four + contract("insj,ijne->isne", grad_scores, key_block) * scale
        )
        key_grad = carried[0] + contract("insj,isne->ijne", grad_scores, query_four) * scale
        value_grad = carried[1] + contract("insj,isne->ijne", probs.astype(jnp.bfloat16), grad_four)
        carried = (
            from_behind(key_grad.astype(jnp.bfloat16), "context", 1).astype(key_grad.dtype),
            from_behind(value_grad.astype(jnp.bfloat16), "context", 1).astype(value_grad.dtype),
        )
    grad_queries = grad_query_four.reshape(-1, features).astype(jnp.bfloat16)
    grad_keys = carried[0].reshape(-1, features).astype(jnp.bfloat16)
    grad_values = carried[1].reshape(-1, features).astype(jnp.bfloat16)
    grad_qbias = jnp.sum(grad_queries.astype(jnp.float32), 0).reshape(heads_here, head_dim).T
    grad_vbias = jnp.sum(grad_values.astype(jnp.float32), 0).reshape(heads_here, head_dim).T
    grad_query = contract("rd,re->de", normed_one, grad_queries)
    grad_key = contract("rd,re->de", normed_one, grad_keys)
    grad_value = contract("rd,re->de", normed_one, grad_values)
    grad_normed_one = lax.psum(
        (
            contract("re,de->rd", grad_queries, query_full)
            + contract("re,de->rd", grad_keys, key_full)
            + contract("re,de->rd", grad_values, value_full)
        ).astype(jnp.bfloat16),
        "tensor",
    ).astype(jnp.float32)
    grad_inputs, grad_gain_one, grad_shift_one = norm_back(
        inputs, gain_one, shift_one, grad_normed_one
    )
    grad_tokens = (grad_inputs + grad_hidden).reshape(tokens.shape)
    shares = (
        lax.psum_scatter(grad_gain_one, "fsdp", scatter_dimension=0, tiled=True).astype(
            jnp.float32
        ),
        lax.psum_scatter(grad_shift_one, "fsdp", scatter_dimension=0, tiled=True).astype(
            jnp.float32
        ),
        lax.psum_scatter(
            grad_query.astype(jnp.bfloat16), "fsdp", scatter_dimension=0, tiled=True
        ).astype(jnp.float32),
        lax.psum_scatter(
            grad_qbias.astype(jnp.bfloat16), "fsdp", scatter_dimension=0, tiled=True
        ).astype(jnp.float32),
        lax.psum_scatter(
            grad_key.astype(jnp.bfloat16), "fsdp", scatter_dimension=0, tiled=True
        ).astype(jnp.float32),
        lax.psum_scatter(
            grad_value.astype(jnp.bfloat16), "fsdp", scatter_dimension=0, tiled=True
        ).astype(jnp.float32),
        lax.psum_scatter(
            grad_vbias.astype(jnp.bfloat16), "fsdp", scatter_dimension=0, tiled=True
        ).astype(jnp.float32),
        lax.psum_scatter(
            grad_outb.astype(jnp.bfloat16), "fsdp", scatter_dimension=0, tiled=True
        ).astype(jnp.float32),
        lax.psum_scatter(grad_gain_two, "fsdp", scatter_dimension=0, tiled=True).astype(
            jnp.float32
        ),
        lax.psum_scatter(grad_shift_two, "fsdp", scatter_dimension=0, tiled=True).astype(
            jnp.float32
        ),
        lax.psum_scatter(
            grad_expand.astype(jnp.bfloat16), "fsdp", scatter_dimension=0, tiled=True
        ).astype(jnp.float32),
        lax.psum_scatter(
            grad_ebias.astype(jnp.bfloat16), "fsdp", scatter_dimension=0, tiled=True
        ).astype(jnp.float32),
        lax.psum_scatter(
            grad_rbias.astype(jnp.bfloat16), "fsdp", scatter_dimension=0, tiled=True
        ).astype(jnp.float32),
        lax.psum_scatter(
            grad_output.astype(jnp.bfloat16), "fsdp", scatter_dimension=1, tiled=True
        ).astype(jnp.float32),
        lax.psum_scatter(
            grad_reduce.astype(jnp.bfloat16), "fsdp", scatter_dimension=1, tiled=True
        ).astype(jnp.float32),
    )
    shares = (
        lax.psum(shares[0].astype(jnp.bfloat16), "context").astype(jnp.float32),
        lax.psum(shares[1].astype(jnp.bfloat16), "context").astype(jnp.float32),
        lax.psum(shares[2].astype(jnp.bfloat16), "context").astype(jnp.float32),
        lax.psum(shares[3].astype(jnp.bfloat16), "context").astype(jnp.float32),
        lax.psum(shares[4].astype(jnp.bfloat16), "context").astype(jnp.float32),
        lax.psum(shares[5].astype(jnp.bfloat16), "context").astype(jnp.float32),
        lax.psum(shares[6].astype(jnp.bfloat16), "context").astype(jnp.float32),
        lax.psum(shares[7].astype(jnp.bfloat16), "context").astype(jnp.float32),
        lax.psum(shares[8].astype(jnp.bfloat16), "context").astype(jnp.float32),
        lax.psum(shares[9].astype(jnp.bfloat16), "context").astype(jnp.float32),
        lax.psum(shares[10].astype(jnp.bfloat16), "context").astype(jnp.float32),
        lax.psum(shares[11].astype(jnp.bfloat16), "context").astype(jnp.float32),
        lax.psum(shares[12].astype(jnp.bfloat16), "context").astype(jnp.float32),
        lax.psum(shares[13].astype(jnp.bfloat16), "context").astype(jnp.float32),
        lax.psum(shares[14].astype(jnp.bfloat16), "context").astype(jnp.float32),
    )
    return (
        output,
        grad_tokens,
        shares[0],
        shares[1],
        shares[2],
        shares[3],
        shares[4],
        shares[5],
        shares[6],
        shares[13],
        shares[7],
        shares[8],
        shares[9],
        shares[10],
        shares[11],
        shares[14],
        shares[12],
    )


def solution(mesh):
    in_specs = (
        P("fsdp", "context", None),
        P("fsdp", "context", None),
        P("fsdp"),
        P("fsdp"),
        P("fsdp"),
        P("fsdp", "tensor"),
        P("fsdp", "tensor"),
        P("fsdp", "tensor"),
        P("fsdp", "tensor"),
        P("fsdp", "tensor"),
        P("tensor", "fsdp"),
        P("fsdp"),
        P("fsdp"),
        P("fsdp"),
        P("fsdp", "tensor"),
        P("fsdp", "tensor"),
        P("tensor", "fsdp"),
        P("fsdp"),
    )
    out_specs = (
        P("fsdp", "context", None),
        P("fsdp", "context", None),
        P("fsdp"),
        P("fsdp"),
        P("fsdp", "tensor"),
        P("fsdp", "tensor"),
        P("fsdp", "tensor"),
        P("fsdp", "tensor"),
        P("fsdp", "tensor"),
        P("tensor", "fsdp"),
        P("fsdp"),
        P("fsdp"),
        P("fsdp"),
        P("fsdp", "tensor"),
        P("fsdp", "tensor"),
        P("tensor", "fsdp"),
        P("fsdp"),
    )
    return jax.shard_map(
        on_device, mesh=mesh, in_specs=in_specs, out_specs=out_specs, check_vma=False
    )
```

profile of v0, /device:TPU:0, one launch (start us, length us, event | category | flops | bytes accessed | tf_op | source)
XLA Modules:
  0.0 487.8 jit_solution(10581630200962446558)
XLA Ops:
  11.8 5.2 %all-gather = bf16[2,1,512]{2,1,0:T(2,128)(2,1)S(1)} all-gather(bf16[1,1,512]{2,1,0:T(2,128)(2,1)S(1)} %reshape.768), channel_id=1, replica_groups=mesh['fsdp'=2,'context'=4,'tensor'=4] {'fsdp'}, dimensions={0}, use_global_device_ids=true | all-gather | bytes 3072 | tf_op jit(solution)/shard_map/all_gather | solution.py:73
  17.7 4.3 all-gather.1
  22.0 7.3 %all_gather.49 = bf16[1024,256]{1,0:T(8,128)(2,1)S(1)} all-gather(bf16[512,256]{1,0:T(8,128)(2,1)} %param.25), channel_id=1, replica_groups=mesh['fsdp'=2,'context'=4,'tensor'=4] {'fsdp'}, dimensions={0}, use_global_device_ids=true | all-gather | bytes 786432 | tf_op jit(solution)/shard_map/all_gather | solution.py:77
  31.6 2.1 collective-permute-start
  33.7 4.3 all-gather.3
  38.2 7.0 %all_gather.50 = bf16[1024,256]{1,0:T(8,128)(2,1)S(1)} all-gather(bf16[512,256]{1,0:T(8,128)(2,1)S(1)} %copy-done.44), channel_id=1, replica_groups=mesh['fsdp'=2,'context'=4,'tensor'=4] {'fsdp'}, dimensions={0}, use_global_device_ids=true | all-gather | bytes 786432 | tf_op jit(solution)/shard_map/all_gather | solution.py:78
  48.8 4.2 all-gather.2
  53.2 8.4 %all_gather.47 = bf16[1024,256]{1,0:T(8,128)(2,1)S(1)} all-gather(bf16[512,256]{1,0:T(8,128)(2,1)S(1)} %copy-done.45), channel_id=1, replica_groups=mesh['fsdp'=2,'context'=4,'tensor'=4] {'fsdp'}, dimensions={0}, use_global_device_ids=true | all-gather | bytes 786432 | tf_op jit(solution)/shard_map/all_gather | solution.py:75
  62.8 7.0 %all_gather.52 = bf16[256,1024]{1,0:T(8,128)(2,1)S(1)} all-gather(bf16[256,512]{1,0:T(8,128)(2,1)S(1)} %copy-done.46), channel_id=1, replica_groups=mesh['fsdp'=2,'context'=4,'tensor'=4] {'fsdp'}, dimensions={1}, use_global_device_ids=true | all-gather | bytes 786432 | tf_op jit(solution)/shard_map/all_gather | solution.py:86
  70.3 1.8 collective-permute-start.2
  73.3 3.8 collective-permute-done.2
  77.1 1.8 collective-permute-done.3
  79.2 4.7 collective-permute-done.4
  89.2 4.3 all-gather.4
  93.6 4.3 all-gather.5
  98.0 4.4 all-gather.6
  102.3 4.4 all-gather.7
  106.8 11.9 %all-reduce.15.cloned.1.call-done = bf16[160,1024]{1,0:T(8,128)(2,1)} async-done(((bf16[160,1024]{1,0:T(8,128)(2,1)}), bf16[160,1024]{1,0:T(8,128)(2,1)}) %all-reduce.15.cloned.1.call-update) | async-done | bytes 327696 | tf_op jit(solution)/shard_map/psum | solution.py:133
  121.3 4.6 multiply_convert_fusion
  125.9 29.8 %all-gather.14.cloned.1.call-done = bf16[1024,1024]{1,0:T(8,128)(2,1)} async-done(((bf16[1024,512]{1,0:T(8,128)(2,1)}), bf16[1024,1024]{1,0:T(8,128)(2,1)}) %all-gather.14.cloned.1.call-update) | async-done | bytes 2097168 | tf_op jit(solution)/shard_map/all_gather | solution.py:87
  155.7 4.6 fusion.168
  163.0 32.2 %all-reduce.17.cloned.1.call-done = bf16[160,1024]{1,0:T(8,128)(2,1)} async-done(((bf16[160,1024]{1,0:T(8,128)(2,1)}), bf16[160,1024]{1,0:T(8,128)(2,1)}) %all-reduce.17.cloned.1.call-update) | async-done | bytes 327696 | tf_op jit(solution)/shard_map/psum | solution.py:154
  196.5 2.0 fusion.44
  202.3 1.7 copy.121
  213.0 1.6 fusion.27
  216.1 2.1 convolution_convert_fusion.2
  218.3 1.9 fusion.28
  223.9 5.0 %collective-permute-done.11 = bf16[1,160,4,64]{1,3,2,0:T(8,128)(2,1)S(1)} collective-permute-done((bf16[1,160,4,64]{1,3,2,0:T(8,128)(2,1)S(1)}, bf16[1,160,4,64]{1,3,2,0:T(8,128)(2,1)S(1)}, u32[]{:S(2)}, u32[]{:S(2)}) %collective-permute-start.11) | collective-permute-done | bytes 81952 | tf_op jit(solution)/shard_map/ppermute | solution.py:14
  229.3 6.4 %collective-permute-done.12 = bf16[1,160,4,64]{1,3,2,0:T(8,128)(2,1)S(1)} collective-permute-done((bf16[1,160,4,64]{1,3,2,0:T(8,128)(2,1)S(1)}, bf16[1,160,4,64]{1,3,2,0:T(8,128)(2,1)S(1)}, u32[]{:S(2)}, u32[]{:S(2)}) %collective-permute-start.12) | collective-permute-done | bytes 81952 | tf_op jit(solution)/shard_map/ppermute | solution.py:14
  237.2 5.4 %collective-permute-done.13 = bf16[1,160,4,64]{1,3,2,0:T(8,128)(2,1)S(1)} collective-permute-done((bf16[1,160,4,64]{1,3,2,0:T(8,128)(2,1)S(1)}, bf16[1,160,4,64]{1,3,2,0:T(8,128)(2,1)S(1)}, u32[]{:S(2)}, u32[]{:S(2)}) %collective-permute-start.13) | collective-permute-done | bytes 81952 | tf_op jit(solution)/shard_map/ppermute | solution.py:14
  244.6 7.7 %collective-permute-done.8 = bf16[1,160,4,64]{1,3,2,0:T(8,128)(2,1)S(1)} collective-permute-done((bf16[1,160,4,64]{1,3,2,0:T(8,128)(2,1)S(1)}, bf16[1,160,4,64]{1,3,2,0:T(8,128)(2,1)S(1)}, u32[]{:S(2)}, u32[]{:S(2)}) %collective-permute-start.8) | collective-permute-done | bytes 81952 | tf_op jit(solution)/shard_map/ppermute | solution.py:14
  252.4 6.8 %collective-permute-done.9 = bf16[1,160,4,64]{1,3,2,0:T(8,128)(2,1)S(1)} collective-permute-done((bf16[1,160,4,64]{1,3,2,0:T(8,128)(2,1)S(1)}, bf16[1,160,4,64]{1,3,2,0:T(8,128)(2,1)S(1)}, u32[]{:S(2)}, u32[]{:S(2)}) %collective-permute-start.9) | collective-permute-done | bytes 81952 | tf_op jit(solution)/shard_map/ppermute | solution.py:14
  260.5 2.2 convolution_convert_fusion.1
  262.8 2.1 convolution_convert_fusion
  273.1 5.4 %reduce-scatter.18.cloned.1.call-done = bf16[512,256]{1,0:T(8,128)(2,1)} async-done(((bf16[1024,256]{1,0:T(8,128)(2,1)}), bf16[512,256]{1,0:T(8,128)(2,1)}) %reduce-scatter.18.cloned.1.call-update) | async-done | bytes 262160 | tf_op jit(solution)/shard_map/reduce_scatter | solution.py:221
  278.5 34.5 %reduce-scatter.24.cloned.1.call-done = bf16[512,1024]{1,0:T(8,128)(2,1)} async-done(((bf16[1024,1024]{1,0:T(8,128)(2,1)}), bf16[512,1024]{1,0:T(8,128)(2,1)}) %reduce-scatter.24.cloned.1.call-update) | async-done | bytes 1048592 | tf_op jit(solution)/shard_map/reduce_scatter | solution.py:239
  313.0 34.5 %reduce-scatter.26.cloned.1.call-done = bf16[1024,512]{1,0:T(8,128)(2,1)} async-done(((bf16[1024,1024]{1,0:T(8,128)(2,1)}), bf16[1024,512]{1,0:T(8,128)(2,1)}) %reduce-scatter.26.cloned.1.call-update) | async-done | bytes 1048592 | tf_op jit(solution)/shard_map/reduce_scatter | solution.py:251
  347.7 4.3 all-gather.8
  353.3 6.2 %reduce-scatter.32.cloned.1.call-done = bf16[64,8]{1,0:T(8,128)(2,1)} async-done(((bf16[128,8]{1,0:T(8,128)(2,1)}), bf16[64,8]{1,0:T(8,128)(2,1)}) %reduce-scatter.32.cloned.1.call-update) | async-done | bytes 1040
  360.3 11.2 %reduce-scatter.28.cloned.1.call-done = bf16[32,4]{1,0:T(8,128)(2,1)} async-done(((bf16[64,4]{1,0:T(8,128)(2,1)}), bf16[32,4]{1,0:T(8,128)(2,1)}) %reduce-scatter.28.cloned.1.call-update) | async-done | bytes 272
  372.3 11.7 %reduce-scatter.30.cloned.1.call-done = bf16[32,4]{1,0:T(8,128)(2,1)} async-done(((bf16[64,4]{1,0:T(8,128)(2,1)}), bf16[32,4]{1,0:T(8,128)(2,1)}) %reduce-scatter.30.cloned.1.call-update) | async-done | bytes 272
  388.5 6.8 %all-reduce.9 = (bf16[1024]{0:T(1024)(128)(2,1)S(1)}, bf16[1024]{0:T(1024)(128)(2,1)S(1)}, bf16[1024]{0:T(1024)(128)(2,1)S(1)}, bf16[1024]{0:T(1024)(128)(2,1)S(...) all-reduce(bf16[1024]{0:T(1024)(128)(2,1)S(1)} %get-tuple-element.1, ...), channel_id=2, replica_groups=mesh['fsdp'=2,'context'=4,'tensor'=4] {'fsdp'}, use_global_device_ids=true, to_apply=%region_22.23.clone | all-reduce | flops 6144 | bytes 24576
  395.7 19.7 %all-reduce.7 = (bf16[512]{0:T(512)(128)(2,1)S(1)}, bf16[512]{0:T(512)(128)(2,1)S(1)}, bf16[32,4]{0,1:T(4,128)(2,1)S(1)}, bf16[32,4]{0,1:T(4,128)(2,1)S(1)}, bf1...) all-reduce(bf16[512]{0:T(512)(128)(2,1)S(1)} %dynamic-slice.1, ...), channel_id=1, replica_groups=mesh['fsdp'=2,'context'=4,'tensor'=4] {'context'}, use_global_device_ids=true, to_apply=%region_23.24 | all-reduce | flops 3840 | bytes 15360 | tf_op jit(solution)/shard_map/psum | solution.py:256
  420.7 2.6 add_bitcast_fusion
  423.3 47.7 %all-reduce.21.cloned.1.call-done = (bf16[512,256]{1,0:T(8,128)(2,1)}, bf16[512,256]{1,0:T(8,128)(2,1)}, bf16[512,256]{1,0:T(8,128)(2,1)}, bf16[256,512]{1,0:T(8...) async-done(((bf16[512,256]{1,0:T(8,128)(2,1)}, bf16[512,256]{1,0:T(8,128)(2,1)}, bf16[512,256]{1,0:T(8,128)(2,1)}, bf16[256,512]{1,0:T(8,128)(2,1)}, ...) | async-done | bytes 3145744 | tf_op jit(solution)/shard_map/psum | solution.py:258
  471.0 1.9 convert_element_type.472
  472.9 1.8 convert_element_type.476
  474.7 1.8 convert_element_type.478
  (393 shorter events, 71.7 us)
Async XLA Ops:
  8.1 110.7 %all-reduce.15.cloned.1.call-start = ((), (), s32[]{:S(2)}) async-start(), calls=%async_computation.9 | async-start | bytes 655360 | tf_op jit(solution)/shard_map/psum | solution.py:133
  9.3 52.3 %copy-start.69 = (f32[160]{0:T(256)}, f32[160]{0:T(256)S(1)}, u32[]{:S(2)}) copy-start(f32[160]{0:T(256)S(1)} %broadcast_multiply_fusion.1) | copy-start | bytes 1924
  11.1 50.5 %copy-start.87 = (f32[160]{0:T(256)}, f32[160]{0:T(256)S(1)}, u32[]{:S(2)}) copy-start(f32[160]{0:T(256)S(1)} %fusion.136) | copy-start | bytes 1924
  17.0 44.6 %copy-start.55 = (f32[2,1,512]{2,1,0:T(1,128)}, f32[2,1,512]{2,1,0:T(1,128)S(1)}, u32[]{:S(2)}) copy-start(f32[2,1,512]{2,1,0:T(1,128)S(1)} %convert_element_type.504) | copy-start | bytes 12292
  22.0 39.6 %copy-start.98 = (f32[2,1,512]{2,1,0:T(1,128)}, f32[2,1,512]{2,1,0:T(1,128)S(1)}, u32[]{:S(2)}) copy-start(f32[2,1,512]{2,1,0:T(1,128)S(1)} %convert_element_type.505) | copy-start | bytes 12292
  31.6 38.7 %collective-permute-start = (bf16[1,160,4,64]{1,3,2,0:T(8,128)(2,1)S(1)}, bf16[1,160,4,64]{1,3,2,0:T(8,128)(2,1)S(1)}, u32[]{:S(2)}, u32[]{:S(2)}) collective-permute-start(bf16[1,160,4,64]{1,3,2,0:T(8,128)(2,1)S(1)} %bitcast.417), channel_id=1, source_target_pairs={{12,0},{0,4},{4,8},{8,12},{13,1},{1,5},{5,9},{9,13},{14,2},{2,6},{... | collective-permute-start | bytes 245768 | tf_op jit(solution)/shard_map/ppermute | solution.py:14
  46.5 38.5 %copy-start.26 = (bf16[160,256]{0,1:T(8,128)(2,1)}, bf16[160,256]{0,1:T(8,128)(2,1)S(1)}, u32[]{:S(2)}) copy-start(bf16[160,256]{0,1:T(8,128)(2,1)S(1)} %copy.112) | copy-start | bytes 245764
  46.5 25.7 %collective-permute-start.1 = (bf16[1,160,4,64]{1,3,2,0:T(8,128)(2,1)S(1)}, bf16[1,160,4,64]{1,3,2,0:T(8,128)(2,1)S(1)}, u32[]{:S(2)}, u32[]{:S(2)}) collective-permute-start(bf16[1,160,4,64]{1,3,2,0:T(8,128)(2,1)S(1)} %bitcast.420), channel_id=1, source_target_pairs={{12,0},{0,4},{4,8},{8,12},{13,1},{1,5},{5,9},{9,13},{14,2},{2,6},{... | collective-permute-start | bytes 245768 | tf_op jit(solution)/shard_map/ppermute | solution.py:14
  70.3 6.8 %collective-permute-start.2 = (bf16[1,160,4,64]{1,3,2,0:T(8,128)(2,1)S(1)}, bf16[1,160,4,64]{1,3,2,0:T(8,128)(2,1)S(1)}, u32[]{:S(2)}, u32[]{:S(2)}) collective-permute-start(bf16[1,160,4,64]{1,3,2,0:T(8,128)(2,1)S(1)} %collective-permute-done), channel_id=1, source_target_pairs={{12,0},{0,4},{4,8},{8,12},{13,1},{1,5},{5,9},{9,13},{14,2},{2,6},{... | collective-permute-start | bytes 245768 | tf_op jit(solution)/shard_map/ppermute | solution.py:14
  72.1 6.8 %collective-permute-start.3 = (bf16[1,160,4,64]{1,3,2,0:T(8,128)(2,1)S(1)}, bf16[1,160,4,64]{1,3,2,0:T(8,128)(2,1)S(1)}, u32[]{:S(2)}, u32[]{:S(2)}) collective-permute-start(bf16[1,160,4,64]{1,3,2,0:T(8,128)(2,1)S(1)} %collective-permute-done.1), channel_id=1, source_target_pairs={{12,0},{0,4},{4,8},{8,12},{13,1},{1,5},{5,9},{9,13},{14,2},{2,6},{... | collective-permute-start | bytes 245768 | tf_op jit(solution)/shard_map/ppermute | solution.py:14
  77.1 6.8 %collective-permute-start.4 = (bf16[1,160,4,64]{1,3,2,0:T(8,128)(2,1)S(1)}, bf16[1,160,4,64]{1,3,2,0:T(8,128)(2,1)S(1)}, u32[]{:S(2)}, u32[]{:S(2)}) collective-permute-start(bf16[1,160,4,64]{1,3,2,0:T(8,128)(2,1)S(1)} %collective-permute-done.2), channel_id=1, source_target_pairs={{12,0},{0,4},{4,8},{8,12},{13,1},{1,5},{5,9},{9,13},{14,2},{2,6},{... | collective-permute-start | bytes 245768 | tf_op jit(solution)/shard_map/ppermute | solution.py:14
  78.9 7.0 %collective-permute-start.5 = (bf16[1,160,4,64]{1,3,2,0:T(8,128)(2,1)S(1)}, bf16[1,160,4,64]{1,3,2,0:T(8,128)(2,1)S(1)}, u32[]{:S(2)}, u32[]{:S(2)}) collective-permute-start(bf16[1,160,4,64]{1,3,2,0:T(8,128)(2,1)S(1)} %collective-permute-done.3), channel_id=1, source_target_pairs={{12,0},{0,4},{4,8},{8,12},{13,1},{1,5},{5,9},{9,13},{14,2},{2,6},{... | collective-permute-start | bytes 245768 | tf_op jit(solution)/shard_map/ppermute | solution.py:14
  88.0 33.3 %all-gather.12.cloned.1.call-start = ((), (), s32[]{:S(2)}) async-start(), calls=%async_computation.10 | async-start | bytes 3145728 | tf_op jit(solution)/shard_map/all_gather | solution.py:83
  88.6 67.1 %all-gather.14.cloned.1.call-start = ((), (), s32[]{:S(2)}) async-start(), calls=%async_computation.11 | async-start | bytes 3145728 | tf_op jit(solution)/shard_map/all_gather | solution.py:87
  89.2 106.0 %all-reduce.17.cloned.1.call-start = ((), (), s32[]{:S(2)}) async-start(), calls=%async_computation.12 | async-start | bytes 655360 | tf_op jit(solution)/shard_map/psum | solution.py:154
  119.9 78.7 %copy-start.67 = (f32[160]{0:T(256)}, f32[160]{0:T(256)S(1)}, u32[]{:S(2)}) copy-start(f32[160]{0:T(256)S(1)} %broadcast_multiply_fusion) | copy-start | bytes 1924
  121.1 77.5 %copy-start.78 = (f32[160]{0:T(256)}, f32[160]{0:T(256)S(1)}, u32[]{:S(2)}) copy-start(f32[160]{0:T(256)S(1)} %fusion.137) | copy-start | bytes 1924
  162.6 110.4 %reduce-scatter.16.cloned.1.call-start = ((), (), s32[]{:S(2)}) async-start(), calls=%async_computation.13 | async-start | bytes 786432 | tf_op jit(solution)/shard_map/reduce_scatter | solution.py:215
  212.9 60.2 %reduce-scatter.22.cloned.1.call-start = ((), (), s32[]{:S(2)}) async-start(), calls=%async_computation.16 | async-start | bytes 786432 | tf_op jit(solution)/shard_map/reduce_scatter | solution.py:248
  214.6 7.1 %collective-permute-start.10 = (bf16[1,160,4,64]{1,3,2,0:T(8,128)(2,1)}, bf16[1,160,4,64]{1,3,2,0:T(8,128)(2,1)S(1)}, u32[]{:S(2)}, u32[]{:S(2)}) collective-permute-start(bf16[1,160,4,64]{1,3,2,0:T(8,128)(2,1)} %fusion.27), channel_id=1, source_target_pairs={{12,0},{0,4},{4,8},{8,12},{13,1},{1,5},{5,9},{9,13},{14,2},{2,6},{... | collective-permute-start | bytes 245768 | tf_op jit(solution)/shard_map/ppermute | solution.py:14
  220.2 15.7 %collective-permute-start.6 = (bf16[1,160,4,64]{1,3,2,0:T(8,128)(2,1)}, bf16[1,160,4,64]{1,3,2,0:T(8,128)(2,1)}, u32[]{:S(2)}, u32[]{:S(2)}) collective-permute-start(bf16[1,160,4,64]{1,3,2,0:T(8,128)(2,1)} %fusion.28), channel_id=1, source_target_pairs={{12,0},{0,4},{4,8},{8,12},{13,1},{1,5},{5,9},{9,13},{14,2},{2,6},{... | collective-permute-start | bytes 245768 | tf_op jit(solution)/shard_map/ppermute | solution.py:14
  221.6 51.5 %reduce-scatter.20.cloned.1.call-start = ((), (), s32[]{:S(2)}) async-start(), calls=%async_computation.15 | async-start | bytes 786432 | tf_op jit(solution)/shard_map/reduce_scatter | solution.py:224
  222.0 6.8 %collective-permute-start.11 = (bf16[1,160,4,64]{1,3,2,0:T(8,128)(2,1)S(1)}, bf16[1,160,4,64]{1,3,2,0:T(8,128)(2,1)S(1)}, u32[]{:S(2)}, u32[]{:S(2)}) collective-permute-start(bf16[1,160,4,64]{1,3,2,0:T(8,128)(2,1)S(1)} %add_convert_fusion.5), channel_id=1, source_target_pairs={{12,0},{0,4},{4,8},{8,12},{13,1},{1,5},{5,9},{9,13},{14,2},{2,6},{... | collective-permute-start | bytes 245768 | tf_op jit(solution)/shard_map/ppermute | solution.py:14
  228.9 6.8 %collective-permute-start.12 = (bf16[1,160,4,64]{1,3,2,0:T(8,128)(2,1)S(1)}, bf16[1,160,4,64]{1,3,2,0:T(8,128)(2,1)S(1)}, u32[]{:S(2)}, u32[]{:S(2)}) collective-permute-start(bf16[1,160,4,64]{1,3,2,0:T(8,128)(2,1)S(1)} %add_convert_fusion.4), channel_id=1, source_target_pairs={{12,0},{0,4},{4,8},{8,12},{13,1},{1,5},{5,9},{9,13},{14,2},{2,6},{... | collective-permute-start | bytes 245768 | tf_op jit(solution)/shard_map/ppermute | solution.py:14
  235.8 6.8 %collective-permute-start.13 = (bf16[1,160,4,64]{1,3,2,0:T(8,128)(2,1)S(1)}, bf16[1,160,4,64]{1,3,2,0:T(8,128)(2,1)S(1)}, u32[]{:S(2)}, u32[]{:S(2)}) collective-permute-start(bf16[1,160,4,64]{1,3,2,0:T(8,128)(2,1)S(1)} %add_convert_fusion.3), channel_id=1, source_target_pairs={{12,0},{0,4},{4,8},{8,12},{13,1},{1,5},{5,9},{9,13},{14,2},{2,6},{... | collective-permute-start | bytes 245768 | tf_op jit(solution)/shard_map/ppermute | solution.py:14
  237.0 7.2 %collective-permute-start.7 = (bf16[1,160,4,64]{1,3,2,0:T(8,128)(2,1)S(1)}, bf16[1,160,4,64]{1,3,2,0:T(8,128)(2,1)S(1)}, u32[]{:S(2)}, u32[]{:S(2)}) collective-permute-start(bf16[1,160,4,64]{1,3,2,0:T(8,128)(2,1)S(1)} %add_convert_fusion.8), channel_id=1, source_target_pairs={{12,0},{0,4},{4,8},{8,12},{13,1},{1,5},{5,9},{9,13},{14,2},{2,6},{... | collective-permute-start | bytes 245768 | tf_op jit(solution)/shard_map/ppermute | solution.py:14
  243.9 34.6 %reduce-scatter.18.cloned.1.call-start = ((), (), s32[]{:S(2)}) async-start(), calls=%async_computation.14 | async-start | bytes 786432 | tf_op jit(solution)/shard_map/reduce_scatter | solution.py:221
  244.3 8.0 %collective-permute-start.8 = (bf16[1,160,4,64]{1,3,2,0:T(8,128)(2,1)S(1)}, bf16[1,160,4,64]{1,3,2,0:T(8,128)(2,1)S(1)}, u32[]{:S(2)}, u32[]{:S(2)}) collective-permute-start(bf16[1,160,4,64]{1,3,2,0:T(8,128)(2,1)S(1)} %add_convert_fusion.7), channel_id=1, source_target_pairs={{12,0},{0,4},{4,8},{8,12},{13,1},{1,5},{5,9},{9,13},{14,2},{2,6},{... | collective-permute-start | bytes 245768 | tf_op jit(solution)/shard_map/ppermute | solution.py:14
  252.3 6.8 %collective-permute-start.9 = (bf16[1,160,4,64]{1,3,2,0:T(8,128)(2,1)S(1)}, bf16[1,160,4,64]{1,3,2,0:T(8,128)(2,1)S(1)}, u32[]{:S(2)}, u32[]{:S(2)}) collective-permute-start(bf16[1,160,4,64]{1,3,2,0:T(8,128)(2,1)S(1)} %add_convert_fusion.6), channel_id=1, source_target_pairs={{12,0},{0,4},{4,8},{8,12},{13,1},{1,5},{5,9},{9,13},{14,2},{2,6},{... | collective-permute-start | bytes 245768 | tf_op jit(solution)/shard_map/ppermute | solution.py:14
  260.4 52.6 %reduce-scatter.24.cloned.1.call-start = ((), (), s32[]{:S(2)}) async-start(), calls=%async_computation.17 | async-start | bytes 3145728 | tf_op jit(solution)/shard_map/reduce_scatter | solution.py:239
  262.7 84.8 %reduce-scatter.26.cloned.1.call-start = ((), (), s32[]{:S(2)}) async-start(), calls=%async_computation.18 | async-start | bytes 3145728 | tf_op jit(solution)/shard_map/reduce_scatter | solution.py:251
  264.9 94.6 %reduce-scatter.32.cloned.1.call-start = ((), (), s32[]{:S(2)}) async-start(), calls=%async_computation.21 | async-start | bytes 49152
  266.4 105.1 %reduce-scatter.28.cloned.1.call-start = ((), (), s32[]{:S(2)}) async-start(), calls=%async_computation.19 | async-start | bytes 24576
  269.4 114.6 %reduce-scatter.30.cloned.1.call-start = ((), (), s32[]{:S(2)}) async-start(), calls=%async_computation.20 | async-start | bytes 24576
  271.8 112.9 %all-reduce.19.cloned.1.call-start = ((), (), s32[]{:S(2)}) async-start(), calls=%async_computation.22 | async-start | bytes 1310720 | tf_op jit(solution)/shard_map/psum | solution.py:141
  273.0 74.8 %copy-start.109 = (bf16[512]{0:T(512)(128)(2,1)S(1)}, bf16[512]{0:T(512)(128)(2,1)}, u32[]{:S(2)}) copy-start(bf16[512]{0:T(512)(128)(2,1)} %param.35) | copy-start | bytes 3076
  273.0 79.1 %copy-start.110 = (u32[32]{0:T(128)S(1)}, u32[32]{0:T(128)}, u32[]{:S(2)}) copy-start(u32[32]{0:T(128)} %constant.149) | copy-start | bytes 388
  273.0 112.8 %copy-start.72 = (f32[160]{0:T(256)S(1)}, f32[160]{0:T(256)}, u32[]{:S(2)}) copy-start(f32[160]{0:T(256)} %copy-done.69) | copy-start | bytes 1924
  273.0 198.0 %all-reduce.21.cloned.1.call-start = ((), (), s32[]{:S(2)}) async-start(), calls=%async_computation.23 | async-start | bytes 6291456 | tf_op jit(solution)/shard_map/psum | solution.py:258
  347.5 39.5 %copy-start.94 = (f32[160]{0:T(256)S(1)}, f32[160]{0:T(256)}, u32[]{:S(2)}) copy-start(f32[160]{0:T(256)} %copy-done.93) | copy-start | bytes 1924
  347.5 39.5 %copy-start.90 = (f32[160]{0:T(256)S(1)}, f32[160]{0:T(256)}, u32[]{:S(2)}) copy-start(f32[160]{0:T(256)} %copy-done.87) | copy-start | bytes 1924
  347.6 40.9 %copy-start.95 = (bf16[1024]{0:T(1024)(128)(2,1)S(1)}, bf16[1024]{0:T(1024)(128)(2,1)}, u32[]{:S(2)}) copy-start(bf16[1024]{0:T(1024)(128)(2,1)} %get-tuple-element.17) | copy-start | bytes 6148
  347.6 40.9 %copy-start.96 = (bf16[1024]{0:T(1024)(128)(2,1)S(1)}, bf16[1024]{0:T(1024)(128)(2,1)}, u32[]{:S(2)}) copy-start(bf16[1024]{0:T(1024)(128)(2,1)} %get-tuple-element.44) | copy-start | bytes 6148
  347.6 41.0 %copy-start.97 = (bf16[1024]{0:T(1024)(128)(2,1)S(1)}, bf16[1024]{0:T(1024)(128)(2,1)}, u32[]{:S(2)}) copy-start(bf16[1024]{0:T(1024)(128)(2,1)} %get-tuple-element.51) | copy-start | bytes 6148
  347.6 73.1 %copy-start.3 = (bf16[160,1024]{1,0:T(8,128)(2,1)S(1)}, bf16[160,1024]{1,0:T(8,128)(2,1)}, u32[]{:S(2)}) copy-start(bf16[160,1024]{1,0:T(8,128)(2,1)} %all-reduce.17.cloned.1.call-done) | copy-start | bytes 983044
  347.6 73.1 %copy-start.77 = (f32[160]{0:T(256)S(1)}, f32[160]{0:T(256)}, u32[]{:S(2)}) copy-start(f32[160]{0:T(256)} %copy-done.76) | copy-start | bytes 1924
  347.6 73.1 %copy-start.80 = (f32[160]{0:T(256)S(1)}, f32[160]{0:T(256)}, u32[]{:S(2)}) copy-start(f32[160]{0:T(256)} %copy-done.78) | copy-start | bytes 1924
  347.6 73.1 %copy-start.92 = (f32[160]{0:T(256)S(1)}, f32[160]{0:T(256)}, u32[]{:S(2)}) copy-start(f32[160]{0:T(256)} %copy-done.91) | copy-start | bytes 1924
  (92 other events, 820.7 us)
Sparse Core Ops, SparseCore 0:
  88.1 30.5 all-reduce.14
  162.7 32.3 all-reduce.16
  275.6 31.1 all-reduce.18
  347.7 123.2 all-reduce.20
Sparse Core Ops, SparseCore 1:
  90.0 31.2 all-gather.11
  122.7 32.9 all-gather.13
  213.0 14.4 reduce-scatter.15
  229.8 14.4 reduce-scatter.21
  246.6 14.4 reduce-scatter.19
  264.0 14.4 reduce-scatter.17
  281.2 31.7 reduce-scatter.23
  315.8 31.7 reduce-scatter.25
  349.6 9.8 reduce-scatter.31
  361.7 9.8 reduce-scatter.27
  374.1 9.8 reduce-scatter.29
where the time goes:
time: 489 us; the launch traced here: 488 us
  waiting for transfers between devices  268 us (55%)
  blocking collectives  96.1 us (20%)
  matrix products  43.3 us (9%)
  other arithmetic  32.3 us (7%)
  between operations  18.4 us (4%)
  local copies, waits for them, and re-layouts  17.4 us (4%)
  starting transfers between devices  12.1 us (2%)
    psum x1, waiting for transfers between devices, on_device(): lax.psum(shares[2].astype(jnp.bfloat16), 'context').astype(jnp.float32)  47.7 us
    ppermute x14, waiting for transfers between devices, from_behind(): return lax.ppermute(block, axis, route)  41.6 us
    reduce_scatter x1, waiting for transfers between devices, on_device(): lax.psum_scatter(grad_reduce.astype(jnp.bfloat16), 'fsdp', scatter_dimens...  34.5 us
    dot_general x36, matrix products, contract(): return jnp.einsum(form, left, right, preferred_element_type=jnp.float32)  34.5 us
    reduce_scatter x1, waiting for transfers between devices, on_device(): lax.psum_scatter(grad_expand.astype(jnp.bfloat16), 'fsdp', scatter_dimens...  34.5 us
    psum x1, waiting for transfers between devices, on_device(): lax.psum(contract('rf,df->rd', grad_expanded, expand_full).astype(jnp.bfl...  32.2 us
    unnamed x18, waiting for transfers between devices  30.4 us
    all_gather x1, waiting for transfers between devices, on_device(): lax.all_gather(reduce_weight, 'fsdp', axis=1, tiled=True)  29.8 us
  transfers between devices with their start and end apart: 29, of which 19 were waited for; matrix products, arithmetic and copies ran while one was open for 10% of the time, Pallas kernels for 0%

commit v1 on v0

v1 whole, which is shorter than its diff:
```python
import jax
import jax.numpy as jnp
from jax import lax
from jax.sharding import PartitionSpec as P

EPS = 1e-06
LOW = jnp.bfloat16
WIDE = jnp.float32


def swap(block, axis, bit):
    return lax.ppermute(block, axis, [(i, i ^ bit) for i in range(lax.axis_size(axis))])


def after(value, *others):
    return lax.optimization_barrier((value, *others))[0]


def pin(value):
    return lax.optimization_barrier(value)


def dot(left, right):
    return lax.dot_general(left, right, (((1,), (0,)), ((), ())), preferred_element_type=WIDE)


def dot_rt(left, right):
    return lax.dot_general(left, right, (((1,), (1,)), ((), ())), preferred_element_type=WIDE)


def dot_lt(left, right):
    return lax.dot_general(left, right, (((0,), (0,)), ((), ())), preferred_element_type=WIDE)


def segments(value, count):
    size = value.shape[1] // count
    return [value[:, i * size : (i + 1) * size] for i in range(count)]


def from_width(value, parts):
    return sum(dot(s, p) for s, p in zip(segments(value, len(parts)), parts))


def to_width(value, parts):
    return jnp.concatenate([dot(value, p) for p in parts], 1)


def from_width_rt(value, parts):
    return sum(dot_rt(s, p) for s, p in zip(segments(value, len(parts)), parts))


def to_width_rt(value, parts):
    return jnp.concatenate([dot_rt(value, p) for p in parts], 1)


def stats(values):
    center = values - jnp.mean(values, -1, keepdims=True)
    return center, lax.rsqrt(jnp.mean(center * center, -1, keepdims=True) + EPS)


def norm_back(xhat, spread, gain, upstream):
    z = upstream * gain
    mean_z = jnp.mean(z, -1, keepdims=True)
    mean_zx = jnp.mean(z * xhat, -1, keepdims=True)
    return (
        spread * (z - mean_z - xhat * mean_zx),
        jnp.sum(upstream * xhat, 0),
        jnp.sum(upstream, 0),
    )


def reorder(blocks, index):
    bit = 1
    while bit < len(blocks):
        flip = (index & bit) != 0
        blocks = [jnp.where(flip, blocks[k ^ bit], blocks[k]) for k in range(len(blocks))]
        bit *= 2
    return blocks


def sum_tensor(value):
    bit = 1
    while bit < lax.axis_size("tensor"):
        value = pin(value)
        value = value.astype(WIDE) + swap(value, "tensor", bit).astype(WIDE)
        bit *= 2
        if bit < lax.axis_size("tensor"):
            value = value.astype(LOW)
    return value


def all_to_all_context(blocks):
    count = len(blocks)
    bit = 1
    blocks = list(blocks)
    while bit < count:
        sent = [k for k in range(count) if k & bit]
        rows = blocks[0].shape[0]
        got = swap(jnp.concatenate([blocks[k] for k in sent], 0), "context", bit)
        for n, k in enumerate(sent):
            blocks[k] = got[n * rows : (n + 1) * rows]
        bit *= 2
    return blocks


def gather_context(block):
    return [block] + [swap(block, "context", k) for k in range(1, lax.axis_size("context"))]


def sum_context(keep, send, place, axis):
    got = swap(send, "context", 1)
    part = pin((keep + got.astype(WIDE)).astype(LOW))
    far = swap(part, "context", 2)
    total = pin((part.astype(WIDE) + far.astype(WIDE)).astype(LOW))
    other = swap(total, "context", 1)
    odd = (place & 1) != 0
    return jnp.concatenate(
        [jnp.where(odd, other, total), jnp.where(odd, total, other)], axis
    ).astype(WIDE)


def halves(value, axis, odd):
    low, high = jnp.split(value, 2, axis)
    return jnp.where(odd, high, low), jnp.where(odd, low, high)


def on_device(
    tokens,
    cotangent,
    valid_count,
    gain_first,
    shift_first,
    query_weight,
    query_bias,
    key_weight,
    value_weight,
    value_bias,
    output_weight,
    output_bias,
    gain_second,
    shift_second,
    expand_weight,
    expand_bias,
    reduce_weight,
    reduce_bias,
):
    images, seq, width = tokens.shape
    ways = lax.axis_size("fsdp")
    pair = ways == 2
    cycle = lax.axis_size("context")
    mine = lax.axis_index("fsdp")
    place = lax.axis_index("context")
    lane = lax.axis_index("tensor")
    odd = (place & 1) != 0
    share = gain_first.shape[0]
    heads_here = query_bias.shape[1]
    head_dim = query_bias.shape[0] * ways
    features = heads_here * head_dim
    group = features // cycle
    scale = head_dim ** (-0.5)
    second = mine == 1

    def turned(value):
        if not pair:
            return value
        low, high = jnp.split(value, 2, -1)
        return jnp.where(second, jnp.concatenate([high, low], -1), value)

    def whole(own, got):
        return jnp.where(
            second, jnp.concatenate([got, own], 0), jnp.concatenate([own, got], 0)
        )

    def head_columns(weight):
        return lax.dynamic_slice_in_dim(weight, place * group, group, 1)

    local = tokens.reshape(seq, width)
    upstream_low = turned(cotangent.reshape(seq, width))

    half = seq // 2
    core = lane & 1
    piece = lax.dynamic_slice_in_dim(local, core * half, half, 0)
    got = jnp.concatenate(gather_context(piece)[1:], 0)

    head_weight = jnp.concatenate(
        [head_columns(w) for w in (query_weight, key_weight, value_weight)], 1
    )
    if pair:
        vectors = (
            gain_first,
            shift_first,
            output_bias,
            gain_second,
            shift_second,
            reduce_bias,
            query_bias.reshape(-1),
            value_bias.reshape(-1),
            expand_bias.reshape(-1),
        )
        flat = jnp.concatenate(vectors)
        columns = head_weight.shape[1]
        lines = -(-flat.shape[0] // columns)
        lines += -lines % 16
        flat = jnp.pad(flat, (0, lines * columns - flat.shape[0])).reshape(lines, columns)
        first = swap(jnp.concatenate([head_weight, flat], 0), "fsdp", 1)
        head_parts = (head_weight, first[:share])
        taken = first[share:].reshape(-1)
        theirs = []
        at = 0
        for v in vectors:
            theirs.append(taken[at : at + v.shape[0]])
            at += v.shape[0]
        gain_one, shift_one, outb_full, gain_two, shift_two, rbias_full = (
            jnp.concatenate([a, b]).astype(WIDE) for a, b in zip(vectors[:6], theirs[:6])
        )
        qbias_full, vbias_full, ebias_full = (
            whole(a, b.reshape(a.shape)).astype(WIDE)
            for a, b in zip((query_bias, value_bias, expand_bias), theirs[6:])
        )
    else:
        gather = lambda v, axis=0: lax.all_gather(v, "fsdp", axis=axis, tiled=True)
        head_parts = (gather(head_weight),)
        gain_one, shift_one, outb_full, gain_two, shift_two, rbias_full = (
            gather(v).astype(WIDE)
            for v in (gain_first, shift_first, output_bias, gain_second, shift_second, reduce_bias)
        )
        qbias_full, vbias_full, ebias_full = (
            gather(v).astype(WIDE) for v in (query_bias, value_bias, expand_bias)
        )

    theirs_rows = swap(got, "tensor", 1)
    upper = core == 1
    blocks = [local]
    for k in range(cycle - 1):
        a, b = got[k * half : (k + 1) * half], theirs_rows[k * half : (k + 1) * half]
        blocks += [jnp.where(upper, b, a), jnp.where(upper, a, b)]
    every = turned(jnp.concatenate(blocks, 0)).astype(WIDE)
    center, spread = stats(every)
    xhat_all = center * spread
    normed_all = (xhat_all * gain_one + shift_one).astype(LOW)

    head_bias = jnp.concatenate(
        [
            head_columns(qbias_full.T.reshape(1, -1)),
            jnp.zeros((1, group), WIDE),
            head_columns(vbias_full.T.reshape(1, -1)),
        ],
        1,
    )
    qkv = (from_width(normed_all, head_parts) + head_bias).astype(LOW)
    positions = jnp.concatenate(
        [(place ^ k) * seq + jnp.arange(seq, dtype=jnp.int32) for k in range(cycle)]
    )
    valid = (positions < valid_count[0])[None, :]
    kept = []
    attended = []
    for h in range(group // head_dim):
        q, k, v = (
            qkv[:, n * group + h * head_dim : n * group + (h + 1) * head_dim] for n in range(3)
        )
        scores = jnp.where(valid, dot_rt(q, k) * scale, -1e30)
        top = jnp.max(scores, -1, keepdims=True)
        raw = jnp.exp(scores - top)
        weights = raw / jnp.sum(raw, -1, keepdims=True)
        probs = weights.astype(LOW)
        attended.append(dot(probs, v))
        kept.append((q, k, v, weights, probs))
    context_all = jnp.concatenate(attended, 1).astype(LOW)
    rows_of = lambda value: [value[k * seq : (k + 1) * seq] for k in range(cycle)]
    context = jnp.concatenate(reorder(all_to_all_context(rows_of(context_all)), place), 1)

    if pair:
        cot_own, cot_other = segments(upstream_low, 2)
        bundle = swap(
            after(jnp.concatenate([output_weight, cot_other], 0), first), "fsdp", 1
        )
        output_parts = (output_weight, bundle[:features])
        cot_got = bundle[features:]
        expand_parts = (expand_weight, swap(after(expand_weight, first), "fsdp", 1))
        reduce_parts = (reduce_weight, swap(after(reduce_weight, qkv), "fsdp", 1))
        qkv_here = jnp.concatenate([query_weight, key_weight, value_weight], 1)
        qkv_parts = (qkv_here, swap(after(qkv_here, context), "fsdp", 1))
    else:
        output_parts = (gather(output_weight, 1),)
        expand_parts = (gather(expand_weight),)
        reduce_parts = (gather(reduce_weight, 1),)
        qkv_parts = (gather(jnp.concatenate([query_weight, key_weight, value_weight], 1)),)

    inputs = turned(local).astype(WIDE)
    branch = sum_tensor(to_width(context, output_parts).astype(LOW)) + outb_full
    hidden = inputs + branch
    center_two, spread_two = stats(hidden)
    xhat_two = center_two * spread_two
    normed_two = (xhat_two * gain_two + shift_two).astype(LOW)
    expanded = from_width(normed_two, expand_parts) + ebias_full.T.reshape(-1)
    cdf = 0.5 * (1.0 + lax.erf(expanded * (2.0**-0.5)))
    activated = (expanded * cdf).astype(LOW)
    slope = cdf + expanded * jnp.exp(-0.5 * expanded * expanded) * 0.3989422804014327
    grad_expanded = (from_width_rt(upstream_low, reduce_parts) * slope).astype(LOW)

    grad_normed_two = sum_tensor(to_width_rt(grad_expanded, expand_parts).astype(LOW))

    if pair:
        near, other = segments(normed_two, 2)
        moved = swap(jnp.concatenate([activated, other], 1), "fsdp", 1)
        units = activated.shape[1]
        act_rows = jnp.concatenate([activated, moved[:, :units]], 0)
        cot_rows = jnp.concatenate([cot_own, cot_got], 0)
        act_keep, act_send = halves(act_rows, 1, odd)
        reduce_send = dot_lt(act_send, cot_rows).astype(LOW)
        reduce_keep = dot_lt(act_keep, cot_rows)
        norm_rows = jnp.concatenate([near, moved[:, units:]], 0)
        ge_rows = jnp.concatenate([grad_expanded, swap(grad_expanded, "fsdp", 1)], 0)
        ge_keep, ge_send = halves(ge_rows, 1, odd)
        expand_send = dot_lt(norm_rows, ge_send).astype(LOW)
        expand_keep = dot_lt(norm_rows, ge_keep)
    else:
        scatter = lambda v, axis: lax.psum_scatter(
            v.astype(LOW), "fsdp", scatter_dimension=axis, tiled=True
        )
        reduce_keep, reduce_send = halves(scatter(dot_lt(activated, upstream_low), 1), 0, odd)
        expand_keep, expand_send = halves(scatter(dot_lt(normed_two, grad_expanded), 0), 1, odd)
    grad_reduce = sum_context(reduce_keep, reduce_send, place, 0)
    grad_expand = sum_context(expand_keep, expand_send, place, 1)

    upstream = upstream_low.astype(WIDE)
    grad_hidden, gain_two_sum, shift_two_sum = norm_back(
        xhat_two, spread_two, gain_two, grad_normed_two
    )
    grad_hidden = grad_hidden + upstream
    grad_branch = pin(grad_hidden.astype(LOW))
    grad_context = from_width_rt(grad_branch, output_parts).astype(LOW)
    grad_heads = all_to_all_context(
        reorder([grad_context[:, k * group : (k + 1) * group] for k in range(cycle)], place)
    )
    grad_all = jnp.concatenate(grad_heads, 0)
    pieces = []
    for h, (q, k, v, weights, probs) in enumerate(kept):
        g = grad_all[:, h * head_dim : (h + 1) * head_dim]
        grad_probs = dot_rt(g, v)
        delta = jnp.sum(weights * grad_probs, -1, keepdims=True)
        grad_scores = (weights * (grad_probs - delta)).astype(LOW)
        pieces.append((dot(grad_scores, k) * scale, dot_lt(grad_scores, q) * scale, dot_lt(probs, g)))
    grad_qkv = pin(
        jnp.concatenate([p[n] for n in range(3) for p in pieces], 1).astype(LOW)
    )

    home = reorder(all_to_all_context(rows_of(grad_qkv)), place)
    home = jnp.concatenate(
        [b[:, n * group : (n + 1) * group] for n in range(3) for b in home], 1
    )
    grad_normed_one = sum_tensor(to_width_rt(home, qkv_parts).astype(LOW))
    center_one, spread_one = stats(inputs)
    grad_inputs, gain_one_sum, shift_one_sum = norm_back(
        center_one * spread_one, spread_one, gain_one, grad_normed_one
    )
    grad_tokens = turned(grad_inputs + grad_hidden).reshape(tokens.shape)

    reduced = sum_tensor(to_width(activated, reduce_parts).astype(LOW)) + rbias_full
    output = turned((hidden + reduced).astype(LOW)).reshape(tokens.shape)

    sums = (
        jnp.sum(grad_branch.astype(WIDE), 0),
        gain_two_sum,
        shift_two_sum,
        jnp.sum(upstream, 0),
    )
    unit_sum = jnp.sum(grad_expanded.astype(WIDE), 0)
    if pair:
        gb_own, gb_other = segments(grad_branch, 2)
        lines = [s.reshape(2, 1, -1) for s in sums]
        unit_lines = unit_sum.reshape(-1, share)
        bottom = [jnp.concatenate([s[n] for s in lines] + [unit_lines], 0) for n in range(2)]
        fill = -(features + bottom[0].shape[0]) % 32
        filler = jnp.zeros((fill, share), WIDE)
        own = jnp.concatenate([dot_lt(context, gb_own), bottom[0], filler], 0)
        away = jnp.concatenate([dot_lt(context, gb_other), bottom[1], filler], 0)
        own = own + swap(away.astype(LOW), "fsdp", 1).astype(WIDE)
    else:
        bottom = [scatter(s, 0).reshape(1, -1) for s in sums]
        unit_lines = lax.psum(unit_sum.astype(LOW), "fsdp").reshape(-1, share)
        own = jnp.concatenate(
            [scatter(dot_lt(context, grad_branch), 1)] + bottom + [unit_lines], 0
        )
        own = jnp.pad(own, ((0, -own.shape[0] % 32), (0, 0))).astype(WIDE)
    keep, send = halves(own, 0, odd)
    own = sum_context(keep, send.astype(LOW), place, 0)
    grad_output = own[:features]
    grad_outb, grad_gain_two, grad_shift_two, grad_rbias = (own[features + n] for n in range(4))
    unit_total = own[features + 4 : features + 4 + unit_lines.shape[0]].reshape(-1)

    def own_rows(value):
        size = value.shape[0] // ways
        return lax.dynamic_slice_in_dim(value, mine * size, size, 0)

    grad_ebias = own_rows(unit_total.reshape(-1, expand_bias.shape[0] * ways).T)

    head_sum = jnp.sum(grad_qkv.astype(WIDE), 0, keepdims=True)
    head_sum = jnp.pad(head_sum, ((0, 15), (0, 0)))
    if pair:
        own_columns, other_columns = segments(normed_all, 2)
        away = jnp.concatenate([dot_lt(other_columns, grad_qkv), head_sum], 0).astype(LOW)
        own = jnp.concatenate([dot_lt(own_columns, grad_qkv), head_sum], 0)
        own = own + swap(away, "fsdp", 1).astype(WIDE)
    else:
        own = jnp.concatenate(
            [scatter(dot_lt(normed_all, grad_qkv), 0), lax.psum(head_sum.astype(LOW), "fsdp")], 0
        )
    heads = reorder(gather_context(pin(own.astype(LOW))), place)
    grad_query, grad_key, grad_value = (
        jnp.concatenate([b[:, n * group : (n + 1) * group] for b in heads], 1).astype(WIDE)
        for n in range(3)
    )
    grad_qbias, grad_vbias = (
        own_rows(g[share].reshape(heads_here, head_dim).T) for g in (grad_query, grad_value)
    )

    last = turned(jnp.stack([gain_one_sum, shift_one_sum]))
    last = jnp.sum(lax.all_gather(last.astype(LOW), ("fsdp", "context")).astype(WIDE), 0)
    last = lax.dynamic_slice_in_dim(last, mine * share, share, 1)
    return (
        output,
        grad_tokens,
        last[0],
        last[1],
        grad_query[:share],
        grad_qbias,
        grad_key[:share],
        grad_value[:share],
        grad_vbias,
        grad_output,
        grad_outb,
        grad_gain_two,
        grad_shift_two,
        grad_expand,
        grad_ebias,
        grad_reduce,
        grad_rbias,
    )


def solution(mesh):
    rows = P("fsdp", "context", None)
    vector = P("fsdp")
    split = P("fsdp", "tensor")
    turned = P("tensor", "fsdp")
    in_specs = (rows, rows, vector, vector, vector, split, split, split, split, split)
    in_specs += (turned, vector, vector, vector, split, split, turned, vector)
    out_specs = (rows, rows, vector, vector, split, split, split, split, split)
    out_specs += (turned, vector, vector, vector, split, split, turned, vector)
    return jax.shard_map(
        on_device, mesh=mesh, in_specs=in_specs, out_specs=out_specs, check_vma=False
    )
```

time: 489 us -> 304 us (0.62)
  waiting for transfers between devices: 268 us -> 121 us
  blocking collectives: 96.1 us -> 30.4 us
  starting transfers between devices: 12.1 us -> 43.7 us
  local copies, waits for them, and re-layouts: 17.4 us -> 40 us
  between operations: 18.4 us -> 2.77 us
  matrix products: 43.3 us -> 31.4 us
    psum x4 -> x0, waiting for transfers between devices: 91.9 us -> none  [the longest x1 47.7 us: on_device(): lax.psum(shares[2].astype(jnp.bfloat16), 'context').astype(jnp.float32)]
    ppermute x14 -> x39, waiting for transfers between devices: 41.6 us -> 121 us  [swap(): lax.ppermute(block, axis, [(i, i ^ bit) for i in range(lax.axis_size(axis...]
    reduce_scatter x6 -> x0, waiting for transfers between devices: 74.5 us -> none  [the longest x1 34.5 us: on_device(): lax.psum_scatter(grad_reduce.astype(jnp.bfloat16), 'fsdp', scatter_dimens...]
    all_gather x13 -> x1, blocking collectives: 69.6 us -> 30.4 us  [on_device(): lax.all_gather(last.astype(LOW), ('fsdp', 'context')).astype(WIDE)]
    ppermute x14 -> x39, starting transfers between devices: 11.3 us -> 43.7 us  [swap(): lax.ppermute(block, axis, [(i, i ^ bit) for i in range(lax.axis_size(axis...]
    unnamed x18 -> x0, waiting for transfers between devices: 30.4 us -> none
    all_gather x2 -> x0, waiting for transfers between devices: 29.9 us -> none  [the longest x1 29.8 us: on_device(): lax.all_gather(reduce_weight, 'fsdp', axis=1, tiled=True)]
    psum x1 -> x0, blocking collectives: 19.7 us -> none  [on_device(): lax.psum(shares[0].astype(jnp.bfloat16), 'context').astype(jnp.float32)]
  transfers between devices with their start and end apart: 29 -> 39, of which waited for: 19 -> 17; matrix products, arithmetic and copies ran while one was open for 10% -> 33% of each run, Pallas kernels for 0% -> 0%
where the time goes in v1:
time: 304 us; the launch traced here: 303 us
  waiting for transfers between devices  121 us (40%)
  starting transfers between devices  43.7 us (14%)
  local copies, waits for them, and re-layouts  40 us (13%)
  other arithmetic  33.5 us (11%)
  matrix products  31.4 us (10%)
  blocking collectives  30.4 us (10%)
    ppermute x39, waiting for transfers between devices, swap(): lax.ppermute(block, axis, [(i, i ^ bit) for i in range(lax.axis_size(axis...  121 us
    ppermute x39, starting transfers between devices, swap(): lax.ppermute(block, axis, [(i, i ^ bit) for i in range(lax.axis_size(axis...  43.7 us
    all_gather x1, blocking collectives, on_device(): lax.all_gather(last.astype(LOW), ('fsdp', 'context')).astype(WIDE)  30.4 us
    unnamed x120, local copies, waits for them, and re-layouts  14.1 us
    dot_general x10, matrix products, dot_lt(): lax.dot_general(left, right, (((0,), (0,)), ((), ())), preferred_element_...  12.8 us
    dot_general x10, matrix products, dot_rt(): lax.dot_general(left, right, (((1,), (1,)), ((), ())), preferred_element_...  11.7 us
    dot_general x10, matrix products, dot(): lax.dot_general(left, right, (((1,), (0,)), ((), ())), preferred_element_...  6.83 us
  transfers between devices with their start and end apart: 39, of which 17 were waited for; matrix products, arithmetic and copies ran while one was open for 33% of the time, Pallas kernels for 0%

profile of v1, /device:TPU:0, one launch (start us, length us, event | category | flops | bytes accessed | tf_op | source)
XLA Modules:
  0.0 303.0 jit_solution(5916147571314506544)
XLA Ops:
  0.7 1.7 dynamic-slice_bitcast_fusion
  2.4 3.0 collective-permute-start
  5.4 2.5 collective-permute-start.2
  25.8 2.6 fusion.95
  39.8 1.8 collective-permute-start.5
  42.3 1.6 collective-permute-done.5
  44.1 2.9 collective-permute-start.6
  50.8 8.1 %collective-permute-done.7 = bf16[416,512]{1,0:T(8,128)(2,1)S(1)} collective-permute-done((bf16[416,512]{1,0:T(8,128)(2,1)S(1)}, bf16[416,512]{1,0:T(8,128)(2,1)S(1)}, u32[]{:S(2)}, u32[]{:S(2)}) %collective-permute-start.7) | collective-permute-done | bytes 426016 | tf_op jit(solution)/shard_map/ppermute | solution.py:12
  61.0 1.5 collective-permute-start.10
  62.7 1.6 collective-permute-start.9
  67.0 1.6 slice.497
  69.2 3.4 %collective-permute-done.9 = bf16[160,1024]{1,0:T(8,128)(2,1)S(1)} collective-permute-done((bf16[160,1024]{1,0:T(8,128)(2,1)S(1)}, bf16[160,1024]{1,0:T(8,128)(2,1)S(1)}, u32[]{:S(2)}, u32[]{:S(2)}) %collective-permute-start.9) | collective-permute-done | bytes 327712 | tf_op jit(solution)/shard_map/ppermute | solution.py:12
  73.4 1.6 fusion.98
  75.7 11.5 %collective-permute-done.10 = bf16[512,1024]{1,0:T(8,128)(2,1)S(1)} collective-permute-done((bf16[512,1024]{1,0:T(8,128)(2,1)}, bf16[512,1024]{1,0:T(8,128)(2,1)S(1)}, u32[]{:S(2)}, u32[]{:S(2)}) %collective-permute-start.10) | collective-permute-done | bytes 1048608 | tf_op jit(solution)/shard_map/ppermute | solution.py:12
  90.5 1.6 convolution_convert_fusion.11
  92.0 17.6 %collective-permute-done.11 = bf16[1024,512]{1,0:T(8,128)(2,1)S(1)} collective-permute-done((bf16[1024,512]{1,0:T(8,128)(2,1)}, bf16[1024,512]{1,0:T(8,128)(2,1)S(1)}, u32[]{:S(2)}, u32[]{:S(2)}) %collective-permute-start.11) | collective-permute-done | bytes 1048608 | tf_op jit(solution)/shard_map/ppermute | solution.py:12
  111.0 1.8 convolution_convert_fusion.9
  112.8 1.6 collective-permute-start.32
  121.3 2.4 convolution_convert_fusion
  126.6 1.6 collective-permute-start.15
  129.9 2.4 convolution_convert_fusion.1
  133.7 3.6 %collective-permute-done.15 = bf16[160,1024]{1,0:T(8,128)(2,1)S(1)} collective-permute-done((bf16[160,1024]{1,0:T(8,128)(2,1)S(1)}, bf16[160,1024]{1,0:T(8,128)(2,1)S(1)}, u32[]{:S(2)}, u32[]{:S(2)}) %collective-permute-start.15) | collective-permute-done | bytes 327712 | tf_op jit(solution)/shard_map/ppermute | solution.py:12
  137.8 4.5 %collective-permute-done.13 = bf16[160,1024]{1,0:T(8,128)(2,1)S(1)} collective-permute-done((bf16[160,1024]{1,0:T(8,128)(2,1)S(1)}, bf16[160,1024]{1,0:T(8,128)(2,1)S(1)}, u32[]{:S(2)}, u32[]{:S(2)}) %collective-permute-start.13) | collective-permute-done | bytes 327712 | tf_op jit(solution)/shard_map/ppermute | solution.py:12
  142.3 1.5 fusion.107
  148.5 2.8 concatenate.271
  152.8 1.8 fusion.51
  154.6 1.9 concatenate.270
  157.1 2.6 fusion.9
  159.7 2.6 collective-permute-start.37
  162.4 8.8 %collective-permute-done.17 = bf16[320,64]{0,1:T(8,128)(2,1)S(1)} collective-permute-done((bf16[320,64]{0,1:T(8,128)(2,1)S(1)}, bf16[320,64]{0,1:T(8,128)(2,1)S(1)}, u32[]{:S(2)}, u32[]{:S(2)}) %collective-permute-start.17) | collective-permute-done | bytes 40992 | tf_op jit(solution)/shard_map/ppermute | solution.py:12
  175.4 2.6 fusion.8
  178.0 1.5 collective-permute-done.18
  179.8 1.8 collective-permute-done.23
  182.8 2.6 collective-permute-start.24
  186.5 32.8 %collective-permute-done.19 = bf16[320,192]{0,1:T(8,128)(2,1)S(1)} collective-permute-done((bf16[320,192]{0,1:T(8,128)(2,1)S(1)}, bf16[320,192]{0,1:T(8,128)(2,1)S(1)}, u32[]{:S(2)}, u32[]{:S(2)}) %collective-permute-start.19) | collective-permute-done | bytes 122912 | tf_op jit(solution)/shard_map/ppermute | solution.py:12
  219.5 1.6 convolution_convert_fusion.7
  221.1 2.4 collective-permute-start.28
  223.5 1.5 convolution_convert_fusion.6
  225.1 1.5 collective-permute-done.28
  226.6 2.4 collective-permute-start.26
  229.2 5.2 %collective-permute-done.25 = bf16[528,192]{0,1:T(8,128)(2,1)S(1)} collective-permute-done((bf16[528,192]{0,1:T(8,128)(2,1)S(1)}, bf16[528,192]{0,1:T(8,128)(2,1)S(1)}, u32[]{:S(2)}, u32[]{:S(2)}) %collective-permute-start.25) | collective-permute-done | bytes 202784 | tf_op jit(solution)/shard_map/ppermute | solution.py:12
  234.3 4.4 %collective-permute-done.26 = bf16[528,192]{0,1:T(8,128)(2,1)S(1)} collective-permute-done((bf16[528,192]{0,1:T(8,128)(2,1)S(1)}, bf16[528,192]{0,1:T(8,128)(2,1)S(1)}, u32[]{:S(2)}, u32[]{:S(2)}) %collective-permute-start.26) | collective-permute-done | bytes 202784 | tf_op jit(solution)/shard_map/ppermute | solution.py:12
  245.5 2.1 collective-permute-start.30
  247.7 1.6 collective-permute-start.22
  250.7 12.7 %collective-permute-done.30 = bf16[144,512]{1,0:T(8,128)(2,1)S(1)} collective-permute-done((bf16[144,512]{1,0:T(8,128)(2,1)S(1)}, bf16[144,512]{1,0:T(8,128)(2,1)S(1)}, u32[]{:S(2)}, u32[]{:S(2)}) %collective-permute-start.30) | collective-permute-done | bytes 147488 | tf_op jit(solution)/shard_map/ppermute | solution.py:12
  266.6 30.4 %all_gather.4 = bf16[8,2,1024]{2,1,0:T(2,128)(2,1)S(1)} all-gather(bf16[1,2,1024]{2,1,0:T(2,128)(2,1)S(1)} %fusion.82), channel_id=1, replica_groups=mesh['fsdp'=2,'context'=4,'tensor'=4] {'fsdp','context'}, dimensions={0}, use_global_device_ids=true | all-gather | bytes 36864 | tf_op jit(solution)/shard_map/all_gather | solution.py:419
  298.7 1.6 maximum_convert_fusion.1
  301.4 1.6 maximum_convert_fusion
  (355 shorter events, 85.3 us)
Async XLA Ops:
  0.7 22.9 %copy-start.11 = (bf16[512,256]{1,0:T(8,128)(2,1)S(1)}, bf16[512,256]{1,0:T(8,128)(2,1)}, u32[]{:S(2)}) copy-start(bf16[512,256]{1,0:T(8,128)(2,1)} %param.26) | copy-start | bytes 786436
  0.7 22.1 %copy-start.10 = (bf16[512,256]{1,0:T(8,128)(2,1)S(1)}, bf16[512,256]{1,0:T(8,128)(2,1)}, u32[]{:S(2)}) copy-start(bf16[512,256]{1,0:T(8,128)(2,1)} %param.25) | copy-start | bytes 786436
  0.7 21.4 %copy-start.9 = (bf16[512,256]{1,0:T(8,128)(2,1)S(1)}, bf16[512,256]{1,0:T(8,128)(2,1)}, u32[]{:S(2)}) copy-start(bf16[512,256]{1,0:T(8,128)(2,1)} %param.23) | copy-start | bytes 786436
  2.4 22.4 %copy-start.2 = (bf16[1,160,1024]{2,1,0:T(8,128)(2,1)S(1)}, bf16[1,160,1024]{2,1,0:T(8,128)(2,1)}, u32[]{:S(2)}) copy-start(bf16[1,160,1024]{2,1,0:T(8,128)(2,1)} %param.18) | copy-start | bytes 983044
  2.4 26.9 %collective-permute-start = (bf16[80,1024]{1,0:T(8,128)(2,1)}, bf16[80,1024]{1,0:T(8,128)(2,1)S(1)}, u32[]{:S(2)}, u32[]{:S(2)}) collective-permute-start(bf16[80,1024]{1,0:T(8,128)(2,1)} %dynamic-slice_bitcast_fusion), channel_id=1, source_target_pairs={{0,4},{4,0},{8,12},{12,8},{1,5},{5,1},{9,13},{13,9},{2,6},{6,2},{1... | collective-permute-start | bytes 491528 | tf_op jit(solution)/shard_map/ppermute | solution.py:12
  5.4 23.8 %collective-permute-start.2 = (bf16[80,1024]{1,0:T(8,128)(2,1)}, bf16[80,1024]{1,0:T(8,128)(2,1)S(1)}, u32[]{:S(2)}, u32[]{:S(2)}) collective-permute-start(bf16[80,1024]{1,0:T(8,128)(2,1)} %dynamic-slice_bitcast_fusion), channel_id=1, source_target_pairs={{0,12},{4,8},{8,4},{12,0},{1,13},{5,9},{9,5},{13,1},{2,14},{6,10},... | collective-permute-start | bytes 491528 | tf_op jit(solution)/shard_map/ppermute | solution.py:12
  7.9 21.4 %collective-permute-start.1 = (bf16[80,1024]{1,0:T(8,128)(2,1)}, bf16[80,1024]{1,0:T(8,128)(2,1)S(1)}, u32[]{:S(2)}, u32[]{:S(2)}) collective-permute-start(bf16[80,1024]{1,0:T(8,128)(2,1)} %dynamic-slice_bitcast_fusion), channel_id=1, source_target_pairs={{0,8},{4,12},{8,0},{12,4},{1,9},{5,13},{9,1},{13,5},{2,10},{6,14},... | collective-permute-start | bytes 491528 | tf_op jit(solution)/shard_map/ppermute | solution.py:12
  20.6 9.9 %collective-permute-start.4 = (bf16[544,192]{1,0:T(8,128)(2,1)}, bf16[544,192]{1,0:T(8,128)(2,1)}, u32[]{:S(2)}, u32[]{:S(2)}) collective-permute-start(bf16[544,192]{1,0:T(8,128)(2,1)} %pad_maximum_fusion.11), channel_id=1, source_target_pairs={{0,16},{16,0},{1,17},{17,1},{2,18},{18,2},{3,19},{19,3},{4,20},{20... | collective-permute-start | bytes 626696 | tf_op jit(solution)/shard_map/ppermute | solution.py:12
  24.3 196.9 %collective-permute-start.20 = (bf16[512,768]{1,0:T(8,128)(2,1)}, bf16[512,768]{1,0:T(8,128)(2,1)}, u32[]{:S(2)}, u32[]{:S(2)}) collective-permute-start(bf16[512,768]{1,0:T(8,128)(2,1)} %constant_dynamic-update-slice_fusion.13), channel_id=1, source_target_pairs={{0,16},{16,0},{1,17},{17,1},{2,18},{18,2},{3,19},{19,3},{4,20},{20... | collective-permute-start | bytes 2359304 | tf_op jit(solution)/shard_map/ppermute | solution.py:12
  30.1 4.4 %collective-permute-start.3 = (bf16[240,1024]{1,0:T(8,128)(2,1)}, bf16[240,1024]{1,0:T(8,128)(2,1)S(1)}, u32[]{:S(2)}, u32[]{:S(2)}) collective-permute-start(bf16[240,1024]{1,0:T(8,128)(2,1)} %pad_maximum_fusion), channel_id=1, source_target_pairs={{0,1},{1,0},{2,3},{3,2},{4,5},{5,4},{6,7},{7,6},{8,9},{9,8},{10,11... | collective-permute-start | bytes 1474568 | tf_op jit(solution)/shard_map/ppermute | solution.py:12
  39.8 4.1 %collective-permute-start.5 = (bf16[320,64]{0,1:T(8,128)(2,1)S(1)}, bf16[320,64]{0,1:T(8,128)(2,1)S(1)}, u32[]{:S(2)}, u32[]{:S(2)}) collective-permute-start(bf16[320,64]{0,1:T(8,128)(2,1)S(1)} %pad_maximum_fusion.25), channel_id=1, source_target_pairs={{0,4},{4,0},{8,12},{12,8},{1,5},{5,1},{9,13},{13,9},{2,6},{6,2},{1... | collective-permute-start | bytes 122888 | tf_op jit(solution)/shard_map/ppermute | solution.py:12
  44.1 5.6 %collective-permute-start.6 = (bf16[320,64]{0,1:T(8,128)(2,1)S(1)}, bf16[320,64]{0,1:T(8,128)(2,1)S(1)}, u32[]{:S(2)}, u32[]{:S(2)}) collective-permute-start(bf16[320,64]{0,1:T(8,128)(2,1)S(1)} %pad_maximum_fusion.26), channel_id=1, source_target_pairs={{0,8},{4,12},{8,0},{12,4},{1,9},{5,13},{9,1},{13,5},{2,10},{6,14},... | collective-permute-start | bytes 122888 | tf_op jit(solution)/shard_map/ppermute | solution.py:12
  47.0 15.6 %copy-start.41 = (bf16[64,8]{0,1:T(8,128)(2,1)S(1)}, bf16[64,8]{0,1:T(8,128)(2,1)}, u32[]{:S(2)}) copy-start(bf16[64,8]{0,1:T(8,128)(2,1)} %param.33) | copy-start | bytes 3076
  48.2 10.7 %collective-permute-start.7 = (bf16[416,512]{1,0:T(8,128)(2,1)S(1)}, bf16[416,512]{1,0:T(8,128)(2,1)S(1)}, u32[]{:S(2)}, u32[]{:S(2)}) collective-permute-start(bf16[416,512]{1,0:T(8,128)(2,1)S(1)} %pad_maximum_fusion.2), channel_id=1, source_target_pairs={{0,16},{16,0},{1,17},{17,1},{2,18},{18,2},{3,19},{19,3},{4,20},{20... | collective-permute-start | bytes 1277960 | tf_op jit(solution)/shard_map/ppermute | solution.py:12
  60.0 2.6 collective-permute-start.8
  61.0 26.2 %collective-permute-start.10 = (bf16[512,1024]{1,0:T(8,128)(2,1)}, bf16[512,1024]{1,0:T(8,128)(2,1)S(1)}, u32[]{:S(2)}, u32[]{:S(2)}) collective-permute-start(bf16[512,1024]{1,0:T(8,128)(2,1)} %param.32), channel_id=1, source_target_pairs={{0,16},{16,0},{1,17},{17,1},{2,18},{18,2},{3,19},{19,3},{4,20},{20... | collective-permute-start | bytes 3145736 | tf_op jit(solution)/shard_map/ppermute | solution.py:12
  62.7 9.9 %collective-permute-start.9 = (bf16[160,1024]{1,0:T(8,128)(2,1)S(1)}, bf16[160,1024]{1,0:T(8,128)(2,1)S(1)}, u32[]{:S(2)}, u32[]{:S(2)}) collective-permute-start(bf16[160,1024]{1,0:T(8,128)(2,1)S(1)} %add_convert_fusion.7), channel_id=1, source_target_pairs={{0,2},{1,3},{2,0},{3,1},{4,6},{5,7},{6,4},{7,5},{8,10},{9,11},{10,... | collective-permute-start | bytes 983048 | tf_op jit(solution)/shard_map/ppermute | solution.py:12
  68.6 41.0 %collective-permute-start.11 = (bf16[1024,512]{1,0:T(8,128)(2,1)}, bf16[1024,512]{1,0:T(8,128)(2,1)S(1)}, u32[]{:S(2)}, u32[]{:S(2)}) collective-permute-start(bf16[1024,512]{1,0:T(8,128)(2,1)} %param.34), channel_id=1, source_target_pairs={{0,16},{16,0},{1,17},{17,1},{2,18},{18,2},{3,19},{19,3},{4,20},{20... | collective-permute-start | bytes 3145736 | tf_op jit(solution)/shard_map/ppermute | solution.py:12
  87.6 22.1 %copy-start.8 = (f32[160,1024]{1,0:T(8,128)S(1)}, f32[160,1024]{1,0:T(8,128)}, u32[]{:S(2)}) copy-start(f32[160,1024]{1,0:T(8,128)} %fusion.95) | copy-start | bytes 1966084
  88.4 31.9 %collective-permute-start.31 = (bf16[160,1536]{1,0:T(8,128)(2,1)}, bf16[160,1536]{1,0:T(8,128)(2,1)}, u32[]{:S(2)}, u32[]{:S(2)}) collective-permute-start(bf16[160,1536]{1,0:T(8,128)(2,1)} %pad_maximum_fusion.1), channel_id=1, source_target_pairs={{0,16},{16,0},{1,17},{17,1},{2,18},{18,2},{3,19},{19,3},{4,20},{20... | collective-permute-start | bytes 1474568 | tf_op jit(solution)/shard_map/ppermute | solution.py:12
  112.8 17.1 %collective-permute-start.32 = (bf16[160,1024]{1,0:T(8,128)(2,1)}, bf16[160,1024]{1,0:T(8,128)(2,1)}, u32[]{:S(2)}, u32[]{:S(2)}) collective-permute-start(bf16[160,1024]{1,0:T(8,128)(2,1)} %get-tuple-element.192), channel_id=1, source_target_pairs={{0,16},{16,0},{1,17},{17,1},{2,18},{18,2},{3,19},{19,3},{4,20},{20... | collective-permute-start | bytes 983048 | tf_op jit(solution)/shard_map/ppermute | solution.py:12
  116.6 8.7 %collective-permute-start.14 = (bf16[160,1024]{1,0:T(8,128)(2,1)}, bf16[160,1024]{1,0:T(8,128)(2,1)}, u32[]{:S(2)}, u32[]{:S(2)}) collective-permute-start(bf16[160,1024]{1,0:T(8,128)(2,1)} %pad_maximum_fusion.7), channel_id=1, source_target_pairs={{0,1},{1,0},{2,3},{3,2},{4,5},{5,4},{6,7},{7,6},{8,9},{9,8},{10,11... | collective-permute-start | bytes 983048 | tf_op jit(solution)/shard_map/ppermute | solution.py:12
  117.7 10.4 %collective-permute-start.12 = (bf16[160,1024]{1,0:T(8,128)(2,1)}, bf16[160,1024]{1,0:T(8,128)(2,1)}, u32[]{:S(2)}, u32[]{:S(2)}) collective-permute-start(bf16[160,1024]{1,0:T(8,128)(2,1)} %pad_maximum_fusion.6), channel_id=1, source_target_pairs={{0,1},{1,0},{2,3},{3,2},{4,5},{5,4},{6,7},{7,6},{8,9},{9,8},{10,11... | collective-permute-start | bytes 983048 | tf_op jit(solution)/shard_map/ppermute | solution.py:12
  123.7 33.4 %collective-permute-start.36 = (bf16[512,512]{1,0:T(8,128)(2,1)}, bf16[512,512]{1,0:T(8,128)(2,1)}, u32[]{:S(2)}, u32[]{:S(2)}) collective-permute-start(bf16[512,512]{1,0:T(8,128)(2,1)} %convolution_convert_fusion), channel_id=1, source_target_pairs={{0,4},{4,0},{8,12},{12,8},{1,5},{5,1},{9,13},{13,9},{2,6},{6,2},{1... | collective-permute-start | bytes 1572872 | tf_op jit(solution)/shard_map/ppermute | solution.py:12
  126.6 10.7 %collective-permute-start.15 = (bf16[160,1024]{1,0:T(8,128)(2,1)S(1)}, bf16[160,1024]{1,0:T(8,128)(2,1)S(1)}, u32[]{:S(2)}, u32[]{:S(2)}) collective-permute-start(bf16[160,1024]{1,0:T(8,128)(2,1)S(1)} %add_convert_fusion.3), channel_id=1, source_target_pairs={{0,2},{1,3},{2,0},{3,1},{4,6},{5,7},{6,4},{7,5},{8,10},{9,11},{10,... | collective-permute-start | bytes 983048 | tf_op jit(solution)/shard_map/ppermute | solution.py:12
  129.3 13.0 %collective-permute-start.13 = (bf16[160,1024]{1,0:T(8,128)(2,1)S(1)}, bf16[160,1024]{1,0:T(8,128)(2,1)S(1)}, u32[]{:S(2)}, u32[]{:S(2)}) collective-permute-start(bf16[160,1024]{1,0:T(8,128)(2,1)S(1)} %add_convert_fusion.5), channel_id=1, source_target_pairs={{0,2},{1,3},{2,0},{3,1},{4,6},{5,7},{6,4},{7,5},{8,10},{9,11},{10,... | collective-permute-start | bytes 983048 | tf_op jit(solution)/shard_map/ppermute | solution.py:12
  132.4 42.9 %collective-permute-start.33 = (bf16[512,512]{1,0:T(8,128)(2,1)}, bf16[512,512]{1,0:T(8,128)(2,1)}, u32[]{:S(2)}, u32[]{:S(2)}) collective-permute-start(bf16[512,512]{1,0:T(8,128)(2,1)} %convolution_convert_fusion.1), channel_id=1, source_target_pairs={{0,4},{4,0},{8,12},{12,8},{1,5},{5,1},{9,13},{13,9},{2,6},{6,2},{1... | collective-permute-start | bytes 1572872 | tf_op jit(solution)/shard_map/ppermute | solution.py:12
  147.0 9.5 %collective-permute-start.16 = (bf16[320,64]{0,1:T(8,128)(2,1)}, bf16[320,64]{0,1:T(8,128)(2,1)S(1)}, u32[]{:S(2)}, u32[]{:S(2)}) collective-permute-start(bf16[320,64]{0,1:T(8,128)(2,1)} %pad_maximum_fusion.27), channel_id=1, source_target_pairs={{0,4},{4,0},{8,12},{12,8},{1,5},{5,1},{9,13},{13,9},{2,6},{6,2},{1... | collective-permute-start | bytes 122888 | tf_op jit(solution)/shard_map/ppermute | solution.py:12
  151.3 31.5 %collective-permute-start.27 = (bf16[288,512]{1,0:T(8,128)(2,1)}, bf16[288,512]{1,0:T(8,128)(2,1)}, u32[]{:S(2)}, u32[]{:S(2)}) collective-permute-start(bf16[288,512]{1,0:T(8,128)(2,1)} %concatenate.271), channel_id=1, source_target_pairs={{0,16},{16,0},{1,17},{17,1},{2,18},{18,2},{3,19},{19,3},{4,20},{20... | collective-permute-start | bytes 884744 | tf_op jit(solution)/shard_map/ppermute | solution.py:12
  156.7 14.5 %copy-start.28 = (bf16[160,64]{0,1:T(8,128)(2,1)S(1)}, bf16[160,64]{0,1:T(8,128)(2,1)}, u32[]{:S(2)}) copy-start(bf16[160,64]{0,1:T(8,128)(2,1)} %get-tuple-element.166) | copy-start | bytes 61444
  156.7 14.5 %collective-permute-start.17 = (bf16[320,64]{0,1:T(8,128)(2,1)S(1)}, bf16[320,64]{0,1:T(8,128)(2,1)S(1)}, u32[]{:S(2)}, u32[]{:S(2)}) collective-permute-start(bf16[320,64]{0,1:T(8,128)(2,1)S(1)} %pad_maximum_fusion.28), channel_id=1, source_target_pairs={{0,8},{4,12},{8,0},{12,4},{1,9},{5,13},{9,1},{13,5},{2,10},{6,14},... | collective-permute-start | bytes 122888 | tf_op jit(solution)/shard_map/ppermute | solution.py:12
  159.7 84.3 %collective-permute-start.37 = (bf16[512,512]{1,0:T(8,128)(2,1)}, bf16[512,512]{1,0:T(8,128)(2,1)}, u32[]{:S(2)}, u32[]{:S(2)}) collective-permute-start(bf16[512,512]{1,0:T(8,128)(2,1)} %fusion.9), channel_id=1, source_target_pairs={{0,8},{4,12},{8,0},{12,4},{1,9},{5,13},{9,1},{13,5},{2,10},{6,14},... | collective-permute-start | bytes 1572872 | tf_op jit(solution)/shard_map/ppermute | solution.py:12
  173.9 5.7 %collective-permute-start.18 = (bf16[320,192]{0,1:T(8,128)(2,1)S(1)}, bf16[320,192]{0,1:T(8,128)(2,1)S(1)}, u32[]{:S(2)}, u32[]{:S(2)}) collective-permute-start(bf16[320,192]{0,1:T(8,128)(2,1)S(1)} %pad_maximum_fusion.21), channel_id=1, source_target_pairs={{0,4},{4,0},{8,12},{12,8},{1,5},{5,1},{9,13},{13,9},{2,6},{6,2},{1... | collective-permute-start | bytes 368648 | tf_op jit(solution)/shard_map/ppermute | solution.py:12
  175.3 6.3 %collective-permute-start.23 = (bf16[528,192]{0,1:T(8,128)(2,1)S(1)}, bf16[528,192]{0,1:T(8,128)(2,1)S(1)}, u32[]{:S(2)}, u32[]{:S(2)}) collective-permute-start(bf16[528,192]{0,1:T(8,128)(2,1)S(1)} %pad_maximum_fusion.16), channel_id=1, source_target_pairs={{0,16},{16,0},{1,17},{17,1},{2,18},{18,2},{3,19},{19,3},{4,20},{20... | collective-permute-start | bytes 608264 | tf_op jit(solution)/shard_map/ppermute | solution.py:12
  179.5 69.7 %collective-permute-start.34 = (bf16[512,512]{1,0:T(8,128)(2,1)}, bf16[512,512]{1,0:T(8,128)(2,1)}, u32[]{:S(2)}, u32[]{:S(2)}) collective-permute-start(bf16[512,512]{1,0:T(8,128)(2,1)} %fusion.8), channel_id=1, source_target_pairs={{0,8},{4,12},{8,0},{12,4},{1,9},{5,13},{9,1},{13,5},{2,10},{6,14},... | collective-permute-start | bytes 1572872 | tf_op jit(solution)/shard_map/ppermute | solution.py:12
  181.6 37.7 %collective-permute-start.19 = (bf16[320,192]{0,1:T(8,128)(2,1)S(1)}, bf16[320,192]{0,1:T(8,128)(2,1)S(1)}, u32[]{:S(2)}, u32[]{:S(2)}) collective-permute-start(bf16[320,192]{0,1:T(8,128)(2,1)S(1)} %pad_maximum_fusion.22), channel_id=1, source_target_pairs={{0,8},{4,12},{8,0},{12,4},{1,9},{5,13},{9,1},{13,5},{2,10},{6,14},... | collective-permute-start | bytes 368648 | tf_op jit(solution)/shard_map/ppermute | solution.py:12
  182.8 46.3 %collective-permute-start.24 = (bf16[528,192]{0,1:T(8,128)(2,1)S(1)}, bf16[528,192]{0,1:T(8,128)(2,1)S(1)}, u32[]{:S(2)}, u32[]{:S(2)}) collective-permute-start(bf16[528,192]{0,1:T(8,128)(2,1)S(1)} %fusion.46), channel_id=1, source_target_pairs={{0,12},{4,8},{8,4},{12,0},{1,13},{5,9},{9,5},{13,1},{2,14},{6,10},... | collective-permute-start | bytes 608264 | tf_op jit(solution)/shard_map/ppermute | solution.py:12
  219.3 15.0 %collective-permute-start.25 = (bf16[528,192]{0,1:T(8,128)(2,1)S(1)}, bf16[528,192]{0,1:T(8,128)(2,1)S(1)}, u32[]{:S(2)}, u32[]{:S(2)}) collective-permute-start(bf16[528,192]{0,1:T(8,128)(2,1)S(1)} %fusion.46), channel_id=1, source_target_pairs={{0,8},{4,12},{8,0},{12,4},{1,9},{5,13},{9,1},{13,5},{2,10},{6,14},... | collective-permute-start | bytes 608264 | tf_op jit(solution)/shard_map/ppermute | solution.py:12
  221.1 5.5 %collective-permute-start.28 = (bf16[144,512]{1,0:T(8,128)(2,1)S(1)}, bf16[144,512]{1,0:T(8,128)(2,1)S(1)}, u32[]{:S(2)}, u32[]{:S(2)}) collective-permute-start(bf16[144,512]{1,0:T(8,128)(2,1)S(1)} %select_convert_fusion), channel_id=1, source_target_pairs={{0,4},{4,0},{8,12},{12,8},{1,5},{5,1},{9,13},{13,9},{2,6},{6,2},{1... | collective-permute-start | bytes 442376 | tf_op jit(solution)/shard_map/ppermute | solution.py:12
  226.6 12.1 %collective-permute-start.26 = (bf16[528,192]{0,1:T(8,128)(2,1)S(1)}, bf16[528,192]{0,1:T(8,128)(2,1)S(1)}, u32[]{:S(2)}, u32[]{:S(2)}) collective-permute-start(bf16[528,192]{0,1:T(8,128)(2,1)S(1)} %fusion.46), channel_id=1, source_target_pairs={{0,4},{4,0},{8,12},{12,8},{1,5},{5,1},{9,13},{13,9},{2,6},{6,2},{1... | collective-permute-start | bytes 608264 | tf_op jit(solution)/shard_map/ppermute | solution.py:12
  229.1 18.5 %collective-permute-start.21 = (bf16[160,1024]{1,0:T(8,128)(2,1)S(1)}, bf16[160,1024]{1,0:T(8,128)(2,1)S(1)}, u32[]{:S(2)}, u32[]{:S(2)}) collective-permute-start(bf16[160,1024]{1,0:T(8,128)(2,1)S(1)} %pad_maximum_fusion.8), channel_id=1, source_target_pairs={{0,1},{1,0},{2,3},{3,2},{4,5},{5,4},{6,7},{7,6},{8,9},{9,8},{10,11... | collective-permute-start | bytes 983048 | tf_op jit(solution)/shard_map/ppermute | solution.py:12
  234.3 11.1 %collective-permute-start.29 = (bf16[144,512]{1,0:T(8,128)(2,1)S(1)}, bf16[144,512]{1,0:T(8,128)(2,1)S(1)}, u32[]{:S(2)}, u32[]{:S(2)}) collective-permute-start(bf16[144,512]{1,0:T(8,128)(2,1)S(1)} %add_convert_fusion.9), channel_id=1, source_target_pairs={{0,8},{4,12},{8,0},{12,4},{1,9},{5,13},{9,1},{13,5},{2,10},{6,14},... | collective-permute-start | bytes 442376 | tf_op jit(solution)/shard_map/ppermute | solution.py:12
  245.4 53.3 %collective-permute-start.38 = (bf16[512,512]{1,0:T(8,128)(2,1)S(1)}, bf16[512,512]{1,0:T(8,128)(2,1)S(1)}, u32[]{:S(2)}, u32[]{:S(2)}) collective-permute-start(bf16[512,512]{1,0:T(8,128)(2,1)S(1)} %add_convert_fusion), channel_id=1, source_target_pairs={{0,4},{4,0},{8,12},{12,8},{1,5},{5,1},{9,13},{13,9},{2,6},{6,2},{1... | collective-permute-start | bytes 1572872 | tf_op jit(solution)/shard_map/ppermute | solution.py:12
  245.5 17.9 %collective-permute-start.30 = (bf16[144,512]{1,0:T(8,128)(2,1)S(1)}, bf16[144,512]{1,0:T(8,128)(2,1)S(1)}, u32[]{:S(2)}, u32[]{:S(2)}) collective-permute-start(bf16[144,512]{1,0:T(8,128)(2,1)S(1)} %add_convert_fusion.8), channel_id=1, source_target_pairs={{0,4},{4,0},{8,12},{12,8},{1,5},{5,1},{9,13},{13,9},{2,6},{6,2},{1... | collective-permute-start | bytes 442376 | tf_op jit(solution)/shard_map/ppermute | solution.py:12
  247.7 18.0 %collective-permute-start.22 = (bf16[160,1024]{1,0:T(8,128)(2,1)S(1)}, bf16[160,1024]{1,0:T(8,128)(2,1)S(1)}, u32[]{:S(2)}, u32[]{:S(2)}) collective-permute-start(bf16[160,1024]{1,0:T(8,128)(2,1)S(1)} %add_convert_fusion.2), channel_id=1, source_target_pairs={{0,2},{1,3},{2,0},{3,1},{4,6},{5,7},{6,4},{7,5},{8,10},{9,11},{10,... | collective-permute-start | bytes 983048 | tf_op jit(solution)/shard_map/ppermute | solution.py:12
  250.6 15.1 %copy-start.34 = (f32[160]{0:T(256)S(1)}, f32[160]{0:T(256)}, u32[]{:S(2)}) copy-start(f32[160]{0:T(256)} %copy-done.33) | copy-start | bytes 1924
  250.6 15.1 %copy-start.38 = (f32[160]{0:T(256)S(1)}, f32[160]{0:T(256)}, u32[]{:S(2)}) copy-start(f32[160]{0:T(256)} %add_rsqrt_fusion.1) | copy-start | bytes 1924
  250.6 49.7 %collective-permute-start.35 = (bf16[512,512]{1,0:T(8,128)(2,1)S(1)}, bf16[512,512]{1,0:T(8,128)(2,1)}, u32[]{:S(2)}, u32[]{:S(2)}) collective-permute-start(bf16[512,512]{1,0:T(8,128)(2,1)S(1)} %add_convert_fusion.1), channel_id=1, source_target_pairs={{0,4},{4,0},{8,12},{12,8},{1,5},{5,1},{9,13},{13,9},{2,6},{6,2},{1... | collective-permute-start | bytes 1572872 | tf_op jit(solution)/shard_map/ppermute | solution.py:12
  (37 other events, 228.4 us)

commit v2 on v1

v2 whole, which is shorter than its diff:
```python
import jax
import jax.numpy as jnp
from jax import lax
from jax.experimental import pallas as pl
from jax.experimental.pallas import tpu as pltpu
from jax.sharding import PartitionSpec as P

EPS = 1e-06
LOW = jnp.bfloat16
WIDE = jnp.float32


def swap(block, axis, bit):
    return lax.ppermute(block, axis, [(i, i ^ bit) for i in range(lax.axis_size(axis))])


def after(value, *others):
    return lax.optimization_barrier((value, *others))[0]


def pin(value):
    return lax.optimization_barrier(value)


def dot(left, right):
    return lax.dot_general(left, right, (((1,), (0,)), ((), ())), preferred_element_type=WIDE)


def dot_rt(left, right):
    return lax.dot_general(left, right, (((1,), (1,)), ((), ())), preferred_element_type=WIDE)


def dot_lt(left, right):
    return lax.dot_general(left, right, (((0,), (0,)), ((), ())), preferred_element_type=WIDE)


def segments(value, count):
    size = value.shape[1] // count
    return [value[:, i * size : (i + 1) * size] for i in range(count)]


def from_width(value, parts):
    return sum(dot(s, p) for s, p in zip(segments(value, len(parts)), parts))


def to_width(value, parts):
    return jnp.concatenate([dot(value, p) for p in parts], 1)


def from_width_rt(value, parts):
    return sum(dot_rt(s, p) for s, p in zip(segments(value, len(parts)), parts))


def to_width_rt(value, parts):
    return jnp.concatenate([dot_rt(value, p) for p in parts], 1)


def stats(values):
    center = values - jnp.mean(values, -1, keepdims=True)
    return center, lax.rsqrt(jnp.mean(center * center, -1, keepdims=True) + EPS)


def norm_back(xhat, spread, gain, upstream):
    z = upstream * gain
    mean_z = jnp.mean(z, -1, keepdims=True)
    mean_zx = jnp.mean(z * xhat, -1, keepdims=True)
    return (
        spread * (z - mean_z - xhat * mean_zx),
        jnp.sum(upstream * xhat, 0),
        jnp.sum(upstream, 0),
    )


def sum_tensor_rows(value):
    rows = value.shape[0] // 2
    value = pin(value)
    value = value[:rows].astype(WIDE) + swap(value[rows:], "tensor", 1).astype(WIDE)
    bit = 2
    while bit < lax.axis_size("tensor"):
        value = pin(value.astype(LOW))
        value = value.astype(WIDE) + swap(value, "tensor", bit).astype(WIDE)
        bit *= 2
    return value


def gather_rows(piece, size):
    mine = [piece] + [swap(piece, "context", k) for k in range(1, lax.axis_size("context"))]
    rows = piece.shape[0]
    theirs = swap(jnp.concatenate(mine, 0), "tensor", 1)
    blocks = []
    for k, own in enumerate(mine):
        blocks += [own, theirs[k * rows : (k + 1) * rows]]
    return jnp.concatenate([b[:size] for b in blocks], 0), [b[size:] for b in blocks]


def params(limit_mb=48):
    return pltpu.CompilerParams(vmem_limit_bytes=limit_mb << 20)


def pack_kernel(query, key, value, *rest):
    vectors, (qbias, vbias, ebias), out, lines, work = rest[:6], rest[6:9], rest[9], rest[10], rest[11]
    share, columns = query.shape
    for n, ref in enumerate((query, key, value)):
        out[:share, n * columns : (n + 1) * columns] = ref[...]
    work[...] = jnp.zeros_like(work)
    for n, ref in enumerate(vectors):
        work[n : n + 1, :share] = ref[...].reshape(1, share).astype(WIDE)
    mine = lax.axis_index("fsdp")

    def placed(ref, total):
        size = ref.shape[0]
        row = lax.broadcasted_iota(jnp.int32, (size, total), 0)
        column = lax.broadcasted_iota(jnp.int32, (size, total), 1)
        return dot_lt(ref[...], (column == row + mine * size).astype(LOW))

    heads, units = qbias.shape[1], ebias.shape[1]
    ways = lax.axis_size("fsdp")
    work[8 : 8 + heads, 0 : qbias.shape[0] * ways] = placed(qbias, qbias.shape[0] * ways)
    work[8 : 8 + heads, 128 : 128 + vbias.shape[0] * ways] = placed(vbias, vbias.shape[0] * ways)
    work[8 : 8 + units, 256 : 256 + ebias.shape[0] * ways] = placed(ebias, ebias.shape[0] * ways)
    lines[...] = work[...]
    out[share:, :] = work[...].astype(LOW)


def pack(query, key, value, vectors, biases):
    share, columns = query.shape
    return pl.pallas_call(
        pack_kernel,
        out_shape=(
            jax.ShapeDtypeStruct((share + 16, 3 * columns), LOW),
            jax.ShapeDtypeStruct((16, 3 * columns), WIDE),
        ),
        scratch_shapes=[pltpu.VMEM((16, 3 * columns), WIDE)],
        compiler_params=params(),
    )(query, key, value, *vectors, *biases)


def head_mask(shape, head, head_dim):
    lane = lax.broadcasted_iota(jnp.int32, shape, 1)
    return (lane >= head * head_dim) & (lane < (head + 1) * head_dim)


def attend_kernel(heads, head_dim, start, rows, qkv, bias, out):
    features = heads * head_dim
    q = qkv[start : start + rows, :features]
    k = qkv[:, features : 2 * features]
    v = qkv[:, 2 * features :]
    scale = head_dim**-0.5
    total = jnp.zeros((rows, features), WIDE)
    for h in range(heads):
        mine = head_mask(q.shape, h, head_dim)
        scores = dot_rt(jnp.where(mine, q, jnp.zeros_like(q)), k) * scale + bias[...]
        top = jnp.max(scores, -1, keepdims=True)
        raw = jnp.exp(scores - top)
        low = jnp.sum(raw, -1, keepdims=True)
        got = dot(raw.astype(LOW), v) / low
        total = jnp.where(mine, got, total)
    out[...] = total.astype(LOW)


def attend(qkv, bias, heads, head_dim, start, rows):
    features = heads * head_dim
    length = qkv.shape[0]
    return pl.pallas_call(
        lambda *refs: attend_kernel(heads, head_dim, start, rows, *refs),
        out_shape=jax.ShapeDtypeStruct((rows, features), LOW),
        compiler_params=params(),
        cost_estimate=pl.CostEstimate(
            flops=4 * rows * length * features,
            bytes_accessed=qkv.size * 2 + rows * features * 2,
            transcendentals=rows * length * heads,
        ),
    )(qkv, bias)


def attend_back_kernel(heads, head_dim, qkv, bias, grad, out):
    features = heads * head_dim
    q = qkv[:, :features]
    k = qkv[:, features : 2 * features]
    v = qkv[:, 2 * features :]
    g = grad[...]
    scale = head_dim**-0.5
    zero = jnp.zeros_like(q)
    shape = q.shape
    totals = [jnp.zeros(shape, WIDE) for _ in range(3)]
    for h in range(heads):
        mine = head_mask(shape, h, head_dim)
        qm = jnp.where(mine, q, zero)
        gm = jnp.where(mine, g, zero)
        scores = dot_rt(k, qm) * scale + bias[...]
        raw = jnp.exp(scores - jnp.max(scores, 0, keepdims=True))
        weights = raw * (1.0 / jnp.sum(raw, 0, keepdims=True))
        grad_probs = dot_rt(v, gm)
        delta = jnp.sum(weights * grad_probs, 0, keepdims=True)
        grad_scores = (weights * (grad_probs - delta)).astype(LOW)
        totals[0] = jnp.where(mine, dot_lt(grad_scores, k) * scale, totals[0])
        totals[1] = jnp.where(mine, dot(grad_scores, q) * scale, totals[1])
        totals[2] = jnp.where(mine, dot(weights.astype(LOW), g), totals[2])
    for n in range(3):
        out[:, n * features : (n + 1) * features] = totals[n].astype(LOW)


def attend_back(qkv, bias, grad, heads, head_dim):
    length, columns = qkv.shape
    return pl.pallas_call(
        lambda *refs: attend_back_kernel(heads, head_dim, *refs),
        out_shape=jax.ShapeDtypeStruct((length, columns), LOW),
        compiler_params=params(),
        cost_estimate=pl.CostEstimate(
            flops=10 * length * length * heads * head_dim,
            bytes_accessed=qkv.size * 4 + grad.size * 2,
            transcendentals=length * length * heads,
        ),
    )(qkv, bias, grad)


def on_device(
    tokens,
    cotangent,
    valid_count,
    gain_first,
    shift_first,
    query_weight,
    query_bias,
    key_weight,
    value_weight,
    value_bias,
    output_weight,
    output_bias,
    gain_second,
    shift_second,
    expand_weight,
    expand_bias,
    reduce_weight,
    reduce_bias,
):
    images, seq, width = tokens.shape
    ways = lax.axis_size("fsdp")
    pair = ways == 2
    cycle = lax.axis_size("context")
    mine = lax.axis_index("fsdp")
    place = lax.axis_index("context")
    core = lax.axis_index("tensor") & 1
    share = gain_first.shape[0]
    heads = query_bias.shape[1]
    head_dim = query_bias.shape[0] * ways
    features = heads * head_dim
    half = seq // 2
    second = mine == 1

    def turned(value):
        if not pair:
            return value
        low, high = jnp.split(value, 2, -1)
        return jnp.where(second, jnp.concatenate([high, low], -1), value)

    def own_piece(value):
        return turned(lax.dynamic_slice_in_dim(value.reshape(seq, width), core * half, half, 0))

    token_piece = own_piece(tokens)
    cot_piece = own_piece(cotangent)
    vectors = (gain_first, shift_first, output_bias, gain_second, shift_second, reduce_bias)
    biases = (query_bias, value_bias, expand_bias)

    every, _ = gather_rows(token_piece, half)
    if pair:
        message, lines = pack(query_weight, key_weight, value_weight, vectors, biases)
        first = swap(message, "fsdp", 1)
        qkv_parts = (message[:share], first[:share])
        their_lines = first[share:].astype(WIDE)
        gain_one, shift_one, outb, gain_two, shift_two, reduceb = (
            jnp.concatenate([lines[n : n + 1, :share], their_lines[n : n + 1, :share]], 1)
            for n in range(6)
        )
        both = lines[8:] + their_lines[8:]
        qbias = both[:heads, :head_dim].reshape(1, -1)
        vbias = both[:heads, 128 : 128 + head_dim].reshape(1, -1)
        units_each = expand_bias.shape[0] * ways
        ebias = both[: expand_bias.shape[1], 256 : 256 + units_each].reshape(1, -1)
    else:
        gather = lambda v, axis=0: lax.all_gather(v, "fsdp", axis=axis, tiled=True)
        qkv_parts = (gather(jnp.concatenate([query_weight, key_weight, value_weight], 1)),)
        gain_one, shift_one, outb, gain_two, shift_two, reduceb = (
            gather(v).astype(WIDE).reshape(1, -1) for v in vectors
        )
        qbias, vbias, ebias = (gather(v).astype(WIDE).T.reshape(1, -1) for v in biases)

    center, spread = stats(every.astype(WIDE))
    xhat_all = center * spread
    normed_all = (xhat_all * gain_one + shift_one).astype(LOW)
    qkv_bias = jnp.concatenate([qbias, jnp.zeros_like(qbias), vbias], 1)
    qkv = (from_width(normed_all, qkv_parts) + qkv_bias).astype(LOW)
    steps = jnp.arange(half, dtype=jnp.int32)
    positions = jnp.concatenate(
        [(place ^ k) * seq + (core ^ j) * half + steps for k in range(cycle) for j in range(2)]
    )
    bias = jnp.where(positions < valid_count[0], 0.0, -1e30).astype(WIDE)
    context_own = attend(qkv, bias[None, :], heads, head_dim, 0, seq)

    if pair:
        output_parts = (output_weight, swap(after(output_weight, first), "fsdp", 1))
        expand_parts = (expand_weight, swap(after(expand_weight, first), "fsdp", 1))
        reduce_parts = (reduce_weight, swap(after(reduce_weight, context_own), "fsdp", 1))
    else:
        output_parts = (gather(output_weight, 1),)
        expand_parts = (gather(expand_weight),)
        reduce_parts = (gather(reduce_weight, 1),)

    branch = sum_tensor_rows(to_width(context_own, output_parts).astype(LOW)) + outb
    hidden = token_piece.astype(WIDE) + branch
    center_two, spread_two = stats(hidden)
    xhat_two = center_two * spread_two
    normed_piece = (xhat_two * gain_two + shift_two).astype(LOW)

    cot_all, _ = gather_rows(after(cot_piece, every), half)
    normed_two, _ = gather_rows(normed_piece, half)
    expanded = from_width(normed_two, expand_parts) + ebias
    cdf = 0.5 * (1.0 + lax.erf(expanded * (2.0**-0.5)))
    activated = (expanded * cdf).astype(LOW)
    slope = cdf + expanded * jnp.exp(-0.5 * expanded * expanded) * 0.3989422804014327
    grad_expanded = (from_width_rt(cot_all, reduce_parts) * slope).astype(LOW)
    grad_normed_two = sum_tensor_rows(to_width_rt(grad_expanded[:seq], expand_parts).astype(LOW))

    def scatter(value, axis):
        return lax.psum_scatter(value.astype(LOW), "fsdp", scatter_dimension=axis, tiled=True)

    def weight_grad(left, right, along):
        if not pair:
            return scatter(dot_lt(left, right), along).astype(WIDE)
        if along:
            own, other = segments(right, 2)
            away = dot_lt(left, other).astype(LOW)
            return dot_lt(left, own) + swap(away, "fsdp", 1).astype(WIDE)
        own, other = segments(left, 2)
        away = dot_lt(other, right).astype(LOW)
        return dot_lt(own, right) + swap(away, "fsdp", 1).astype(WIDE)

    grad_reduce = weight_grad(activated, cot_all, 1)
    grad_expand = weight_grad(normed_two, grad_expanded, 0)

    upstream = cot_piece.astype(WIDE)
    grad_hidden, gain_two_sum, shift_two_sum = norm_back(
        xhat_two, spread_two, gain_two, grad_normed_two
    )
    grad_hidden = grad_hidden + upstream
    tail = jnp.stack([gain_two_sum, shift_two_sum] + [jnp.zeros_like(gain_two_sum)] * 14)
    grad_branch, tails = gather_rows(
        jnp.concatenate([grad_hidden, tail], 0).astype(LOW), half
    )
    norm_sums = sum(t[:2].astype(WIDE) for t in tails)
    grad_context = from_width_rt(grad_branch, output_parts).astype(LOW)
    grad_qkv = attend_back(qkv, bias[:, None], grad_context, heads, head_dim)

    grad_normed_one = sum_tensor_rows(to_width_rt(grad_qkv[:seq], qkv_parts).astype(LOW))
    center_one, spread_one = stats(token_piece.astype(WIDE))
    grad_inputs, _, _ = norm_back(center_one * spread_one, spread_one, gain_one, grad_normed_one)

    def both_cores(value):
        theirs = swap(value, "tensor", 1)
        upper = core == 1
        return turned(
            jnp.concatenate([jnp.where(upper, theirs, value), jnp.where(upper, value, theirs)], 0)
        ).reshape(tokens.shape)

    grad_tokens = both_cores(grad_inputs + grad_hidden)

    reduced = sum_tensor_rows(
        to_width(after(activated[:seq], grad_branch), reduce_parts).astype(LOW)
    )
    output = both_cores((hidden + reduced + reduceb).astype(LOW))

    def own_rows(value):
        size = value.shape[0] // ways
        return lax.dynamic_slice_in_dim(value, mine * size, size, 0)

    context_rest = attend(
        after(qkv, branch), bias[None, :], heads, head_dim, seq, (cycle - 1) * seq
    )
    context_all = jnp.concatenate([context_own, context_rest], 0)
    sums = jnp.concatenate(
        [
            jnp.sum(grad_branch.astype(WIDE), 0, keepdims=True),
            norm_sums,
            jnp.sum(cot_all.astype(WIDE), 0, keepdims=True),
        ],
        0,
    )
    unit_sum = jnp.sum(grad_expanded.astype(WIDE), 0).reshape(-1, share)
    if pair:
        branch_own, branch_other = segments(grad_branch, 2)
        sums_own, sums_other = segments(sums, 2)
        filler = jnp.zeros((-(features + 4 + unit_sum.shape[0]) % 16, share), WIDE)
        own = jnp.concatenate([dot_lt(context_all, branch_own), sums_own, unit_sum, filler], 0)
        away = jnp.concatenate(
            [dot_lt(context_all, branch_other), sums_other, unit_sum, filler], 0
        )
        own = own + swap(away.astype(LOW), "fsdp", 1).astype(WIDE)
        grad_output, sums, unit_sum = (
            own[:features],
            own[features : features + 4],
            own[features + 4 : features + 4 + unit_sum.shape[0]],
        )
    else:
        grad_output = scatter(dot_lt(context_all, grad_branch), 1).astype(WIDE)
        sums = scatter(sums, 1).astype(WIDE)
        unit_sum = lax.psum(unit_sum, "fsdp")
    grad_ebias = own_rows(unit_sum.reshape(-1, expand_bias.shape[0] * ways).T)

    head_sum = jnp.sum(grad_qkv.astype(WIDE), 0, keepdims=True)
    grad_all = to_width_rt(grad_qkv, qkv_parts)
    first_sums = jnp.stack([jnp.sum(grad_all * xhat_all, 0), jnp.sum(grad_all, 0)])
    if pair:
        columns = 3 * features
        own_side, other_side = segments(first_sums, 2)
        wide = lambda v: jnp.pad(v, ((0, 0), (0, columns - share)))
        filler = jnp.zeros((13, columns), WIDE)
        normed_own, normed_other = segments(normed_all, 2)
        own = jnp.concatenate([dot_lt(normed_own, grad_qkv), head_sum, wide(own_side), filler], 0)
        away = jnp.concatenate(
            [dot_lt(normed_other, grad_qkv), head_sum, wide(other_side), filler], 0
        )
        own = own + swap(away.astype(LOW), "fsdp", 1).astype(WIDE)
        grad_weights, head_sum = own[:share], own[share]
        first_sums = own[share + 1 : share + 3, :share]
    else:
        grad_weights = scatter(dot_lt(normed_all, grad_qkv), 0).astype(WIDE)
        head_sum = lax.psum(head_sum, "fsdp")[0]
        first_sums = scatter(first_sums, 1).astype(WIDE)
    bit = 1
    while bit < lax.axis_size("tensor"):
        first_sums = first_sums + swap(first_sums, "tensor", bit)
        bit *= 2
    grad_query, grad_key, grad_value = (
        grad_weights[:, n * features : (n + 1) * features] for n in range(3)
    )
    grad_qbias, grad_vbias = (
        own_rows(head_sum[n * features : (n + 1) * features].reshape(heads, head_dim).T)
        for n in (0, 2)
    )
    return (
        output,
        grad_tokens,
        first_sums[0],
        first_sums[1],
        grad_query,
        grad_qbias,
        grad_key,
        grad_value,
        grad_vbias,
        grad_output,
        sums[0],
        sums[1],
        sums[2],
        grad_expand,
        grad_ebias,
        grad_reduce,
        sums[3],
    )


def solution(mesh):
    rows = P("fsdp", "context", None)
    vector = P("fsdp")
    split = P("fsdp", "tensor")
    turned = P("tensor", "fsdp")
    in_specs = (rows, rows, vector, vector, vector, split, split, split, split, split)
    in_specs += (turned, vector, vector, vector, split, split, turned, vector)
    out_specs = (rows, rows, vector, vector, split, split, split, split, split)
    out_specs += (turned, vector, vector, vector, split, split, turned, vector)
    return jax.shard_map(
        on_device, mesh=mesh, in_specs=in_specs, out_specs=out_specs, check_vma=False
    )
```

time: 304 us -> 234 us (0.77)
  waiting for transfers between devices: 121 us -> 86.3 us
  blocking collectives: 30.4 us -> 0 us
  other arithmetic: 33.5 us -> 18.3 us
  Pallas kernels: 0 us -> 12 us
  starting transfers between devices: 43.7 us -> 39.7 us
    ppermute x39 -> x36, waiting for transfers between devices: 121 us -> 86.3 us  [swap(): lax.ppermute(block, axis, [(i, i ^ bit) for i in range(lax.axis_size(axis...]
    all_gather x1 -> x0, blocking collectives: 30.4 us -> none  [on_device(): lax.all_gather(last.astype(LOW), ('fsdp', 'context')).astype(WIDE)]
    convert_element_type x23 -> x6, other arithmetic: 13.6 us -> 0.99 us  [the longest x1 0.74 us: on_device(): their_lines = first[share:].astype(WIDE)]
    pallas_call x0 -> x4, Pallas kernels: none -> 12 us  [the longest x1 7.59 us: attend_back(): pl.pallas_call(lambda *refs: attend_back_kernel(heads, head_dim, *refs),...]
    concatenate x6 -> x16, local copies, waits for them, and re-layouts: 5.84 us -> 13.3 us  [the longest x1 6.67 us: gather_rows(): theirs = swap(jnp.concatenate(mine, 0), 'tensor', 1)]
    slice x33 -> x15, local copies, waits for them, and re-layouts: 9.98 us -> 4.87 us  [the longest x1 1.17 us: on_device(): grad_weights[:, n * features:(n + 1) * features]]
    ppermute x39 -> x36, starting transfers between devices: 43.7 us -> 39.7 us  [swap(): lax.ppermute(block, axis, [(i, i ^ bit) for i in range(lax.axis_size(axis...]
    unnamed x120 -> x123, local copies, waits for them, and re-layouts: 14.1 us -> 18 us
  transfers between devices with their start and end apart: 39 -> 36, of which waited for: 17 -> 13; matrix products, arithmetic and copies ran while one was open for 33% -> 25% of each run, Pallas kernels for 0% -> 2%
where the time goes in v2:
time: 234 us; the launch traced here: 231 us
  waiting for transfers between devices  86.3 us (37%)
  local copies, waits for them, and re-layouts  40.5 us (17%)
  starting transfers between devices  39.7 us (17%)
  matrix products  31.3 us (13%)
  other arithmetic  18.3 us (8%)
  Pallas kernels  12 us (5%)
  between operations  2.71 us (1%)
    ppermute x36, waiting for transfers between devices, swap(): lax.ppermute(block, axis, [(i, i ^ bit) for i in range(lax.axis_size(axis...  86.3 us
    ppermute x36, starting transfers between devices, swap(): lax.ppermute(block, axis, [(i, i ^ bit) for i in range(lax.axis_size(axis...  39.7 us
    unnamed x123, local copies, waits for them, and re-layouts  18 us
    dot_general x8, matrix products, dot_lt(): lax.dot_general(left, right, (((0,), (0,)), ((), ())), preferred_element_...  15.6 us
    dot_general x10, matrix products, dot_rt(): lax.dot_general(left, right, (((1,), (1,)), ((), ())), preferred_element_...  9.6 us
    pallas_call x1, Pallas kernels, attend_back(): pl.pallas_call(lambda *refs: attend_back_kernel(heads, head_dim, *refs),...  7.59 us
    concatenate x1, local copies, waits for them, and re-layouts, gather_rows(): theirs = swap(jnp.concatenate(mine, 0), 'tensor', 1)  6.67 us
    dot_general x8, matrix products, dot(): lax.dot_general(left, right, (((1,), (0,)), ((), ())), preferred_element_...  6.11 us
  transfers between devices with their start and end apart: 36, of which 13 were waited for; matrix products, arithmetic and copies ran while one was open for 25% of the time, Pallas kernels for 2%

profile of v2, /device:TPU:0, one launch (start us, length us, event | category | flops | bytes accessed | tf_op | source)
XLA Modules:
  0.0 230.9 jit_solution(11486805072363114542)
XLA Ops:
  0.7 1.0 dynamic-slice_bitcast_fusion.1
  1.7 1.1 convert_reduce_fusion.5
  2.8 5.1 %collective-permute-start.2 = (bf16[80,1024]{1,0:T(8,128)(2,1)S(1)}, bf16[80,1024]{1,0:T(8,128)(2,1)S(1)}, u32[]{:S(2)}, u32[]{:S(2)}) collective-permute-start(bf16[80,1024]{1,0:T(8,128)(2,1)S(1)} %get-tuple-element.44), channel_id=1, source_target_pairs={{0,12},{4,8},{8,4},{12,0},{1,13},{5,9},{9,5},{13,1},{2,14},{6,10},... | collective-permute-start | bytes 491528 | tf_op jit(solution)/shard_map/ppermute | solution.py:14
  15.2 1.6 collective-permute-start.4
  23.8 10.7 %collective-permute-done.4 = bf16[528,768]{1,0:T(8,128)(2,1)} collective-permute-done((bf16[528,768]{1,0:T(8,128)(2,1)S(1)}, bf16[528,768]{1,0:T(8,128)(2,1)}, u32[]{:S(2)}, u32[]{:S(2)}) %collective-permute-start.4) | collective-permute-done | bytes 811040 | tf_op jit(solution)/shard_map/ppermute | solution.py:14
  35.5 1.5 collective-permute-start.5
  43.4 2.3 fusion.23
  46.4 1.7 shard_map.306
  49.4 3.5 %collective-permute-start.15 = (bf16[80,1024]{1,0:T(8,128)(2,1)S(1)}, bf16[80,1024]{1,0:T(8,128)(2,1)S(1)}, u32[]{:S(2)}, u32[]{:S(2)}) collective-permute-start(bf16[80,1024]{1,0:T(8,128)(2,1)S(1)} %maximum_select_fusion.3), channel_id=1, source_target_pairs={{0,12},{4,8},{8,4},{12,0},{1,13},{5,9},{9,5},{13,1},{2,14},{6,10},... | collective-permute-start | bytes 491528 | tf_op jit(solution)/shard_map/ppermute | solution.py:14
  53.9 1.6 collective-permute-start.7
  55.5 2.9 %collective-permute-done.15 = bf16[80,1024]{1,0:T(8,128)(2,1)S(1)} collective-permute-done((bf16[80,1024]{1,0:T(8,128)(2,1)S(1)}, bf16[80,1024]{1,0:T(8,128)(2,1)S(1)}, u32[]{:S(2)}, u32[]{:S(2)}) %collective-permute-start.15) | collective-permute-done | bytes 163872 | tf_op jit(solution)/shard_map/ppermute | solution.py:14
  58.4 8.7 %collective-permute-done.14 = bf16[80,1024]{1,0:T(8,128)(2,1)S(1)} collective-permute-done((bf16[80,1024]{1,0:T(8,128)(2,1)S(1)}, bf16[80,1024]{1,0:T(8,128)(2,1)S(1)}, u32[]{:S(2)}, u32[]{:S(2)}) %collective-permute-start.14) | collective-permute-done | bytes 163872 | tf_op jit(solution)/shard_map/ppermute | solution.py:14
  68.3 2.4 %collective-permute-start.10 = (bf16[80,1024]{1,0:T(8,128)(2,1)S(1)}, bf16[80,1024]{1,0:T(8,128)(2,1)S(1)}, u32[]{:S(2)}, u32[]{:S(2)}) collective-permute-start(bf16[80,1024]{1,0:T(8,128)(2,1)S(1)} %get-tuple-element.49), channel_id=1, source_target_pairs={{0,12},{4,8},{8,4},{12,0},{1,13},{5,9},{9,5},{13,1},{2,14},{6,10},... | collective-permute-start | bytes 491528 | tf_op jit(solution)/shard_map/ppermute | solution.py:14
  70.7 2.0 collective-permute-start.8
  73.4 2.5 %shard_map.308 = bf16[480,256]{1,0:T(8,128)(2,1)S(1)} custom-call(bf16[640,768]{1,0:T(8,128)(2,1)S(1)} %add_convert_fusion.refs_0_, f32[1,640]{1,0:T(1,128)S(1)} %compare_select_fusion.refs_1_), custom_call_target="tpu_custom_call" | custom-call | flops 314572800 | bytes 1228800 | tf_op jit(solution)/shard_map/pallas_call | solution.py:164
  75.9 1.4 collective-permute-done.10
  77.3 1.5 collective-permute-start.17
  78.8 5.7 %collective-permute-done.9 = bf16[80,1024]{1,0:T(8,128)(2,1)S(1)} collective-permute-done((bf16[80,1024]{1,0:T(8,128)(2,1)S(1)}, bf16[80,1024]{1,0:T(8,128)(2,1)S(1)}, u32[]{:S(2)}, u32[]{:S(2)}) %collective-permute-start.9) | collective-permute-done | bytes 163872 | tf_op jit(solution)/shard_map/ppermute | solution.py:14
  84.8 16.8 %collective-permute-done.17 = bf16[1024,512]{1,0:T(8,128)(2,1)S(1)} collective-permute-done((bf16[1024,512]{1,0:T(8,128)(2,1)S(1)}, bf16[1024,512]{1,0:T(8,128)(2,1)S(1)}, u32[]{:S(2)}, u32[]{:S(2)}) %collective-permute-start.17) | collective-permute-done | bytes 1048608 | tf_op jit(solution)/shard_map/ppermute | solution.py:14
  103.6 1.2 multiply_convert_fusion
  104.9 2.5 %convert_reduce_fusion.1 = (f32[1024]{0:T(1024)}, bf16[640,1024]{1,0:T(8,128)(2,1)S(1)}) fusion(f32[640,1024]{1,0:T(8,128)S(1)} %get-tuple-element.90, f32[640,1024]{1,0:T(8,128)S(1)} %fusion.39, bf16[1024,512]{1,0:T(8,128)(2,1)S(1)} %copy-done.26, bf16[640,1024]{1,0:T(8,128)(2,1)S(1)} %slice_dynamic-update-slice_fusion.7), kind=kOutput, calls=%fused_computation.18 | convolution fusion | flops 679607296 | bytes 8261632 | tf_op jit(solution)/shard_map/dot_general | solution.py:30
  108.5 2.0 convolution_convert_fusion.1
  110.5 1.5 collective-permute-start.34
  112.0 1.6 collective-permute-start.19
  113.6 2.0 convolution_convert_fusion
  116.1 2.3 collective-permute-done.19
  119.7 2.0 concatenate.246
  121.6 4.4 %collective-permute-start.20 = (bf16[96,1024]{1,0:T(8,128)(2,1)}, bf16[96,1024]{1,0:T(8,128)(2,1)}, u32[]{:S(2)}, u32[]{:S(2)}) collective-permute-start(bf16[96,1024]{1,0:T(8,128)(2,1)} %concatenate.246), channel_id=1, source_target_pairs={{0,4},{4,0},{8,12},{12,8},{1,5},{5,1},{9,13},{13,9},{2,6},{6,2},{1... | collective-permute-start | bytes 589832 | tf_op jit(solution)/shard_map/ppermute | solution.py:14
  126.1 2.4 %collective-permute-start.22 = (bf16[96,1024]{1,0:T(8,128)(2,1)}, bf16[96,1024]{1,0:T(8,128)(2,1)}, u32[]{:S(2)}, u32[]{:S(2)}) collective-permute-start(bf16[96,1024]{1,0:T(8,128)(2,1)} %concatenate.246), channel_id=1, source_target_pairs={{0,12},{4,8},{8,4},{12,0},{1,13},{5,9},{9,5},{13,1},{2,14},{6,10},... | collective-permute-start | bytes 589832 | tf_op jit(solution)/shard_map/ppermute | solution.py:14
  128.4 1.2 add_rsqrt_fusion.1
  129.6 2.1 collective-permute-done.20
  131.7 9.9 %collective-permute-done.21 = bf16[96,1024]{1,0:T(8,128)(2,1)} collective-permute-done((bf16[96,1024]{1,0:T(8,128)(2,1)}, bf16[96,1024]{1,0:T(8,128)(2,1)}, u32[]{:S(2)}, u32[]{:S(2)}) %collective-permute-start.21) | collective-permute-done | bytes 196640 | tf_op jit(solution)/shard_map/ppermute | solution.py:14
  141.6 6.7 %concatenate.247 = bf16[384,1024]{1,0:T(8,128)(2,1)} concatenate(bf16[80,1024]{1,0:T(8,128)(2,1)S(1)} %get-tuple-element.46, bf16[1,1024]{1,0:T(2,128)(2,1)S(1)} %stack.17, bf16[1,1024]{1,0:T(2,128)(2,1)S(1)} %stack.18, bf16[2,1024]{1,0:T(2,128)(2,1)S(1)} %concatenate.243, bf16[4,1024]{1,0:T(4,128)(2,1)S(1)} %concatenate.244, bf16[8,1024]{1,0:T(8,128)(2,1)S(1)} %concatenate.245, ...), dimensions={0} | concatenate | bytes 1572864 | tf_op jit(solution)/shard_map/concatenate | solution.py:89
  148.3 2.1 convert_reduce_fusion.2
  152.1 4.3 %convert_add_fusion.1 = f32[512,1024]{1,0:T(8,128)} fusion(bf16[512,1024]{1,0:T(8,128)(2,1)} %collective-permute-done.34, bf16[640,1024]{1,0:T(8,128)(2,1)} %copy-done.32, bf16[640,1024]{1,0:T(8,128)(2,1)} %copy-done.24), kind=kOutput, calls=%fused_computation.28 | convolution fusion | flops 672137216 | bytes 5111808 | tf_op jit(solution)/shard_map/dot_general | solution.py:34
  156.4 2.4 %collective-permute-done.35 = bf16[1024,512]{1,0:T(8,128)(2,1)} collective-permute-done((bf16[1024,512]{1,0:T(8,128)(2,1)}, bf16[1024,512]{1,0:T(8,128)(2,1)}, u32[]{:S(2)}, u32[]{:S(2)}) %collective-permute-start.35) | collective-permute-done | bytes 1048608 | tf_op jit(solution)/shard_map/ppermute | solution.py:14
  158.8 3.6 %convert_add_fusion = f32[1024,512]{1,0:T(8,128)} fusion(bf16[1024,512]{1,0:T(8,128)(2,1)} %collective-permute-done.35, bf16[640,1024]{1,0:T(8,128)(2,1)S(1)} %copy-done.23, bf16[640,1024]{1,0:T(8,128)(2,1)S(1)} %copy-done.21), kind=kOutput, calls=%fused_computation.27 | convolution fusion | flops 672137216 | bytes 5111808 | tf_op jit(solution)/shard_map/dot_general | solution.py:34
  169.7 7.6 %shard_map.307 = bf16[640,768]{1,0:T(8,128)(2,1)S(1)} custom-call(bf16[640,768]{1,0:T(8,128)(2,1)S(1)} %add_convert_fusion.refs_0_, f32[640,1]{1,0:T(8,128)S(1)} %broadcast_select_fusion.refs_1_, bf16[640,256]{1,0:T(8,128)(2,1)S(1)} %fusion.17.refs_2_), custom_call_target="tpu_custom_call" | custom-call | flops 1048576000 | bytes 2293760 | tf_op jit(solution)/shard_map/pallas_call | solution.py:205
  179.1 2.0 fusion.50
  185.3 1.5 convolution_convert_fusion.4
  187.4 1.8 fusion.20
  190.2 1.5 collective-permute-start.30
  192.5 1.6 collective-permute-start.25
  194.8 21.5 %collective-permute-done.33 = bf16[272,512]{1,0:T(8,128)(2,1)S(1)} collective-permute-done((bf16[272,512]{1,0:T(8,128)(2,1)S(1)}, bf16[272,512]{1,0:T(8,128)(2,1)S(1)}, u32[]{:S(2)}, u32[]{:S(2)}) %collective-permute-start.33) | collective-permute-done | bytes 278560 | tf_op jit(solution)/shard_map/ppermute | solution.py:14
  222.7 1.4 maximum_add_fusion
  224.2 1.2 fusion.100
  226.6 1.6 collective-permute-start.32
  228.8 1.4 collective-permute-done.32
  (308 shorter events, 56.8 us)
Async XLA Ops:
  0.7 10.3 %copy-start = (bf16[512,256]{1,0:T(8,128)(2,1)S(1)}, bf16[512,256]{1,0:T(8,128)(2,1)}, u32[]{:S(2)}) copy-start(bf16[512,256]{1,0:T(8,128)(2,1)} %query.1) | copy-start | bytes 786436
  0.7 17.5 %copy-start.31 = (bf16[1,160,1024]{2,1,0:T(8,128)(2,1)S(1)}, bf16[1,160,1024]{2,1,0:T(8,128)(2,1)}, u32[]{:S(2)}) copy-start(bf16[1,160,1024]{2,1,0:T(8,128)(2,1)} %param.19) | copy-start | bytes 983044
  2.8 20.1 %copy-start.13 = (bf16[80,1024]{1,0:T(8,128)(2,1)}, bf16[80,1024]{1,0:T(8,128)(2,1)S(1)}, u32[]{:S(2)}) copy-start(bf16[80,1024]{1,0:T(8,128)(2,1)S(1)} %get-tuple-element.44) | copy-start | bytes 491524
  2.8 20.1 %collective-permute-start.2 = (bf16[80,1024]{1,0:T(8,128)(2,1)S(1)}, bf16[80,1024]{1,0:T(8,128)(2,1)S(1)}, u32[]{:S(2)}, u32[]{:S(2)}) collective-permute-start(bf16[80,1024]{1,0:T(8,128)(2,1)S(1)} %get-tuple-element.44), channel_id=1, source_target_pairs={{0,12},{4,8},{8,4},{12,0},{1,13},{5,9},{9,5},{13,1},{2,14},{6,10},... | collective-permute-start | bytes 491528 | tf_op jit(solution)/shard_map/ppermute | solution.py:14
  7.9 15.0 %collective-permute-start.1 = (bf16[80,1024]{1,0:T(8,128)(2,1)S(1)}, bf16[80,1024]{1,0:T(8,128)(2,1)S(1)}, u32[]{:S(2)}, u32[]{:S(2)}) collective-permute-start(bf16[80,1024]{1,0:T(8,128)(2,1)S(1)} %get-tuple-element.44), channel_id=1, source_target_pairs={{0,8},{4,12},{8,0},{12,4},{1,9},{5,13},{9,1},{13,5},{2,10},{6,14},... | collective-permute-start | bytes 491528 | tf_op jit(solution)/shard_map/ppermute | solution.py:14
  8.0 15.0 %collective-permute-start = (bf16[80,1024]{1,0:T(8,128)(2,1)S(1)}, bf16[80,1024]{1,0:T(8,128)(2,1)S(1)}, u32[]{:S(2)}, u32[]{:S(2)}) collective-permute-start(bf16[80,1024]{1,0:T(8,128)(2,1)S(1)} %get-tuple-element.44), channel_id=1, source_target_pairs={{0,4},{4,0},{8,12},{12,8},{1,5},{5,1},{9,13},{13,9},{2,6},{6,2},{1... | collective-permute-start | bytes 491528 | tf_op jit(solution)/shard_map/ppermute | solution.py:14
  15.2 19.4 %collective-permute-start.4 = (bf16[528,768]{1,0:T(8,128)(2,1)S(1)}, bf16[528,768]{1,0:T(8,128)(2,1)}, u32[]{:S(2)}, u32[]{:S(2)}) collective-permute-start(bf16[528,768]{1,0:T(8,128)(2,1)S(1)} %get-tuple-element.26), channel_id=1, source_target_pairs={{0,16},{16,0},{1,17},{17,1},{2,18},{18,2},{3,19},{19,3},{4,20},{20... | collective-permute-start | bytes 2433032 | tf_op jit(solution)/shard_map/ppermute | solution.py:14
  22.9 12.5 %copy-start.30 = (bf16[80,1024]{1,0:T(8,128)(2,1)}, bf16[80,1024]{1,0:T(8,128)(2,1)S(1)}, u32[]{:S(2)}) copy-start(bf16[80,1024]{1,0:T(8,128)(2,1)S(1)} %collective-permute-done) | copy-start | bytes 491524
  23.8 13.2 %collective-permute-start.3 = (bf16[320,1024]{1,0:T(8,128)(2,1)}, bf16[320,1024]{1,0:T(8,128)(2,1)}, u32[]{:S(2)}, u32[]{:S(2)}) collective-permute-start(bf16[320,1024]{1,0:T(8,128)(2,1)} %pad_maximum_fusion.1), channel_id=1, source_target_pairs={{0,1},{1,0},{2,3},{3,2},{4,5},{5,4},{6,7},{7,6},{8,9},{9,8},{10,11... | collective-permute-start | bytes 1966088 | tf_op jit(solution)/shard_map/ppermute | solution.py:14
  35.5 12.9 %collective-permute-start.5 = (bf16[256,512]{1,0:T(8,128)(2,1)}, bf16[256,512]{1,0:T(8,128)(2,1)S(1)}, u32[]{:S(2)}, u32[]{:S(2)}) collective-permute-start(bf16[256,512]{1,0:T(8,128)(2,1)} %param.28), channel_id=1, source_target_pairs={{0,16},{16,0},{1,17},{17,1},{2,18},{18,2},{3,19},{19,3},{4,20},{20... | collective-permute-start | bytes 786440 | tf_op jit(solution)/shard_map/ppermute | solution.py:14
  48.6 18.6 %copy-start.14 = (bf16[80,1024]{1,0:T(8,128)(2,1)S(1)}, bf16[80,1024]{1,0:T(8,128)(2,1)}, u32[]{:S(2)}) copy-start(bf16[80,1024]{1,0:T(8,128)(2,1)} %copy-done.13) | copy-start | bytes 491524
  48.6 18.6 %copy-start.42 = (f32[80]{0:T(128)S(1)}, f32[80]{0:T(128)}, u32[]{:S(2)}) copy-start(f32[80]{0:T(128)} %broadcast_multiply_fusion.3) | copy-start | bytes 964
  48.7 5.2 %collective-permute-start.6 = (bf16[80,1024]{1,0:T(8,128)(2,1)S(1)}, bf16[80,1024]{1,0:T(8,128)(2,1)S(1)}, u32[]{:S(2)}, u32[]{:S(2)}) collective-permute-start(bf16[80,1024]{1,0:T(8,128)(2,1)S(1)} %slice.405), channel_id=1, source_target_pairs={{0,1},{1,0},{2,3},{3,2},{4,5},{5,4},{6,7},{7,6},{8,9},{9,8},{10,11... | collective-permute-start | bytes 491528 | tf_op jit(solution)/shard_map/ppermute | solution.py:14
  48.8 54.0 %collective-permute-start.12 = (bf16[512,1024]{1,0:T(8,128)(2,1)S(1)}, bf16[512,1024]{1,0:T(8,128)(2,1)S(1)}, u32[]{:S(2)}, u32[]{:S(2)}) collective-permute-start(bf16[512,1024]{1,0:T(8,128)(2,1)S(1)} %copy-done.17), channel_id=1, source_target_pairs={{0,16},{16,0},{1,17},{17,1},{2,18},{18,2},{3,19},{19,3},{4,20},{20... | collective-permute-start | bytes 3145736 | tf_op jit(solution)/shard_map/ppermute | solution.py:14
  49.4 9.0 %collective-permute-start.15 = (bf16[80,1024]{1,0:T(8,128)(2,1)S(1)}, bf16[80,1024]{1,0:T(8,128)(2,1)S(1)}, u32[]{:S(2)}, u32[]{:S(2)}) collective-permute-start(bf16[80,1024]{1,0:T(8,128)(2,1)S(1)} %maximum_select_fusion.3), channel_id=1, source_target_pairs={{0,12},{4,8},{8,4},{12,0},{1,13},{5,9},{9,5},{13,1},{2,14},{6,10},... | collective-permute-start | bytes 491528 | tf_op jit(solution)/shard_map/ppermute | solution.py:14
  52.9 14.1 %collective-permute-start.14 = (bf16[80,1024]{1,0:T(8,128)(2,1)S(1)}, bf16[80,1024]{1,0:T(8,128)(2,1)S(1)}, u32[]{:S(2)}, u32[]{:S(2)}) collective-permute-start(bf16[80,1024]{1,0:T(8,128)(2,1)S(1)} %maximum_select_fusion.3), channel_id=1, source_target_pairs={{0,8},{4,12},{8,0},{12,4},{1,9},{5,13},{9,1},{13,5},{2,10},{6,14},... | collective-permute-start | bytes 491528 | tf_op jit(solution)/shard_map/ppermute | solution.py:14
  52.9 14.1 %collective-permute-start.13 = (bf16[80,1024]{1,0:T(8,128)(2,1)S(1)}, bf16[80,1024]{1,0:T(8,128)(2,1)S(1)}, u32[]{:S(2)}, u32[]{:S(2)}) collective-permute-start(bf16[80,1024]{1,0:T(8,128)(2,1)S(1)} %maximum_select_fusion.3), channel_id=1, source_target_pairs={{0,4},{4,0},{8,12},{12,8},{1,5},{5,1},{9,13},{13,9},{2,6},{6,2},{1... | collective-permute-start | bytes 491528 | tf_op jit(solution)/shard_map/ppermute | solution.py:14
  53.9 13.3 %collective-permute-start.7 = (bf16[80,1024]{1,0:T(8,128)(2,1)S(1)}, bf16[80,1024]{1,0:T(8,128)(2,1)S(1)}, u32[]{:S(2)}, u32[]{:S(2)}) collective-permute-start(bf16[80,1024]{1,0:T(8,128)(2,1)S(1)} %add_convert_fusion.6), channel_id=1, source_target_pairs={{0,2},{1,3},{2,0},{3,1},{4,6},{5,7},{6,4},{7,5},{8,10},{9,11},{10,... | collective-permute-start | bytes 491528 | tf_op jit(solution)/shard_map/ppermute | solution.py:14
  67.1 17.5 %collective-permute-start.16 = (bf16[320,1024]{1,0:T(8,128)(2,1)S(1)}, bf16[320,1024]{1,0:T(8,128)(2,1)S(1)}, u32[]{:S(2)}, u32[]{:S(2)}) collective-permute-start(bf16[320,1024]{1,0:T(8,128)(2,1)S(1)} %pad_maximum_fusion.3), channel_id=1, source_target_pairs={{0,1},{1,0},{2,3},{3,2},{4,5},{5,4},{6,7},{7,6},{8,9},{9,8},{10,11... | collective-permute-start | bytes 1966088 | tf_op jit(solution)/shard_map/ppermute | solution.py:14
  68.3 9.0 %collective-permute-start.10 = (bf16[80,1024]{1,0:T(8,128)(2,1)S(1)}, bf16[80,1024]{1,0:T(8,128)(2,1)S(1)}, u32[]{:S(2)}, u32[]{:S(2)}) collective-permute-start(bf16[80,1024]{1,0:T(8,128)(2,1)S(1)} %get-tuple-element.49), channel_id=1, source_target_pairs={{0,12},{4,8},{8,4},{12,0},{1,13},{5,9},{9,5},{13,1},{2,14},{6,10},... | collective-permute-start | bytes 491528 | tf_op jit(solution)/shard_map/ppermute | solution.py:14
  70.7 13.7 %collective-permute-start.9 = (bf16[80,1024]{1,0:T(8,128)(2,1)S(1)}, bf16[80,1024]{1,0:T(8,128)(2,1)S(1)}, u32[]{:S(2)}, u32[]{:S(2)}) collective-permute-start(bf16[80,1024]{1,0:T(8,128)(2,1)S(1)} %get-tuple-element.49), channel_id=1, source_target_pairs={{0,8},{4,12},{8,0},{12,4},{1,9},{5,13},{9,1},{13,5},{2,10},{6,14},... | collective-permute-start | bytes 491528 | tf_op jit(solution)/shard_map/ppermute | solution.py:14
  70.7 13.7 %collective-permute-start.8 = (bf16[80,1024]{1,0:T(8,128)(2,1)S(1)}, bf16[80,1024]{1,0:T(8,128)(2,1)S(1)}, u32[]{:S(2)}, u32[]{:S(2)}) collective-permute-start(bf16[80,1024]{1,0:T(8,128)(2,1)S(1)} %get-tuple-element.49), channel_id=1, source_target_pairs={{0,4},{4,0},{8,12},{12,8},{1,5},{5,1},{9,13},{13,9},{2,6},{6,2},{1... | collective-permute-start | bytes 491528 | tf_op jit(solution)/shard_map/ppermute | solution.py:14
  77.3 24.3 %collective-permute-start.17 = (bf16[1024,512]{1,0:T(8,128)(2,1)S(1)}, bf16[1024,512]{1,0:T(8,128)(2,1)S(1)}, u32[]{:S(2)}, u32[]{:S(2)}) collective-permute-start(bf16[1024,512]{1,0:T(8,128)(2,1)S(1)} %copy-done.26), channel_id=1, source_target_pairs={{0,16},{16,0},{1,17},{17,1},{2,18},{18,2},{3,19},{19,3},{4,20},{20... | collective-permute-start | bytes 3145736 | tf_op jit(solution)/shard_map/ppermute | solution.py:14
  84.5 18.1 %collective-permute-start.11 = (bf16[320,1024]{1,0:T(8,128)(2,1)S(1)}, bf16[320,1024]{1,0:T(8,128)(2,1)S(1)}, u32[]{:S(2)}, u32[]{:S(2)}) collective-permute-start(bf16[320,1024]{1,0:T(8,128)(2,1)S(1)} %pad_maximum_fusion.2), channel_id=1, source_target_pairs={{0,1},{1,0},{2,3},{3,2},{4,5},{5,4},{6,7},{7,6},{8,9},{9,8},{10,11... | collective-permute-start | bytes 1966088 | tf_op jit(solution)/shard_map/ppermute | solution.py:14
  84.8 28.9 %copy-start.20 = (bf16[640,1024]{1,0:T(8,128)(2,1)}, bf16[640,1024]{1,0:T(8,128)(2,1)S(1)}, u32[]{:S(2)}) copy-start(bf16[640,1024]{1,0:T(8,128)(2,1)S(1)} %slice_dynamic-update-slice_fusion.7) | copy-start | bytes 3932164
  108.4 3.6 %collective-permute-start.18 = (bf16[80,1024]{1,0:T(8,128)(2,1)S(1)}, bf16[80,1024]{1,0:T(8,128)(2,1)S(1)}, u32[]{:S(2)}, u32[]{:S(2)}) collective-permute-start(bf16[80,1024]{1,0:T(8,128)(2,1)S(1)} %slice.425), channel_id=1, source_target_pairs={{0,1},{1,0},{2,3},{3,2},{4,5},{5,4},{6,7},{7,6},{8,9},{9,8},{10,11... | collective-permute-start | bytes 491528 | tf_op jit(solution)/shard_map/ppermute | solution.py:14
  110.5 41.6 %collective-permute-start.34 = (bf16[512,1024]{1,0:T(8,128)(2,1)}, bf16[512,1024]{1,0:T(8,128)(2,1)}, u32[]{:S(2)}, u32[]{:S(2)}) collective-permute-start(bf16[512,1024]{1,0:T(8,128)(2,1)} %convolution_convert_fusion.1), channel_id=1, source_target_pairs={{0,16},{16,0},{1,17},{17,1},{2,18},{18,2},{3,19},{19,3},{4,20},{20... | collective-permute-start | bytes 3145736 | tf_op jit(solution)/shard_map/ppermute | solution.py:14
  112.0 6.4 %collective-permute-start.19 = (bf16[80,1024]{1,0:T(8,128)(2,1)S(1)}, bf16[80,1024]{1,0:T(8,128)(2,1)S(1)}, u32[]{:S(2)}, u32[]{:S(2)}) collective-permute-start(bf16[80,1024]{1,0:T(8,128)(2,1)S(1)} %add_convert_fusion.4), channel_id=1, source_target_pairs={{0,2},{1,3},{2,0},{3,1},{4,6},{5,7},{6,4},{7,5},{8,10},{9,11},{10,... | collective-permute-start | bytes 491528 | tf_op jit(solution)/shard_map/ppermute | solution.py:14
  115.6 43.2 %collective-permute-start.35 = (bf16[1024,512]{1,0:T(8,128)(2,1)}, bf16[1024,512]{1,0:T(8,128)(2,1)}, u32[]{:S(2)}, u32[]{:S(2)}) collective-permute-start(bf16[1024,512]{1,0:T(8,128)(2,1)} %convolution_convert_fusion), channel_id=1, source_target_pairs={{0,16},{16,0},{1,17},{17,1},{2,18},{18,2},{3,19},{19,3},{4,20},{20... | collective-permute-start | bytes 3145736 | tf_op jit(solution)/shard_map/ppermute | solution.py:14
  121.6 10.1 %collective-permute-start.20 = (bf16[96,1024]{1,0:T(8,128)(2,1)}, bf16[96,1024]{1,0:T(8,128)(2,1)}, u32[]{:S(2)}, u32[]{:S(2)}) collective-permute-start(bf16[96,1024]{1,0:T(8,128)(2,1)} %concatenate.246), channel_id=1, source_target_pairs={{0,4},{4,0},{8,12},{12,8},{1,5},{5,1},{9,13},{13,9},{2,6},{6,2},{1... | collective-permute-start | bytes 589832 | tf_op jit(solution)/shard_map/ppermute | solution.py:14
  126.1 15.5 %collective-permute-start.21 = (bf16[96,1024]{1,0:T(8,128)(2,1)}, bf16[96,1024]{1,0:T(8,128)(2,1)}, u32[]{:S(2)}, u32[]{:S(2)}) collective-permute-start(bf16[96,1024]{1,0:T(8,128)(2,1)} %concatenate.246), channel_id=1, source_target_pairs={{0,8},{4,12},{8,0},{12,4},{1,9},{5,13},{9,1},{13,5},{2,10},{6,14},... | collective-permute-start | bytes 589832 | tf_op jit(solution)/shard_map/ppermute | solution.py:14
  126.1 15.5 %collective-permute-start.22 = (bf16[96,1024]{1,0:T(8,128)(2,1)}, bf16[96,1024]{1,0:T(8,128)(2,1)}, u32[]{:S(2)}, u32[]{:S(2)}) collective-permute-start(bf16[96,1024]{1,0:T(8,128)(2,1)} %concatenate.246), channel_id=1, source_target_pairs={{0,12},{4,8},{8,4},{12,0},{1,13},{5,9},{9,5},{13,1},{2,14},{6,10},... | collective-permute-start | bytes 589832 | tf_op jit(solution)/shard_map/ppermute | solution.py:14
  148.3 14.1 %collective-permute-start.23 = (bf16[384,1024]{1,0:T(8,128)(2,1)}, bf16[384,1024]{1,0:T(8,128)(2,1)}, u32[]{:S(2)}, u32[]{:S(2)}) collective-permute-start(bf16[384,1024]{1,0:T(8,128)(2,1)} %concatenate.247), channel_id=1, source_target_pairs={{0,1},{1,0},{2,3},{3,2},{4,5},{5,4},{6,7},{7,6},{8,9},{9,8},{10,11... | collective-permute-start | bytes 2359304 | tf_op jit(solution)/shard_map/ppermute | solution.py:14
  185.2 7.3 %collective-permute-start.24 = (bf16[80,1024]{1,0:T(8,128)(2,1)S(1)}, bf16[80,1024]{1,0:T(8,128)(2,1)S(1)}, u32[]{:S(2)}, u32[]{:S(2)}) collective-permute-start(bf16[80,1024]{1,0:T(8,128)(2,1)S(1)} %slice.434), channel_id=1, source_target_pairs={{0,1},{1,0},{2,3},{3,2},{4,5},{5,4},{6,7},{7,6},{8,9},{9,8},{10,11... | collective-permute-start | bytes 491528 | tf_op jit(solution)/shard_map/ppermute | solution.py:14
  186.9 7.3 %collective-permute-start.27 = (bf16[80,1024]{1,0:T(8,128)(2,1)S(1)}, bf16[80,1024]{1,0:T(8,128)(2,1)S(1)}, u32[]{:S(2)}, u32[]{:S(2)}) collective-permute-start(bf16[80,1024]{1,0:T(8,128)(2,1)S(1)} %slice.440), channel_id=1, source_target_pairs={{0,1},{1,0},{2,3},{3,2},{4,5},{5,4},{6,7},{7,6},{8,9},{9,8},{10,11... | collective-permute-start | bytes 491528 | tf_op jit(solution)/shard_map/ppermute | solution.py:14
  190.0 26.3 %slice-start = ((f32[4,1024]{1,0:T(4,128)}), f32[4,512]{1,0:T(4,128)S(1)}, s32[]{:S(2)}) async-start(f32[4,1024]{1,0:T(4,128)} %copy-done.33), calls=%async_computation | async-start | bytes 16384 | tf_op jit(solution)/shard_map/slice | solution.py:39
  190.0 26.3 %copy-start.37 = (f32[272]{0:T(512)S(1)}, f32[272]{0:T(512)}, u32[]{:S(2)}) copy-start(f32[272]{0:T(512)} %pad.17.clone) | copy-start | bytes 3268
  190.2 31.8 %collective-permute-start.30 = (bf16[528,768]{1,0:T(8,128)(2,1)S(1)}, bf16[528,768]{1,0:T(8,128)(2,1)}, u32[]{:S(2)}, u32[]{:S(2)}) collective-permute-start(bf16[528,768]{1,0:T(8,128)(2,1)S(1)} %fusion.19), channel_id=1, source_target_pairs={{0,16},{16,0},{1,17},{17,1},{2,18},{18,2},{3,19},{19,3},{4,20},{20... | collective-permute-start | bytes 2433032 | tf_op jit(solution)/shard_map/ppermute | solution.py:14
  191.9 24.4 %collective-permute-start.33 = (bf16[272,512]{1,0:T(8,128)(2,1)S(1)}, bf16[272,512]{1,0:T(8,128)(2,1)S(1)}, u32[]{:S(2)}, u32[]{:S(2)}) collective-permute-start(bf16[272,512]{1,0:T(8,128)(2,1)S(1)} %maximum_maximum_fusion), channel_id=1, source_target_pairs={{0,16},{16,0},{1,17},{17,1},{2,18},{18,2},{3,19},{19,3},{4,20},{20... | collective-permute-start | bytes 835592 | tf_op jit(solution)/shard_map/ppermute | solution.py:14
  192.5 26.0 %collective-permute-start.25 = (bf16[80,1024]{1,0:T(8,128)(2,1)S(1)}, bf16[80,1024]{1,0:T(8,128)(2,1)S(1)}, u32[]{:S(2)}, u32[]{:S(2)}) collective-permute-start(bf16[80,1024]{1,0:T(8,128)(2,1)S(1)} %add_convert_fusion.3), channel_id=1, source_target_pairs={{0,2},{1,3},{2,0},{3,1},{4,6},{5,7},{6,4},{7,5},{8,10},{9,11},{10,... | collective-permute-start | bytes 491528 | tf_op jit(solution)/shard_map/ppermute | solution.py:14
  194.2 24.4 %copy-start.34 = (f32[1,1024]{1,0:T(1,128)S(1)}, f32[1,1024]{1,0:T(1,128)}, u32[]{:S(2)}) copy-start(f32[1,1024]{1,0:T(1,128)} %pad_maximum_fusion.20) | copy-start | bytes 12292
  194.2 24.5 %copy-start.43 = (f32[80]{0:T(128)S(1)}, f32[80]{0:T(128)}, u32[]{:S(2)}) copy-start(f32[80]{0:T(128)} %broadcast_multiply_fusion.3) | copy-start | bytes 964
  194.2 24.5 %copy-start.45 = (f32[80]{0:T(128)S(1)}, f32[80]{0:T(128)}, u32[]{:S(2)}) copy-start(f32[80]{0:T(128)} %add_rsqrt_fusion.1) | copy-start | bytes 964
  194.2 24.5 %collective-permute-start.28 = (bf16[80,1024]{1,0:T(8,128)(2,1)S(1)}, bf16[80,1024]{1,0:T(8,128)(2,1)S(1)}, u32[]{:S(2)}, u32[]{:S(2)}) collective-permute-start(bf16[80,1024]{1,0:T(8,128)(2,1)S(1)} %add_convert_fusion.1), channel_id=1, source_target_pairs={{0,2},{1,3},{2,0},{3,1},{4,6},{5,7},{6,4},{7,5},{8,10},{9,11},{10,... | collective-permute-start | bytes 491528 | tf_op jit(solution)/shard_map/ppermute | solution.py:14
  218.6 1.5 collective-permute-start.26
  219.2 1.8 collective-permute-start.29
  225.3 1.3 collective-permute-start.31
  226.6 3.7 %collective-permute-start.32 = (f32[2,512]{1,0:T(2,128)S(1)}, f32[2,512]{1,0:T(2,128)S(1)}, u32[]{:S(2)}, u32[]{:S(2)}) collective-permute-start(f32[2,512]{1,0:T(2,128)S(1)} %slice_add_fusion.1), channel_id=1, source_target_pairs={{0,2},{1,3},{2,0},{3,1},{4,6},{5,7},{6,4},{7,5},{8,10},{9,11},{10,... | collective-permute-start | bytes 12296 | tf_op jit(solution)/shard_map/ppermute | solution.py:14
  (36 other events, 108.8 us)

commit v3 on v2

v3 whole, which is shorter than its diff:
```python
import jax
import jax.numpy as jnp
from jax import lax
from jax.experimental import pallas as pl
from jax.experimental.pallas import tpu as pltpu
from jax.sharding import PartitionSpec as P

EPS = 1e-06
LOW = jnp.bfloat16
WIDE = jnp.float32


def swap(block, axis, bit):
    return lax.ppermute(block, axis, [(i, i ^ bit) for i in range(lax.axis_size(axis))])


def after(value, *others):
    return lax.optimization_barrier((value, *others))[0]


def pin(value):
    return lax.optimization_barrier(value)


def dot(left, right):
    return lax.dot_general(left, right, (((1,), (0,)), ((), ())), preferred_element_type=WIDE)


def dot_rt(left, right):
    return lax.dot_general(left, right, (((1,), (1,)), ((), ())), preferred_element_type=WIDE)


def dot_lt(left, right):
    return lax.dot_general(left, right, (((0,), (0,)), ((), ())), preferred_element_type=WIDE)


def segments(value, count):
    size = value.shape[1] // count
    return [value[:, i * size : (i + 1) * size] for i in range(count)]


def from_width(value, parts):
    return sum(dot(s, p) for s, p in zip(segments(value, len(parts)), parts))


def to_width(value, parts):
    return jnp.concatenate([dot(value, p) for p in parts], 1)


def from_width_rt(value, parts):
    return sum(dot_rt(s, p) for s, p in zip(segments(value, len(parts)), parts))


def to_width_rt(value, parts):
    return jnp.concatenate([dot_rt(value, p) for p in parts], 1)


def sum_cores(keep, send):
    return (keep.astype(WIDE) + swap(send, "tensor", 1).astype(WIDE)).astype(LOW)


def last_terms(keep, send):
    value = pin(sum_cores(keep, send))
    bit = 2
    while True:
        got = swap(value, "tensor", bit)
        bit *= 2
        if bit >= lax.axis_size("tensor"):
            return value, got
        value = pin((value.astype(WIDE) + got.astype(WIDE)).astype(LOW))


def spread_context(piece):
    return [piece] + [swap(piece, "context", k) for k in range(1, lax.axis_size("context"))]


def woven(mine, theirs):
    return [block for both in zip(mine, theirs) for block in both]


def gather_pieces(piece):
    mine = spread_context(piece)
    return woven(mine, [swap(m, "tensor", 1) for m in mine])


def kernel(body, out_shape, *args, flops=0, moved=0, scratch=(), in_specs=None):
    extra = {} if in_specs is None else {"in_specs": in_specs}
    return pl.pallas_call(
        body,
        out_shape=out_shape,
        scratch_shapes=list(scratch),
        compiler_params=pltpu.CompilerParams(vmem_limit_bytes=48 << 20),
        cost_estimate=pl.CostEstimate(flops=flops, bytes_accessed=moved, transcendentals=0),
        **extra,
    )(*args)


def low(*shape):
    return jax.ShapeDtypeStruct(shape, LOW)


def wide(*shape):
    return jax.ShapeDtypeStruct(shape, WIDE)


QBIAS, VBIAS, EBIAS = 6, 7, 8


def pack_body(*refs):
    sources, (lines, message), copies = refs[:9], refs[9:11], refs[11:20]
    arrived = refs[20]
    moves = [
        pltpu.make_async_copy(s, c, arrived.at[n]) for n, (s, c) in enumerate(zip(sources, copies))
    ]
    for m in moves:
        m.start()
    lines[...] = jnp.zeros_like(lines)
    for m in moves:
        m.wait()
    ways = lax.axis_size("fsdp")
    mine = lax.axis_index("fsdp")
    for n, ref in enumerate(copies[:6]):
        lines[n : n + 1, : ref.shape[0]] = ref[...].reshape(1, -1).astype(WIDE)
    for n, ref in zip((QBIAS, VBIAS, EBIAS), copies[6:]):
        groups, size = ref.shape
        each = size * ways
        row = lax.broadcasted_iota(jnp.int32, (size, groups * each), 0)
        column = lax.broadcasted_iota(jnp.int32, (size, groups * each), 1)
        within = column
        for g in range(1, groups):
            within = jnp.where(column >= g * each, column - g * each, within)
        tiled = dot(ref[...], (within == row + mine * size).astype(LOW))
        group = lax.broadcasted_iota(jnp.int32, tiled.shape, 0)
        column = lax.broadcasted_iota(jnp.int32, tiled.shape, 1)
        keep = (column >= group * each) & (column < (group + 1) * each)
        lines[n : n + 1, : groups * each] = jnp.sum(
            jnp.where(keep, tiled, 0.0), 0, keepdims=True
        )
    message[...] = lines[...].astype(LOW)


def merge_body(own, got, out):
    share = own.shape[1] // 2
    theirs = got[...].astype(WIDE)
    out[...] = own[...] + theirs
    out[:QBIAS, :share] = own[:QBIAS, :share]
    out[:QBIAS, share:] = theirs[:QBIAS, :share]


def normed_rows(values):
    center = values - jnp.mean(values, -1, keepdims=True)
    return center * lax.rsqrt(jnp.mean(center * center, -1, keepdims=True) + EPS)


def norm_back_rows(values, gain, upstream):
    center = values - jnp.mean(values, -1, keepdims=True)
    spread = lax.rsqrt(jnp.mean(center * center, -1, keepdims=True) + EPS)
    xhat = center * spread
    z = upstream * gain
    grad = spread * (
        z - jnp.mean(z, -1, keepdims=True) - xhat * jnp.mean(z * xhat, -1, keepdims=True)
    )
    return grad, xhat


def head_mask(shape, head, head_dim):
    lane = lax.broadcasted_iota(jnp.int32, shape, 1)
    return (lane >= head * head_dim) & (lane < (head + 1) * head_dim)


def attend_rows(heads, head_dim, start, rows, qkv, bias):
    features = heads * head_dim
    q = qkv[start : start + rows, :features]
    k = qkv[:, features : 2 * features]
    v = qkv[:, 2 * features :]
    scale = head_dim**-0.5
    total = jnp.zeros((rows, features), WIDE)
    for h in range(heads):
        mine = head_mask(q.shape, h, head_dim)
        scores = dot_rt(jnp.where(mine, q, jnp.zeros_like(q)), k) * scale + bias[...]
        raw = jnp.exp(scores - jnp.max(scores, -1, keepdims=True))
        got = dot(raw.astype(LOW), v) / jnp.sum(raw, -1, keepdims=True)
        total = jnp.where(mine, got, total)
    return total.astype(LOW)


def first_body(heads, head_dim, blocks, ways, *refs):
    pieces, refs = refs[:blocks], refs[blocks:]
    vec, bias = refs[:2]
    weights = [refs[2 + n * ways : 2 + (n + 1) * ways] for n in range(3)]
    outs = refs[2 + 3 * ways : 2 + 4 * ways]
    xhat, normed, qkv, context, keep, send = refs[2 + 4 * ways :]
    rows = pieces[0].shape[0]
    features = heads * head_dim
    for n, piece in enumerate(pieces):
        part = normed_rows(piece[...].astype(WIDE))
        xhat[n * rows : (n + 1) * rows, :] = part.astype(LOW)
        normed[n * rows : (n + 1) * rows, :] = (part * vec[0:1, :] + vec[1:2, :]).astype(LOW)
    size = normed.shape[1] // ways
    for n, row in enumerate((QBIAS, None, VBIAS)):
        got = sum(
            dot(normed[:, i * size : (i + 1) * size], w[...]) for i, w in enumerate(weights[n])
        )
        if row is not None:
            got = got + vec[row : row + 1, :features]
        qkv[:, n * features : (n + 1) * features] = got.astype(LOW)
    context[...] = attend_rows(heads, head_dim, 0, 2 * rows, qkv, bias)
    for i, w in enumerate(outs):
        part = dot(context[...], w[...]).astype(LOW)
        keep[:, i * size : (i + 1) * size] = part[:rows]
        send[:, i * size : (i + 1) * size] = part[rows:]


def rest_body(heads, head_dim, start, qkv, bias, out):
    out[...] = attend_rows(heads, head_dim, start, out.shape[0], qkv, bias)


def second_body(tokens, near, far, vec, hidden, normed):
    total = tokens[...].astype(WIDE) + (near[...].astype(WIDE) + far[...].astype(WIDE))
    total = total + vec[2:3, :]
    hidden[...] = total
    normed[...] = (normed_rows(total) * vec[3:4, :] + vec[4:5, :]).astype(LOW)


def second_back_body(near, far, hidden, cot, vec, grad_hidden, grad_branch, sums):
    upstream = near[...].astype(WIDE) + far[...].astype(WIDE)
    grad, xhat = norm_back_rows(hidden[...], vec[3:4, :], upstream)
    total = grad + cot[...].astype(WIDE)
    grad_hidden[...] = total
    grad_branch[...] = total.astype(LOW)
    sums[...] = jnp.zeros_like(sums)
    sums[0:1, :] = jnp.sum(upstream * xhat, 0, keepdims=True)
    sums[1:2, :] = jnp.sum(upstream, 0, keepdims=True)


def attend_back_body(heads, head_dim, blocks, ways, *refs):
    pieces, refs = refs[:blocks], refs[blocks:]
    qkv, bias = refs[:2]
    outs = refs[2 : 2 + ways]
    weights = [refs[2 + (n + 1) * ways : 2 + (n + 2) * ways] for n in range(3)]
    branch, grad_qkv, keep, send, sums, head_sums = refs[2 + 4 * ways :]
    rows = pieces[0].shape[0]
    features = heads * head_dim
    for n, piece in enumerate(pieces):
        branch[n * rows : (n + 1) * rows, :] = piece[...]
    size = branch.shape[1] // ways
    g = sum(
        dot_rt(branch[:, i * size : (i + 1) * size], w[...]) for i, w in enumerate(outs)
    ).astype(LOW)
    q = qkv[:, :features]
    k = qkv[:, features : 2 * features]
    v = qkv[:, 2 * features :]
    scale = head_dim**-0.5
    zero = jnp.zeros_like(q)
    totals = [jnp.zeros(q.shape, WIDE) for _ in range(3)]
    for h in range(heads):
        mine = head_mask(q.shape, h, head_dim)
        scores = dot_rt(k, jnp.where(mine, q, zero)) * scale + bias[...]
        raw = jnp.exp(scores - jnp.max(scores, 0, keepdims=True))
        probs = raw * (1.0 / jnp.sum(raw, 0, keepdims=True))
        grad_probs = dot_rt(v, jnp.where(mine, g, zero))
        delta = jnp.sum(probs * grad_probs, 0, keepdims=True)
        grad_scores = (probs * (grad_probs - delta)).astype(LOW)
        totals[0] = jnp.where(mine, dot_lt(grad_scores, k) * scale, totals[0])
        totals[1] = jnp.where(mine, dot(grad_scores, q) * scale, totals[1])
        totals[2] = jnp.where(mine, dot(probs.astype(LOW), g), totals[2])
    head_sums[...] = jnp.zeros_like(head_sums)
    for n in range(3):
        part = totals[n].astype(LOW)
        grad_qkv[:, n * features : (n + 1) * features] = part
        head_sums[0:1, n * features : (n + 1) * features] = jnp.sum(
            part.astype(WIDE), 0, keepdims=True
        )
    for i in range(ways):
        part = sum(
            dot_rt(grad_qkv[: 2 * rows, n * features : (n + 1) * features], weights[n][i][...])
            for n in range(3)
        ).astype(LOW)
        keep[:, i * size : (i + 1) * size] = part[:rows]
        send[:, i * size : (i + 1) * size] = part[rows:]
    sums[...] = jnp.zeros_like(sums)
    sums[0:1, :] = jnp.sum(branch[...].astype(WIDE), 0, keepdims=True)


def first_sums_body(ways, grad_qkv, xhat, *refs):
    weights = [refs[n * ways : (n + 1) * ways] for n in range(3)]
    out = refs[3 * ways]
    features = grad_qkv.shape[1] // 3
    size = xhat.shape[1] // ways
    out[...] = jnp.zeros_like(out)
    for i in range(ways):
        part = sum(
            dot_rt(grad_qkv[:, n * features : (n + 1) * features], weights[n][i][...])
            for n in range(3)
        )
        columns = slice(i * size, (i + 1) * size)
        out[0:1, columns] = jnp.sum(part * xhat[:, columns].astype(WIDE), 0, keepdims=True)
        out[1:2, columns] = jnp.sum(part, 0, keepdims=True)


def first_back_body(near, far, tokens, grad_hidden, vec, out):
    upstream = near[...].astype(WIDE) + far[...].astype(WIDE)
    grad, _ = norm_back_rows(tokens[...].astype(WIDE), vec[0:1, :], upstream)
    out[...] = grad + grad_hidden[...]


def on_device(
    tokens,
    cotangent,
    valid_count,
    gain_first,
    shift_first,
    query_weight,
    query_bias,
    key_weight,
    value_weight,
    value_bias,
    output_weight,
    output_bias,
    gain_second,
    shift_second,
    expand_weight,
    expand_bias,
    reduce_weight,
    reduce_bias,
):
    images, seq, width = tokens.shape
    ways = lax.axis_size("fsdp")
    pair = ways == 2
    parts = 2 if pair else 1
    cycle = lax.axis_size("context")
    mine = lax.axis_index("fsdp")
    place = lax.axis_index("context")
    core = lax.axis_index("tensor") & 1
    share = gain_first.shape[0]
    heads = query_bias.shape[1]
    head_dim = query_bias.shape[0] * ways
    features = heads * head_dim
    units = expand_weight.shape[1]
    half = seq // 2
    blocks = 2 * cycle
    length = cycle * seq
    second = mine == 1

    def turned(value):
        if not pair:
            return value
        left, right = jnp.split(value, 2, -1)
        return jnp.where(second, jnp.concatenate([right, left], -1), value)

    def piece_of(value, which):
        return turned(lax.dynamic_slice_in_dim(value.reshape(seq, width), which * half, half, 0))

    token_piece = piece_of(tokens, core)
    mine_tokens = spread_context(token_piece)
    token_pieces = woven(
        mine_tokens,
        [piece_of(tokens, 1 - core)] + [swap(m, "tensor", 1) for m in mine_tokens[1:]],
    )
    vectors = (gain_first, shift_first, output_bias, gain_second, shift_second, reduce_bias)
    biases = (query_bias, value_bias, expand_bias)
    thirds = (query_weight, key_weight, value_weight)

    if pair:
        across = lambda v: swap(v, "fsdp", 1)
        qkv_parts = [(w, across(w)) for w in thirds]
        lines, message = kernel(
            pack_body,
            (wide(16, width), low(16, width)),
            *vectors,
            *(b.T for b in biases),
            in_specs=[pl.BlockSpec(memory_space=pl.ANY)] * 9,
            scratch=[pltpu.VMEM(v.shape, LOW) for v in vectors]
            + [pltpu.VMEM(b.shape[::-1], LOW) for b in biases]
            + [pltpu.SemaphoreType.DMA((9,))],
        )
        vec = kernel(merge_body, wide(16, width), lines, across(message))
        output_parts = (output_weight, across(output_weight))
    else:
        gather = lambda v, axis=0: lax.all_gather(v, "fsdp", axis=axis, tiled=True)
        qkv_parts = [(gather(w),) for w in thirds]
        rows = [gather(v).reshape(1, -1) for v in vectors]
        rows += [gather(b).T.reshape(1, -1) for b in biases]
        vec = jnp.concatenate(
            [jnp.pad(r, ((0, 0), (0, width - r.shape[1]))) for r in rows]
            + [jnp.zeros((16 - len(rows), width), LOW)],
            0,
        ).astype(WIDE)
        output_parts = (gather(output_weight, 1),)
    flat_qkv = [w for group in qkv_parts for w in group]

    steps = jnp.arange(half, dtype=jnp.int32)
    positions = jnp.concatenate(
        [(place ^ k) * seq + (core ^ j) * half + steps for k in range(cycle) for j in range(2)]
    )
    bias = jnp.where(positions < valid_count[0], 0.0, -1e30).astype(WIDE)
    xhat_all, normed_all, qkv, context_own, keep, send = kernel(
        lambda *refs: first_body(heads, head_dim, blocks, parts, *refs),
        (
            low(length, width),
            low(length, width),
            low(length, 3 * features),
            low(seq, features),
            low(half, width),
            low(half, width),
        ),
        *token_pieces,
        vec,
        bias[None, :],
        *flat_qkv,
        *output_parts,
        flops=6 * length * width * features,
        moved=10 * length * width,
    )

    if pair:
        expand_parts = (expand_weight, across(after(expand_weight, flat_qkv[-1])))
        reduce_parts = (reduce_weight, across(after(reduce_weight, keep)))
    else:
        expand_parts = (gather(expand_weight),)
        reduce_parts = (gather(reduce_weight, 1),)

    near, far = last_terms(keep, send)
    hidden, normed_piece = kernel(
        second_body, (wide(half, width), low(half, width)), token_piece, near, far, vec
    )

    cot_piece = piece_of(cotangent, core)
    cot_all = jnp.concatenate(gather_pieces(after(cot_piece, mine_tokens[-1])), 0)
    normed_two = jnp.concatenate(gather_pieces(normed_piece), 0)
    expanded = from_width(normed_two, expand_parts) + vec[EBIAS : EBIAS + 1, :units]
    cdf = 0.5 * (1.0 + lax.erf(expanded * (2.0**-0.5)))
    activated = (expanded * cdf).astype(LOW)
    slope = cdf + expanded * jnp.exp(-0.5 * expanded * expanded) * 0.3989422804014327
    grad_expanded = (from_width_rt(cot_all, reduce_parts) * slope).astype(LOW)
    near, far = last_terms(
        to_width_rt(grad_expanded[:half], expand_parts).astype(LOW),
        to_width_rt(grad_expanded[half:seq], expand_parts).astype(LOW),
    )
    grad_hidden, grad_piece, norm_sums = kernel(
        second_back_body,
        (wide(half, width), low(half, width), wide(8, width)),
        near,
        far,
        hidden,
        cot_piece,
        vec,
    )

    def scatter(value, axis):
        return lax.psum_scatter(value.astype(LOW), "fsdp", scatter_dimension=axis, tiled=True)

    def weight_grad(left, right, along):
        if not pair:
            return scatter(dot_lt(left, right), along).astype(WIDE)
        if along:
            own, other = segments(right, 2)
            away = across(dot_lt(left, other).astype(LOW))
            return pin(dot_lt(left, own)) + away.astype(WIDE)
        own, other = segments(left, 2)
        away = across(dot_lt(other, right).astype(LOW))
        return pin(dot_lt(own, right)) + away.astype(WIDE)

    grad_reduce = weight_grad(activated, cot_all, 1)
    grad_expand = weight_grad(normed_two, grad_expanded, 0)

    grad_branch, grad_qkv, keep, send, branch_sum, head_sum = kernel(
        lambda *refs: attend_back_body(heads, head_dim, blocks, parts, *refs),
        (
            low(length, width),
            low(length, 3 * features),
            low(half, width),
            low(half, width),
            wide(8, width),
            wide(8, 3 * features),
        ),
        *gather_pieces(grad_piece),
        qkv,
        bias[:, None],
        *output_parts,
        *flat_qkv,
        flops=10 * length * length * features,
        moved=8 * length * width,
    )
    near, far = last_terms(keep, send)
    grad_token_piece = kernel(
        first_back_body, wide(half, width), near, far, token_piece, grad_hidden, vec
    )

    def both_cores(value):
        theirs = swap(value, "tensor", 1)
        upper = core == 1
        return turned(
            jnp.concatenate([jnp.where(upper, theirs, value), jnp.where(upper, value, theirs)], 0)
        ).reshape(tokens.shape)

    grad_tokens = both_cores(grad_token_piece)

    normed_sides = segments(normed_all, parts)
    if pair:
        away = across(dot_lt(normed_sides[1], grad_qkv).astype(LOW))
        grad_weights = pin(dot_lt(normed_sides[0], grad_qkv)) + away.astype(WIDE)
    else:
        grad_weights = scatter(dot_lt(normed_all, grad_qkv), 0).astype(WIDE)
    grad_query, grad_key, grad_value = (
        grad_weights[:, n * features : (n + 1) * features] for n in range(3)
    )

    near, far = last_terms(
        to_width(after(activated[:half], grad_piece), reduce_parts).astype(LOW),
        to_width(after(activated[half:seq], grad_piece), reduce_parts).astype(LOW),
    )
    reduced = near.astype(WIDE) + far.astype(WIDE) + vec[5:6, :]
    output = both_cores((hidden + reduced).astype(LOW))

    def own_rows(value):
        size = value.shape[0] // ways
        return lax.dynamic_slice_in_dim(value, mine * size, size, 0)

    context_rest = kernel(
        lambda *refs: rest_body(heads, head_dim, seq, *refs),
        low(length - seq, features),
        after(qkv, near),
        bias[None, :],
    )
    context_all = jnp.concatenate([context_own, context_rest], 0)
    grad_output = weight_grad(context_all, grad_branch, 1)

    first_sums = kernel(
        lambda *refs: first_sums_body(parts, *refs), wide(8, width), grad_qkv, xhat_all, *flat_qkv
    )[:2]
    bit = 1
    while bit < lax.axis_size("tensor"):
        first_sums = first_sums + swap(first_sums, "tensor", bit)
        bit *= 2
    norm_sums = norm_sums[:2] + swap(norm_sums[:2], "tensor", 1)
    bit = 1
    while bit < cycle:
        norm_sums = norm_sums + swap(norm_sums, "context", bit)
        bit *= 2
    cot_sum = jnp.sum(cot_all.astype(WIDE), 0, keepdims=True)
    unit_sum = jnp.sum(grad_expanded.astype(WIDE), 0, keepdims=True)
    sums = jnp.concatenate([first_sums, norm_sums, branch_sum[:1], cot_sum], 0)
    plain = jnp.concatenate(
        [jnp.pad(head_sum[:1], ((0, 0), (0, width - 3 * features))), unit_sum], 0
    )
    if pair:
        own, other = segments(sums, 2)
        got = across(jnp.concatenate([other, *segments(plain, 2)], 0))
        sums = own + got[:6]
        plain = plain + jnp.concatenate([got[6:8], got[8:10]], 1)
    else:
        sums = scatter(sums, 1).astype(WIDE)
        plain = lax.psum(plain, "fsdp")
    grad_ebias = own_rows(plain[1].reshape(-1, expand_bias.shape[0] * ways).T)
    grad_qbias, grad_vbias = (
        own_rows(plain[0, n * features : (n + 1) * features].reshape(heads, head_dim).T)
        for n in (0, 2)
    )
    return (
        output,
        grad_tokens,
        sums[0],
        sums[1],
        grad_query,
        grad_qbias,
        grad_key,
        grad_value,
        grad_vbias,
        grad_output,
        sums[4],
        sums[2],
        sums[3],
        grad_expand,
        grad_ebias,
        grad_reduce,
        sums[5],
    )


def solution(mesh):
    rows = P("fsdp", "context", None)
    vector = P("fsdp")
    split = P("fsdp", "tensor")
    turned = P("tensor", "fsdp")
    in_specs = (rows, rows, vector, vector, vector, split, split, split, split, split)
    in_specs += (turned, vector, vector, vector, split, split, turned, vector)
    out_specs = (rows, rows, vector, vector, split, split, split, split, split)
    out_specs += (turned, vector, vector, vector, split, split, turned, vector)
    return jax.shard_map(
        on_device, mesh=mesh, in_specs=in_specs, out_specs=out_specs, check_vma=False
    )
```

time: 234 us -> 199 us (0.85); the launches traced: 231 us -> 198 us
  local copies, waits for them, and re-layouts: 40.5 us -> 7.55 us
  matrix products: 31.3 us -> 22.6 us
  other arithmetic: 18.3 us -> 10.7 us
  starting transfers between devices: 39.7 us -> 46 us
  Pallas kernels: 12 us -> 18.2 us
  waiting for transfers between devices: 86.3 us -> 91.1 us
    unnamed x123 -> x58, local copies, waits for them, and re-layouts: 18 us -> 1.35 us
    concatenate x14 -> x2, local copies, waits for them, and re-layouts: 13.1 us -> 0.02 us  [the longest x1 0.01 us: on_device(): jnp.concatenate(gather_pieces(after(cot_piece, mine_tokens[-1])), 0)]
    ppermute x36 -> x54, starting transfers between devices: 39.7 us -> 46 us  [swap(): lax.ppermute(block, axis, [(i, i ^ bit) for i in range(lax.axis_size(axis...]
    pallas_call x4 -> x9, Pallas kernels: 12 us -> 18.2 us  [kernel(): pl.pallas_call(body, out_shape=out_shape, scratch_shapes=list(scratch), c...]
    reduce_sum x11 -> x1, other arithmetic: 6.33 us -> 0.23 us  [on_device(): cot_sum = jnp.sum(cot_all.astype(WIDE), 0, keepdims=True)]
    dot_general x10 -> x6, matrix products: 9.6 us -> 4.61 us  [dot_rt(): lax.dot_general(left, right, (((1,), (1,)), ((), ())), preferred_element_...]
    ppermute x36 -> x54, waiting for transfers between devices: 86.3 us -> 91.1 us  [swap(): lax.ppermute(block, axis, [(i, i ^ bit) for i in range(lax.axis_size(axis...]
    add x5 -> x9, other arithmetic: 2.56 us -> 7.1 us  [the longest x2 3.88 us: weight_grad(): return pin(dot_lt(left, own)) + away.astype(WIDE)]
  transfers between devices with their start and end apart: 36 -> 54, of which waited for: 13 -> 21; matrix products, arithmetic and copies ran while one was open for 25% -> 15% of each run, Pallas kernels for 2% -> 9%
where the time goes in v3:
time: 199 us; the launch traced here: 198 us
  waiting for transfers between devices  91.1 us (46%)
  starting transfers between devices  46 us (23%)
  matrix products  22.6 us (11%)
  Pallas kernels  18.2 us (9%)
  other arithmetic  10.7 us (5%)
  local copies, waits for them, and re-layouts  7.55 us (4%)
  between operations  2.28 us (1%)
    ppermute x54, waiting for transfers between devices, swap(): lax.ppermute(block, axis, [(i, i ^ bit) for i in range(lax.axis_size(axis...  91.1 us
    ppermute x54, starting transfers between devices, swap(): lax.ppermute(block, axis, [(i, i ^ bit) for i in range(lax.axis_size(axis...  46 us
    pallas_call x9, Pallas kernels, kernel(): pl.pallas_call(body, out_shape=out_shape, scratch_shapes=list(scratch), c...  18.2 us
    dot_general x8, matrix products, dot_lt(): lax.dot_general(left, right, (((0,), (0,)), ((), ())), preferred_element_...  14.7 us
    dot_general x6, matrix products, dot_rt(): lax.dot_general(left, right, (((1,), (1,)), ((), ())), preferred_element_...  4.61 us
  transfers between devices with their start and end apart: 54, of which 21 were waited for; matrix products, arithmetic and copies ran while one was open for 15% of the time, Pallas kernels for 9%

profile of v3, /device:TPU:0, one launch (start us, length us, event | category | flops | bytes accessed | tf_op | source)
XLA Modules:
  0.0 198.4 jit_solution(3453219405265750222)
XLA Ops:
  2.0 3.1 %collective-permute-start = (bf16[80,1024]{1,0:T(8,128)(2,1)S(1)}, bf16[80,1024]{1,0:T(8,128)(2,1)S(1)}, u32[]{:S(2)}, u32[]{:S(2)}) collective-permute-start(bf16[80,1024]{1,0:T(8,128)(2,1)S(1)} %maximum_select_fusion.2.refs_0_.tokens), channel_id=1, source_target_pairs={{0,4},{4,0},{8,12},{12,8},{1,5},{5,1},{9,13},{13,9},{2,6},{6,2},{1... | collective-permute-start | bytes 491528 | tf_op jit(solution)/shard_map/ppermute | solution.py:14
  5.1 2.6 %collective-permute-start.2 = (bf16[80,1024]{1,0:T(8,128)(2,1)S(1)}, bf16[80,1024]{1,0:T(8,128)(2,1)S(1)}, u32[]{:S(2)}, u32[]{:S(2)}) collective-permute-start(bf16[80,1024]{1,0:T(8,128)(2,1)S(1)} %maximum_select_fusion.2.refs_0_.tokens), channel_id=1, source_target_pairs={{0,8},{4,12},{8,0},{12,4},{1,9},{5,13},{9,1},{13,5},{2,10},{6,14},... | collective-permute-start | bytes 491528 | tf_op jit(solution)/shard_map/ppermute | solution.py:14
  8.0 1.8 collective-permute-start.6
  12.3 1.8 collective-permute-start.8
  14.4 5.7 %collective-permute-done.2.refs_4_ = bf16[80,1024]{1,0:T(8,128)(2,1)S(1)} collective-permute-done((bf16[80,1024]{1,0:T(8,128)(2,1)S(1)}, bf16[80,1024]{1,0:T(8,128)(2,1)S(1)}, u32[]{:S(2)}, u32[]{:S(2)}) %collective-permute-start.2) | collective-permute-done | bytes 163872 | tf_op jit(solution)/shard_map/ppermute | solution.py:14
  20.1 1.5 collective-permute-start.10
  23.2 1.4 collective-permute-done.8.refs_13_.refs_15_.refs_5_
  24.7 5.6 %collective-permute-done.9.refs_15_.refs_17_.refs_7_ = bf16[512,256]{1,0:T(8,128)(2,1)S(1)} collective-permute-done((bf16[512,256]{1,0:T(8,128)(2,1)S(1)}, bf16[512,256]{1,0:T(8,128)(2,1)S(1)}, u32[]{:S(2)}, u32[]{:S(2)}) %collective-permute-start.9) | collective-permute-done | bytes 262176 | tf_op jit(solution)/shard_map/ppermute | solution.py:14
  30.3 3.7 %collective-permute-done.10.refs_17_.refs_11_ = bf16[256,512]{1,0:T(8,128)(2,1)S(1)} collective-permute-done((bf16[256,512]{1,0:T(8,128)(2,1)S(1)}, bf16[256,512]{1,0:T(8,128)(2,1)S(1)}, u32[]{:S(2)}, u32[]{:S(2)}) %collective-permute-start.10) | collective-permute-done | bytes 262176 | tf_op jit(solution)/shard_map/ppermute | solution.py:14
  34.6 3.5 %collective-permute-start.24 = (bf16[80,1024]{1,0:T(8,128)(2,1)S(1)}, bf16[80,1024]{1,0:T(8,128)(2,1)S(1)}, u32[]{:S(2)}, u32[]{:S(2)}) collective-permute-start(bf16[80,1024]{1,0:T(8,128)(2,1)S(1)} %maximum_select_fusion.4.cot), channel_id=1, source_target_pairs={{0,8},{4,12},{8,0},{12,4},{1,9},{5,13},{9,1},{13,5},{2,10},{6,14},... | collective-permute-start | bytes 491528 | tf_op jit(solution)/shard_map/ppermute | solution.py:14
  39.1 4.7 %shard_map.307 = (bf16[640,1024]{1,0:T(8,128)(2,1)S(1)}, bf16[640,1024]{1,0:T(8,128)(2,1)}, bf16[640,768]{1,0:T(8,128)(2,1)S(1)}, bf16[160,256]{1,0:T(8,128)(2,1...) custom-call(bf16[80,1024]{1,0:T(8,128)(2,1)S(1)} %maximum_select_fusion.2.refs_0_.tokens, ...), custom_call_target="tpu_custom_call" | custom-call | flops 1006632960 | bytes 6553600 | tf_op jit(solution)/shard_map/pallas_call | solution.py:88
  44.4 4.7 %collective-permute-done.24 = bf16[80,1024]{1,0:T(8,128)(2,1)S(1)} collective-permute-done((bf16[80,1024]{1,0:T(8,128)(2,1)S(1)}, bf16[80,1024]{1,0:T(8,128)(2,1)S(1)}, u32[]{:S(2)}, u32[]{:S(2)}) %collective-permute-start.24) | collective-permute-done | bytes 163872 | tf_op jit(solution)/shard_map/ppermute | solution.py:14
  49.7 1.6 collective-permute-start.12
  51.4 4.5 %collective-permute-done.12.far = bf16[80,1024]{1,0:T(8,128)(2,1)S(1)} collective-permute-done((bf16[80,1024]{1,0:T(8,128)(2,1)S(1)}, bf16[80,1024]{1,0:T(8,128)(2,1)S(1)}, u32[]{:S(2)}, u32[]{:S(2)}) %collective-permute-start.12) | collective-permute-done | bytes 163872 | tf_op jit(solution)/shard_map/ppermute | solution.py:14
  56.2 2.4 %collective-permute-start.14 = (bf16[80,1024]{1,0:T(8,128)(2,1)S(1)}, bf16[80,1024]{1,0:T(8,128)(2,1)S(1)}, u32[]{:S(2)}, u32[]{:S(2)}) collective-permute-start(bf16[80,1024]{1,0:T(8,128)(2,1)S(1)} %get-tuple-element.47), channel_id=1, source_target_pairs={{0,4},{4,0},{8,12},{12,8},{1,5},{5,1},{9,13},{13,9},{2,6},{6,2},{1... | collective-permute-start | bytes 491528 | tf_op jit(solution)/shard_map/ppermute | solution.py:14
  59.6 1.4 collective-permute-start.18
  61.9 4.5 %collective-permute-done.14 = bf16[80,1024]{1,0:T(8,128)(2,1)S(1)} collective-permute-done((bf16[80,1024]{1,0:T(8,128)(2,1)S(1)}, bf16[80,1024]{1,0:T(8,128)(2,1)S(1)}, u32[]{:S(2)}, u32[]{:S(2)}) %collective-permute-start.14) | collective-permute-done | bytes 163872 | tf_op jit(solution)/shard_map/ppermute | solution.py:14
  66.4 7.2 %collective-permute-done.16 = bf16[80,1024]{1,0:T(8,128)(2,1)S(1)} collective-permute-done((bf16[80,1024]{1,0:T(8,128)(2,1)S(1)}, bf16[80,1024]{1,0:T(8,128)(2,1)S(1)}, u32[]{:S(2)}, u32[]{:S(2)}) %collective-permute-start.16) | collective-permute-done | bytes 163872 | tf_op jit(solution)/shard_map/ppermute | solution.py:14
  76.5 1.2 multiply_convert_fusion
  77.7 2.3 %fusion.15 = f32[1024,512]{1,0:T(8,128)} fusion(bf16[640,1024]{1,0:T(8,128)(2,1)S(1)} %get-tuple-element.102, bf16[640,1024]{1,0:T(8,128)(2,1)S(1)} %constant_dynamic-update-slice_fusion.8), kind=kOutput, calls=%fused_computation.39 | convolution fusion | flops 671088640 | bytes 4063232 | tf_op jit(solution)/shard_map/dot_general | solution.py:34
  80.1 2.0 %convolution_convert_fusion = bf16[1024,512]{1,0:T(8,128)(2,1)} fusion(bf16[640,1024]{1,0:T(8,128)(2,1)S(1)} %get-tuple-element.102, bf16[640,1024]{1,0:T(8,128)(2,1)S(1)} %constant_dynamic-update-slice_fusion.8), kind=kOutput, calls=%fused_computation.15 | convolution fusion | flops 671612928 | bytes 3014656 | tf_op jit(solution)/shard_map/dot_general | solution.py:34
  82.1 4.2 %collective-permute-done.28 = bf16[1024,512]{1,0:T(8,128)(2,1)S(1)} collective-permute-done((bf16[1024,512]{1,0:T(8,128)(2,1)S(1)}, bf16[1024,512]{1,0:T(8,128)(2,1)S(1)}, u32[]{:S(2)}, u32[]{:S(2)}) %collective-permute-start.28) | collective-permute-done | bytes 1048608 | tf_op jit(solution)/shard_map/ppermute | solution.py:14
  87.2 1.9 convert_reduce_fusion
  90.0 2.3 %fusion.21 = f32[512,1024]{1,0:T(8,128)} fusion(bf16[640,1024]{1,0:T(8,128)(2,1)S(1)} %get-tuple-element.105, bf16[640,1024]{1,0:T(8,128)(2,1)S(1)} %constant_dynamic-update-slice_fusion), kind=kOutput, calls=%fused_computation.45 | convolution fusion | flops 671088640 | bytes 4063232 | tf_op jit(solution)/shard_map/dot_general | solution.py:34
  94.4 1.6 collective-permute-start.30
  95.9 2.0 convolution_convert_fusion.1
  97.9 2.8 %collective-permute-done.30.far = bf16[80,1024]{1,0:T(8,128)(2,1)S(1)} collective-permute-done((bf16[80,1024]{1,0:T(8,128)(2,1)S(1)}, bf16[80,1024]{1,0:T(8,128)(2,1)S(1)}, u32[]{:S(2)}, u32[]{:S(2)}) %collective-permute-start.30) | collective-permute-done | bytes 163872 | tf_op jit(solution)/shard_map/ppermute | solution.py:14
  101.9 2.1 %collective-permute-start.37 = (bf16[80,1024]{1,0:T(8,128)(2,1)S(1)}, bf16[80,1024]{1,0:T(8,128)(2,1)S(1)}, u32[]{:S(2)}, u32[]{:S(2)}) collective-permute-start(bf16[80,1024]{1,0:T(8,128)(2,1)S(1)} %get-tuple-element.51.refs_0_), channel_id=1, source_target_pairs={{0,8},{4,12},{8,0},{12,4},{1,9},{5,13},{9,1},{13,5},{2,10},{6,14},... | collective-permute-start | bytes 491528 | tf_op jit(solution)/shard_map/ppermute | solution.py:14
  104.0 1.5 collective-permute-start.39
  107.4 4.7 %collective-permute-done.47 = f32[2,1024]{1,0:T(2,128)S(1)} collective-permute-done((f32[2,1024]{1,0:T(2,128)S(1)}, f32[2,1024]{1,0:T(2,128)S(1)}, u32[]{:S(2)}, u32[]{:S(2)}) %collective-permute-start.47) | collective-permute-done | bytes 8224 | tf_op jit(solution)/shard_map/ppermute | solution.py:14
  112.1 3.4 %collective-permute-start.48 = (f32[2,1024]{1,0:T(2,128)S(1)}, f32[2,1024]{1,0:T(2,128)S(1)}, u32[]{:S(2)}, u32[]{:S(2)}) collective-permute-start(f32[2,1024]{1,0:T(2,128)S(1)} %add.316), channel_id=1, source_target_pairs={{0,8},{4,12},{8,0},{12,4},{1,9},{5,13},{9,1},{13,5},{2,10},{6,14},... | collective-permute-start | bytes 24584 | tf_op jit(solution)/shard_map/ppermute | solution.py:14
  115.8 3.0 %collective-permute-done.48 = f32[2,1024]{1,0:T(2,128)S(1)} collective-permute-done((f32[2,1024]{1,0:T(2,128)S(1)}, f32[2,1024]{1,0:T(2,128)S(1)}, u32[]{:S(2)}, u32[]{:S(2)}) %collective-permute-start.48) | collective-permute-done | bytes 8224 | tf_op jit(solution)/shard_map/ppermute | solution.py:14
  120.6 2.5 %shard_map.313 = bf16[480,256]{1,0:T(8,128)(2,1)S(1)} custom-call(bf16[640,768]{1,0:T(8,128)(2,1)S(1)} %get-tuple-element.65.refs_8_.refs_0_, f32[1,640]{1,0:T(1,128)S(1)} %compare_select_fusion.1.refs_9_.refs_1_), custom_call_target="tpu_custom_call" | custom-call | tf_op jit(solution)/shard_map/pallas_call | solution.py:88
  123.1 1.5 collective-permute-start.52
  124.6 1.5 collective-permute-start.32
  126.1 8.5 %shard_map.310 = (bf16[640,1024]{1,0:T(8,128)(2,1)}, bf16[640,768]{1,0:T(8,128)(2,1)S(1)}, bf16[80,1024]{1,0:T(8,128)(2,1)S(1)}, bf16[80,1024]{1,0:T(8,128)(2,1)...) custom-call(bf16[80,1024]{1,0:T(8,128)(2,1)S(1)} %get-tuple-element.51.refs_0_, ...), custom_call_target="tpu_custom_call" | custom-call | flops 1048576000 | bytes 5242880 | tf_op jit(solution)/shard_map/pallas_call | solution.py:88
  134.7 2.0 fusion.10
  136.6 1.8 convolution_convert_fusion.2
  138.4 1.2 fusion.7
  140.7 1.2 shard_map.312
  143.7 3.1 %collective-permute-done.45 = f32[2,1024]{1,0:T(2,128)S(1)} collective-permute-done((f32[2,1024]{1,0:T(2,128)S(1)}, f32[2,1024]{1,0:T(2,128)S(1)}, u32[]{:S(2)}, u32[]{:S(2)}) %collective-permute-start.45) | collective-permute-done | bytes 8224 | tf_op jit(solution)/shard_map/ppermute | solution.py:14
  148.2 17.2 %collective-permute-done.49 = f32[10,512]{1,0:T(8,128)S(1)} collective-permute-done((f32[10,512]{1,0:T(8,128)S(1)}, f32[10,512]{1,0:T(8,128)S(1)}, u32[]{:S(2)}, u32[]{:S(2)}) %collective-permute-start.49) | collective-permute-done | bytes 20512 | tf_op jit(solution)/shard_map/ppermute | solution.py:14
  168.8 1.5 collective-permute-start.51
  170.3 1.6 collective-permute-start.42
  172.8 15.2 %collective-permute-done.51 = bf16[256,512]{1,0:T(8,128)(2,1)S(1)} collective-permute-done((bf16[256,512]{1,0:T(8,128)(2,1)}, bf16[256,512]{1,0:T(8,128)(2,1)S(1)}, u32[]{:S(2)}, u32[]{:S(2)}) %collective-permute-start.51) | collective-permute-done | bytes 262176 | tf_op jit(solution)/shard_map/ppermute | solution.py:14
  188.9 3.0 %convert_add_fusion = f32[1024,512]{1,0:T(8,128)} fusion(f32[1024,512]{1,0:T(8,128)S(1)} %copy-done.17, bf16[1024,512]{1,0:T(8,128)(2,1)} %collective-permute-done.53), kind=kLoop, calls=%fused_computation.12 | loop fusion | flops 1048576 | bytes 5242880 | tf_op jit(solution)/shard_map/add | solution.py:459
  192.3 3.0 %convert_add_fusion.1 = f32[512,1024]{1,0:T(8,128)} fusion(f32[512,1024]{1,0:T(8,128)S(1)} %copy-done.16, bf16[512,1024]{1,0:T(8,128)(2,1)} %collective-permute-done.52), kind=kLoop, calls=%fused_computation.13 | loop fusion | flops 1048576 | bytes 5242880 | tf_op jit(solution)/shard_map/add | solution.py:462
  197.3 1.2 fusion.53
  (217 shorter events, 33.4 us)
Async XLA Ops:
  2.0 12.2 %collective-permute-start = (bf16[80,1024]{1,0:T(8,128)(2,1)S(1)}, bf16[80,1024]{1,0:T(8,128)(2,1)S(1)}, u32[]{:S(2)}, u32[]{:S(2)}) collective-permute-start(bf16[80,1024]{1,0:T(8,128)(2,1)S(1)} %maximum_select_fusion.2.refs_0_.tokens), channel_id=1, source_target_pairs={{0,4},{4,0},{8,12},{12,8},{1,5},{5,1},{9,13},{13,9},{2,6},{6,2},{1... | collective-permute-start | bytes 491528 | tf_op jit(solution)/shard_map/ppermute | solution.py:14
  5.1 15.0 %collective-permute-start.2 = (bf16[80,1024]{1,0:T(8,128)(2,1)S(1)}, bf16[80,1024]{1,0:T(8,128)(2,1)S(1)}, u32[]{:S(2)}, u32[]{:S(2)}) collective-permute-start(bf16[80,1024]{1,0:T(8,128)(2,1)S(1)} %maximum_select_fusion.2.refs_0_.tokens), channel_id=1, source_target_pairs={{0,8},{4,12},{8,0},{12,4},{1,9},{5,13},{9,1},{13,5},{2,10},{6,14},... | collective-permute-start | bytes 491528 | tf_op jit(solution)/shard_map/ppermute | solution.py:14
  7.7 15.0 %collective-permute-start.4 = (bf16[80,1024]{1,0:T(8,128)(2,1)S(1)}, bf16[80,1024]{1,0:T(8,128)(2,1)}, u32[]{:S(2)}, u32[]{:S(2)}) collective-permute-start(bf16[80,1024]{1,0:T(8,128)(2,1)S(1)} %maximum_select_fusion.2.refs_0_.tokens), channel_id=1, source_target_pairs={{0,12},{4,8},{8,4},{12,0},{1,13},{5,9},{9,5},{13,1},{2,14},{6,10},... | collective-permute-start | bytes 491528 | tf_op jit(solution)/shard_map/ppermute | solution.py:14
  8.0 4.3 %collective-permute-start.6 = (bf16[16,1024]{1,0:T(8,128)(2,1)S(1)}, bf16[16,1024]{1,0:T(8,128)(2,1)S(1)}, u32[]{:S(2)}, u32[]{:S(2)}) collective-permute-start(bf16[16,1024]{1,0:T(8,128)(2,1)S(1)} %get-tuple-element.43), channel_id=1, source_target_pairs={{0,16},{16,0},{1,17},{17,1},{2,18},{18,2},{3,19},{19,3},{4,20},{20... | collective-permute-start | bytes 98312 | tf_op jit(solution)/shard_map/ppermute | solution.py:14
  9.8 12.9 %collective-permute-start.7 = (bf16[512,256]{1,0:T(8,128)(2,1)S(1)}, bf16[512,256]{1,0:T(8,128)(2,1)S(1)}, u32[]{:S(2)}, u32[]{:S(2)}) collective-permute-start(bf16[512,256]{1,0:T(8,128)(2,1)S(1)} %copy-done), channel_id=1, source_target_pairs={{0,16},{16,0},{1,17},{17,1},{2,18},{18,2},{3,19},{19,3},{4,20},{20... | collective-permute-start | bytes 786440 | tf_op jit(solution)/shard_map/ppermute | solution.py:14
  12.3 12.4 %collective-permute-start.8 = (bf16[512,256]{1,0:T(8,128)(2,1)S(1)}, bf16[512,256]{1,0:T(8,128)(2,1)S(1)}, u32[]{:S(2)}, u32[]{:S(2)}) collective-permute-start(bf16[512,256]{1,0:T(8,128)(2,1)S(1)} %copy-done.1), channel_id=1, source_target_pairs={{0,16},{16,0},{1,17},{17,1},{2,18},{18,2},{3,19},{19,3},{4,20},{20... | collective-permute-start | bytes 786440 | tf_op jit(solution)/shard_map/ppermute | solution.py:14
  14.1 16.1 %collective-permute-start.9 = (bf16[512,256]{1,0:T(8,128)(2,1)S(1)}, bf16[512,256]{1,0:T(8,128)(2,1)S(1)}, u32[]{:S(2)}, u32[]{:S(2)}) collective-permute-start(bf16[512,256]{1,0:T(8,128)(2,1)S(1)} %copy-done.2), channel_id=1, source_target_pairs={{0,16},{16,0},{1,17},{17,1},{2,18},{18,2},{3,19},{19,3},{4,20},{20... | collective-permute-start | bytes 786440 | tf_op jit(solution)/shard_map/ppermute | solution.py:14
  20.1 13.9 %collective-permute-start.10 = (bf16[256,512]{1,0:T(8,128)(2,1)S(1)}, bf16[256,512]{1,0:T(8,128)(2,1)S(1)}, u32[]{:S(2)}, u32[]{:S(2)}) collective-permute-start(bf16[256,512]{1,0:T(8,128)(2,1)S(1)} %copy-done.3), channel_id=1, source_target_pairs={{0,16},{16,0},{1,17},{17,1},{2,18},{18,2},{3,19},{19,3},{4,20},{20... | collective-permute-start | bytes 786440 | tf_op jit(solution)/shard_map/ppermute | solution.py:14
  22.7 12.0 %collective-permute-start.1 = (bf16[80,1024]{1,0:T(8,128)(2,1)S(1)}, bf16[80,1024]{1,0:T(8,128)(2,1)S(1)}, u32[]{:S(2)}, u32[]{:S(2)}) collective-permute-start(bf16[80,1024]{1,0:T(8,128)(2,1)S(1)} %collective-permute-done.refs_2_), channel_id=1, source_target_pairs={{0,1},{1,0},{2,3},{3,2},{4,5},{5,4},{6,7},{7,6},{8,9},{9,8},{10,11... | collective-permute-start | bytes 491528 | tf_op jit(solution)/shard_map/ppermute | solution.py:14
  22.7 15.4 %collective-permute-start.3 = (bf16[80,1024]{1,0:T(8,128)(2,1)S(1)}, bf16[80,1024]{1,0:T(8,128)(2,1)S(1)}, u32[]{:S(2)}, u32[]{:S(2)}) collective-permute-start(bf16[80,1024]{1,0:T(8,128)(2,1)S(1)} %collective-permute-done.2.refs_4_), channel_id=1, source_target_pairs={{0,1},{1,0},{2,3},{3,2},{4,5},{5,4},{6,7},{7,6},{8,9},{9,8},{10,11... | collective-permute-start | bytes 491528 | tf_op jit(solution)/shard_map/ppermute | solution.py:14
  24.7 13.8 %collective-permute-start.5 = (bf16[80,1024]{1,0:T(8,128)(2,1)}, bf16[80,1024]{1,0:T(8,128)(2,1)S(1)}, u32[]{:S(2)}, u32[]{:S(2)}) collective-permute-start(bf16[80,1024]{1,0:T(8,128)(2,1)} %collective-permute-done.4.refs_6_), channel_id=1, source_target_pairs={{0,1},{1,0},{2,3},{3,2},{4,5},{5,4},{6,7},{7,6},{8,9},{9,8},{10,11... | collective-permute-start | bytes 491528 | tf_op jit(solution)/shard_map/ppermute | solution.py:14
  30.3 13.6 %collective-permute-start.21 = (bf16[80,1024]{1,0:T(8,128)(2,1)S(1)}, bf16[80,1024]{1,0:T(8,128)(2,1)S(1)}, u32[]{:S(2)}, u32[]{:S(2)}) collective-permute-start(bf16[80,1024]{1,0:T(8,128)(2,1)S(1)} %maximum_select_fusion.4.cot), channel_id=1, source_target_pairs={{0,1},{1,0},{2,3},{3,2},{4,5},{5,4},{6,7},{7,6},{8,9},{9,8},{10,11... | collective-permute-start | bytes 491528 | tf_op jit(solution)/shard_map/ppermute | solution.py:14
  34.0 9.9 %collective-permute-start.22 = (bf16[80,1024]{1,0:T(8,128)(2,1)S(1)}, bf16[80,1024]{1,0:T(8,128)(2,1)S(1)}, u32[]{:S(2)}, u32[]{:S(2)}) collective-permute-start(bf16[80,1024]{1,0:T(8,128)(2,1)S(1)} %maximum_select_fusion.4.cot), channel_id=1, source_target_pairs={{0,4},{4,0},{8,12},{12,8},{1,5},{5,1},{9,13},{13,9},{2,6},{6,2},{1... | collective-permute-start | bytes 491528 | tf_op jit(solution)/shard_map/ppermute | solution.py:14
  34.6 14.5 %collective-permute-start.24 = (bf16[80,1024]{1,0:T(8,128)(2,1)S(1)}, bf16[80,1024]{1,0:T(8,128)(2,1)S(1)}, u32[]{:S(2)}, u32[]{:S(2)}) collective-permute-start(bf16[80,1024]{1,0:T(8,128)(2,1)S(1)} %maximum_select_fusion.4.cot), channel_id=1, source_target_pairs={{0,8},{4,12},{8,0},{12,4},{1,9},{5,13},{9,1},{13,5},{2,10},{6,14},... | collective-permute-start | bytes 491528 | tf_op jit(solution)/shard_map/ppermute | solution.py:14
  38.1 11.0 %collective-permute-start.26 = (bf16[80,1024]{1,0:T(8,128)(2,1)S(1)}, bf16[80,1024]{1,0:T(8,128)(2,1)S(1)}, u32[]{:S(2)}, u32[]{:S(2)}) collective-permute-start(bf16[80,1024]{1,0:T(8,128)(2,1)S(1)} %maximum_select_fusion.4.cot), channel_id=1, source_target_pairs={{0,12},{4,8},{8,4},{12,0},{1,13},{5,9},{9,5},{13,1},{2,14},{6,10},... | collective-permute-start | bytes 491528 | tf_op jit(solution)/shard_map/ppermute | solution.py:14
  38.4 36.9 %collective-permute-start.20 = (bf16[512,1024]{1,0:T(8,128)(2,1)}, bf16[512,1024]{1,0:T(8,128)(2,1)S(1)}, u32[]{:S(2)}, u32[]{:S(2)}) collective-permute-start(bf16[512,1024]{1,0:T(8,128)(2,1)} %param.32), channel_id=1, source_target_pairs={{0,16},{16,0},{1,17},{17,1},{2,18},{18,2},{3,19},{19,3},{4,20},{20... | collective-permute-start | bytes 3145736 | tf_op jit(solution)/shard_map/ppermute | solution.py:14
  43.9 5.8 %collective-permute-start.11 = (bf16[80,1024]{1,0:T(8,128)(2,1)S(1)}, bf16[80,1024]{1,0:T(8,128)(2,1)S(1)}, u32[]{:S(2)}, u32[]{:S(2)}) collective-permute-start(bf16[80,1024]{1,0:T(8,128)(2,1)S(1)} %get-tuple-element.45), channel_id=1, source_target_pairs={{0,1},{1,0},{2,3},{3,2},{4,5},{5,4},{6,7},{7,6},{8,9},{9,8},{10,11... | collective-permute-start | bytes 491528 | tf_op jit(solution)/shard_map/ppermute | solution.py:14
  43.9 7.4 %collective-permute-start.23 = (bf16[80,1024]{1,0:T(8,128)(2,1)S(1)}, bf16[80,1024]{1,0:T(8,128)(2,1)S(1)}, u32[]{:S(2)}, u32[]{:S(2)}) collective-permute-start(bf16[80,1024]{1,0:T(8,128)(2,1)S(1)} %collective-permute-done.22), channel_id=1, source_target_pairs={{0,1},{1,0},{2,3},{3,2},{4,5},{5,4},{6,7},{7,6},{8,9},{9,8},{10,11... | collective-permute-start | bytes 491528 | tf_op jit(solution)/shard_map/ppermute | solution.py:14
  49.1 2.3 %collective-permute-start.27 = (bf16[80,1024]{1,0:T(8,128)(2,1)S(1)}, bf16[80,1024]{1,0:T(8,128)(2,1)S(1)}, u32[]{:S(2)}, u32[]{:S(2)}) collective-permute-start(bf16[80,1024]{1,0:T(8,128)(2,1)S(1)} %collective-permute-done.26), channel_id=1, source_target_pairs={{0,1},{1,0},{2,3},{3,2},{4,5},{5,4},{6,7},{7,6},{8,9},{9,8},{10,11... | collective-permute-start | bytes 491528 | tf_op jit(solution)/shard_map/ppermute | solution.py:14
  49.7 6.2 %collective-permute-start.12 = (bf16[80,1024]{1,0:T(8,128)(2,1)S(1)}, bf16[80,1024]{1,0:T(8,128)(2,1)S(1)}, u32[]{:S(2)}, u32[]{:S(2)}) collective-permute-start(bf16[80,1024]{1,0:T(8,128)(2,1)S(1)} %add_convert_fusion.4.near), channel_id=1, source_target_pairs={{0,2},{1,3},{2,0},{3,1},{4,6},{5,7},{6,4},{7,5},{8,10},{9,11},{10,... | collective-permute-start | bytes 491528 | tf_op jit(solution)/shard_map/ppermute | solution.py:14
  56.2 5.2 %collective-permute-start.13 = (bf16[80,1024]{1,0:T(8,128)(2,1)S(1)}, bf16[80,1024]{1,0:T(8,128)(2,1)S(1)}, u32[]{:S(2)}, u32[]{:S(2)}) collective-permute-start(bf16[80,1024]{1,0:T(8,128)(2,1)S(1)} %get-tuple-element.47), channel_id=1, source_target_pairs={{0,1},{1,0},{2,3},{3,2},{4,5},{5,4},{6,7},{7,6},{8,9},{9,8},{10,11... | collective-permute-start | bytes 491528 | tf_op jit(solution)/shard_map/ppermute | solution.py:14
  56.2 10.2 %collective-permute-start.14 = (bf16[80,1024]{1,0:T(8,128)(2,1)S(1)}, bf16[80,1024]{1,0:T(8,128)(2,1)S(1)}, u32[]{:S(2)}, u32[]{:S(2)}) collective-permute-start(bf16[80,1024]{1,0:T(8,128)(2,1)S(1)} %get-tuple-element.47), channel_id=1, source_target_pairs={{0,4},{4,0},{8,12},{12,8},{1,5},{5,1},{9,13},{13,9},{2,6},{6,2},{1... | collective-permute-start | bytes 491528 | tf_op jit(solution)/shard_map/ppermute | solution.py:14
  58.6 15.0 %collective-permute-start.16 = (bf16[80,1024]{1,0:T(8,128)(2,1)S(1)}, bf16[80,1024]{1,0:T(8,128)(2,1)S(1)}, u32[]{:S(2)}, u32[]{:S(2)}) collective-permute-start(bf16[80,1024]{1,0:T(8,128)(2,1)S(1)} %get-tuple-element.47), channel_id=1, source_target_pairs={{0,8},{4,12},{8,0},{12,4},{1,9},{5,13},{9,1},{13,5},{2,10},{6,14},... | collective-permute-start | bytes 491528 | tf_op jit(solution)/shard_map/ppermute | solution.py:14
  59.6 14.0 %collective-permute-start.18 = (bf16[80,1024]{1,0:T(8,128)(2,1)S(1)}, bf16[80,1024]{1,0:T(8,128)(2,1)S(1)}, u32[]{:S(2)}, u32[]{:S(2)}) collective-permute-start(bf16[80,1024]{1,0:T(8,128)(2,1)S(1)} %get-tuple-element.47), channel_id=1, source_target_pairs={{0,12},{4,8},{8,4},{12,0},{1,13},{5,9},{9,5},{13,1},{2,14},{6,10},... | collective-permute-start | bytes 491528 | tf_op jit(solution)/shard_map/ppermute | solution.py:14
  61.3 25.0 %collective-permute-start.28 = (bf16[1024,512]{1,0:T(8,128)(2,1)S(1)}, bf16[1024,512]{1,0:T(8,128)(2,1)S(1)}, u32[]{:S(2)}, u32[]{:S(2)}) collective-permute-start(bf16[1024,512]{1,0:T(8,128)(2,1)S(1)} %copy-done.15), channel_id=1, source_target_pairs={{0,16},{16,0},{1,17},{17,1},{2,18},{18,2},{3,19},{19,3},{4,20},{20... | collective-permute-start | bytes 3145736 | tf_op jit(solution)/shard_map/ppermute | solution.py:14
  66.4 7.7 %collective-permute-start.15 = (bf16[80,1024]{1,0:T(8,128)(2,1)S(1)}, bf16[80,1024]{1,0:T(8,128)(2,1)S(1)}, u32[]{:S(2)}, u32[]{:S(2)}) collective-permute-start(bf16[80,1024]{1,0:T(8,128)(2,1)S(1)} %collective-permute-done.14), channel_id=1, source_target_pairs={{0,1},{1,0},{2,3},{3,2},{4,5},{5,4},{6,7},{7,6},{8,9},{9,8},{10,11... | collective-permute-start | bytes 491528 | tf_op jit(solution)/shard_map/ppermute | solution.py:14
  94.4 6.3 %collective-permute-start.30 = (bf16[80,1024]{1,0:T(8,128)(2,1)S(1)}, bf16[80,1024]{1,0:T(8,128)(2,1)S(1)}, u32[]{:S(2)}, u32[]{:S(2)}) collective-permute-start(bf16[80,1024]{1,0:T(8,128)(2,1)S(1)} %add_convert_fusion.3.near), channel_id=1, source_target_pairs={{0,2},{1,3},{2,0},{3,1},{4,6},{5,7},{6,4},{7,5},{8,10},{9,11},{10,... | collective-permute-start | bytes 491528 | tf_op jit(solution)/shard_map/ppermute | solution.py:14
  101.0 18.5 %collective-permute-start.35 = (bf16[80,1024]{1,0:T(8,128)(2,1)S(1)}, bf16[80,1024]{1,0:T(8,128)(2,1)S(1)}, u32[]{:S(2)}, u32[]{:S(2)}) collective-permute-start(bf16[80,1024]{1,0:T(8,128)(2,1)S(1)} %get-tuple-element.51.refs_0_), channel_id=1, source_target_pairs={{0,4},{4,0},{8,12},{12,8},{1,5},{5,1},{9,13},{13,9},{2,6},{6,2},{1... | collective-permute-start | bytes 491528 | tf_op jit(solution)/shard_map/ppermute | solution.py:14
  101.9 18.1 %collective-permute-start.37 = (bf16[80,1024]{1,0:T(8,128)(2,1)S(1)}, bf16[80,1024]{1,0:T(8,128)(2,1)S(1)}, u32[]{:S(2)}, u32[]{:S(2)}) collective-permute-start(bf16[80,1024]{1,0:T(8,128)(2,1)S(1)} %get-tuple-element.51.refs_0_), channel_id=1, source_target_pairs={{0,8},{4,12},{8,0},{12,4},{1,9},{5,13},{9,1},{13,5},{2,10},{6,14},... | collective-permute-start | bytes 491528 | tf_op jit(solution)/shard_map/ppermute | solution.py:14
  104.0 16.1 %collective-permute-start.39 = (bf16[80,1024]{1,0:T(8,128)(2,1)S(1)}, bf16[80,1024]{1,0:T(8,128)(2,1)S(1)}, u32[]{:S(2)}, u32[]{:S(2)}) collective-permute-start(bf16[80,1024]{1,0:T(8,128)(2,1)S(1)} %get-tuple-element.51.refs_0_), channel_id=1, source_target_pairs={{0,12},{4,8},{8,4},{12,0},{1,13},{5,9},{9,5},{13,1},{2,14},{6,10},... | collective-permute-start | bytes 491528 | tf_op jit(solution)/shard_map/ppermute | solution.py:14
  106.2 13.2 %collective-permute-start.31 = (bf16[80,1024]{1,0:T(8,128)(2,1)S(1)}, bf16[80,1024]{1,0:T(8,128)(2,1)S(1)}, u32[]{:S(2)}, u32[]{:S(2)}) collective-permute-start(bf16[80,1024]{1,0:T(8,128)(2,1)S(1)} %pad_maximum_fusion.6), channel_id=1, source_target_pairs={{0,1},{1,0},{2,3},{3,2},{4,5},{5,4},{6,7},{7,6},{8,9},{9,8},{10,11... | collective-permute-start | bytes 491528 | tf_op jit(solution)/shard_map/ppermute | solution.py:14
  107.0 5.0 %collective-permute-start.47 = (f32[2,1024]{1,0:T(2,128)S(1)}, f32[2,1024]{1,0:T(2,128)S(1)}, u32[]{:S(2)}, u32[]{:S(2)}) collective-permute-start(f32[2,1024]{1,0:T(2,128)S(1)} %slice_add_fusion.2), channel_id=1, source_target_pairs={{0,4},{4,0},{8,12},{12,8},{1,5},{5,1},{9,13},{13,9},{2,6},{6,2},{1... | collective-permute-start | bytes 24584 | tf_op jit(solution)/shard_map/ppermute | solution.py:14
  112.1 6.8 %collective-permute-start.48 = (f32[2,1024]{1,0:T(2,128)S(1)}, f32[2,1024]{1,0:T(2,128)S(1)}, u32[]{:S(2)}, u32[]{:S(2)}) collective-permute-start(f32[2,1024]{1,0:T(2,128)S(1)} %add.316), channel_id=1, source_target_pairs={{0,8},{4,12},{8,0},{12,4},{1,9},{5,13},{9,1},{13,5},{2,10},{6,14},... | collective-permute-start | bytes 24584 | tf_op jit(solution)/shard_map/ppermute | solution.py:14
  118.9 70.0 %collective-permute-start.53 = (bf16[1024,512]{1,0:T(8,128)(2,1)}, bf16[1024,512]{1,0:T(8,128)(2,1)}, u32[]{:S(2)}, u32[]{:S(2)}) collective-permute-start(bf16[1024,512]{1,0:T(8,128)(2,1)} %convolution_convert_fusion), channel_id=1, source_target_pairs={{0,16},{16,0},{1,17},{17,1},{2,18},{18,2},{3,19},{19,3},{4,20},{20... | collective-permute-start | bytes 3145736 | tf_op jit(solution)/shard_map/ppermute | solution.py:14
  119.4 3.6 %collective-permute-start.34 = (bf16[80,1024]{1,0:T(8,128)(2,1)S(1)}, bf16[80,1024]{1,0:T(8,128)(2,1)S(1)}, u32[]{:S(2)}, u32[]{:S(2)}) collective-permute-start(bf16[80,1024]{1,0:T(8,128)(2,1)S(1)} %get-tuple-element.51.refs_0_), channel_id=1, source_target_pairs={{0,1},{1,0},{2,3},{3,2},{4,5},{5,4},{6,7},{7,6},{8,9},{9,8},{10,11... | collective-permute-start | bytes 491528 | tf_op jit(solution)/shard_map/ppermute | solution.py:14
  119.5 5.1 %collective-permute-start.36 = (bf16[80,1024]{1,0:T(8,128)(2,1)S(1)}, bf16[80,1024]{1,0:T(8,128)(2,1)S(1)}, u32[]{:S(2)}, u32[]{:S(2)}) collective-permute-start(bf16[80,1024]{1,0:T(8,128)(2,1)S(1)} %collective-permute-done.35.refs_2_), channel_id=1, source_target_pairs={{0,1},{1,0},{2,3},{3,2},{4,5},{5,4},{6,7},{7,6},{8,9},{9,8},{10,11... | collective-permute-start | bytes 491528 | tf_op jit(solution)/shard_map/ppermute | solution.py:14
  120.0 6.1 %collective-permute-start.38 = (bf16[80,1024]{1,0:T(8,128)(2,1)S(1)}, bf16[80,1024]{1,0:T(8,128)(2,1)S(1)}, u32[]{:S(2)}, u32[]{:S(2)}) collective-permute-start(bf16[80,1024]{1,0:T(8,128)(2,1)S(1)} %collective-permute-done.37.refs_4_), channel_id=1, source_target_pairs={{0,1},{1,0},{2,3},{3,2},{4,5},{5,4},{6,7},{7,6},{8,9},{9,8},{10,11... | collective-permute-start | bytes 491528 | tf_op jit(solution)/shard_map/ppermute | solution.py:14
  120.1 6.0 %collective-permute-start.40 = (bf16[80,1024]{1,0:T(8,128)(2,1)S(1)}, bf16[80,1024]{1,0:T(8,128)(2,1)S(1)}, u32[]{:S(2)}, u32[]{:S(2)}) collective-permute-start(bf16[80,1024]{1,0:T(8,128)(2,1)S(1)} %collective-permute-done.39.refs_6_), channel_id=1, source_target_pairs={{0,1},{1,0},{2,3},{3,2},{4,5},{5,4},{6,7},{7,6},{8,9},{9,8},{10,11... | collective-permute-start | bytes 491528 | tf_op jit(solution)/shard_map/ppermute | solution.py:14
  123.1 69.2 %collective-permute-start.52 = (bf16[512,1024]{1,0:T(8,128)(2,1)}, bf16[512,1024]{1,0:T(8,128)(2,1)}, u32[]{:S(2)}, u32[]{:S(2)}) collective-permute-start(bf16[512,1024]{1,0:T(8,128)(2,1)} %convolution_convert_fusion.1), channel_id=1, source_target_pairs={{0,16},{16,0},{1,17},{17,1},{2,18},{18,2},{3,19},{19,3},{4,20},{20... | collective-permute-start | bytes 3145736 | tf_op jit(solution)/shard_map/ppermute | solution.py:14
  124.6 23.0 %collective-permute-start.32 = (bf16[80,1024]{1,0:T(8,128)(2,1)S(1)}, bf16[80,1024]{1,0:T(8,128)(2,1)S(1)}, u32[]{:S(2)}, u32[]{:S(2)}) collective-permute-start(bf16[80,1024]{1,0:T(8,128)(2,1)S(1)} %add_convert_fusion.2), channel_id=1, source_target_pairs={{0,2},{1,3},{2,0},{3,1},{4,6},{5,7},{6,4},{7,5},{8,10},{9,11},{10,... | collective-permute-start | bytes 491528 | tf_op jit(solution)/shard_map/ppermute | solution.py:14
  143.2 3.7 %collective-permute-start.45 = (f32[2,1024]{1,0:T(2,128)S(1)}, f32[2,1024]{1,0:T(2,128)S(1)}, u32[]{:S(2)}, u32[]{:S(2)}) collective-permute-start(f32[2,1024]{1,0:T(2,128)S(1)} %slice_add_fusion.1), channel_id=1, source_target_pairs={{0,2},{1,3},{2,0},{3,1},{4,6},{5,7},{6,4},{7,5},{8,10},{9,11},{10,... | collective-permute-start | bytes 24584 | tf_op jit(solution)/shard_map/ppermute | solution.py:14
  146.9 18.5 %collective-permute-start.49 = (f32[10,512]{1,0:T(8,128)S(1)}, f32[10,512]{1,0:T(8,128)S(1)}, u32[]{:S(2)}, u32[]{:S(2)}) collective-permute-start(f32[10,512]{1,0:T(8,128)S(1)} %pad_maximum_fusion.8), channel_id=1, source_target_pairs={{0,16},{16,0},{1,17},{17,1},{2,18},{18,2},{3,19},{19,3},{4,20},{20... | collective-permute-start | bytes 61448 | tf_op jit(solution)/shard_map/ppermute | solution.py:14
  147.6 22.7 %collective-permute-start.33 = (bf16[80,1024]{1,0:T(8,128)(2,1)S(1)}, bf16[80,1024]{1,0:T(8,128)(2,1)S(1)}, u32[]{:S(2)}, u32[]{:S(2)}) collective-permute-start(bf16[80,1024]{1,0:T(8,128)(2,1)S(1)} %add_convert_fusion.1), channel_id=1, source_target_pairs={{0,1},{1,0},{2,3},{3,2},{4,5},{5,4},{6,7},{7,6},{8,9},{9,8},{10,11... | collective-permute-start | bytes 491528 | tf_op jit(solution)/shard_map/ppermute | solution.py:14
  147.7 21.1 %collective-permute-start.41 = (bf16[80,1024]{1,0:T(8,128)(2,1)S(1)}, bf16[80,1024]{1,0:T(8,128)(2,1)S(1)}, u32[]{:S(2)}, u32[]{:S(2)}) collective-permute-start(bf16[80,1024]{1,0:T(8,128)(2,1)S(1)} %get-tuple-element.56), channel_id=1, source_target_pairs={{0,1},{1,0},{2,3},{3,2},{4,5},{5,4},{6,7},{7,6},{8,9},{9,8},{10,11... | collective-permute-start | bytes 491528 | tf_op jit(solution)/shard_map/ppermute | solution.py:14
  165.4 30.9 %collective-permute-start.50 = (bf16[512,768]{1,0:T(8,128)(2,1)}, bf16[512,768]{1,0:T(8,128)(2,1)S(1)}, u32[]{:S(2)}, u32[]{:S(2)}) collective-permute-start(bf16[512,768]{1,0:T(8,128)(2,1)} %convolution_convert_fusion.2), channel_id=1, source_target_pairs={{0,16},{16,0},{1,17},{17,1},{2,18},{18,2},{3,19},{19,3},{4,20},{20... | collective-permute-start | bytes 2359304 | tf_op jit(solution)/shard_map/ppermute | solution.py:14
  168.8 19.2 %collective-permute-start.51 = (bf16[256,512]{1,0:T(8,128)(2,1)}, bf16[256,512]{1,0:T(8,128)(2,1)S(1)}, u32[]{:S(2)}, u32[]{:S(2)}) collective-permute-start(bf16[256,512]{1,0:T(8,128)(2,1)} %convolution_convert_fusion.3), channel_id=1, source_target_pairs={{0,16},{16,0},{1,17},{17,1},{2,18},{18,2},{3,19},{19,3},{4,20},{20... | collective-permute-start | bytes 786440 | tf_op jit(solution)/shard_map/ppermute | solution.py:14
  170.3 21.6 %collective-permute-start.42 = (bf16[80,1024]{1,0:T(8,128)(2,1)S(1)}, bf16[80,1024]{1,0:T(8,128)(2,1)S(1)}, u32[]{:S(2)}, u32[]{:S(2)}) collective-permute-start(bf16[80,1024]{1,0:T(8,128)(2,1)S(1)} %add_convert_fusion.near), channel_id=1, source_target_pairs={{0,2},{1,3},{2,0},{3,1},{4,6},{5,7},{6,4},{7,5},{8,10},{9,11},{10,... | collective-permute-start | bytes 491528 | tf_op jit(solution)/shard_map/ppermute | solution.py:14
  192.2 3.1 %collective-permute-start.43 = (f32[80,1024]{1,0:T(8,128)S(1)}, f32[80,1024]{1,0:T(8,128)S(1)}, u32[]{:S(2)}, u32[]{:S(2)}) collective-permute-start(f32[80,1024]{1,0:T(8,128)S(1)} %shard_map.311), channel_id=1, source_target_pairs={{0,1},{1,0},{2,3},{3,2},{4,5},{5,4},{6,7},{7,6},{8,9},{9,8},{10,11... | collective-permute-start | bytes 983048 | tf_op jit(solution)/shard_map/ppermute | solution.py:14
  (28 other events, 196.5 us)

commit v4 on v3

v4 whole, which is shorter than its diff:
```python
import jax
import jax.numpy as jnp
from jax import lax
from jax.experimental import pallas as pl
from jax.experimental.pallas import tpu as pltpu
from jax.sharding import PartitionSpec as P

EPS = 1e-06
LOW = jnp.bfloat16
WIDE = jnp.float32


def swap(block, axis, bit):
    return lax.ppermute(block, axis, [(i, i ^ bit) for i in range(lax.axis_size(axis))])


def after(value, *others):
    return lax.optimization_barrier((value, *others))[0]


def pin(value):
    return lax.optimization_barrier(value)


def dot(left, right):
    return lax.dot_general(left, right, (((1,), (0,)), ((), ())), preferred_element_type=WIDE)


def dot_rt(left, right):
    return lax.dot_general(left, right, (((1,), (1,)), ((), ())), preferred_element_type=WIDE)


def dot_lt(left, right):
    return lax.dot_general(left, right, (((0,), (0,)), ((), ())), preferred_element_type=WIDE)


def segments(value, count):
    size = value.shape[1] // count
    return [value[:, i * size : (i + 1) * size] for i in range(count)]


def sum_cores(keep, send):
    return (keep.astype(WIDE) + swap(send, "tensor", 1).astype(WIDE)).astype(LOW)


def last_terms(keep, send):
    value = pin(sum_cores(keep, send))
    bit = 2
    while True:
        got = swap(value, "tensor", bit)
        bit *= 2
        if bit >= lax.axis_size("tensor"):
            return value, got
        value = pin((value.astype(WIDE) + got.astype(WIDE)).astype(LOW))


def spread_context(piece):
    return [piece] + [swap(piece, "context", k) for k in range(1, lax.axis_size("context"))]


def woven(mine, theirs):
    return [block for both in zip(mine, theirs) for block in both]


class Late:
    def __init__(self, ref, copy):
        self.ref, self.copy, self.shape = ref, copy, ref.shape

    def wait(self):
        if self.copy is not None:
            self.copy.wait()
            self.copy = None

    def __getitem__(self, index):
        self.wait()
        return self.ref[index]


def kernel(body, out_shape, *args, count=None, flops=0, moved=0, staged=False, limit=48):
    scalars = [] if count is None else [count]
    first, last = len(scalars), len(scalars) + len(args)

    def run(*refs):
        buffers, arrived = refs[-len(args) - 1 : -1], refs[-1]
        inputs = []
        for n, (source, buffer) in enumerate(zip(refs[first:last], buffers)):
            copy = pltpu.make_async_copy(source, buffer, arrived.at[n])
            copy.start()
            inputs.append(Late(buffer, copy))
        body(*refs[:first], *inputs, *refs[last : -len(args) - 1])
        for late in inputs:
            late.wait()

    scratch = [pltpu.VMEM(a.shape, a.dtype) for a in args] + [pltpu.SemaphoreType.DMA((len(args),))]
    space = pltpu.HBM if staged else pltpu.VMEM
    return pl.pallas_call(
        run if staged else body,
        out_shape=out_shape,
        in_specs=[pl.BlockSpec(memory_space=pltpu.SMEM)] * first
        + [pl.BlockSpec(memory_space=space)] * len(args),
        scratch_shapes=scratch if staged else (),
        compiler_params=pltpu.CompilerParams(vmem_limit_bytes=limit << 20),
        cost_estimate=pl.CostEstimate(flops=flops, bytes_accessed=moved, transcendentals=0),
    )(*scalars, *args)


def low(*shape):
    return jax.ShapeDtypeStruct(shape, LOW)


def wide(*shape):
    return jax.ShapeDtypeStruct(shape, WIDE)


QBIAS, VBIAS, EBIAS = 6, 7, 8


def pack_body(*refs):
    weights, vectors, biases = refs[:3], refs[3:9], refs[9:12]
    message, lines = refs[12:]
    ways = lax.axis_size("fsdp")
    mine = lax.axis_index("fsdp")
    share, columns = weights[0].shape
    lines[...] = jnp.zeros_like(lines)
    for n, ref in enumerate(vectors):
        lines[n : n + 1, :share] = ref[...].reshape(1, -1).astype(WIDE)
    for n, ref in zip((QBIAS, VBIAS, EBIAS), biases):
        groups, size = ref.shape
        each = size * ways
        row = lax.broadcasted_iota(jnp.int32, (size, groups * each), 0)
        column = lax.broadcasted_iota(jnp.int32, (size, groups * each), 1)
        within = column
        for g in range(1, groups):
            within = jnp.where(column >= g * each, column - g * each, within)
        tiled = dot(ref[...], (within == row + mine * size).astype(LOW))
        group = lax.broadcasted_iota(jnp.int32, tiled.shape, 0)
        column = lax.broadcasted_iota(jnp.int32, tiled.shape, 1)
        keep = (column >= group * each) & (column < (group + 1) * each)
        flat = jnp.sum(jnp.where(keep, tiled, 0.0), 0, keepdims=True)
        for at in range(0, groups * each, share):
            part = flat[:, at : at + share]
            lines[n + at // share : n + at // share + 1, : part.shape[1]] = part
    message[share:, :] = lines[...].astype(LOW)
    for n, w in enumerate(weights):
        message[:share, n * columns : (n + 1) * columns] = w[...]


def merge(own, got, out):
    share = out.shape[1] // 2
    out[...] = jnp.zeros_like(out)
    mine, theirs = own[...], got[got.shape[0] - own.shape[0] :, :].astype(WIDE)
    out[:QBIAS, :share] = mine[:QBIAS, :share]
    out[:QBIAS, share:] = theirs[:QBIAS, :share]
    both = mine + theirs
    out[QBIAS : EBIAS + 1, :share] = both[QBIAS : EBIAS + 1, :share]
    out[EBIAS : EBIAS + 1, share:] = both[EBIAS + 1 : EBIAS + 2, :share]


def normed_rows(values):
    center = values - jnp.mean(values, -1, keepdims=True)
    return center * lax.rsqrt(jnp.mean(center * center, -1, keepdims=True) + EPS)


def norm_back_rows(values, gain, upstream):
    center = values - jnp.mean(values, -1, keepdims=True)
    spread = lax.rsqrt(jnp.mean(center * center, -1, keepdims=True) + EPS)
    xhat = center * spread
    z = upstream * gain
    grad = spread * (
        z - jnp.mean(z, -1, keepdims=True) - xhat * jnp.mean(z * xhat, -1, keepdims=True)
    )
    return grad, xhat


def third_of(message, n, size, features):
    return message[:size, n * features : (n + 1) * features]


def key_bias(count, shape, axis, seq):
    step = lax.broadcasted_iota(jnp.int32, shape, axis)
    place = lax.axis_index("context")
    core = lax.axis_index("tensor") & 1
    half = seq // 2
    position = step
    for b in range(shape[axis] // half):
        start = (place ^ (b // 2)) * seq + (core ^ (b % 2)) * half
        position = jnp.where(step >= b * half, step + (start - b * half), position)
    return jnp.where(position < count[0], 0.0, -1e30).astype(WIDE)


def head_mask(shape, head, head_dim):
    lane = lax.broadcasted_iota(jnp.int32, shape, 1)
    return (lane >= head * head_dim) & (lane < (head + 1) * head_dim)


def attend_rows(heads, head_dim, start, rows, qkv, bias):
    features = heads * head_dim
    q = qkv[start : start + rows, :features]
    k = qkv[:, features : 2 * features]
    v = qkv[:, 2 * features :]
    scale = head_dim**-0.5
    total = jnp.zeros((rows, features), WIDE)
    for h in range(heads):
        mine = head_mask(q.shape, h, head_dim)
        scores = dot_rt(jnp.where(mine, q, jnp.zeros_like(q)), k) * scale + bias
        raw = jnp.exp(scores - jnp.max(scores, -1, keepdims=True))
        got = dot(raw.astype(LOW), v) / jnp.sum(raw, -1, keepdims=True)
        total = jnp.where(mine, got, total)
    return total.astype(LOW)


def first_body(heads, head_dim, blocks, ways, count, *refs):
    pieces, refs = refs[:blocks], refs[blocks:]
    packed, lines, refs = refs[:ways], refs[ways], refs[ways + 1 :]
    vec, xhat, normed, qkv, context = refs
    rows = pieces[0].shape[0]
    if ways == 2:
        merge(lines, packed[1], vec)
    else:
        vec[...] = lines[...]
    features = heads * head_dim
    for n, piece in enumerate(pieces):
        part = normed_rows(piece[...].astype(WIDE))
        xhat[n * rows : (n + 1) * rows, :] = part.astype(LOW)
        normed[n * rows : (n + 1) * rows, :] = (part * vec[0:1, :] + vec[1:2, :]).astype(LOW)
    size = normed.shape[1] // ways
    for n, row in enumerate((QBIAS, None, VBIAS)):
        got = sum(
            dot(normed[:, i * size : (i + 1) * size], third_of(w, n, size, features))
            for i, w in enumerate(packed)
        )
        if row is not None:
            got = got + vec[row : row + 1, :features]
        qkv[:, n * features : (n + 1) * features] = got.astype(LOW)
    bias = key_bias(count, (1, blocks * rows), 1, 2 * rows)
    context[...] = attend_rows(heads, head_dim, 0, 2 * rows, qkv, bias)


def out_body(ways, *refs):
    context, weights, (keep, send) = refs[0], refs[1 : 1 + ways], refs[1 + ways :]
    rows, size = keep.shape[0], keep.shape[1] // ways
    for i, w in enumerate(weights):
        part = dot(context[...], w[...]).astype(LOW)
        keep[:, i * size : (i + 1) * size] = part[:rows]
        send[:, i * size : (i + 1) * size] = part[rows:]


def rest_body(heads, head_dim, start, count, qkv, out):
    bias = key_bias(count, (1, qkv.shape[0]), 1, start)
    out[...] = attend_rows(heads, head_dim, start, out.shape[0], qkv, bias)


def second_body(tokens, near, far, vec, hidden, normed):
    total = tokens[...].astype(WIDE) + (near[...].astype(WIDE) + far[...].astype(WIDE))
    total = total + vec[2:3, :]
    hidden[...] = total
    normed[...] = (normed_rows(total) * vec[3:4, :] + vec[4:5, :]).astype(LOW)


def forward_body(blocks, ways, *refs):
    normed, cots, refs = refs[:blocks], refs[blocks : 2 * blocks], refs[2 * blocks :]
    vec, expand, reduce = refs[0], refs[1 : 1 + ways], refs[1 + ways : 1 + 2 * ways]
    normed_all, cot_all, act, grad, keep, send, out_keep, out_send, unit_sum, cot_sum = refs[
        1 + 2 * ways :
    ]
    rows = normed[0].shape[0]
    size = normed_all.shape[1] // ways
    units = act.shape[1]
    total = jnp.zeros((1, normed_all.shape[1]), WIDE)
    for n in range(blocks):
        normed_all[n * rows : (n + 1) * rows, :] = normed[n][...]
        cot_all[n * rows : (n + 1) * rows, :] = cots[n][...]
        total = total + jnp.sum(cots[n][...].astype(WIDE), 0, keepdims=True)
    cot_sum[...] = total
    step = min(256, units, size)
    back = [jnp.zeros((2 * rows, size), WIDE) for _ in range(ways)]
    out = [jnp.zeros((2 * rows, size), WIDE) for _ in range(ways)]
    for at in range(0, units, step):
        columns = slice(at, at + step)
        expands = [w[:, columns] for w in expand]
        reduces = [w[columns, :] for w in reduce]
        sides = [slice(i * size, (i + 1) * size) for i in range(ways)]
        value = sum(dot(normed_all[:, c], w) for c, w in zip(sides, expands))
        value = value + vec[EBIAS : EBIAS + 1, columns]
        cdf = 0.5 * (1.0 + lax.erf(value * (2.0**-0.5)))
        act[:, columns] = (value * cdf).astype(LOW)
        slope = cdf + value * jnp.exp(-0.5 * value * value) * 0.3989422804014327
        part = sum(dot_rt(cot_all[:, c], w) for c, w in zip(sides, reduces))
        part = (part * slope).astype(LOW)
        grad[:, columns] = part
        unit_sum[0:1, columns] = jnp.sum(part.astype(WIDE), 0, keepdims=True)
        own = act[: 2 * rows, columns]
        for i in range(ways):
            back[i] = back[i] + dot_rt(part[: 2 * rows], expands[i])
            out[i] = out[i] + dot(own, reduces[i])
    for i, c in enumerate(sides):
        keep[:, c] = back[i][:rows].astype(LOW)
        send[:, c] = back[i][rows:].astype(LOW)
        out_keep[:, c] = out[i][:rows].astype(LOW)
        out_send[:, c] = out[i][rows:].astype(LOW)


def second_back_body(near, far, hidden, cot, vec, grad_hidden, grad_branch, sums):
    upstream = near[...].astype(WIDE) + far[...].astype(WIDE)
    grad, xhat = norm_back_rows(hidden[...], vec[3:4, :], upstream)
    total = grad + cot[...].astype(WIDE)
    grad_hidden[...] = total
    grad_branch[...] = total.astype(LOW)
    sums[0:1, :] = jnp.sum(upstream * xhat, 0, keepdims=True)
    sums[1:2, :] = jnp.sum(upstream, 0, keepdims=True)


def attend_back_body(heads, head_dim, blocks, ways, count, *refs):
    pieces, refs = refs[:blocks], refs[blocks:]
    outs, qkv, packed = refs[:ways], refs[ways], refs[ways + 1 : 2 * ways + 1]
    normed = refs[2 * ways + 1]
    branch, grad_qkv, keep, send, sums, head_sums, away = refs[2 * ways + 2 :]
    rows = pieces[0].shape[0]
    features = heads * head_dim
    for n, piece in enumerate(pieces):
        branch[n * rows : (n + 1) * rows, :] = piece[...]
    size = branch.shape[1] // ways
    g = sum(
        dot_rt(branch[:, i * size : (i + 1) * size], w[...]) for i, w in enumerate(outs)
    ).astype(LOW)
    bias = key_bias(count, (branch.shape[0], 1), 0, 2 * rows)
    q = qkv[:, :features]
    k = qkv[:, features : 2 * features]
    v = qkv[:, 2 * features :]
    scale = head_dim**-0.5
    zero = jnp.zeros_like(q)
    totals = [jnp.zeros(q.shape, WIDE) for _ in range(3)]
    for h in range(heads):
        mine = head_mask(q.shape, h, head_dim)
        scores = dot_rt(k, jnp.where(mine, q, zero)) * scale + bias
        raw = jnp.exp(scores - jnp.max(scores, 0, keepdims=True))
        probs = raw * (1.0 / jnp.sum(raw, 0, keepdims=True))
        grad_probs = dot_rt(v, jnp.where(mine, g, zero))
        delta = jnp.sum(probs * grad_probs, 0, keepdims=True)
        grad_scores = (probs * (grad_probs - delta)).astype(LOW)
        totals[0] = jnp.where(mine, dot_lt(grad_scores, k) * scale, totals[0])
        totals[1] = jnp.where(mine, dot(grad_scores, q) * scale, totals[1])
        totals[2] = jnp.where(mine, dot(probs.astype(LOW), g), totals[2])
    for n in range(3):
        part = totals[n].astype(LOW)
        grad_qkv[:, n * features : (n + 1) * features] = part
        head_sums[0:1, n * features : (n + 1) * features] = jnp.sum(
            part.astype(WIDE), 0, keepdims=True
        )
    for i in range(ways):
        part = sum(
            dot_rt(
                grad_qkv[: 2 * rows, n * features : (n + 1) * features],
                third_of(packed[i], n, size, features),
            )
            for n in range(3)
        ).astype(LOW)
        keep[:, i * size : (i + 1) * size] = part[:rows]
        send[:, i * size : (i + 1) * size] = part[rows:]
    sums[...] = jnp.sum(branch[...].astype(WIDE), 0, keepdims=True)
    away[...] = dot_lt(normed[:, normed.shape[1] - away.shape[0] :], grad_qkv[...]).astype(LOW)


def first_sums_body(ways, grad_qkv, xhat, *refs):
    packed, out = refs[:ways], refs[ways]
    features = grad_qkv.shape[1] // 3
    size = xhat.shape[1] // ways
    for i in range(ways):
        part = sum(
            dot_rt(
                grad_qkv[:, n * features : (n + 1) * features],
                third_of(packed[i], n, size, features),
            )
            for n in range(3)
        )
        columns = slice(i * size, (i + 1) * size)
        out[0:1, columns] = jnp.sum(part * xhat[:, columns].astype(WIDE), 0, keepdims=True)
        out[1:2, columns] = jnp.sum(part, 0, keepdims=True)


def thirds_body(own, got, *outs):
    size = outs[0].shape[1]
    for n, out in enumerate(outs):
        columns = slice(n * size, (n + 1) * size)
        out[...] = own[:, columns] + got[:, columns].astype(WIDE)


def first_back_body(near, far, tokens, grad_hidden, vec, out):
    upstream = near[...].astype(WIDE) + far[...].astype(WIDE)
    grad, _ = norm_back_rows(tokens[...].astype(WIDE), vec[0:1, :], upstream)
    out[...] = grad + grad_hidden[...]


def on_device(
    tokens,
    cotangent,
    valid_count,
    gain_first,
    shift_first,
    query_weight,
    query_bias,
    key_weight,
    value_weight,
    value_bias,
    output_weight,
    output_bias,
    gain_second,
    shift_second,
    expand_weight,
    expand_bias,
    reduce_weight,
    reduce_bias,
):
    images, seq, width = tokens.shape
    ways = lax.axis_size("fsdp")
    pair = ways == 2
    parts = 2 if pair else 1
    cycle = lax.axis_size("context")
    mine = lax.axis_index("fsdp")
    place = lax.axis_index("context")
    core = lax.axis_index("tensor") & 1
    share = gain_first.shape[0]
    heads = query_bias.shape[1]
    head_dim = query_bias.shape[0] * ways
    features = heads * head_dim
    units = expand_weight.shape[1]
    half = seq // 2
    blocks = 2 * cycle
    length = cycle * seq
    second = mine == 1

    def turned(value):
        if not pair:
            return value
        left, right = jnp.split(value, 2, -1)
        return jnp.where(second, jnp.concatenate([right, left], -1), value)

    def piece_of(value, which):
        return turned(lax.dynamic_slice_in_dim(value.reshape(seq, width), which * half, half, 0))

    token_piece = piece_of(tokens, core)
    mine_tokens = spread_context(token_piece)
    token_pieces = woven(
        mine_tokens,
        [piece_of(tokens, 1 - core)] + [swap(m, "tensor", 1) for m in mine_tokens[1:]],
    )
    vectors = (gain_first, shift_first, output_bias, gain_second, shift_second, reduce_bias)
    biases = (query_bias, value_bias, expand_bias)
    thirds = (query_weight, key_weight, value_weight)

    if pair:
        across = lambda v: swap(v, "fsdp", 1)
        message, lines = kernel(
            pack_body,
            (low(share + 16, 3 * features), wide(16, 3 * features)),
            after(query_weight, token_piece),
            key_weight,
            value_weight,
            *vectors,
            *(b.T for b in biases),
            staged=True,
            limit=62,
        )
        first = across(message)
        packed = (message, first)
        output_parts = (output_weight, across(after(output_weight, message)))
        expand_parts = (expand_weight, across(after(expand_weight, first)))
        reduce_parts = (reduce_weight, across(after(reduce_weight, first)))
    else:
        gather = lambda v, axis=0: lax.all_gather(v, "fsdp", axis=axis, tiled=True)
        rows = [gather(v).reshape(1, -1) for v in vectors]
        rows += [gather(b).T.reshape(1, -1) for b in biases]
        lines = jnp.concatenate(
            [jnp.pad(r, ((0, 0), (0, width - r.shape[1]))) for r in rows]
            + [jnp.zeros((16 - len(rows), width), LOW)],
            0,
        ).astype(WIDE)
        packed = (jnp.concatenate([gather(w) for w in thirds], 1),)
        output_parts = (gather(output_weight, 1),)
        expand_parts = (gather(expand_weight),)
        reduce_parts = (gather(reduce_weight, 1),)

    vec, xhat_all, normed_all, qkv, context_own = kernel(
        lambda *refs: first_body(heads, head_dim, blocks, parts, *refs),
        (
            wide(16, width),
            low(length, width),
            low(length, width),
            low(length, 3 * features),
            low(seq, features),
        ),
        *token_pieces,
        *packed,
        lines,
        count=valid_count,
        flops=6 * length * width * features,
        moved=10 * length * width,
    )
    keep, send = kernel(
        lambda *refs: out_body(parts, *refs),
        (low(half, width), low(half, width)),
        context_own,
        *output_parts,
    )
    cot_piece = piece_of(cotangent, core)
    mine_cots = spread_context(after(cot_piece, mine_tokens[-1]))
    cots = woven(mine_cots, [swap(m, "tensor", 1) for m in mine_cots])
    near, far = last_terms(keep, send)
    near = after(near, *cots)
    hidden, normed_piece = kernel(
        second_body, (wide(half, width), low(half, width)), token_piece, near, far, vec
    )

    context_rest = kernel(
        lambda *refs: rest_body(heads, head_dim, seq, *refs),
        low(length - seq, features),
        after(qkv, near),
        count=valid_count,
    )
    mine_normed = spread_context(normed_piece)
    theirs = [swap(m, "tensor", 1) for m in mine_normed[:1]]
    mine_normed[1:] = [after(m, context_rest, expand_parts[-1]) for m in mine_normed[1:]]
    theirs += [swap(m, "tensor", 1) for m in mine_normed[1:]]
    (
        normed_two,
        cot_all,
        activated,
        grad_expanded,
        keep,
        send,
        out_keep,
        out_send,
        unit_sum,
        cot_sum,
    ) = kernel(
        lambda *refs: forward_body(blocks, parts, *refs),
        (low(length, width),) * 2
        + (low(length, units),) * 2
        + (low(half, width),) * 4
        + (wide(1, units), wide(1, width)),
        *woven(mine_normed, theirs),
        *cots,
        vec,
        *expand_parts,
        *reduce_parts,
        flops=10 * length * width * units,
        moved=12 * length * width,
        staged=True,
        limit=62,
    )
    near, far = last_terms(keep, send)
    grad_hidden, grad_piece, norm_sums = kernel(
        second_back_body,
        (wide(half, width), low(half, width), wide(2, width)),
        near,
        far,
        hidden,
        cot_piece,
        vec,
    )

    def scatter(value, axis):
        return lax.psum_scatter(value.astype(LOW), "fsdp", scatter_dimension=axis, tiled=True)

    def weight_grad(left, right, along):
        if not pair:
            return scatter(dot_lt(left, right), along).astype(WIDE)
        if along:
            own, other = segments(right, 2)
            away = across(dot_lt(left, other).astype(LOW))
            return pin(dot_lt(left, own)) + away.astype(WIDE)
        own, other = segments(left, 2)
        away = across(dot_lt(other, right).astype(LOW))
        return pin(dot_lt(own, right)) + away.astype(WIDE)

    if pair:
        many = units // 2
        act_half = lax.dynamic_slice_in_dim(activated, (place & 1) * many, many, 1)
        cot_own, cot_other = segments(cot_all, 2)
        normed_own, normed_other = segments(normed_two, 2)
        reduce_got = across(dot_lt(act_half, cot_other).astype(LOW))
        reduce_half = pin((dot_lt(act_half, cot_own) + reduce_got.astype(WIDE)).astype(LOW))
        expand_got = across(dot_lt(normed_other, grad_expanded).astype(LOW))
        grad_expand = pin(dot_lt(normed_own, grad_expanded)) + expand_got.astype(WIDE)

        def both_halves(value, theirs, axis):
            odd = (place & 1) != 0
            return jnp.concatenate(
                [jnp.where(odd, theirs, value), jnp.where(odd, value, theirs)], axis
            ).astype(WIDE)

    else:
        grad_reduce = weight_grad(activated, cot_all, 1)
        grad_expand = weight_grad(normed_two, grad_expanded, 0)

    mine_grads = spread_context(grad_piece)
    theirs = [swap(m, "tensor", 1) for m in mine_grads[:1]]
    if pair:
        mine_grads[1:] = [after(m, reduce_got) for m in mine_grads[1:]]
    theirs += [swap(m, "tensor", 1) for m in mine_grads[1:]]
    grad_branch, grad_qkv, keep, send, branch_sum, head_sum, away = kernel(
        lambda *refs: attend_back_body(heads, head_dim, blocks, parts, *refs),
        (
            low(length, width),
            low(length, 3 * features),
            low(half, width),
            low(half, width),
            wide(1, width),
            wide(1, 3 * features),
            low(width // parts, 3 * features),
        ),
        *woven(mine_grads, theirs),
        *output_parts,
        qkv,
        *packed,
        normed_all,
        count=valid_count,
        flops=10 * length * length * features,
        moved=8 * length * width,
    )
    if pair:
        qkv_got = across(away)
    near, far = last_terms(keep, send)
    if pair:
        reduce_theirs = swap(after(reduce_half, mine_grads[-1]), "context", 1)
        qkv_far = far
        near = after(near, reduce_theirs, expand_got, qkv_got)
        grad_reduce = both_halves(reduce_half, reduce_theirs, 0)
    grad_token_piece = kernel(
        first_back_body, wide(half, width), near, far, token_piece, grad_hidden, vec
    )

    def both_cores(value):
        theirs = swap(value, "tensor", 1)
        upper = core == 1
        return turned(
            jnp.concatenate([jnp.where(upper, theirs, value), jnp.where(upper, value, theirs)], 0)
        ).reshape(tokens.shape)

    grad_tokens = both_cores(grad_token_piece)

    if pair:
        grad_query, grad_key, grad_value = kernel(
            thirds_body,
            (wide(share, features),) * 3,
            dot_lt(segments(normed_all, 2)[0], grad_qkv),
            qkv_got,
        )
    else:
        grad_weights = scatter(dot_lt(normed_all, grad_qkv), 0).astype(WIDE)
        grad_query, grad_key, grad_value = jnp.split(grad_weights, 3, 1)

    near, far = last_terms(after(out_keep, grad_piece), after(out_send, grad_piece))
    reduced = near.astype(WIDE) + far.astype(WIDE) + vec[5:6, :]
    output = both_cores((hidden + reduced).astype(LOW))

    def own_rows(value):
        size = value.shape[0] // ways
        return lax.dynamic_slice_in_dim(value, mine * size, size, 0)

    context_all = jnp.concatenate([context_own, context_rest], 0)
    if pair:
        context_all = after(context_all, qkv_far)
    grad_output = weight_grad(context_all, grad_branch, 1)

    first_sums = kernel(
        lambda *refs: first_sums_body(parts, *refs), wide(2, width), grad_qkv, xhat_all, *packed
    )
    bit = 1
    while bit < lax.axis_size("tensor"):
        first_sums = first_sums + swap(first_sums, "tensor", bit)
        bit *= 2
    norm_sums = after(norm_sums, mine_grads[-1])
    norm_sums = norm_sums + swap(norm_sums, "tensor", 1)
    bit = 1
    while bit < cycle:
        norm_sums = norm_sums + swap(norm_sums, "context", bit)
        bit *= 2
    sums = jnp.concatenate([first_sums, norm_sums, branch_sum, cot_sum], 0)
    plain = jnp.concatenate(
        [jnp.pad(head_sum, ((0, 0), (0, width - 3 * features))), unit_sum], 0
    )
    if pair:
        own, other = segments(sums, 2)
        got = across(jnp.concatenate([other, *segments(plain, 2)], 0))
        sums = own + got[:6]
        plain = plain + jnp.concatenate([got[6:8], got[8:10]], 1)
    else:
        sums = scatter(sums, 1).astype(WIDE)
        plain = lax.psum(plain, "fsdp")
    grad_ebias = own_rows(plain[1].reshape(-1, expand_bias.shape[0] * ways).T)
    grad_qbias, grad_vbias = (
        own_rows(plain[0, n * features : (n + 1) * features].reshape(heads, head_dim).T)
        for n in (0, 2)
    )
    return (
        output,
        grad_tokens,
        sums[0],
        sums[1],
        grad_query,
        grad_qbias,
        grad_key,
        grad_value,
        grad_vbias,
        grad_output,
        sums[4],
        sums[2],
        sums[3],
        grad_expand,
        grad_ebias,
        grad_reduce,
        sums[5],
    )


def solution(mesh):
    rows = P("fsdp", "context", None)
    vector = P("fsdp")
    split = P("fsdp", "tensor")
    turned = P("tensor", "fsdp")
    in_specs = (rows, rows, vector, vector, vector, split, split, split, split, split)
    in_specs += (turned, vector, vector, vector, split, split, turned, vector)
    out_specs = (rows, rows, vector, vector, split, split, split, split, split)
    out_specs += (turned, vector, vector, vector, split, split, turned, vector)
    return jax.shard_map(
        on_device, mesh=mesh, in_specs=in_specs, out_specs=out_specs, check_vma=False
    )
```

time: 199 us -> 177 us (0.89)
  waiting for transfers between devices: 91.1 us -> 58.9 us
  Pallas kernels: 18.2 us -> 34.8 us
  matrix products: 22.6 us -> 10.7 us
  starting transfers between devices: 46 us -> 53 us
  local copies, waits for them, and re-layouts: 7.55 us -> 5.51 us
    ppermute x54 -> x52, waiting for transfers between devices: 91.1 us -> 58.9 us  [swap(): lax.ppermute(block, axis, [(i, i ^ bit) for i in range(lax.axis_size(axis...]
    pallas_call x9 -> x11, Pallas kernels: 18.2 us -> 34.8 us  [kernel(): pl.pallas_call(run if staged else body, out_shape=out_shape, in_specs=[pl...]
    dot_general x12 -> x0, matrix products: 7.84 us -> none  [the longest x6 4.61 us: dot_rt(): lax.dot_general(left, right, (((1,), (1,)), ((), ())), preferred_element_...]
    ppermute x54 -> x52, starting transfers between devices: 46 us -> 53 us  [swap(): lax.ppermute(block, axis, [(i, i ^ bit) for i in range(lax.axis_size(axis...]
    dot_general x8 -> x7, matrix products: 14.7 us -> 10.7 us  [dot_lt(): lax.dot_general(left, right, (((0,), (0,)), ((), ())), preferred_element_...]
    add x2 -> x1, other arithmetic: 3.88 us -> 0.87 us  [weight_grad(): return pin(dot_lt(left, own)) + away.astype(WIDE)]
  transfers between devices with their start and end apart: 54 -> 52, of which waited for: 21 -> 18; matrix products, arithmetic and copies ran while one was open for 15% -> 13% of each run, Pallas kernels for 9% -> 13%
where the time goes in v4:
time: 177 us
  waiting for transfers between devices  58.9 us (33%)
  starting transfers between devices  53 us (30%)
  Pallas kernels  34.8 us (20%)
  other arithmetic  11.7 us (7%)
  matrix products  10.7 us (6%)
  local copies, waits for them, and re-layouts  5.51 us (3%)
  between operations  2.11 us (1%)
    ppermute x52, waiting for transfers between devices, swap(): lax.ppermute(block, axis, [(i, i ^ bit) for i in range(lax.axis_size(axis...  58.9 us
    ppermute x52, starting transfers between devices, swap(): lax.ppermute(block, axis, [(i, i ^ bit) for i in range(lax.axis_size(axis...  53 us
    pallas_call x11, Pallas kernels, kernel(): pl.pallas_call(run if staged else body, out_shape=out_shape, in_specs=[pl...  34.8 us
    dot_general x7, matrix products, dot_lt(): lax.dot_general(left, right, (((0,), (0,)), ((), ())), preferred_element_...  10.7 us
  transfers between devices with their start and end apart: 52, of which 18 were waited for; matrix products, arithmetic and copies ran while one was open for 13% of the time, Pallas kernels for 13%

profile of v4, /device:TPU:0, one launch (start us, length us, event | category | flops | bytes accessed | tf_op | source)
XLA Modules:
  0.0 176.8 jit_solution(8170787487700510204)
XLA Ops:
  1.8 2.5 %shard_map.305 = (bf16[528,768]{1,0:T(8,128)(2,1)}, f32[16,768]{1,0:T(8,128)}) custom-call(bf16[512,256]{1,0:T(8,128)(2,1)} %refs_0_.3, bf16[512,256]{1,0:T(8,128)(2,1)} %refs_1_.2, bf16[512,256]{1,0:T(8,128)(2,1)} %refs_2_.1, bf16[512]{0:T(512)(128)(2,1)} %refs_3_.1, bf16[512]{0:T(512)(128)(2,1)} %refs_4_.1, bf16[512]{0:T(512)(128)(2,1)} %refs_5_.1, ...), custom_call_target="tpu_custom_call" | custom-call | tf_op jit(solution)/shard_map/pallas_call | solution.py:96
  4.3 3.0 %collective-permute-start.6 = (bf16[528,768]{1,0:T(8,128)(2,1)}, bf16[528,768]{1,0:T(8,128)(2,1)S(1)}, u32[]{:S(2)}, u32[]{:S(2)}) collective-permute-start(bf16[528,768]{1,0:T(8,128)(2,1)} %get-tuple-element.71.refs_9_.refs_12_.refs_2_), channel_id=1, source_target_pairs={{0,16},{16,0},{1,17},{17,1},{2,18},{18,2},{3,19},{19,3},{4,20},{20... | collective-permute-start | bytes 2433032 | tf_op jit(solution)/shard_map/ppermute | solution.py:14
  7.3 3.6 %collective-permute-start.4 = (bf16[80,1024]{1,0:T(8,128)(2,1)S(1)}, bf16[80,1024]{1,0:T(8,128)(2,1)S(1)}, u32[]{:S(2)}, u32[]{:S(2)}) collective-permute-start(bf16[80,1024]{1,0:T(8,128)(2,1)S(1)} %maximum_select_fusion.2.refs_1_.tokens), channel_id=1, source_target_pairs={{0,12},{4,8},{8,4},{12,0},{1,13},{5,9},{9,5},{13,1},{2,14},{6,10},... | collective-permute-start | bytes 491528 | tf_op jit(solution)/shard_map/ppermute | solution.py:14
  12.1 4.2 %collective-permute-done.4.refs_7_ = bf16[80,1024]{1,0:T(8,128)(2,1)S(1)} collective-permute-done((bf16[80,1024]{1,0:T(8,128)(2,1)S(1)}, bf16[80,1024]{1,0:T(8,128)(2,1)S(1)}, u32[]{:S(2)}, u32[]{:S(2)}) %collective-permute-start.4) | collective-permute-done | bytes 163872 | tf_op jit(solution)/shard_map/ppermute | solution.py:14
  16.3 8.2 %collective-permute-done.2.refs_5_ = bf16[80,1024]{1,0:T(8,128)(2,1)S(1)} collective-permute-done((bf16[80,1024]{1,0:T(8,128)(2,1)S(1)}, bf16[80,1024]{1,0:T(8,128)(2,1)S(1)}, u32[]{:S(2)}, u32[]{:S(2)}) %collective-permute-start.2) | collective-permute-done | bytes 163872 | tf_op jit(solution)/shard_map/ppermute | solution.py:14
  25.0 1.4 collective-permute-done.6.refs_10_.refs_13_.refs_3_
  26.4 2.1 %collective-permute-start.19 = (bf16[512,1024]{1,0:T(8,128)(2,1)}, bf16[512,1024]{1,0:T(8,128)(2,1)S(1)}, u32[]{:S(2)}, u32[]{:S(2)}) collective-permute-start(bf16[512,1024]{1,0:T(8,128)(2,1)} %refs_17_.1), channel_id=1, source_target_pairs={{0,16},{16,0},{1,17},{17,1},{2,18},{18,2},{3,19},{19,3},{4,20},{20... | collective-permute-start | bytes 3145736 | tf_op jit(solution)/shard_map/ppermute | solution.py:14
  29.3 4.2 %collective-permute-start.14 = (bf16[80,1024]{1,0:T(8,128)(2,1)S(1)}, bf16[80,1024]{1,0:T(8,128)(2,1)S(1)}, u32[]{:S(2)}, u32[]{:S(2)}) collective-permute-start(bf16[80,1024]{1,0:T(8,128)(2,1)S(1)} %maximum_select_fusion.4.refs_8_.cot), channel_id=1, source_target_pairs={{0,12},{4,8},{8,4},{12,0},{1,13},{5,9},{9,5},{13,1},{2,14},{6,10},... | collective-permute-start | bytes 491528 | tf_op jit(solution)/shard_map/ppermute | solution.py:14
  33.5 3.5 %shard_map.306 = (f32[16,1024]{1,0:T(8,128)S(1)}, bf16[640,1024]{1,0:T(8,128)(2,1)S(1)}, bf16[640,1024]{1,0:T(8,128)(2,1)}, bf16[640,768]{1,0:T(8,128)(2,1)S(1)}, bf16[160,256]{1,0:T(8,128)(2,1)S(1)}) custom-call(s32[1]{0:T(128)S(6)} %copy.35.refs_0_, bf16[80,1024]{1,0:T(8,128)(2,1)S(1)} %maximum_select_fusion.2.refs_1_.tokens, ...), custom_call_target="tpu_custom_call" | custom-call | flops 1006632960 | bytes 6553600 | tf_op jit(solution)/shard_map/pallas_call | solution.py:96
  37.0 1.4 shard_map.307
  39.1 4.0 %collective-permute-start.10 = (bf16[80,1024]{1,0:T(8,128)(2,1)S(1)}, bf16[80,1024]{1,0:T(8,128)(2,1)S(1)}, u32[]{:S(2)}, u32[]{:S(2)}) collective-permute-start(bf16[80,1024]{1,0:T(8,128)(2,1)S(1)} %maximum_select_fusion.4.refs_8_.cot), channel_id=1, source_target_pairs={{0,4},{4,0},{8,12},{12,8},{1,5},{5,1},{9,13},{13,9},{2,6},{6,2},{1... | collective-permute-start | bytes 491528 | tf_op jit(solution)/shard_map/ppermute | solution.py:14
  43.1 1.8 %collective-permute-done.12.refs_12_ = bf16[80,1024]{1,0:T(8,128)(2,1)S(1)} collective-permute-done((bf16[80,1024]{1,0:T(8,128)(2,1)S(1)}, bf16[80,1024]{1,0:T(8,128)(2,1)S(1)}, u32[]{:S(2)}, u32[]{:S(2)}) %collective-permute-start.12) | collective-permute-done | bytes 163872 | tf_op jit(solution)/shard_map/ppermute | solution.py:14
  45.5 2.7 %collective-permute-done.10.refs_10_ = bf16[80,1024]{1,0:T(8,128)(2,1)S(1)} collective-permute-done((bf16[80,1024]{1,0:T(8,128)(2,1)S(1)}, bf16[80,1024]{1,0:T(8,128)(2,1)S(1)}, u32[]{:S(2)}, u32[]{:S(2)}) %collective-permute-start.10) | collective-permute-done | bytes 163872 | tf_op jit(solution)/shard_map/ppermute | solution.py:14
  48.7 1.5 collective-permute-start.16
  50.2 4.6 %collective-permute-done.16.far = bf16[80,1024]{1,0:T(8,128)(2,1)S(1)} collective-permute-done((bf16[80,1024]{1,0:T(8,128)(2,1)S(1)}, bf16[80,1024]{1,0:T(8,128)(2,1)S(1)}, u32[]{:S(2)}, u32[]{:S(2)}) %collective-permute-start.16) | collective-permute-done | bytes 163872 | tf_op jit(solution)/shard_map/ppermute | solution.py:14
  55.8 2.1 %collective-permute-start.23 = (bf16[80,1024]{1,0:T(8,128)(2,1)S(1)}, bf16[80,1024]{1,0:T(8,128)(2,1)}, u32[]{:S(2)}, u32[]{:S(2)}) collective-permute-start(bf16[80,1024]{1,0:T(8,128)(2,1)S(1)} %get-tuple-element.81.refs_0_), channel_id=1, source_target_pairs={{0,12},{4,8},{8,4},{12,0},{1,13},{5,9},{9,5},{13,1},{2,14},{6,10},... | collective-permute-start | bytes 491528 | tf_op jit(solution)/shard_map/ppermute | solution.py:14
  57.9 2.3 %collective-permute-start.18 = (bf16[80,1024]{1,0:T(8,128)(2,1)S(1)}, bf16[80,1024]{1,0:T(8,128)(2,1)}, u32[]{:S(2)}, u32[]{:S(2)}) collective-permute-start(bf16[80,1024]{1,0:T(8,128)(2,1)S(1)} %get-tuple-element.81.refs_0_), channel_id=1, source_target_pairs={{0,4},{4,0},{8,12},{12,8},{1,5},{5,1},{9,13},{13,9},{2,6},{6,2},{1... | collective-permute-start | bytes 491528 | tf_op jit(solution)/shard_map/ppermute | solution.py:14
  60.2 2.4 %shard_map.309 = bf16[480,256]{1,0:T(8,128)(2,1)S(1)} custom-call(s32[1]{0:T(128)S(6)} %copy.35.refs_0_, bf16[640,768]{1,0:T(8,128)(2,1)S(1)} %get-tuple-element.83.refs_1_.refs_11_), custom_call_target="tpu_custom_call" | custom-call | tf_op jit(solution)/shard_map/pallas_call | solution.py:96
  63.3 1.6 collective-permute-done.23.refs_6_
  64.9 6.9 %collective-permute-done.21.refs_4_ = bf16[80,1024]{1,0:T(8,128)(2,1)} collective-permute-done((bf16[80,1024]{1,0:T(8,128)(2,1)S(1)}, bf16[80,1024]{1,0:T(8,128)(2,1)}, u32[]{:S(2)}, u32[]{:S(2)}) %collective-permute-start.21) | collective-permute-done | bytes 163872 | tf_op jit(solution)/shard_map/ppermute | solution.py:14
  72.3 3.9 %collective-permute-done.25.refs_20_ = bf16[1024,512]{1,0:T(8,128)(2,1)} collective-permute-done((bf16[1024,512]{1,0:T(8,128)(2,1)}, bf16[1024,512]{1,0:T(8,128)(2,1)}, u32[]{:S(2)}, u32[]{:S(2)}) %collective-permute-start.25) | collective-permute-done | bytes 1048608 | tf_op jit(solution)/shard_map/ppermute | solution.py:14
  76.3 10.2 %shard_map.310 = (bf16[640,1024]{1,0:T(8,128)(2,1)}, bf16[640,1024]{1,0:T(8,128)(2,1)}, bf16[640,1024]{1,0:T(8,128)(2,1)}, bf16[640,1024]{1,0:T(8,128)(2,1)}, bf...) custom-call(bf16[80,1024]{1,0:T(8,128)(2,1)} %copy-done.22, ...), custom_call_target="tpu_custom_call" | custom-call | flops 6710886400 | bytes 7864320 | tf_op jit(solution)/shard_map/pallas_call | solution.py:96
  86.7 2.0 %convolution_convert_fusion.1 = bf16[512,512]{1,0:T(8,128)(2,1)S(1)} fusion(bf16[640,1024]{1,0:T(8,128)(2,1)} %get-tuple-element.97, bf16[640,1024]{1,0:T(8,128)(2,1)} %get-tuple-element.96, s32[]{:T(128)S(6)} %select_n.104), kind=kOutput, calls=%fused_computation.3 | convolution fusion | flops 335806464 | bytes 1835012 | tf_op jit(solution)/shard_map/dot_general | solution.py:34
  88.6 1.8 %collective-permute-start.33 = (bf16[512,512]{1,0:T(8,128)(2,1)S(1)}, bf16[512,512]{1,0:T(8,128)(2,1)S(1)}, u32[]{:S(2)}, u32[]{:S(2)}) collective-permute-start(bf16[512,512]{1,0:T(8,128)(2,1)S(1)} %convolution_convert_fusion.1), channel_id=1, source_target_pairs={{0,16},{16,0},{1,17},{17,1},{2,18},{18,2},{3,19},{19,3},{4,20},{20... | collective-permute-start | bytes 1572872 | tf_op jit(solution)/shard_map/ppermute | solution.py:14
  90.5 1.6 collective-permute-start.27
  92.9 4.0 %collective-permute-done.27.far = bf16[80,1024]{1,0:T(8,128)(2,1)S(1)} collective-permute-done((bf16[80,1024]{1,0:T(8,128)(2,1)S(1)}, bf16[80,1024]{1,0:T(8,128)(2,1)S(1)}, u32[]{:S(2)}, u32[]{:S(2)}) %collective-permute-start.27) | collective-permute-done | bytes 163872 | tf_op jit(solution)/shard_map/ppermute | solution.py:14
  97.2 3.7 %collective-permute-start.37 = (bf16[80,1024]{1,0:T(8,128)(2,1)S(1)}, bf16[80,1024]{1,0:T(8,128)(2,1)S(1)}, u32[]{:S(2)}, u32[]{:S(2)}) collective-permute-start(bf16[80,1024]{1,0:T(8,128)(2,1)S(1)} %get-tuple-element.92.refs_1_), channel_id=1, source_target_pairs={{0,12},{4,8},{8,4},{12,0},{1,13},{5,9},{9,5},{13,1},{2,14},{6,10},... | collective-permute-start | bytes 491528 | tf_op jit(solution)/shard_map/ppermute | solution.py:14
  100.9 3.8 %fusion.1 = f32[512,1024]{1,0:T(8,128)} fusion(bf16[640,1024]{1,0:T(8,128)(2,1)} %get-tuple-element.106, bf16[640,1024]{1,0:T(8,128)(2,1)S(1)} %copy-done.42), kind=kOutput, calls=%fused_computation.10 | convolution fusion | flops 671088640 | bytes 4063232 | tf_op jit(solution)/shard_map/dot_general | solution.py:34
  105.2 2.0 %convolution_convert_fusion = bf16[512,1024]{1,0:T(8,128)(2,1)} fusion(bf16[640,1024]{1,0:T(8,128)(2,1)S(1)} %copy-done.43, bf16[640,1024]{1,0:T(8,128)(2,1)S(1)} %copy-done.42), kind=kOutput, calls=%fused_computation.1 | convolution fusion | flops 671612928 | bytes 3014656 | tf_op jit(solution)/shard_map/dot_general | solution.py:34
  107.8 3.7 %collective-permute-start.35 = (bf16[80,1024]{1,0:T(8,128)(2,1)S(1)}, bf16[80,1024]{1,0:T(8,128)(2,1)S(1)}, u32[]{:S(2)}, u32[]{:S(2)}) collective-permute-start(bf16[80,1024]{1,0:T(8,128)(2,1)S(1)} %get-tuple-element.92.refs_1_), channel_id=1, source_target_pairs={{0,8},{4,12},{8,0},{12,4},{1,9},{5,13},{9,1},{13,5},{2,10},{6,14},... | collective-permute-start | bytes 491528 | tf_op jit(solution)/shard_map/ppermute | solution.py:14
  111.5 2.1 %collective-permute-start.48 = (f32[2,1024]{1,0:T(2,128)S(1)}, f32[2,1024]{1,0:T(2,128)S(1)}, u32[]{:S(2)}, u32[]{:S(2)}) collective-permute-start(f32[2,1024]{1,0:T(2,128)S(1)} %add.92), channel_id=1, source_target_pairs={{0,4},{4,0},{8,12},{12,8},{1,5},{5,1},{9,13},{13,9},{2,6},{6,2},{1... | collective-permute-start | bytes 24584 | tf_op jit(solution)/shard_map/ppermute | solution.py:14
  113.6 1.6 collective-permute-start.29
  115.2 4.8 %collective-permute-done.48 = f32[2,1024]{1,0:T(2,128)S(1)} collective-permute-done((f32[2,1024]{1,0:T(2,128)S(1)}, f32[2,1024]{1,0:T(2,128)S(1)}, u32[]{:S(2)}, u32[]{:S(2)}) %collective-permute-start.48) | collective-permute-done | bytes 8224 | tf_op jit(solution)/shard_map/ppermute | solution.py:14
  120.0 1.4 collective-permute-start.49
  121.5 1.4 fusion
  126.0 1.5 collective-permute-start.40
  127.5 11.4 %shard_map.312 = (bf16[640,1024]{1,0:T(8,128)(2,1)}, bf16[640,768]{1,0:T(8,128)(2,1)S(1)}, bf16[80,1024]{1,0:T(8,128)(2,1)S(1)}, bf16[80,1024]{1,0:T(8,128)(2,1)...) custom-call(s32[1]{0:T(128)S(6)} %copy.35.refs_0_, ...), custom_call_target="tpu_custom_call" | custom-call | flops 1048576000 | bytes 5242880 | tf_op jit(solution)/shard_map/pallas_call | solution.py:96
  141.6 1.5 collective-permute-start.46
  143.2 2.1 %collective-permute-done.46 = f32[2,1024]{1,0:T(2,128)S(1)} collective-permute-done((f32[2,1024]{1,0:T(2,128)S(1)}, f32[2,1024]{1,0:T(2,128)S(1)}, u32[]{:S(2)}, u32[]{:S(2)}) %collective-permute-start.46) | collective-permute-done | bytes 8224 | tf_op jit(solution)/shard_map/ppermute | solution.py:14
  145.4 1.5 collective-permute-start.50
  147.8 1.5 collective-permute-done.50
  149.4 1.5 collective-permute-start.42
  154.2 1.6 collective-permute-start.43
  156.7 2.9 %collective-permute-done.43.far = bf16[80,1024]{1,0:T(8,128)(2,1)S(1)} collective-permute-done((bf16[80,1024]{1,0:T(8,128)(2,1)S(1)}, bf16[80,1024]{1,0:T(8,128)(2,1)S(1)}, u32[]{:S(2)}, u32[]{:S(2)}) %collective-permute-start.43) | collective-permute-done | bytes 163872 | tf_op jit(solution)/shard_map/ppermute | solution.py:14
  161.2 3.0 %convert_add_fusion = f32[512,1024]{1,0:T(8,128)} fusion(f32[512,1024]{1,0:T(8,128)S(1)} %copy-done.25, bf16[512,1024]{1,0:T(8,128)(2,1)} %collective-permute-done.41), kind=kLoop, calls=%fused_computation | loop fusion | flops 1048576 | bytes 5242880 | tf_op jit(solution)/shard_map/add | solution.py:584
  165.5 4.5 %collective-permute-done.42.got = bf16[512,768]{1,0:T(8,128)(2,1)S(1)} collective-permute-done((bf16[512,768]{1,0:T(8,128)(2,1)}, bf16[512,768]{1,0:T(8,128)(2,1)S(1)}, u32[]{:S(2)}, u32[]{:S(2)}) %collective-permute-start.42) | collective-permute-done | bytes 786464 | tf_op jit(solution)/shard_map/ppermute | solution.py:14
  170.5 1.6 maximum_convert_fusion
  172.1 1.5 collective-permute-done.51
  (211 shorter events, 26.6 us)
Async XLA Ops:
  4.3 22.1 %collective-permute-start.6 = (bf16[528,768]{1,0:T(8,128)(2,1)}, bf16[528,768]{1,0:T(8,128)(2,1)S(1)}, u32[]{:S(2)}, u32[]{:S(2)}) collective-permute-start(bf16[528,768]{1,0:T(8,128)(2,1)} %get-tuple-element.71.refs_9_.refs_12_.refs_2_), channel_id=1, source_target_pairs={{0,16},{16,0},{1,17},{17,1},{2,18},{18,2},{3,19},{19,3},{4,20},{20... | collective-permute-start | bytes 2433032 | tf_op jit(solution)/shard_map/ppermute | solution.py:14
  7.3 9.0 %collective-permute-start.4 = (bf16[80,1024]{1,0:T(8,128)(2,1)S(1)}, bf16[80,1024]{1,0:T(8,128)(2,1)S(1)}, u32[]{:S(2)}, u32[]{:S(2)}) collective-permute-start(bf16[80,1024]{1,0:T(8,128)(2,1)S(1)} %maximum_select_fusion.2.refs_1_.tokens), channel_id=1, source_target_pairs={{0,12},{4,8},{8,4},{12,0},{1,13},{5,9},{9,5},{13,1},{2,14},{6,10},... | collective-permute-start | bytes 491528 | tf_op jit(solution)/shard_map/ppermute | solution.py:14
  10.9 13.6 %collective-permute-start.2 = (bf16[80,1024]{1,0:T(8,128)(2,1)S(1)}, bf16[80,1024]{1,0:T(8,128)(2,1)S(1)}, u32[]{:S(2)}, u32[]{:S(2)}) collective-permute-start(bf16[80,1024]{1,0:T(8,128)(2,1)S(1)} %maximum_select_fusion.2.refs_1_.tokens), channel_id=1, source_target_pairs={{0,8},{4,12},{8,0},{12,4},{1,9},{5,13},{9,1},{13,5},{2,10},{6,14},... | collective-permute-start | bytes 491528 | tf_op jit(solution)/shard_map/ppermute | solution.py:14
  10.9 13.6 %collective-permute-start = (bf16[80,1024]{1,0:T(8,128)(2,1)S(1)}, bf16[80,1024]{1,0:T(8,128)(2,1)S(1)}, u32[]{:S(2)}, u32[]{:S(2)}) collective-permute-start(bf16[80,1024]{1,0:T(8,128)(2,1)S(1)} %maximum_select_fusion.2.refs_1_.tokens), channel_id=1, source_target_pairs={{0,4},{4,0},{8,12},{12,8},{1,5},{5,1},{9,13},{13,9},{2,6},{6,2},{1... | collective-permute-start | bytes 491528 | tf_op jit(solution)/shard_map/ppermute | solution.py:14
  11.7 25.3 %collective-permute-start.7 = (bf16[256,512]{1,0:T(8,128)(2,1)}, bf16[256,512]{1,0:T(8,128)(2,1)S(1)}, u32[]{:S(2)}, u32[]{:S(2)}) collective-permute-start(bf16[256,512]{1,0:T(8,128)(2,1)} %refs_9_.1), channel_id=1, source_target_pairs={{0,16},{16,0},{1,17},{17,1},{2,18},{18,2},{3,19},{19,3},{4,20},{20... | collective-permute-start | bytes 786440 | tf_op jit(solution)/shard_map/ppermute | solution.py:14
  16.3 12.9 %collective-permute-start.5 = (bf16[80,1024]{1,0:T(8,128)(2,1)S(1)}, bf16[80,1024]{1,0:T(8,128)(2,1)S(1)}, u32[]{:S(2)}, u32[]{:S(2)}) collective-permute-start(bf16[80,1024]{1,0:T(8,128)(2,1)S(1)} %collective-permute-done.4.refs_7_), channel_id=1, source_target_pairs={{0,1},{1,0},{2,3},{3,2},{4,5},{5,4},{6,7},{7,6},{8,9},{9,8},{10,11... | collective-permute-start | bytes 491528 | tf_op jit(solution)/shard_map/ppermute | solution.py:14
  24.5 4.8 %collective-permute-start.3 = (bf16[80,1024]{1,0:T(8,128)(2,1)S(1)}, bf16[80,1024]{1,0:T(8,128)(2,1)S(1)}, u32[]{:S(2)}, u32[]{:S(2)}) collective-permute-start(bf16[80,1024]{1,0:T(8,128)(2,1)S(1)} %collective-permute-done.2.refs_5_), channel_id=1, source_target_pairs={{0,1},{1,0},{2,3},{3,2},{4,5},{5,4},{6,7},{7,6},{8,9},{9,8},{10,11... | collective-permute-start | bytes 491528 | tf_op jit(solution)/shard_map/ppermute | solution.py:14
  24.5 9.0 %collective-permute-start.1 = (bf16[80,1024]{1,0:T(8,128)(2,1)S(1)}, bf16[80,1024]{1,0:T(8,128)(2,1)S(1)}, u32[]{:S(2)}, u32[]{:S(2)}) collective-permute-start(bf16[80,1024]{1,0:T(8,128)(2,1)S(1)} %collective-permute-done.refs_3_), channel_id=1, source_target_pairs={{0,1},{1,0},{2,3},{3,2},{4,5},{5,4},{6,7},{7,6},{8,9},{9,8},{10,11... | collective-permute-start | bytes 491528 | tf_op jit(solution)/shard_map/ppermute | solution.py:14
  26.4 38.5 %collective-permute-start.19 = (bf16[512,1024]{1,0:T(8,128)(2,1)}, bf16[512,1024]{1,0:T(8,128)(2,1)S(1)}, u32[]{:S(2)}, u32[]{:S(2)}) collective-permute-start(bf16[512,1024]{1,0:T(8,128)(2,1)} %refs_17_.1), channel_id=1, source_target_pairs={{0,16},{16,0},{1,17},{17,1},{2,18},{18,2},{3,19},{19,3},{4,20},{20... | collective-permute-start | bytes 3145736 | tf_op jit(solution)/shard_map/ppermute | solution.py:14
  29.2 47.1 %collective-permute-start.25 = (bf16[1024,512]{1,0:T(8,128)(2,1)}, bf16[1024,512]{1,0:T(8,128)(2,1)}, u32[]{:S(2)}, u32[]{:S(2)}) collective-permute-start(bf16[1024,512]{1,0:T(8,128)(2,1)} %refs_19_.1), channel_id=1, source_target_pairs={{0,16},{16,0},{1,17},{17,1},{2,18},{18,2},{3,19},{19,3},{4,20},{20... | collective-permute-start | bytes 3145736 | tf_op jit(solution)/shard_map/ppermute | solution.py:14
  29.3 9.8 %collective-permute-start.14 = (bf16[80,1024]{1,0:T(8,128)(2,1)S(1)}, bf16[80,1024]{1,0:T(8,128)(2,1)S(1)}, u32[]{:S(2)}, u32[]{:S(2)}) collective-permute-start(bf16[80,1024]{1,0:T(8,128)(2,1)S(1)} %maximum_select_fusion.4.refs_8_.cot), channel_id=1, source_target_pairs={{0,12},{4,8},{8,4},{12,0},{1,13},{5,9},{9,5},{13,1},{2,14},{6,10},... | collective-permute-start | bytes 491528 | tf_op jit(solution)/shard_map/ppermute | solution.py:14
  33.5 11.4 %collective-permute-start.12 = (bf16[80,1024]{1,0:T(8,128)(2,1)S(1)}, bf16[80,1024]{1,0:T(8,128)(2,1)S(1)}, u32[]{:S(2)}, u32[]{:S(2)}) collective-permute-start(bf16[80,1024]{1,0:T(8,128)(2,1)S(1)} %maximum_select_fusion.4.refs_8_.cot), channel_id=1, source_target_pairs={{0,8},{4,12},{8,0},{12,4},{1,9},{5,13},{9,1},{13,5},{2,10},{6,14},... | collective-permute-start | bytes 491528 | tf_op jit(solution)/shard_map/ppermute | solution.py:14
  39.1 5.9 %collective-permute-start.8 = (bf16[80,1024]{1,0:T(8,128)(2,1)S(1)}, bf16[80,1024]{1,0:T(8,128)(2,1)S(1)}, u32[]{:S(2)}, u32[]{:S(2)}) collective-permute-start(bf16[80,1024]{1,0:T(8,128)(2,1)S(1)} %get-tuple-element.76), channel_id=1, source_target_pairs={{0,1},{1,0},{2,3},{3,2},{4,5},{5,4},{6,7},{7,6},{8,9},{9,8},{10,11... | collective-permute-start | bytes 491528 | tf_op jit(solution)/shard_map/ppermute | solution.py:14
  39.1 9.1 %collective-permute-start.10 = (bf16[80,1024]{1,0:T(8,128)(2,1)S(1)}, bf16[80,1024]{1,0:T(8,128)(2,1)S(1)}, u32[]{:S(2)}, u32[]{:S(2)}) collective-permute-start(bf16[80,1024]{1,0:T(8,128)(2,1)S(1)} %maximum_select_fusion.4.refs_8_.cot), channel_id=1, source_target_pairs={{0,4},{4,0},{8,12},{12,8},{1,5},{5,1},{9,13},{13,9},{2,6},{6,2},{1... | collective-permute-start | bytes 491528 | tf_op jit(solution)/shard_map/ppermute | solution.py:14
  44.9 3.2 %collective-permute-start.9 = (bf16[80,1024]{1,0:T(8,128)(2,1)S(1)}, bf16[80,1024]{1,0:T(8,128)(2,1)S(1)}, u32[]{:S(2)}, u32[]{:S(2)}) collective-permute-start(bf16[80,1024]{1,0:T(8,128)(2,1)S(1)} %maximum_select_fusion.4.refs_8_.cot), channel_id=1, source_target_pairs={{0,1},{1,0},{2,3},{3,2},{4,5},{5,4},{6,7},{7,6},{8,9},{9,8},{10,11... | collective-permute-start | bytes 491528 | tf_op jit(solution)/shard_map/ppermute | solution.py:14
  45.0 3.7 %collective-permute-start.15 = (bf16[80,1024]{1,0:T(8,128)(2,1)S(1)}, bf16[80,1024]{1,0:T(8,128)(2,1)S(1)}, u32[]{:S(2)}, u32[]{:S(2)}) collective-permute-start(bf16[80,1024]{1,0:T(8,128)(2,1)S(1)} %collective-permute-done.14.refs_14_), channel_id=1, source_target_pairs={{0,1},{1,0},{2,3},{3,2},{4,5},{5,4},{6,7},{7,6},{8,9},{9,8},{10,11... | collective-permute-start | bytes 491528 | tf_op jit(solution)/shard_map/ppermute | solution.py:14
  48.7 6.2 %collective-permute-start.16 = (bf16[80,1024]{1,0:T(8,128)(2,1)S(1)}, bf16[80,1024]{1,0:T(8,128)(2,1)S(1)}, u32[]{:S(2)}, u32[]{:S(2)}) collective-permute-start(bf16[80,1024]{1,0:T(8,128)(2,1)S(1)} %add_convert_fusion.4.near), channel_id=1, source_target_pairs={{0,2},{1,3},{2,0},{3,1},{4,6},{5,7},{6,4},{7,5},{8,10},{9,11},{10,... | collective-permute-start | bytes 491528 | tf_op jit(solution)/shard_map/ppermute | solution.py:14
  55.8 9.1 %collective-permute-start.23 = (bf16[80,1024]{1,0:T(8,128)(2,1)S(1)}, bf16[80,1024]{1,0:T(8,128)(2,1)}, u32[]{:S(2)}, u32[]{:S(2)}) collective-permute-start(bf16[80,1024]{1,0:T(8,128)(2,1)S(1)} %get-tuple-element.81.refs_0_), channel_id=1, source_target_pairs={{0,12},{4,8},{8,4},{12,0},{1,13},{5,9},{9,5},{13,1},{2,14},{6,10},... | collective-permute-start | bytes 491528 | tf_op jit(solution)/shard_map/ppermute | solution.py:14
  57.9 13.9 %collective-permute-start.21 = (bf16[80,1024]{1,0:T(8,128)(2,1)S(1)}, bf16[80,1024]{1,0:T(8,128)(2,1)}, u32[]{:S(2)}, u32[]{:S(2)}) collective-permute-start(bf16[80,1024]{1,0:T(8,128)(2,1)S(1)} %get-tuple-element.81.refs_0_), channel_id=1, source_target_pairs={{0,8},{4,12},{8,0},{12,4},{1,9},{5,13},{9,1},{13,5},{2,10},{6,14},... | collective-permute-start | bytes 491528 | tf_op jit(solution)/shard_map/ppermute | solution.py:14
  57.9 13.9 %collective-permute-start.18 = (bf16[80,1024]{1,0:T(8,128)(2,1)S(1)}, bf16[80,1024]{1,0:T(8,128)(2,1)}, u32[]{:S(2)}, u32[]{:S(2)}) collective-permute-start(bf16[80,1024]{1,0:T(8,128)(2,1)S(1)} %get-tuple-element.81.refs_0_), channel_id=1, source_target_pairs={{0,4},{4,0},{8,12},{12,8},{1,5},{5,1},{9,13},{13,9},{2,6},{6,2},{1... | collective-permute-start | bytes 491528 | tf_op jit(solution)/shard_map/ppermute | solution.py:14
  64.9 7.5 %collective-permute-start.17 = (bf16[80,1024]{1,0:T(8,128)(2,1)S(1)}, bf16[80,1024]{1,0:T(8,128)(2,1)}, u32[]{:S(2)}, u32[]{:S(2)}) collective-permute-start(bf16[80,1024]{1,0:T(8,128)(2,1)S(1)} %get-tuple-element.81.refs_0_), channel_id=1, source_target_pairs={{0,1},{1,0},{2,3},{3,2},{4,5},{5,4},{6,7},{7,6},{8,9},{9,8},{10,11... | collective-permute-start | bytes 491528 | tf_op jit(solution)/shard_map/ppermute | solution.py:14
  71.8 4.4 %collective-permute-start.20 = (bf16[80,1024]{1,0:T(8,128)(2,1)}, bf16[80,1024]{1,0:T(8,128)(2,1)}, u32[]{:S(2)}, u32[]{:S(2)}) collective-permute-start(bf16[80,1024]{1,0:T(8,128)(2,1)} %collective-permute-done.18.refs_2_), channel_id=1, source_target_pairs={{0,1},{1,0},{2,3},{3,2},{4,5},{5,4},{6,7},{7,6},{8,9},{9,8},{10,11... | collective-permute-start | bytes 491528 | tf_op jit(solution)/shard_map/ppermute | solution.py:14
  71.8 4.4 %collective-permute-start.22 = (bf16[80,1024]{1,0:T(8,128)(2,1)}, bf16[80,1024]{1,0:T(8,128)(2,1)}, u32[]{:S(2)}, u32[]{:S(2)}) collective-permute-start(bf16[80,1024]{1,0:T(8,128)(2,1)} %collective-permute-done.21.refs_4_), channel_id=1, source_target_pairs={{0,1},{1,0},{2,3},{3,2},{4,5},{5,4},{6,7},{7,6},{8,9},{9,8},{10,11... | collective-permute-start | bytes 491528 | tf_op jit(solution)/shard_map/ppermute | solution.py:14
  72.3 3.9 %collective-permute-start.24 = (bf16[80,1024]{1,0:T(8,128)(2,1)}, bf16[80,1024]{1,0:T(8,128)(2,1)}, u32[]{:S(2)}, u32[]{:S(2)}) collective-permute-start(bf16[80,1024]{1,0:T(8,128)(2,1)} %collective-permute-done.23.refs_6_), channel_id=1, source_target_pairs={{0,1},{1,0},{2,3},{3,2},{4,5},{5,4},{6,7},{7,6},{8,9},{9,8},{10,11... | collective-permute-start | bytes 491528 | tf_op jit(solution)/shard_map/ppermute | solution.py:14
  86.5 3.9 %collective-permute-start.26 = (bf16[80,1024]{1,0:T(8,128)(2,1)}, bf16[80,1024]{1,0:T(8,128)(2,1)S(1)}, u32[]{:S(2)}, u32[]{:S(2)}) collective-permute-start(bf16[80,1024]{1,0:T(8,128)(2,1)} %get-tuple-element.91), channel_id=1, source_target_pairs={{0,1},{1,0},{2,3},{3,2},{4,5},{5,4},{6,7},{7,6},{8,9},{9,8},{10,11... | collective-permute-start | bytes 491528 | tf_op jit(solution)/shard_map/ppermute | solution.py:14
  88.6 16.0 %collective-permute-start.33 = (bf16[512,512]{1,0:T(8,128)(2,1)S(1)}, bf16[512,512]{1,0:T(8,128)(2,1)S(1)}, u32[]{:S(2)}, u32[]{:S(2)}) collective-permute-start(bf16[512,512]{1,0:T(8,128)(2,1)S(1)} %convolution_convert_fusion.1), channel_id=1, source_target_pairs={{0,16},{16,0},{1,17},{17,1},{2,18},{18,2},{3,19},{19,3},{4,20},{20... | collective-permute-start | bytes 1572872 | tf_op jit(solution)/shard_map/ppermute | solution.py:14
  90.5 6.3 %collective-permute-start.27 = (bf16[80,1024]{1,0:T(8,128)(2,1)S(1)}, bf16[80,1024]{1,0:T(8,128)(2,1)S(1)}, u32[]{:S(2)}, u32[]{:S(2)}) collective-permute-start(bf16[80,1024]{1,0:T(8,128)(2,1)S(1)} %add_convert_fusion.3.near), channel_id=1, source_target_pairs={{0,2},{1,3},{2,0},{3,1},{4,6},{5,7},{6,4},{7,5},{8,10},{9,11},{10,... | collective-permute-start | bytes 491528 | tf_op jit(solution)/shard_map/ppermute | solution.py:14
  97.2 7.5 %collective-permute-start.37 = (bf16[80,1024]{1,0:T(8,128)(2,1)S(1)}, bf16[80,1024]{1,0:T(8,128)(2,1)S(1)}, u32[]{:S(2)}, u32[]{:S(2)}) collective-permute-start(bf16[80,1024]{1,0:T(8,128)(2,1)S(1)} %get-tuple-element.92.refs_1_), channel_id=1, source_target_pairs={{0,12},{4,8},{8,4},{12,0},{1,13},{5,9},{9,5},{13,1},{2,14},{6,10},... | collective-permute-start | bytes 491528 | tf_op jit(solution)/shard_map/ppermute | solution.py:14
  104.6 8.9 %collective-permute-start.28 = (bf16[80,1024]{1,0:T(8,128)(2,1)S(1)}, bf16[80,1024]{1,0:T(8,128)(2,1)S(1)}, u32[]{:S(2)}, u32[]{:S(2)}) collective-permute-start(bf16[80,1024]{1,0:T(8,128)(2,1)S(1)} %copy-done.39), channel_id=1, source_target_pairs={{0,1},{1,0},{2,3},{3,2},{4,5},{5,4},{6,7},{7,6},{8,9},{9,8},{10,11... | collective-permute-start | bytes 491528 | tf_op jit(solution)/shard_map/ppermute | solution.py:14
  104.7 6.8 %collective-permute-start.47 = (f32[2,1024]{1,0:T(2,128)S(1)}, f32[2,1024]{1,0:T(2,128)S(1)}, u32[]{:S(2)}, u32[]{:S(2)}) collective-permute-start(f32[2,1024]{1,0:T(2,128)S(1)} %get-tuple-element.113), channel_id=1, source_target_pairs={{0,1},{1,0},{2,3},{3,2},{4,5},{5,4},{6,7},{7,6},{8,9},{9,8},{10,11... | collective-permute-start | bytes 24584 | tf_op jit(solution)/shard_map/ppermute | solution.py:14
  107.2 53.8 %collective-permute-start.41 = (bf16[512,1024]{1,0:T(8,128)(2,1)}, bf16[512,1024]{1,0:T(8,128)(2,1)}, u32[]{:S(2)}, u32[]{:S(2)}) collective-permute-start(bf16[512,1024]{1,0:T(8,128)(2,1)} %convolution_convert_fusion), channel_id=1, source_target_pairs={{0,16},{16,0},{1,17},{17,1},{2,18},{18,2},{3,19},{19,3},{4,20},{20... | collective-permute-start | bytes 3145736 | tf_op jit(solution)/shard_map/ppermute | solution.py:14
  107.8 15.1 %collective-permute-start.35 = (bf16[80,1024]{1,0:T(8,128)(2,1)S(1)}, bf16[80,1024]{1,0:T(8,128)(2,1)S(1)}, u32[]{:S(2)}, u32[]{:S(2)}) collective-permute-start(bf16[80,1024]{1,0:T(8,128)(2,1)S(1)} %get-tuple-element.92.refs_1_), channel_id=1, source_target_pairs={{0,8},{4,12},{8,0},{12,4},{1,9},{5,13},{9,1},{13,5},{2,10},{6,14},... | collective-permute-start | bytes 491528 | tf_op jit(solution)/shard_map/ppermute | solution.py:14
  111.5 11.4 %collective-permute-start.32 = (bf16[80,1024]{1,0:T(8,128)(2,1)S(1)}, bf16[80,1024]{1,0:T(8,128)(2,1)S(1)}, u32[]{:S(2)}, u32[]{:S(2)}) collective-permute-start(bf16[80,1024]{1,0:T(8,128)(2,1)S(1)} %get-tuple-element.92.refs_1_), channel_id=1, source_target_pairs={{0,4},{4,0},{8,12},{12,8},{1,5},{5,1},{9,13},{13,9},{2,6},{6,2},{1... | collective-permute-start | bytes 491528 | tf_op jit(solution)/shard_map/ppermute | solution.py:14
  111.5 8.5 %collective-permute-start.48 = (f32[2,1024]{1,0:T(2,128)S(1)}, f32[2,1024]{1,0:T(2,128)S(1)}, u32[]{:S(2)}, u32[]{:S(2)}) collective-permute-start(f32[2,1024]{1,0:T(2,128)S(1)} %add.92), channel_id=1, source_target_pairs={{0,4},{4,0},{8,12},{12,8},{1,5},{5,1},{9,13},{13,9},{2,6},{6,2},{1... | collective-permute-start | bytes 24584 | tf_op jit(solution)/shard_map/ppermute | solution.py:14
  113.6 11.0 %collective-permute-start.29 = (bf16[80,1024]{1,0:T(8,128)(2,1)S(1)}, bf16[80,1024]{1,0:T(8,128)(2,1)S(1)}, u32[]{:S(2)}, u32[]{:S(2)}) collective-permute-start(bf16[80,1024]{1,0:T(8,128)(2,1)S(1)} %add_convert_fusion.2), channel_id=1, source_target_pairs={{0,2},{1,3},{2,0},{3,1},{4,6},{5,7},{6,4},{7,5},{8,10},{9,11},{10,... | collective-permute-start | bytes 491528 | tf_op jit(solution)/shard_map/ppermute | solution.py:14
  120.0 4.6 %collective-permute-start.49 = (f32[2,1024]{1,0:T(2,128)S(1)}, f32[2,1024]{1,0:T(2,128)S(1)}, u32[]{:S(2)}, u32[]{:S(2)}) collective-permute-start(f32[2,1024]{1,0:T(2,128)S(1)} %add.93), channel_id=1, source_target_pairs={{0,8},{4,12},{8,0},{12,4},{1,9},{5,13},{9,1},{13,5},{2,10},{6,14},... | collective-permute-start | bytes 24584 | tf_op jit(solution)/shard_map/ppermute | solution.py:14
  122.9 3.1 %collective-permute-start.31 = (bf16[80,1024]{1,0:T(8,128)(2,1)S(1)}, bf16[80,1024]{1,0:T(8,128)(2,1)S(1)}, u32[]{:S(2)}, u32[]{:S(2)}) collective-permute-start(bf16[80,1024]{1,0:T(8,128)(2,1)S(1)} %get-tuple-element.92.refs_1_), channel_id=1, source_target_pairs={{0,1},{1,0},{2,3},{3,2},{4,5},{5,4},{6,7},{7,6},{8,9},{9,8},{10,11... | collective-permute-start | bytes 491528 | tf_op jit(solution)/shard_map/ppermute | solution.py:14
  122.9 4.6 %collective-permute-start.38 = (bf16[80,1024]{1,0:T(8,128)(2,1)S(1)}, bf16[80,1024]{1,0:T(8,128)(2,1)S(1)}, u32[]{:S(2)}, u32[]{:S(2)}) collective-permute-start(bf16[80,1024]{1,0:T(8,128)(2,1)S(1)} %collective-permute-done.37.refs_7_), channel_id=1, source_target_pairs={{0,1},{1,0},{2,3},{3,2},{4,5},{5,4},{6,7},{7,6},{8,9},{9,8},{10,11... | collective-permute-start | bytes 491528 | tf_op jit(solution)/shard_map/ppermute | solution.py:14
  124.6 2.8 %collective-permute-start.34 = (bf16[80,1024]{1,0:T(8,128)(2,1)S(1)}, bf16[80,1024]{1,0:T(8,128)(2,1)S(1)}, u32[]{:S(2)}, u32[]{:S(2)}) collective-permute-start(bf16[80,1024]{1,0:T(8,128)(2,1)S(1)} %collective-permute-done.32.refs_3_), channel_id=1, source_target_pairs={{0,1},{1,0},{2,3},{3,2},{4,5},{5,4},{6,7},{7,6},{8,9},{9,8},{10,11... | collective-permute-start | bytes 491528 | tf_op jit(solution)/shard_map/ppermute | solution.py:14
  126.0 38.2 %collective-permute-start.40 = (bf16[512,512]{1,0:T(8,128)(2,1)}, bf16[512,512]{1,0:T(8,128)(2,1)}, u32[]{:S(2)}, u32[]{:S(2)}) collective-permute-start(bf16[512,512]{1,0:T(8,128)(2,1)} %fusion), channel_id=1, source_target_pairs={{0,4},{4,0},{8,12},{12,8},{1,5},{5,1},{9,13},{13,9},{2,6},{6,2},{1... | collective-permute-start | bytes 1572872 | tf_op jit(solution)/shard_map/ppermute | solution.py:14
  127.5 25.5 %collective-permute-start.30 = (bf16[80,1024]{1,0:T(8,128)(2,1)}, bf16[80,1024]{1,0:T(8,128)(2,1)}, u32[]{:S(2)}, u32[]{:S(2)}) collective-permute-start(bf16[80,1024]{1,0:T(8,128)(2,1)} %add_convert_fusion.1), channel_id=1, source_target_pairs={{0,1},{1,0},{2,3},{3,2},{4,5},{5,4},{6,7},{7,6},{8,9},{9,8},{10,11... | collective-permute-start | bytes 491528 | tf_op jit(solution)/shard_map/ppermute | solution.py:14
  141.6 3.7 %collective-permute-start.46 = (f32[2,1024]{1,0:T(2,128)S(1)}, f32[2,1024]{1,0:T(2,128)S(1)}, u32[]{:S(2)}, u32[]{:S(2)}) collective-permute-start(f32[2,1024]{1,0:T(2,128)S(1)} %add.90), channel_id=1, source_target_pairs={{0,2},{1,3},{2,0},{3,1},{4,6},{5,7},{6,4},{7,5},{8,10},{9,11},{10,... | collective-permute-start | bytes 24584 | tf_op jit(solution)/shard_map/ppermute | solution.py:14
  145.4 4.0 %collective-permute-start.50 = (f32[10,512]{1,0:T(8,128)S(1)}, f32[10,512]{1,0:T(8,128)S(1)}, u32[]{:S(2)}, u32[]{:S(2)}) collective-permute-start(f32[10,512]{1,0:T(8,128)S(1)} %pad_maximum_fusion.4), channel_id=1, source_target_pairs={{0,16},{16,0},{1,17},{17,1},{2,18},{18,2},{3,19},{19,3},{4,20},{20... | collective-permute-start | bytes 61448 | tf_op jit(solution)/shard_map/ppermute | solution.py:14
  147.8 6.4 %collective-permute-start.39 = (bf16[80,1024]{1,0:T(8,128)(2,1)}, bf16[80,1024]{1,0:T(8,128)(2,1)S(1)}, u32[]{:S(2)}, u32[]{:S(2)}) collective-permute-start(bf16[80,1024]{1,0:T(8,128)(2,1)} %get-tuple-element.103), channel_id=1, source_target_pairs={{0,1},{1,0},{2,3},{3,2},{4,5},{5,4},{6,7},{7,6},{8,9},{9,8},{10,11... | collective-permute-start | bytes 491528 | tf_op jit(solution)/shard_map/ppermute | solution.py:14
  149.4 20.7 %collective-permute-start.42 = (bf16[512,768]{1,0:T(8,128)(2,1)}, bf16[512,768]{1,0:T(8,128)(2,1)S(1)}, u32[]{:S(2)}, u32[]{:S(2)}) collective-permute-start(bf16[512,768]{1,0:T(8,128)(2,1)} %get-tuple-element.107), channel_id=1, source_target_pairs={{0,16},{16,0},{1,17},{17,1},{2,18},{18,2},{3,19},{19,3},{4,20},{20... | collective-permute-start | bytes 2359304 | tf_op jit(solution)/shard_map/ppermute | solution.py:14
  154.2 5.4 %collective-permute-start.43 = (bf16[80,1024]{1,0:T(8,128)(2,1)S(1)}, bf16[80,1024]{1,0:T(8,128)(2,1)S(1)}, u32[]{:S(2)}, u32[]{:S(2)}) collective-permute-start(bf16[80,1024]{1,0:T(8,128)(2,1)S(1)} %add_convert_fusion.near), channel_id=1, source_target_pairs={{0,2},{1,3},{2,0},{3,1},{4,6},{5,7},{6,4},{7,5},{8,10},{9,11},{10,... | collective-permute-start | bytes 491528 | tf_op jit(solution)/shard_map/ppermute | solution.py:14
  160.4 13.2 %collective-permute-start.51 = (bf16[256,512]{1,0:T(8,128)(2,1)S(1)}, bf16[256,512]{1,0:T(8,128)(2,1)S(1)}, u32[]{:S(2)}, u32[]{:S(2)}) collective-permute-start(bf16[256,512]{1,0:T(8,128)(2,1)S(1)} %convolution_convert_fusion.2), channel_id=1, source_target_pairs={{0,16},{16,0},{1,17},{17,1},{2,18},{18,2},{3,19},{19,3},{4,20},{20... | collective-permute-start | bytes 786440 | tf_op jit(solution)/shard_map/ppermute | solution.py:14
  170.4 5.4 %collective-permute-start.44 = (f32[80,1024]{1,0:T(8,128)S(1)}, f32[80,1024]{1,0:T(8,128)S(1)}, u32[]{:S(2)}, u32[]{:S(2)}) collective-permute-start(f32[80,1024]{1,0:T(8,128)S(1)} %shard_map.313), channel_id=1, source_target_pairs={{0,1},{1,0},{2,3},{3,2},{4,5},{5,4},{6,7},{7,6},{8,9},{9,8},{10,11... | collective-permute-start | bytes 983048 | tf_op jit(solution)/shard_map/ppermute | solution.py:14
  (50 other events, 593.1 us)

commit v5 on v4

--- a/solution.py
+++ b/solution.py
@@ -113,6 +113,7 @@
 
 
 QBIAS, VBIAS, EBIAS = 6, 7, 8
+FIRST_COST = 20_000_000_000
 
 
 def pack_body(*refs):
@@ -260,18 +261,18 @@
 def forward_body(blocks, ways, *refs):
     normed, cots, refs = refs[:blocks], refs[blocks : 2 * blocks], refs[2 * blocks :]
     vec, expand, reduce = refs[0], refs[1 : 1 + ways], refs[1 + ways : 1 + 2 * ways]
-    normed_all, cot_all, act, grad, keep, send, out_keep, out_send, unit_sum, cot_sum = refs[
+    normed_all, cot_all, act, grad, keep, send, out_keep, out_send, unit_sum, cot_sum, *aways = refs[
         1 + 2 * ways :
     ]
     rows = normed[0].shape[0]
     size = normed_all.shape[1] // ways
     units = act.shape[1]
-    total = jnp.zeros((1, normed_all.shape[1]), WIDE)
+    place = lax.axis_index("context")
     for n in range(blocks):
         normed_all[n * rows : (n + 1) * rows, :] = normed[n][...]
+    for n in range(blocks):
         cot_all[n * rows : (n + 1) * rows, :] = cots[n][...]
-        total = total + jnp.sum(cots[n][...].astype(WIDE), 0, keepdims=True)
-    cot_sum[...] = total
+    cot_sum[...] = jnp.sum(cot_all[...].astype(WIDE), 0, keepdims=True)
     step = min(256, units, size)
     back = [jnp.zeros((2 * rows, size), WIDE) for _ in range(ways)]
     out = [jnp.zeros((2 * rows, size), WIDE) for _ in range(ways)]
@@ -298,27 +299,39 @@
         send[:, c] = back[i][rows:].astype(LOW)
         out_keep[:, c] = out[i][:rows].astype(LOW)
         out_send[:, c] = out[i][rows:].astype(LOW)
-
-
-def second_back_body(near, far, hidden, cot, vec, grad_hidden, grad_branch, sums):
+    if aways:
+        many = units // 2
+        chosen = pl.ds(pl.multiple_of((place & 1) * many, many), many)
+        aways[0][...] = dot_lt(act[:, chosen], cot_all[:, size:]).astype(LOW)
+        aways[1][...] = dot_lt(normed_all[:, size:], grad[...]).astype(LOW)
+
+
+def second_back_body(near, far, hidden, cot, vec, grad_hidden, grad_branch):
     upstream = near[...].astype(WIDE) + far[...].astype(WIDE)
     grad, xhat = norm_back_rows(hidden[...], vec[3:4, :], upstream)
     total = grad + cot[...].astype(WIDE)
     grad_hidden[...] = total
-    grad_branch[...] = total.astype(LOW)
-    sums[0:1, :] = jnp.sum(upstream * xhat, 0, keepdims=True)
-    sums[1:2, :] = jnp.sum(upstream, 0, keepdims=True)
+    rows = total.shape[0]
+    grad_branch[:rows, :] = total.astype(LOW)
+    below = jnp.zeros((grad_branch.shape[0] - rows, total.shape[1]), WIDE)
+    line = lax.broadcasted_iota(jnp.int32, below.shape, 0)
+    below = jnp.where(line == 0, jnp.sum(upstream * xhat, 0, keepdims=True), below)
+    below = jnp.where(line == 1, jnp.sum(upstream, 0, keepdims=True), below)
+    grad_branch[rows:, :] = below.astype(LOW)
 
 
 def attend_back_body(heads, head_dim, blocks, ways, count, *refs):
     pieces, refs = refs[:blocks], refs[blocks:]
     outs, qkv, packed = refs[:ways], refs[ways], refs[ways + 1 : 2 * ways + 1]
-    normed = refs[2 * ways + 1]
-    branch, grad_qkv, keep, send, sums, head_sums, away = refs[2 * ways + 2 :]
-    rows = pieces[0].shape[0]
+    normed, contexts = refs[2 * ways + 1], refs[2 * ways + 2 : 2 * ways + 4]
+    branch, grad_qkv, keep, send, sums, norm_sums, head_sums, away = refs[2 * ways + 4 :]
+    rows = keep.shape[0]
     features = heads * head_dim
+    below = jnp.zeros((pieces[0].shape[0] - rows, branch.shape[1]), WIDE)
     for n, piece in enumerate(pieces):
-        branch[n * rows : (n + 1) * rows, :] = piece[...]
+        branch[n * rows : (n + 1) * rows, :] = piece[:rows, :]
+        below = below + piece[rows:, :].astype(WIDE)
+    norm_sums[...] = below[:2]
     size = branch.shape[1] // ways
     g = sum(
         dot_rt(branch[:, i * size : (i + 1) * size], w[...]) for i, w in enumerate(outs)
@@ -358,7 +371,15 @@
         keep[:, i * size : (i + 1) * size] = part[:rows]
         send[:, i * size : (i + 1) * size] = part[rows:]
     sums[...] = jnp.sum(branch[...].astype(WIDE), 0, keepdims=True)
-    away[...] = dot_lt(normed[:, normed.shape[1] - away.shape[0] :], grad_qkv[...]).astype(LOW)
+    other = normed.shape[1] - away.shape[0]
+    away[:, : 3 * features] = dot_lt(normed[:, other:], grad_qkv[...]).astype(LOW)
+    first = contexts[0].shape[0]
+    part = dot_lt(contexts[0][...], branch[:first, other:])
+    part = (part + dot_lt(contexts[1][...], branch[first:, other:])).astype(LOW)
+    for n in range(away.shape[0] // features):
+        away[n * features : (n + 1) * features, 3 * features :] = part[
+            :, n * features : (n + 1) * features
+        ]
 
 
 def first_sums_body(ways, grad_qkv, xhat, *refs):
@@ -378,11 +399,14 @@
         out[1:2, columns] = jnp.sum(part, 0, keepdims=True)
 
 
-def thirds_body(own, got, *outs):
-    size = outs[0].shape[1]
-    for n, out in enumerate(outs):
+def last_body(own, own_out, got, query, key, value, out):
+    size = query.shape[1]
+    for n, ref in enumerate((query, key, value)):
         columns = slice(n * size, (n + 1) * size)
-        out[...] = own[:, columns] + got[:, columns].astype(WIDE)
+        ref[...] = own[:, columns] + got[:, columns].astype(WIDE)
+    for n in range(out.shape[1] // size):
+        columns = slice(n * size, (n + 1) * size)
+        out[:, columns] = own_out[:, columns] + got[columns, 3 * size :].astype(WIDE)
 
 
 def first_back_body(near, far, tokens, grad_hidden, vec, out):
@@ -439,11 +463,6 @@
         return turned(lax.dynamic_slice_in_dim(value.reshape(seq, width), which * half, half, 0))
 
     token_piece = piece_of(tokens, core)
-    mine_tokens = spread_context(token_piece)
-    token_pieces = woven(
-        mine_tokens,
-        [piece_of(tokens, 1 - core)] + [swap(m, "tensor", 1) for m in mine_tokens[1:]],
-    )
     vectors = (gain_first, shift_first, output_bias, gain_second, shift_second, reduce_bias)
     biases = (query_bias, value_bias, expand_bias)
     thirds = (query_weight, key_weight, value_weight)
@@ -464,7 +483,6 @@
         first = across(message)
         packed = (message, first)
         output_parts = (output_weight, across(after(output_weight, message)))
-        expand_parts = (expand_weight, across(after(expand_weight, first)))
         reduce_parts = (reduce_weight, across(after(reduce_weight, first)))
     else:
         gather = lambda v, axis=0: lax.all_gather(v, "fsdp", axis=axis, tiled=True)
@@ -480,6 +498,18 @@
         expand_parts = (gather(expand_weight),)
         reduce_parts = (gather(reduce_weight, 1),)
 
+    mine_tokens = spread_context(token_piece)
+    token_pieces = woven(
+        mine_tokens,
+        [piece_of(tokens, 1 - core)]
+        + [swap(after(m, packed[-1]), "tensor", 1) for m in mine_tokens[1:]],
+    )
+    cot_piece = piece_of(cotangent, core)
+    mine_cots = spread_context(after(cot_piece, *mine_tokens[1:]))
+    mine_cots = list(lax.optimization_barrier(tuple(mine_cots)))
+    if pair:
+        expand_parts = (expand_weight, across(after(expand_weight, mine_tokens[1])))
+
     vec, xhat_all, normed_all, qkv, context_own = kernel(
         lambda *refs: first_body(heads, head_dim, blocks, parts, *refs),
         (
@@ -493,8 +523,7 @@
         *packed,
         lines,
         count=valid_count,
-        flops=6 * length * width * features,
-        moved=10 * length * width,
+        flops=FIRST_COST,
     )
     keep, send = kernel(
         lambda *refs: out_body(parts, *refs),
@@ -502,11 +531,10 @@
         context_own,
         *output_parts,
     )
-    cot_piece = piece_of(cotangent, core)
-    mine_cots = spread_context(after(cot_piece, mine_tokens[-1]))
+    near, far = last_terms(keep, send)
+    far, *mine_cots = lax.optimization_barrier((far, *mine_cots))
+    far = after(far, expand_parts[-1])
     cots = woven(mine_cots, [swap(m, "tensor", 1) for m in mine_cots])
-    near, far = last_terms(keep, send)
-    near = after(near, *cots)
     hidden, normed_piece = kernel(
         second_body, (wide(half, width), low(half, width)), token_piece, near, far, vec
     )
@@ -532,12 +560,14 @@
         out_send,
         unit_sum,
         cot_sum,
+        *aways,
     ) = kernel(
         lambda *refs: forward_body(blocks, parts, *refs),
         (low(length, width),) * 2
         + (low(length, units),) * 2
         + (low(half, width),) * 4
-        + (wide(1, units), wide(1, width)),
+        + (wide(1, units), wide(1, width))
+        + ((low(units // 2, share), low(share, units)) if pair else ()),
         *woven(mine_normed, theirs),
         *cots,
         vec,
@@ -549,9 +579,13 @@
         limit=62,
     )
     near, far = last_terms(keep, send)
-    grad_hidden, grad_piece, norm_sums = kernel(
+    if pair:
+        many = units // 2
+        act_half = lax.dynamic_slice_in_dim(activated, (place & 1) * many, many, 1)
+        cot_own, normed_own = segments(cot_all, 2)[0], segments(normed_two, 2)[0]
+    grad_hidden, grad_piece = kernel(
         second_back_body,
-        (wide(half, width), low(half, width), wide(2, width)),
+        (wide(half, width), low(half + 16, width)),
         near,
         far,
         hidden,
@@ -574,14 +608,7 @@
         return pin(dot_lt(own, right)) + away.astype(WIDE)
 
     if pair:
-        many = units // 2
-        act_half = lax.dynamic_slice_in_dim(activated, (place & 1) * many, many, 1)
-        cot_own, cot_other = segments(cot_all, 2)
-        normed_own, normed_other = segments(normed_two, 2)
-        reduce_got = across(dot_lt(act_half, cot_other).astype(LOW))
-        reduce_half = pin((dot_lt(act_half, cot_own) + reduce_got.astype(WIDE)).astype(LOW))
-        expand_got = across(dot_lt(normed_other, grad_expanded).astype(LOW))
-        grad_expand = pin(dot_lt(normed_own, grad_expanded)) + expand_got.astype(WIDE)
+        reduce_got, expand_got = (across(a) for a in aways)
 
         def both_halves(value, theirs, axis):
             odd = (place & 1) != 0
@@ -594,11 +621,16 @@
         grad_expand = weight_grad(normed_two, grad_expanded, 0)
 
     mine_grads = spread_context(grad_piece)
+    out_near, out_far = last_terms(after(out_keep, grad_piece), after(out_send, grad_piece))
+    ready = [out_far]
     theirs = [swap(m, "tensor", 1) for m in mine_grads[:1]]
     if pair:
-        mine_grads[1:] = [after(m, reduce_got) for m in mine_grads[1:]]
+        *mine_grads[1:], reduce_got = lax.optimization_barrier((*mine_grads[1:], reduce_got))
+        reduce_half = pin((dot_lt(act_half, cot_own) + reduce_got.astype(WIDE)).astype(LOW))
+        expand_own = pin(dot_lt(after(normed_own, grad_piece), grad_expanded))
+        ready += [reduce_half, expand_own]
     theirs += [swap(m, "tensor", 1) for m in mine_grads[1:]]
-    grad_branch, grad_qkv, keep, send, branch_sum, head_sum, away = kernel(
+    grad_branch, grad_qkv, keep, send, branch_sum, norm_sums, head_sum, away = kernel(
         lambda *refs: attend_back_body(heads, head_dim, blocks, parts, *refs),
         (
             low(length, width),
@@ -606,26 +638,32 @@
             low(half, width),
             low(half, width),
             wide(1, width),
+            wide(2, width),
             wide(1, 3 * features),
-            low(width // parts, 3 * features),
+            low(width // parts, 4 * features),
         ),
         *woven(mine_grads, theirs),
         *output_parts,
-        qkv,
+        after(qkv, *ready),
         *packed,
         normed_all,
+        context_own,
+        context_rest,
         count=valid_count,
         flops=10 * length * length * features,
         moved=8 * length * width,
     )
     if pair:
         qkv_got = across(away)
+    if pair:
+        send = after(send, expand_got)
     near, far = last_terms(keep, send)
-    if pair:
-        reduce_theirs = swap(after(reduce_half, mine_grads[-1]), "context", 1)
-        qkv_far = far
-        near = after(near, reduce_theirs, expand_got, qkv_got)
-        grad_reduce = both_halves(reduce_half, reduce_theirs, 0)
+    gn_far = far
+    if pair:
+        grad_reduce = both_halves(
+            reduce_half, swap(after(reduce_half, head_sum), "context", 1), 0
+        )
+        grad_expand = expand_own + expand_got.astype(WIDE)
     grad_token_piece = kernel(
         first_back_body, wide(half, width), near, far, token_piece, grad_hidden, vec
     )
@@ -639,42 +677,33 @@
 
     grad_tokens = both_cores(grad_token_piece)
 
-    if pair:
-        grad_query, grad_key, grad_value = kernel(
-            thirds_body,
-            (wide(share, features),) * 3,
-            dot_lt(segments(normed_all, 2)[0], grad_qkv),
+    reduced = out_near.astype(WIDE) + out_far.astype(WIDE) + vec[5:6, :]
+    output = both_cores((hidden + reduced).astype(LOW))
+
+    if pair:
+        grad_query, grad_key, grad_value, grad_output = kernel(
+            last_body,
+            (wide(share, features),) * 3 + (wide(features, share),),
+            dot_lt(segments(normed_all, 2)[0], after(grad_qkv, gn_far)),
+            dot_lt(jnp.concatenate([context_own, context_rest], 0), after(segments(grad_branch, 2)[0], gn_far)),
             qkv_got,
         )
     else:
         grad_weights = scatter(dot_lt(normed_all, grad_qkv), 0).astype(WIDE)
         grad_query, grad_key, grad_value = jnp.split(grad_weights, 3, 1)
-
-    near, far = last_terms(after(out_keep, grad_piece), after(out_send, grad_piece))
-    reduced = near.astype(WIDE) + far.astype(WIDE) + vec[5:6, :]
-    output = both_cores((hidden + reduced).astype(LOW))
+        context_all = jnp.concatenate([context_own, context_rest], 0)
+        grad_output = scatter(dot_lt(context_all, grad_branch), 1).astype(WIDE)
 
     def own_rows(value):
         size = value.shape[0] // ways
         return lax.dynamic_slice_in_dim(value, mine * size, size, 0)
 
-    context_all = jnp.concatenate([context_own, context_rest], 0)
-    if pair:
-        context_all = after(context_all, qkv_far)
-    grad_output = weight_grad(context_all, grad_branch, 1)
-
     first_sums = kernel(
-        lambda *refs: first_sums_body(parts, *refs), wide(2, width), grad_qkv, xhat_all, *packed
+        lambda *refs: first_sums_body(parts, *refs), wide(2, width), after(grad_qkv, gn_far), xhat_all, *packed
     )
     bit = 1
     while bit < lax.axis_size("tensor"):
         first_sums = first_sums + swap(first_sums, "tensor", bit)
-        bit *= 2
-    norm_sums = after(norm_sums, mine_grads[-1])
-    norm_sums = norm_sums + swap(norm_sums, "tensor", 1)
-    bit = 1
-    while bit < cycle:
-        norm_sums = norm_sums + swap(norm_sums, "context", bit)
         bit *= 2
     sums = jnp.concatenate([first_sums, norm_sums, branch_sum, cot_sum], 0)
     plain = jnp.concatenate(

time: 177 us -> 167 us (0.944)
  starting transfers between devices: 53 us -> 45.5 us
  matrix products: 10.7 us -> 4.28 us
  other arithmetic: 11.7 us -> 6.58 us
  waiting for transfers between devices: 58.9 us -> 62.7 us
  local copies, waits for them, and re-layouts: 5.51 us -> 9.05 us
  Pallas kernels: 34.8 us -> 36.8 us
    ppermute x52 -> x48, starting transfers between devices: 53 us -> 45.5 us  [swap(): lax.ppermute(block, axis, [(i, i ^ bit) for i in range(lax.axis_size(axis...]
    dot_general x7 -> x4, matrix products: 10.7 us -> 4.28 us  [dot_lt(): lax.dot_general(left, right, (((0,), (0,)), ((), ())), preferred_element_...]
    ppermute x52 -> x48, waiting for transfers between devices: 58.9 us -> 62.7 us  [swap(): lax.ppermute(block, axis, [(i, i ^ bit) for i in range(lax.axis_size(axis...]
    slice x2 -> x4, local copies, waits for them, and re-layouts: 0.01 us -> 2.28 us  [segments(): return [value[:, i * size:(i + 1) * size] for i in range(count)]]
    add x5 -> x1, other arithmetic: 3.88 us -> 1.62 us  [on_device(): grad_expand = expand_own + expand_got.astype(WIDE)]
    pallas_call x11, Pallas kernels: 34.8 us -> 36.8 us  [kernel(): pl.pallas_call(run if staged else body, out_shape=out_shape, in_specs=[pl...]
  transfers between devices with their start and end apart: 52 -> 48, of which waited for: 18 -> 20; matrix products, arithmetic and copies ran while one was open for 13% -> 9% of each run, Pallas kernels for 13% -> 12%
where the time goes in v5:
time: 167 us
  waiting for transfers between devices  62.7 us (38%)
  starting transfers between devices  45.5 us (27%)
  Pallas kernels  36.8 us (22%)
  local copies, waits for them, and re-layouts  9.05 us (5%)
  other arithmetic  6.58 us (4%)
  matrix products  4.28 us (3%)
  between operations  2.04 us (1%)
    ppermute x48, waiting for transfers between devices, swap(): lax.ppermute(block, axis, [(i, i ^ bit) for i in range(lax.axis_size(axis...  62.7 us
    ppermute x48, starting transfers between devices, swap(): lax.ppermute(block, axis, [(i, i ^ bit) for i in range(lax.axis_size(axis...  45.5 us
    pallas_call x11, Pallas kernels, kernel(): pl.pallas_call(run if staged else body, out_shape=out_shape, in_specs=[pl...  36.8 us
    dot_general x4, matrix products, dot_lt(): lax.dot_general(left, right, (((0,), (0,)), ((), ())), preferred_element_...  4.28 us
  transfers between devices with their start and end apart: 48, of which 20 were waited for; matrix products, arithmetic and copies ran while one was open for 9% of the time, Pallas kernels for 12%

profile of v5, /device:TPU:0, one launch (start us, length us, event | category | flops | bytes accessed | tf_op | source)
XLA Modules:
  0.0 166.9 jit_solution(16152604604538574381)
XLA Ops:
  0.7 1.1 dynamic-slice_bitcast_fusion.1
  1.8 2.5 %shard_map.305 = (bf16[528,768]{1,0:T(8,128)(2,1)}, f32[16,768]{1,0:T(8,128)}) custom-call(bf16[512,256]{1,0:T(8,128)(2,1)} %refs_0_.3, bf16[512,256]{1,0:T(8,128)(2,1)} %refs_1_.2, bf16[512,256]{1,0:T(8,128)(2,1)} %refs_2_.1, bf16[512]{0:T(512)(128)(2,1)} %refs_3_.1, bf16[512]{0:T(512)(128)(2,1)} %refs_4_.1, bf16[512]{0:T(512)(128)(2,1)} %refs_5_.1, ...), custom_call_target="tpu_custom_call" | custom-call | tf_op jit(solution)/shard_map/pallas_call | solution.py:96
  4.4 3.0 %collective-permute-start.1 = (bf16[528,768]{1,0:T(8,128)(2,1)}, bf16[528,768]{1,0:T(8,128)(2,1)S(1)}, u32[]{:S(2)}, u32[]{:S(2)}) collective-permute-start(bf16[528,768]{1,0:T(8,128)(2,1)} %get-tuple-element.89.refs_9_.refs_12_.refs_2_), channel_id=1, source_target_pairs={{0,16},{16,0},{1,17},{17,1},{2,18},{18,2},{3,19},{19,3},{4,20},{20... | collective-permute-start | bytes 2433032 | tf_op jit(solution)/shard_map/ppermute | solution.py:14
  7.4 1.6 collective-permute-start
  8.9 2.6 %collective-permute-start.3 = (bf16[80,1024]{1,0:T(8,128)(2,1)S(1)}, bf16[80,1024]{1,0:T(8,128)(2,1)S(1)}, u32[]{:S(2)}, u32[]{:S(2)}) collective-permute-start(bf16[80,1024]{1,0:T(8,128)(2,1)S(1)} %maximum_select_fusion.2.refs_1_.tokens), channel_id=1, source_target_pairs={{0,8},{4,12},{8,0},{12,4},{1,9},{5,13},{9,1},{13,5},{2,10},{6,14},... | collective-permute-start | bytes 491528 | tf_op jit(solution)/shard_map/ppermute | solution.py:14
  12.8 2.4 %collective-permute-done.refs_3_ = bf16[80,1024]{1,0:T(8,128)(2,1)S(1)} collective-permute-done((bf16[80,1024]{1,0:T(8,128)(2,1)S(1)}, bf16[80,1024]{1,0:T(8,128)(2,1)S(1)}, u32[]{:S(2)}, u32[]{:S(2)}) %collective-permute-start) | collective-permute-done | bytes 163872 | tf_op jit(solution)/shard_map/ppermute | solution.py:14
  15.2 11.2 %collective-permute-done.1.refs_10_.refs_13_.refs_3_ = bf16[528,768]{1,0:T(8,128)(2,1)S(1)} collective-permute-done((bf16[528,768]{1,0:T(8,128)(2,1)}, bf16[528,768]{1,0:T(8,128)(2,1)S(1)}, u32[]{:S(2)}, u32[]{:S(2)}) %collective-permute-start.1) | collective-permute-done | bytes 811040 | tf_op jit(solution)/shard_map/ppermute | solution.py:14
  27.2 2.1 %collective-permute-start.13 = (bf16[512,1024]{1,0:T(8,128)(2,1)S(1)}, bf16[512,1024]{1,0:T(8,128)(2,1)S(1)}, u32[]{:S(2)}, u32[]{:S(2)}) collective-permute-start(bf16[512,1024]{1,0:T(8,128)(2,1)S(1)} %copy-done.25), channel_id=1, source_target_pairs={{0,16},{16,0},{1,17},{17,1},{2,18},{18,2},{3,19},{19,3},{4,20},{20... | collective-permute-start | bytes 3145736 | tf_op jit(solution)/shard_map/ppermute | solution.py:14
  29.3 3.5 %shard_map.306 = (f32[16,1024]{1,0:T(8,128)S(1)}, bf16[640,1024]{1,0:T(8,128)(2,1)S(1)}, bf16[640,1024]{1,0:T(8,128)(2,1)}, bf16[640,768]{1,0:T(8,128)(2,1)S(1)}, bf16[160,256]{1,0:T(8,128)(2,1)S(1)}) custom-call(s32[1]{0:T(128)S(6)} %copy.35.refs_0_, bf16[80,1024]{1,0:T(8,128)(2,1)S(1)} %maximum_select_fusion.2.refs_1_.tokens, ...), custom_call_target="tpu_custom_call" | custom-call | flops 20000000000 | tf_op jit(solution)/shard_map/pallas_call | solution.py:96
  32.9 1.4 shard_map.307
  35.1 1.2 collective-permute-start.25
  36.2 1.6 collective-permute-start.10
  37.8 2.6 %collective-permute-start.11 = (bf16[80,1024]{1,0:T(8,128)(2,1)S(1)}, bf16[80,1024]{1,0:T(8,128)(2,1)S(1)}, u32[]{:S(2)}, u32[]{:S(2)}) collective-permute-start(bf16[80,1024]{1,0:T(8,128)(2,1)S(1)} %get-tuple-element.114.refs_8_.cot), channel_id=1, source_target_pairs={{0,8},{4,12},{8,0},{12,4},{1,9},{5,13},{9,1},{13,5},{2,10},{6,14},... | collective-permute-start | bytes 491528 | tf_op jit(solution)/shard_map/ppermute | solution.py:14
  40.7 4.4 %collective-permute-done.10.refs_10_ = bf16[80,1024]{1,0:T(8,128)(2,1)S(1)} collective-permute-done((bf16[80,1024]{1,0:T(8,128)(2,1)S(1)}, bf16[80,1024]{1,0:T(8,128)(2,1)S(1)}, u32[]{:S(2)}, u32[]{:S(2)}) %collective-permute-start.10) | collective-permute-done | bytes 163872 | tf_op jit(solution)/shard_map/ppermute | solution.py:14
  45.1 1.5 collective-permute-start.9
  46.6 6.3 %collective-permute-done.11.refs_12_ = bf16[80,1024]{1,0:T(8,128)(2,1)S(1)} collective-permute-done((bf16[80,1024]{1,0:T(8,128)(2,1)S(1)}, bf16[80,1024]{1,0:T(8,128)(2,1)S(1)}, u32[]{:S(2)}, u32[]{:S(2)}) %collective-permute-start.11) | collective-permute-done | bytes 163872 | tf_op jit(solution)/shard_map/ppermute | solution.py:14
  52.9 1.5 collective-permute-done.13.refs_18_
  55.4 1.8 %collective-permute-start.15 = (bf16[80,1024]{1,0:T(8,128)(2,1)S(1)}, bf16[80,1024]{1,0:T(8,128)(2,1)S(1)}, u32[]{:S(2)}, u32[]{:S(2)}) collective-permute-start(bf16[80,1024]{1,0:T(8,128)(2,1)S(1)} %get-tuple-element.108.refs_0_), channel_id=1, source_target_pairs={{0,4},{4,0},{8,12},{12,8},{1,5},{5,1},{9,13},{13,9},{2,6},{6,2},{1... | collective-permute-start | bytes 491528 | tf_op jit(solution)/shard_map/ppermute | solution.py:14
  57.2 2.6 %collective-permute-start.17 = (bf16[80,1024]{1,0:T(8,128)(2,1)S(1)}, bf16[80,1024]{1,0:T(8,128)(2,1)S(1)}, u32[]{:S(2)}, u32[]{:S(2)}) collective-permute-start(bf16[80,1024]{1,0:T(8,128)(2,1)S(1)} %get-tuple-element.108.refs_0_), channel_id=1, source_target_pairs={{0,8},{4,12},{8,0},{12,4},{1,9},{5,13},{9,1},{13,5},{2,10},{6,14},... | collective-permute-start | bytes 491528 | tf_op jit(solution)/shard_map/ppermute | solution.py:14
  59.8 2.9 %collective-permute-done.15.refs_2_ = bf16[80,1024]{1,0:T(8,128)(2,1)S(1)} collective-permute-done((bf16[80,1024]{1,0:T(8,128)(2,1)S(1)}, bf16[80,1024]{1,0:T(8,128)(2,1)S(1)}, u32[]{:S(2)}, u32[]{:S(2)}) %collective-permute-start.15) | collective-permute-done | bytes 163872 | tf_op jit(solution)/shard_map/ppermute | solution.py:14
  62.7 9.0 %collective-permute-done.17.refs_4_ = bf16[80,1024]{1,0:T(8,128)(2,1)S(1)} collective-permute-done((bf16[80,1024]{1,0:T(8,128)(2,1)S(1)}, bf16[80,1024]{1,0:T(8,128)(2,1)S(1)}, u32[]{:S(2)}, u32[]{:S(2)}) %collective-permute-start.17) | collective-permute-done | bytes 163872 | tf_op jit(solution)/shard_map/ppermute | solution.py:14
  72.2 2.4 %shard_map.309.refs_16_ = bf16[480,256]{1,0:T(8,128)(2,1)S(1)} custom-call(s32[1]{0:T(128)S(6)} %copy.35.refs_0_, bf16[640,768]{1,0:T(8,128)(2,1)S(1)} %get-tuple-element.136.refs_1_.refs_11_), custom_call_target="tpu_custom_call" | custom-call | tf_op jit(solution)/shard_map/pallas_call | solution.py:96
  78.4 10.8 %shard_map.310 = (bf16[640,1024]{1,0:T(8,128)(2,1)}, bf16[640,1024]{1,0:T(8,128)(2,1)}, bf16[640,1024]{1,0:T(8,128)(2,1)}, bf16[640,1024]{1,0:T(8,128)(2,1)}, bf...) custom-call(bf16[80,1024]{1,0:T(8,128)(2,1)} %copy-done.18, ...), custom_call_target="tpu_custom_call" | custom-call | flops 6710886400 | bytes 7864320 | tf_op jit(solution)/shard_map/pallas_call | solution.py:96
  89.7 1.3 collective-permute-done.26
  90.9 1.0 add_convert_fusion.3.near
  91.9 1.6 collective-permute-start.27
  93.5 1.5 collective-permute-start.35
  95.1 1.1 slice.65
  96.8 1.6 collective-permute-done.27.far
  98.8 2.1 %collective-permute-start.32 = (bf16[96,1024]{1,0:T(8,128)(2,1)S(1)}, bf16[96,1024]{1,0:T(8,128)(2,1)S(1)}, u32[]{:S(2)}, u32[]{:S(2)}) collective-permute-start(bf16[96,1024]{1,0:T(8,128)(2,1)S(1)} %get-tuple-element.122.refs_1_), channel_id=1, source_target_pairs={{0,4},{4,0},{8,12},{12,8},{1,5},{5,1},{9,13},{13,9},{2,6},{6,2},{1... | collective-permute-start | bytes 589832 | tf_op jit(solution)/shard_map/ppermute | solution.py:14
  100.9 1.1 collective-permute-start.33
  101.9 2.5 %fusion.24 = f32[512,1024]{1,0:T(8,128)S(1)} fusion(bf16[640,512]{1,0:T(8,128)(2,1)S(1)} %slice.65, bf16[640,1024]{1,0:T(8,128)(2,1)} %get-tuple-element.135), kind=kOutput, calls=%fused_computation.62 | convolution fusion | flops 671088640 | bytes 4063232 | tf_op jit(solution)/shard_map/dot_general | solution.py:34
  104.4 1.5 collective-permute-start.34
  105.9 2.7 %collective-permute-done.35 = bf16[512,512]{1,0:T(8,128)(2,1)S(1)} collective-permute-done((bf16[512,512]{1,0:T(8,128)(2,1)}, bf16[512,512]{1,0:T(8,128)(2,1)S(1)}, u32[]{:S(2)}, u32[]{:S(2)}) %collective-permute-start.35) | collective-permute-done | bytes 524320 | tf_op jit(solution)/shard_map/ppermute | solution.py:14
  109.2 1.5 collective-permute-start.29
  110.8 5.6 %collective-permute-done.33.refs_5_ = bf16[96,1024]{1,0:T(8,128)(2,1)S(1)} collective-permute-done((bf16[96,1024]{1,0:T(8,128)(2,1)S(1)}, bf16[96,1024]{1,0:T(8,128)(2,1)S(1)}, u32[]{:S(2)}, u32[]{:S(2)}) %collective-permute-start.33) | collective-permute-done | bytes 196640 | tf_op jit(solution)/shard_map/ppermute | solution.py:14
  119.1 11.5 %shard_map.312 = (bf16[640,1024]{1,0:T(8,128)(2,1)}, bf16[640,768]{1,0:T(8,128)(2,1)S(1)}, bf16[80,1024]{1,0:T(8,128)(2,1)S(1)}, bf16[80,1024]{1,0:T(8,128)(2,1)...) custom-call(s32[1]{0:T(128)S(6)} %copy.35.refs_0_, ...), custom_call_target="tpu_custom_call" | custom-call | flops 1048576000 | bytes 5242880 | tf_op jit(solution)/shard_map/pallas_call | solution.py:96
  130.5 1.1 slice.74
  131.7 1.5 collective-permute-start.46
  133.2 4.5 %collective-permute-start.47 = (bf16[512,512]{1,0:T(8,128)(2,1)S(1)}, bf16[512,512]{1,0:T(8,128)(2,1)S(1)}, u32[]{:S(2)}, u32[]{:S(2)}) collective-permute-start(bf16[512,512]{1,0:T(8,128)(2,1)S(1)} %fusion), channel_id=1, source_target_pairs={{0,4},{4,0},{8,12},{12,8},{1,5},{5,1},{9,13},{13,9},{2,6},{6,2},{1... | collective-permute-start | bytes 1572872 | tf_op jit(solution)/shard_map/ppermute | solution.py:14
  138.6 1.6 convert_add_fusion
  140.3 1.6 collective-permute-start.41
  141.9 7.7 %collective-permute-done.47 = bf16[512,512]{1,0:T(8,128)(2,1)S(1)} collective-permute-done((bf16[512,512]{1,0:T(8,128)(2,1)S(1)}, bf16[512,512]{1,0:T(8,128)(2,1)S(1)}, u32[]{:S(2)}, u32[]{:S(2)}) %collective-permute-start.47) | collective-permute-done | bytes 524320 | tf_op jit(solution)/shard_map/ppermute | solution.py:14
  149.7 1.2 shard_map.314
  151.1 1.6 maximum_convert_fusion
  152.7 1.6 collective-permute-start.44
  157.5 3.0 %collective-permute-done.45 = f32[10,512]{1,0:T(8,128)S(1)} collective-permute-done((f32[10,512]{1,0:T(8,128)S(1)}, f32[10,512]{1,0:T(8,128)S(1)}, u32[]{:S(2)}, u32[]{:S(2)}) %collective-permute-start.45) | collective-permute-done | bytes 20512 | tf_op jit(solution)/shard_map/ppermute | solution.py:14
  164.3 2.6 %shard_map.315 = (f32[512,256]{1,0:T(8,128)}, f32[512,256]{1,0:T(8,128)}, f32[512,256]{1,0:T(8,128)}, f32[256,512]{1,0:T(8,128)}) custom-call(f32[512,768]{1,0:T(8,128)S(1)} %fusion.1.own, f32[256,512]{1,0:T(8,128)S(1)} %fusion.8.own_out, bf16[512,1024]{1,0:T(8,128)(2,1)} %collective-permute-done.46.got), custom_call_target="tpu_custom_call" | custom-call | tf_op jit(solution)/shard_map/pallas_call | solution.py:96
  (195 shorter events, 20.5 us)
Async XLA Ops:
  4.4 22.1 %collective-permute-start.1 = (bf16[528,768]{1,0:T(8,128)(2,1)}, bf16[528,768]{1,0:T(8,128)(2,1)S(1)}, u32[]{:S(2)}, u32[]{:S(2)}) collective-permute-start(bf16[528,768]{1,0:T(8,128)(2,1)} %get-tuple-element.89.refs_9_.refs_12_.refs_2_), channel_id=1, source_target_pairs={{0,16},{16,0},{1,17},{17,1},{2,18},{18,2},{3,19},{19,3},{4,20},{20... | collective-permute-start | bytes 2433032 | tf_op jit(solution)/shard_map/ppermute | solution.py:14
  7.4 7.9 %collective-permute-start = (bf16[80,1024]{1,0:T(8,128)(2,1)S(1)}, bf16[80,1024]{1,0:T(8,128)(2,1)S(1)}, u32[]{:S(2)}, u32[]{:S(2)}) collective-permute-start(bf16[80,1024]{1,0:T(8,128)(2,1)S(1)} %maximum_select_fusion.2.refs_1_.tokens), channel_id=1, source_target_pairs={{0,4},{4,0},{8,12},{12,8},{1,5},{5,1},{9,13},{13,9},{2,6},{6,2},{1... | collective-permute-start | bytes 491528 | tf_op jit(solution)/shard_map/ppermute | solution.py:14
  8.9 17.5 %collective-permute-start.3 = (bf16[80,1024]{1,0:T(8,128)(2,1)S(1)}, bf16[80,1024]{1,0:T(8,128)(2,1)S(1)}, u32[]{:S(2)}, u32[]{:S(2)}) collective-permute-start(bf16[80,1024]{1,0:T(8,128)(2,1)S(1)} %maximum_select_fusion.2.refs_1_.tokens), channel_id=1, source_target_pairs={{0,8},{4,12},{8,0},{12,4},{1,9},{5,13},{9,1},{13,5},{2,10},{6,14},... | collective-permute-start | bytes 491528 | tf_op jit(solution)/shard_map/ppermute | solution.py:14
  11.5 15.5 %collective-permute-start.5 = (bf16[80,1024]{1,0:T(8,128)(2,1)S(1)}, bf16[80,1024]{1,0:T(8,128)(2,1)S(1)}, u32[]{:S(2)}, u32[]{:S(2)}) collective-permute-start(bf16[80,1024]{1,0:T(8,128)(2,1)S(1)} %maximum_select_fusion.2.refs_1_.tokens), channel_id=1, source_target_pairs={{0,12},{4,8},{8,4},{12,0},{1,13},{5,9},{9,5},{13,1},{2,14},{6,10},... | collective-permute-start | bytes 491528 | tf_op jit(solution)/shard_map/ppermute | solution.py:14
  11.8 21.1 %collective-permute-start.7 = (bf16[256,512]{1,0:T(8,128)(2,1)}, bf16[256,512]{1,0:T(8,128)(2,1)S(1)}, u32[]{:S(2)}, u32[]{:S(2)}) collective-permute-start(bf16[256,512]{1,0:T(8,128)(2,1)} %refs_9_.1), channel_id=1, source_target_pairs={{0,16},{16,0},{1,17},{17,1},{2,18},{18,2},{3,19},{19,3},{4,20},{20... | collective-permute-start | bytes 786440 | tf_op jit(solution)/shard_map/ppermute | solution.py:14
  26.5 2.8 %collective-permute-start.2 = (bf16[80,1024]{1,0:T(8,128)(2,1)S(1)}, bf16[80,1024]{1,0:T(8,128)(2,1)S(1)}, u32[]{:S(2)}, u32[]{:S(2)}) collective-permute-start(bf16[80,1024]{1,0:T(8,128)(2,1)S(1)} %collective-permute-done.refs_3_), channel_id=1, source_target_pairs={{0,1},{1,0},{2,3},{3,2},{4,5},{5,4},{6,7},{7,6},{8,9},{9,8},{10,11... | collective-permute-start | bytes 491528 | tf_op jit(solution)/shard_map/ppermute | solution.py:14
  26.5 2.8 %collective-permute-start.4 = (bf16[80,1024]{1,0:T(8,128)(2,1)S(1)}, bf16[80,1024]{1,0:T(8,128)(2,1)S(1)}, u32[]{:S(2)}, u32[]{:S(2)}) collective-permute-start(bf16[80,1024]{1,0:T(8,128)(2,1)S(1)} %collective-permute-done.3.refs_5_), channel_id=1, source_target_pairs={{0,1},{1,0},{2,3},{3,2},{4,5},{5,4},{6,7},{7,6},{8,9},{9,8},{10,11... | collective-permute-start | bytes 491528 | tf_op jit(solution)/shard_map/ppermute | solution.py:14
  27.0 2.3 %collective-permute-start.6 = (bf16[80,1024]{1,0:T(8,128)(2,1)S(1)}, bf16[80,1024]{1,0:T(8,128)(2,1)S(1)}, u32[]{:S(2)}, u32[]{:S(2)}) collective-permute-start(bf16[80,1024]{1,0:T(8,128)(2,1)S(1)} %collective-permute-done.5.refs_7_), channel_id=1, source_target_pairs={{0,1},{1,0},{2,3},{3,2},{4,5},{5,4},{6,7},{7,6},{8,9},{9,8},{10,11... | collective-permute-start | bytes 491528 | tf_op jit(solution)/shard_map/ppermute | solution.py:14
  27.2 27.2 %collective-permute-start.13 = (bf16[512,1024]{1,0:T(8,128)(2,1)S(1)}, bf16[512,1024]{1,0:T(8,128)(2,1)S(1)}, u32[]{:S(2)}, u32[]{:S(2)}) collective-permute-start(bf16[512,1024]{1,0:T(8,128)(2,1)S(1)} %copy-done.25), channel_id=1, source_target_pairs={{0,16},{16,0},{1,17},{17,1},{2,18},{18,2},{3,19},{19,3},{4,20},{20... | collective-permute-start | bytes 3145736 | tf_op jit(solution)/shard_map/ppermute | solution.py:14
  34.9 5.5 %collective-permute-start.8 = (bf16[80,1024]{1,0:T(8,128)(2,1)S(1)}, bf16[80,1024]{1,0:T(8,128)(2,1)S(1)}, u32[]{:S(2)}, u32[]{:S(2)}) collective-permute-start(bf16[80,1024]{1,0:T(8,128)(2,1)S(1)} %get-tuple-element.97), channel_id=1, source_target_pairs={{0,1},{1,0},{2,3},{3,2},{4,5},{5,4},{6,7},{7,6},{8,9},{9,8},{10,11... | collective-permute-start | bytes 491528 | tf_op jit(solution)/shard_map/ppermute | solution.py:14
  35.1 42.6 %collective-permute-start.25 = (bf16[1024,512]{1,0:T(8,128)(2,1)S(1)}, bf16[1024,512]{1,0:T(8,128)(2,1)}, u32[]{:S(2)}, u32[]{:S(2)}) collective-permute-start(bf16[1024,512]{1,0:T(8,128)(2,1)S(1)} %copy-done.26), channel_id=1, source_target_pairs={{0,16},{16,0},{1,17},{17,1},{2,18},{18,2},{3,19},{19,3},{4,20},{20... | collective-permute-start | bytes 3145736 | tf_op jit(solution)/shard_map/ppermute | solution.py:14
  36.2 8.8 %collective-permute-start.10 = (bf16[80,1024]{1,0:T(8,128)(2,1)S(1)}, bf16[80,1024]{1,0:T(8,128)(2,1)S(1)}, u32[]{:S(2)}, u32[]{:S(2)}) collective-permute-start(bf16[80,1024]{1,0:T(8,128)(2,1)S(1)} %get-tuple-element.114.refs_8_.cot), channel_id=1, source_target_pairs={{0,4},{4,0},{8,12},{12,8},{1,5},{5,1},{9,13},{13,9},{2,6},{6,2},{1... | collective-permute-start | bytes 491528 | tf_op jit(solution)/shard_map/ppermute | solution.py:14
  37.8 15.0 %collective-permute-start.11 = (bf16[80,1024]{1,0:T(8,128)(2,1)S(1)}, bf16[80,1024]{1,0:T(8,128)(2,1)S(1)}, u32[]{:S(2)}, u32[]{:S(2)}) collective-permute-start(bf16[80,1024]{1,0:T(8,128)(2,1)S(1)} %get-tuple-element.114.refs_8_.cot), channel_id=1, source_target_pairs={{0,8},{4,12},{8,0},{12,4},{1,9},{5,13},{9,1},{13,5},{2,10},{6,14},... | collective-permute-start | bytes 491528 | tf_op jit(solution)/shard_map/ppermute | solution.py:14
  40.4 12.4 %collective-permute-start.12 = (bf16[80,1024]{1,0:T(8,128)(2,1)S(1)}, bf16[80,1024]{1,0:T(8,128)(2,1)S(1)}, u32[]{:S(2)}, u32[]{:S(2)}) collective-permute-start(bf16[80,1024]{1,0:T(8,128)(2,1)S(1)} %get-tuple-element.114.refs_8_.cot), channel_id=1, source_target_pairs={{0,12},{4,8},{8,4},{12,0},{1,13},{5,9},{9,5},{13,1},{2,14},{6,10},... | collective-permute-start | bytes 491528 | tf_op jit(solution)/shard_map/ppermute | solution.py:14
  45.1 7.8 %collective-permute-start.9 = (bf16[80,1024]{1,0:T(8,128)(2,1)S(1)}, bf16[80,1024]{1,0:T(8,128)(2,1)S(1)}, u32[]{:S(2)}, u32[]{:S(2)}) collective-permute-start(bf16[80,1024]{1,0:T(8,128)(2,1)S(1)} %add_convert_fusion.4.near), channel_id=1, source_target_pairs={{0,2},{1,3},{2,0},{3,1},{4,6},{5,7},{6,4},{7,5},{8,10},{9,11},{10,... | collective-permute-start | bytes 491528 | tf_op jit(solution)/shard_map/ppermute | solution.py:14
  55.4 7.3 %collective-permute-start.15 = (bf16[80,1024]{1,0:T(8,128)(2,1)S(1)}, bf16[80,1024]{1,0:T(8,128)(2,1)S(1)}, u32[]{:S(2)}, u32[]{:S(2)}) collective-permute-start(bf16[80,1024]{1,0:T(8,128)(2,1)S(1)} %get-tuple-element.108.refs_0_), channel_id=1, source_target_pairs={{0,4},{4,0},{8,12},{12,8},{1,5},{5,1},{9,13},{13,9},{2,6},{6,2},{1... | collective-permute-start | bytes 491528 | tf_op jit(solution)/shard_map/ppermute | solution.py:14
  57.2 14.5 %collective-permute-start.17 = (bf16[80,1024]{1,0:T(8,128)(2,1)S(1)}, bf16[80,1024]{1,0:T(8,128)(2,1)S(1)}, u32[]{:S(2)}, u32[]{:S(2)}) collective-permute-start(bf16[80,1024]{1,0:T(8,128)(2,1)S(1)} %get-tuple-element.108.refs_0_), channel_id=1, source_target_pairs={{0,8},{4,12},{8,0},{12,4},{1,9},{5,13},{9,1},{13,5},{2,10},{6,14},... | collective-permute-start | bytes 491528 | tf_op jit(solution)/shard_map/ppermute | solution.py:14
  59.8 11.9 %collective-permute-start.19 = (bf16[80,1024]{1,0:T(8,128)(2,1)S(1)}, bf16[80,1024]{1,0:T(8,128)(2,1)S(1)}, u32[]{:S(2)}, u32[]{:S(2)}) collective-permute-start(bf16[80,1024]{1,0:T(8,128)(2,1)S(1)} %get-tuple-element.108.refs_0_), channel_id=1, source_target_pairs={{0,12},{4,8},{8,4},{12,0},{1,13},{5,9},{9,5},{13,1},{2,14},{6,10},... | collective-permute-start | bytes 491528 | tf_op jit(solution)/shard_map/ppermute | solution.py:14
  59.8 15.5 %collective-permute-start.14 = (bf16[80,1024]{1,0:T(8,128)(2,1)S(1)}, bf16[80,1024]{1,0:T(8,128)(2,1)S(1)}, u32[]{:S(2)}, u32[]{:S(2)}) collective-permute-start(bf16[80,1024]{1,0:T(8,128)(2,1)S(1)} %get-tuple-element.108.refs_0_), channel_id=1, source_target_pairs={{0,1},{1,0},{2,3},{3,2},{4,5},{5,4},{6,7},{7,6},{8,9},{9,8},{10,11... | collective-permute-start | bytes 491528 | tf_op jit(solution)/shard_map/ppermute | solution.py:14
  62.7 12.8 %collective-permute-start.21 = (bf16[80,1024]{1,0:T(8,128)(2,1)S(1)}, bf16[80,1024]{1,0:T(8,128)(2,1)S(1)}, u32[]{:S(2)}, u32[]{:S(2)}) collective-permute-start(bf16[80,1024]{1,0:T(8,128)(2,1)S(1)} %get-tuple-element.114.refs_8_.cot), channel_id=1, source_target_pairs={{0,1},{1,0},{2,3},{3,2},{4,5},{5,4},{6,7},{7,6},{8,9},{9,8},{10,11... | collective-permute-start | bytes 491528 | tf_op jit(solution)/shard_map/ppermute | solution.py:14
  71.7 4.3 %collective-permute-start.22 = (bf16[80,1024]{1,0:T(8,128)(2,1)S(1)}, bf16[80,1024]{1,0:T(8,128)(2,1)S(1)}, u32[]{:S(2)}, u32[]{:S(2)}) collective-permute-start(bf16[80,1024]{1,0:T(8,128)(2,1)S(1)} %collective-permute-done.10.refs_10_), channel_id=1, source_target_pairs={{0,1},{1,0},{2,3},{3,2},{4,5},{5,4},{6,7},{7,6},{8,9},{9,8},{10,11... | collective-permute-start | bytes 491528 | tf_op jit(solution)/shard_map/ppermute | solution.py:14
  71.7 4.4 %collective-permute-start.23 = (bf16[80,1024]{1,0:T(8,128)(2,1)S(1)}, bf16[80,1024]{1,0:T(8,128)(2,1)S(1)}, u32[]{:S(2)}, u32[]{:S(2)}) collective-permute-start(bf16[80,1024]{1,0:T(8,128)(2,1)S(1)} %collective-permute-done.11.refs_12_), channel_id=1, source_target_pairs={{0,1},{1,0},{2,3},{3,2},{4,5},{5,4},{6,7},{7,6},{8,9},{9,8},{10,11... | collective-permute-start | bytes 491528 | tf_op jit(solution)/shard_map/ppermute | solution.py:14
  75.3 1.5 collective-permute-start.24
  75.5 1.5 collective-permute-start.16
  76.0 1.5 collective-permute-start.18
  76.1 1.5 collective-permute-start.20
  89.2 1.7 %collective-permute-start.26 = (bf16[80,1024]{1,0:T(8,128)(2,1)}, bf16[80,1024]{1,0:T(8,128)(2,1)S(1)}, u32[]{:S(2)}, u32[]{:S(2)}) collective-permute-start(bf16[80,1024]{1,0:T(8,128)(2,1)} %get-tuple-element.121), channel_id=1, source_target_pairs={{0,1},{1,0},{2,3},{3,2},{4,5},{5,4},{6,7},{7,6},{8,9},{9,8},{10,11... | collective-permute-start | bytes 491528 | tf_op jit(solution)/shard_map/ppermute | solution.py:14
  91.9 6.5 %collective-permute-start.27 = (bf16[80,1024]{1,0:T(8,128)(2,1)S(1)}, bf16[80,1024]{1,0:T(8,128)(2,1)S(1)}, u32[]{:S(2)}, u32[]{:S(2)}) collective-permute-start(bf16[80,1024]{1,0:T(8,128)(2,1)S(1)} %add_convert_fusion.3.near), channel_id=1, source_target_pairs={{0,2},{1,3},{2,0},{3,1},{4,6},{5,7},{6,4},{7,5},{8,10},{9,11},{10,... | collective-permute-start | bytes 491528 | tf_op jit(solution)/shard_map/ppermute | solution.py:14
  93.5 15.1 %collective-permute-start.35 = (bf16[512,512]{1,0:T(8,128)(2,1)}, bf16[512,512]{1,0:T(8,128)(2,1)S(1)}, u32[]{:S(2)}, u32[]{:S(2)}) collective-permute-start(bf16[512,512]{1,0:T(8,128)(2,1)} %get-tuple-element.126), channel_id=1, source_target_pairs={{0,16},{16,0},{1,17},{17,1},{2,18},{18,2},{3,19},{19,3},{4,20},{20... | collective-permute-start | bytes 1572872 | tf_op jit(solution)/shard_map/ppermute | solution.py:14
  96.2 42.4 %collective-permute-start.39 = (bf16[512,1024]{1,0:T(8,128)(2,1)}, bf16[512,1024]{1,0:T(8,128)(2,1)S(1)}, u32[]{:S(2)}, u32[]{:S(2)}) collective-permute-start(bf16[512,1024]{1,0:T(8,128)(2,1)} %get-tuple-element.140), channel_id=1, source_target_pairs={{0,16},{16,0},{1,17},{17,1},{2,18},{18,2},{3,19},{19,3},{4,20},{20... | collective-permute-start | bytes 3145736 | tf_op jit(solution)/shard_map/ppermute | solution.py:14
  98.8 10.5 %collective-permute-start.32 = (bf16[96,1024]{1,0:T(8,128)(2,1)S(1)}, bf16[96,1024]{1,0:T(8,128)(2,1)S(1)}, u32[]{:S(2)}, u32[]{:S(2)}) collective-permute-start(bf16[96,1024]{1,0:T(8,128)(2,1)S(1)} %get-tuple-element.122.refs_1_), channel_id=1, source_target_pairs={{0,4},{4,0},{8,12},{12,8},{1,5},{5,1},{9,13},{13,9},{2,6},{6,2},{1... | collective-permute-start | bytes 589832 | tf_op jit(solution)/shard_map/ppermute | solution.py:14
  100.9 15.5 %collective-permute-start.33 = (bf16[96,1024]{1,0:T(8,128)(2,1)S(1)}, bf16[96,1024]{1,0:T(8,128)(2,1)S(1)}, u32[]{:S(2)}, u32[]{:S(2)}) collective-permute-start(bf16[96,1024]{1,0:T(8,128)(2,1)S(1)} %get-tuple-element.122.refs_1_), channel_id=1, source_target_pairs={{0,8},{4,12},{8,0},{12,4},{1,9},{5,13},{9,1},{13,5},{2,10},{6,14},... | collective-permute-start | bytes 589832 | tf_op jit(solution)/shard_map/ppermute | solution.py:14
  101.9 2.5 %collective-permute-start.28 = (bf16[80,1024]{1,0:T(8,128)(2,1)S(1)}, bf16[80,1024]{1,0:T(8,128)(2,1)S(1)}, u32[]{:S(2)}, u32[]{:S(2)}) collective-permute-start(bf16[80,1024]{1,0:T(8,128)(2,1)S(1)} %copy-done.31), channel_id=1, source_target_pairs={{0,1},{1,0},{2,3},{3,2},{4,5},{5,4},{6,7},{7,6},{8,9},{9,8},{10,11... | collective-permute-start | bytes 491528 | tf_op jit(solution)/shard_map/ppermute | solution.py:14
  104.4 11.9 %collective-permute-start.34 = (bf16[96,1024]{1,0:T(8,128)(2,1)S(1)}, bf16[96,1024]{1,0:T(8,128)(2,1)S(1)}, u32[]{:S(2)}, u32[]{:S(2)}) collective-permute-start(bf16[96,1024]{1,0:T(8,128)(2,1)S(1)} %get-tuple-element.122.refs_1_), channel_id=1, source_target_pairs={{0,12},{4,8},{8,4},{12,0},{1,13},{5,9},{9,5},{13,1},{2,14},{6,10},... | collective-permute-start | bytes 589832 | tf_op jit(solution)/shard_map/ppermute | solution.py:14
  108.6 9.1 %collective-permute-start.31 = (bf16[96,1024]{1,0:T(8,128)(2,1)S(1)}, bf16[96,1024]{1,0:T(8,128)(2,1)S(1)}, u32[]{:S(2)}, u32[]{:S(2)}) collective-permute-start(bf16[96,1024]{1,0:T(8,128)(2,1)S(1)} %get-tuple-element.122.refs_1_), channel_id=1, source_target_pairs={{0,1},{1,0},{2,3},{3,2},{4,5},{5,4},{6,7},{7,6},{8,9},{9,8},{10,11... | collective-permute-start | bytes 589832 | tf_op jit(solution)/shard_map/ppermute | solution.py:14
  109.2 8.3 %collective-permute-start.29 = (bf16[80,1024]{1,0:T(8,128)(2,1)S(1)}, bf16[80,1024]{1,0:T(8,128)(2,1)S(1)}, u32[]{:S(2)}, u32[]{:S(2)}) collective-permute-start(bf16[80,1024]{1,0:T(8,128)(2,1)S(1)} %add_convert_fusion.2), channel_id=1, source_target_pairs={{0,2},{1,3},{2,0},{3,1},{4,6},{5,7},{6,4},{7,5},{8,10},{9,11},{10,... | collective-permute-start | bytes 491528 | tf_op jit(solution)/shard_map/ppermute | solution.py:14
  116.3 1.9 %collective-permute-start.36 = (bf16[96,1024]{1,0:T(8,128)(2,1)S(1)}, bf16[96,1024]{1,0:T(8,128)(2,1)S(1)}, u32[]{:S(2)}, u32[]{:S(2)}) collective-permute-start(bf16[96,1024]{1,0:T(8,128)(2,1)S(1)} %collective-permute-done.32.refs_3_), channel_id=1, source_target_pairs={{0,1},{1,0},{2,3},{3,2},{4,5},{5,4},{6,7},{7,6},{8,9},{9,8},{10,11... | collective-permute-start | bytes 589832 | tf_op jit(solution)/shard_map/ppermute | solution.py:14
  116.3 1.9 %collective-permute-start.37 = (bf16[96,1024]{1,0:T(8,128)(2,1)S(1)}, bf16[96,1024]{1,0:T(8,128)(2,1)S(1)}, u32[]{:S(2)}, u32[]{:S(2)}) collective-permute-start(bf16[96,1024]{1,0:T(8,128)(2,1)S(1)} %collective-permute-done.33.refs_5_), channel_id=1, source_target_pairs={{0,1},{1,0},{2,3},{3,2},{4,5},{5,4},{6,7},{7,6},{8,9},{9,8},{10,11... | collective-permute-start | bytes 589832 | tf_op jit(solution)/shard_map/ppermute | solution.py:14
  117.5 1.5 collective-permute-start.38
  117.7 20.0 %collective-permute-start.30 = (bf16[80,1024]{1,0:T(8,128)(2,1)S(1)}, bf16[80,1024]{1,0:T(8,128)(2,1)S(1)}, u32[]{:S(2)}, u32[]{:S(2)}) collective-permute-start(bf16[80,1024]{1,0:T(8,128)(2,1)S(1)} %add_convert_fusion.1), channel_id=1, source_target_pairs={{0,1},{1,0},{2,3},{3,2},{4,5},{5,4},{6,7},{7,6},{8,9},{9,8},{10,11... | collective-permute-start | bytes 491528 | tf_op jit(solution)/shard_map/ppermute | solution.py:14
  131.7 32.6 %collective-permute-start.46 = (bf16[512,1024]{1,0:T(8,128)(2,1)}, bf16[512,1024]{1,0:T(8,128)(2,1)}, u32[]{:S(2)}, u32[]{:S(2)}) collective-permute-start(bf16[512,1024]{1,0:T(8,128)(2,1)} %get-tuple-element.153), channel_id=1, source_target_pairs={{0,16},{16,0},{1,17},{17,1},{2,18},{18,2},{3,19},{19,3},{4,20},{20... | collective-permute-start | bytes 3145736 | tf_op jit(solution)/shard_map/ppermute | solution.py:14
  133.2 16.5 %collective-permute-start.47 = (bf16[512,512]{1,0:T(8,128)(2,1)S(1)}, bf16[512,512]{1,0:T(8,128)(2,1)S(1)}, u32[]{:S(2)}, u32[]{:S(2)}) collective-permute-start(bf16[512,512]{1,0:T(8,128)(2,1)S(1)} %fusion), channel_id=1, source_target_pairs={{0,4},{4,0},{8,12},{12,8},{1,5},{5,1},{9,13},{13,9},{2,6},{6,2},{1... | collective-permute-start | bytes 1572872 | tf_op jit(solution)/shard_map/ppermute | solution.py:14
  138.6 1.6 collective-permute-start.40
  140.3 9.4 %collective-permute-start.41 = (bf16[80,1024]{1,0:T(8,128)(2,1)S(1)}, bf16[80,1024]{1,0:T(8,128)(2,1)S(1)}, u32[]{:S(2)}, u32[]{:S(2)}) collective-permute-start(bf16[80,1024]{1,0:T(8,128)(2,1)S(1)} %add_convert_fusion.near), channel_id=1, source_target_pairs={{0,2},{1,3},{2,0},{3,1},{4,6},{5,7},{6,4},{7,5},{8,10},{9,11},{10,... | collective-permute-start | bytes 491528 | tf_op jit(solution)/shard_map/ppermute | solution.py:14
  151.0 1.7 %collective-permute-start.43 = (f32[2,1024]{1,0:T(2,128)S(1)}, f32[2,1024]{1,0:T(2,128)S(1)}, u32[]{:S(2)}, u32[]{:S(2)}) collective-permute-start(f32[2,1024]{1,0:T(2,128)S(1)} %shard_map.314), channel_id=1, source_target_pairs={{0,1},{1,0},{2,3},{3,2},{4,5},{5,4},{6,7},{7,6},{8,9},{9,8},{10,11... | collective-permute-start | bytes 24584 | tf_op jit(solution)/shard_map/ppermute | solution.py:14
  152.7 3.7 %collective-permute-start.44 = (f32[2,1024]{1,0:T(2,128)S(1)}, f32[2,1024]{1,0:T(2,128)S(1)}, u32[]{:S(2)}, u32[]{:S(2)}) collective-permute-start(f32[2,1024]{1,0:T(2,128)S(1)} %add.78), channel_id=1, source_target_pairs={{0,2},{1,3},{2,0},{3,1},{4,6},{5,7},{6,4},{7,5},{8,10},{9,11},{10,... | collective-permute-start | bytes 24584 | tf_op jit(solution)/shard_map/ppermute | solution.py:14
  155.5 7.8 %collective-permute-start.42 = (f32[80,1024]{1,0:T(8,128)S(1)}, f32[80,1024]{1,0:T(8,128)S(1)}, u32[]{:S(2)}, u32[]{:S(2)}) collective-permute-start(f32[80,1024]{1,0:T(8,128)S(1)} %shard_map.313), channel_id=1, source_target_pairs={{0,1},{1,0},{2,3},{3,2},{4,5},{5,4},{6,7},{7,6},{8,9},{9,8},{10,11... | collective-permute-start | bytes 983048 | tf_op jit(solution)/shard_map/ppermute | solution.py:14
  156.5 4.0 %collective-permute-start.45 = (f32[10,512]{1,0:T(8,128)S(1)}, f32[10,512]{1,0:T(8,128)S(1)}, u32[]{:S(2)}, u32[]{:S(2)}) collective-permute-start(f32[10,512]{1,0:T(8,128)S(1)} %pad_maximum_fusion.3), channel_id=1, source_target_pairs={{0,16},{16,0},{1,17},{17,1},{2,18},{18,2},{3,19},{19,3},{4,20},{20... | collective-permute-start | bytes 61448 | tf_op jit(solution)/shard_map/ppermute | solution.py:14
  (45 other events, 548.8 us)

commit v6 on v5

--- a/solution.py
+++ b/solution.py
@@ -113,7 +113,7 @@
 
 
 QBIAS, VBIAS, EBIAS = 6, 7, 8
-FIRST_COST = 20_000_000_000
+FIRST_COST = 1_000_000_000
 
 
 def pack_body(*refs):
@@ -214,14 +214,14 @@
     pieces, refs = refs[:blocks], refs[blocks:]
     packed, lines, refs = refs[:ways], refs[ways], refs[ways + 1 :]
     vec, xhat, normed, qkv, context = refs
-    rows = pieces[0].shape[0]
+    rows = pieces[0].shape[0] // 2
     if ways == 2:
         merge(lines, packed[1], vec)
     else:
         vec[...] = lines[...]
     features = heads * head_dim
     for n, piece in enumerate(pieces):
-        part = normed_rows(piece[...].astype(WIDE))
+        part = normed_rows(piece[:rows, :].astype(WIDE))
         xhat[n * rows : (n + 1) * rows, :] = part.astype(LOW)
         normed[n * rows : (n + 1) * rows, :] = (part * vec[0:1, :] + vec[1:2, :]).astype(LOW)
     size = normed.shape[1] // ways
@@ -252,7 +252,7 @@
 
 
 def second_body(tokens, near, far, vec, hidden, normed):
-    total = tokens[...].astype(WIDE) + (near[...].astype(WIDE) + far[...].astype(WIDE))
+    total = tokens[: near.shape[0], :].astype(WIDE) + (near[...].astype(WIDE) + far[...].astype(WIDE))
     total = total + vec[2:3, :]
     hidden[...] = total
     normed[...] = (normed_rows(total) * vec[3:4, :] + vec[4:5, :]).astype(LOW)
@@ -271,7 +271,7 @@
     for n in range(blocks):
         normed_all[n * rows : (n + 1) * rows, :] = normed[n][...]
     for n in range(blocks):
-        cot_all[n * rows : (n + 1) * rows, :] = cots[n][...]
+        cot_all[n * rows : (n + 1) * rows, :] = cots[n][rows:, :]
     cot_sum[...] = jnp.sum(cot_all[...].astype(WIDE), 0, keepdims=True)
     step = min(256, units, size)
     back = [jnp.zeros((2 * rows, size), WIDE) for _ in range(ways)]
@@ -309,7 +309,7 @@
 def second_back_body(near, far, hidden, cot, vec, grad_hidden, grad_branch):
     upstream = near[...].astype(WIDE) + far[...].astype(WIDE)
     grad, xhat = norm_back_rows(hidden[...], vec[3:4, :], upstream)
-    total = grad + cot[...].astype(WIDE)
+    total = grad + cot[grad.shape[0] :, :].astype(WIDE)
     grad_hidden[...] = total
     rows = total.shape[0]
     grad_branch[:rows, :] = total.astype(LOW)
@@ -399,7 +399,9 @@
         out[1:2, columns] = jnp.sum(part, 0, keepdims=True)
 
 
-def last_body(own, own_out, got, query, key, value, out):
+def last_body(own, own_out, got, sums, plain, lines, *outs):
+    query, key, value, out = outs[:4]
+    vectors, (qbias, vbias, ebias) = outs[4:10], outs[10:]
     size = query.shape[1]
     for n, ref in enumerate((query, key, value)):
         columns = slice(n * size, (n + 1) * size)
@@ -407,11 +409,26 @@
     for n in range(out.shape[1] // size):
         columns = slice(n * size, (n + 1) * size)
         out[:, columns] = own_out[:, columns] + got[columns, 3 * size :].astype(WIDE)
+    count = len(vectors)
+    total = sums[...] + lines[:count, :]
+    for n, ref in enumerate(vectors):
+        ref[...] = total[n : n + 1, :].reshape(ref.shape)
+    heads, units = (
+        plain[n : n + 1, :]
+        + jnp.concatenate([lines[count + n : count + n + 1, :], lines[count + 2 + n : count + 3 + n, :]], 1)
+        for n in range(2)
+    )
+    upper = lax.axis_index("fsdp") == 1
+    for ref, row, start in ((qbias, heads, 0), (vbias, heads, 2 * size), (ebias, units, 0)):
+        groups, half = ref.shape
+        for g in range(groups):
+            at = start + 2 * g * half
+            ref[g : g + 1, :] = jnp.where(upper, row[:, at + half : at + 2 * half], row[:, at : at + half])
 
 
 def first_back_body(near, far, tokens, grad_hidden, vec, out):
     upstream = near[...].astype(WIDE) + far[...].astype(WIDE)
-    grad, _ = norm_back_rows(tokens[...].astype(WIDE), vec[0:1, :], upstream)
+    grad, _ = norm_back_rows(tokens[: near.shape[0], :].astype(WIDE), vec[0:1, :], upstream)
     out[...] = grad + grad_hidden[...]
 
 
@@ -462,7 +479,10 @@
     def piece_of(value, which):
         return turned(lax.dynamic_slice_in_dim(value.reshape(seq, width), which * half, half, 0))
 
-    token_piece = piece_of(tokens, core)
+    def pieces_of(which):
+        return jnp.concatenate([piece_of(tokens, which), piece_of(cotangent, which)], 0)
+
+    own_piece = pieces_of(core)
     vectors = (gain_first, shift_first, output_bias, gain_second, shift_second, reduce_bias)
     biases = (query_bias, value_bias, expand_bias)
     thirds = (query_weight, key_weight, value_weight)
@@ -472,7 +492,7 @@
         message, lines = kernel(
             pack_body,
             (low(share + 16, 3 * features), wide(16, 3 * features)),
-            after(query_weight, token_piece),
+            after(query_weight, own_piece),
             key_weight,
             value_weight,
             *vectors,
@@ -498,15 +518,12 @@
         expand_parts = (gather(expand_weight),)
         reduce_parts = (gather(reduce_weight, 1),)
 
-    mine_tokens = spread_context(token_piece)
-    token_pieces = woven(
+    mine_tokens = spread_context(own_piece)
+    both_pieces = woven(
         mine_tokens,
-        [piece_of(tokens, 1 - core)]
+        [pieces_of(1 - core)]
         + [swap(after(m, packed[-1]), "tensor", 1) for m in mine_tokens[1:]],
     )
-    cot_piece = piece_of(cotangent, core)
-    mine_cots = spread_context(after(cot_piece, *mine_tokens[1:]))
-    mine_cots = list(lax.optimization_barrier(tuple(mine_cots)))
     if pair:
         expand_parts = (expand_weight, across(after(expand_weight, mine_tokens[1])))
 
@@ -519,7 +536,7 @@
             low(length, 3 * features),
             low(seq, features),
         ),
-        *token_pieces,
+        *both_pieces,
         *packed,
         lines,
         count=valid_count,
@@ -532,22 +549,20 @@
         *output_parts,
     )
     near, far = last_terms(keep, send)
-    far, *mine_cots = lax.optimization_barrier((far, *mine_cots))
-    far = after(far, expand_parts[-1])
-    cots = woven(mine_cots, [swap(m, "tensor", 1) for m in mine_cots])
-    hidden, normed_piece = kernel(
-        second_body, (wide(half, width), low(half, width)), token_piece, near, far, vec
-    )
-
     context_rest = kernel(
         lambda *refs: rest_body(heads, head_dim, seq, *refs),
         low(length - seq, features),
         after(qkv, near),
         count=valid_count,
     )
+    far = after(far, context_rest)
+    hidden, normed_piece = kernel(
+        second_body, (wide(half, width), low(half, width)), own_piece, near, far, vec
+    )
+
     mine_normed = spread_context(normed_piece)
     theirs = [swap(m, "tensor", 1) for m in mine_normed[:1]]
-    mine_normed[1:] = [after(m, context_rest, expand_parts[-1]) for m in mine_normed[1:]]
+    mine_normed[1:] = [after(m, expand_parts[-1]) for m in mine_normed[1:]]
     theirs += [swap(m, "tensor", 1) for m in mine_normed[1:]]
     (
         normed_two,
@@ -569,7 +584,7 @@
         + (wide(1, units), wide(1, width))
         + ((low(units // 2, share), low(share, units)) if pair else ()),
         *woven(mine_normed, theirs),
-        *cots,
+        *both_pieces,
         vec,
         *expand_parts,
         *reduce_parts,
@@ -589,7 +604,7 @@
         near,
         far,
         hidden,
-        cot_piece,
+        own_piece,
         vec,
     )
 
@@ -625,8 +640,8 @@
     ready = [out_far]
     theirs = [swap(m, "tensor", 1) for m in mine_grads[:1]]
     if pair:
-        *mine_grads[1:], reduce_got = lax.optimization_barrier((*mine_grads[1:], reduce_got))
         reduce_half = pin((dot_lt(act_half, cot_own) + reduce_got.astype(WIDE)).astype(LOW))
+        mine_grads[1:] = lax.optimization_barrier((*mine_grads[1:], reduce_got))[:-1]
         expand_own = pin(dot_lt(after(normed_own, grad_piece), grad_expanded))
         ready += [reduce_half, expand_own]
     theirs += [swap(m, "tensor", 1) for m in mine_grads[1:]]
@@ -660,12 +675,10 @@
     near, far = last_terms(keep, send)
     gn_far = far
     if pair:
-        grad_reduce = both_halves(
-            reduce_half, swap(after(reduce_half, head_sum), "context", 1), 0
-        )
+        reduce_theirs = swap(reduce_half, "context", 1)
         grad_expand = expand_own + expand_got.astype(WIDE)
     grad_token_piece = kernel(
-        first_back_body, wide(half, width), near, far, token_piece, grad_hidden, vec
+        first_back_body, wide(half, width), near, far, own_piece, grad_hidden, vec
     )
 
     def both_cores(value):
@@ -680,24 +693,12 @@
     reduced = out_near.astype(WIDE) + out_far.astype(WIDE) + vec[5:6, :]
     output = both_cores((hidden + reduced).astype(LOW))
 
-    if pair:
-        grad_query, grad_key, grad_value, grad_output = kernel(
-            last_body,
-            (wide(share, features),) * 3 + (wide(features, share),),
-            dot_lt(segments(normed_all, 2)[0], after(grad_qkv, gn_far)),
-            dot_lt(jnp.concatenate([context_own, context_rest], 0), after(segments(grad_branch, 2)[0], gn_far)),
-            qkv_got,
-        )
-    else:
+    if not pair:
         grad_weights = scatter(dot_lt(normed_all, grad_qkv), 0).astype(WIDE)
         grad_query, grad_key, grad_value = jnp.split(grad_weights, 3, 1)
         context_all = jnp.concatenate([context_own, context_rest], 0)
         grad_output = scatter(dot_lt(context_all, grad_branch), 1).astype(WIDE)
 
-    def own_rows(value):
-        size = value.shape[0] // ways
-        return lax.dynamic_slice_in_dim(value, mine * size, size, 0)
-
     first_sums = kernel(
         lambda *refs: first_sums_body(parts, *refs), wide(2, width), after(grad_qkv, gn_far), xhat_all, *packed
     )
@@ -705,23 +706,47 @@
     while bit < lax.axis_size("tensor"):
         first_sums = first_sums + swap(first_sums, "tensor", bit)
         bit *= 2
+    if pair:
+        grad_reduce = both_halves(reduce_half, after(reduce_theirs, gn_far), 0)
     sums = jnp.concatenate([first_sums, norm_sums, branch_sum, cot_sum], 0)
     plain = jnp.concatenate(
         [jnp.pad(head_sum, ((0, 0), (0, width - 3 * features))), unit_sum], 0
     )
     if pair:
         own, other = segments(sums, 2)
-        got = across(jnp.concatenate([other, *segments(plain, 2)], 0))
-        sums = own + got[:6]
-        plain = plain + jnp.concatenate([got[6:8], got[8:10]], 1)
+        lines = across(jnp.concatenate([other, *segments(plain, 2)], 0))
+        grads = kernel(
+            last_body,
+            (wide(share, features),) * 3
+            + (wide(features, share),)
+            + (wide(share),) * 6
+            + (wide(heads, head_dim // 2),) * 2
+            + (wide(expand_bias.shape[1], expand_bias.shape[0]),),
+            after(dot_lt(segments(after(normed_all, gn_far), 2)[0], grad_qkv), grad_tokens, output),
+            dot_lt(
+                jnp.concatenate([context_own, context_rest], 0),
+                segments(after(grad_branch, gn_far), 2)[0],
+            ),
+            qkv_got,
+            own,
+            plain,
+            lines,
+        )
+        grad_query, grad_key, grad_value, grad_output, *sums = grads[:10]
+        grad_qbias, grad_vbias, grad_ebias = (g.T for g in grads[10:])
     else:
         sums = scatter(sums, 1).astype(WIDE)
         plain = lax.psum(plain, "fsdp")
-    grad_ebias = own_rows(plain[1].reshape(-1, expand_bias.shape[0] * ways).T)
-    grad_qbias, grad_vbias = (
-        own_rows(plain[0, n * features : (n + 1) * features].reshape(heads, head_dim).T)
-        for n in (0, 2)
-    )
+
+        def own_rows(value):
+            size = value.shape[0] // ways
+            return lax.dynamic_slice_in_dim(value, mine * size, size, 0)
+
+        grad_ebias = own_rows(plain[1].reshape(-1, expand_bias.shape[0] * ways).T)
+        grad_qbias, grad_vbias = (
+            own_rows(plain[0, n * features : (n + 1) * features].reshape(heads, head_dim).T)
+            for n in (0, 2)
+        )
     return (
         output,
         grad_tokens,

time: 167 us -> 161 us (0.964)
  starting transfers between devices: 45.5 us -> 40.4 us
  Pallas kernels: 36.8 us -> 34.9 us
  other arithmetic: 6.58 us -> 8.44 us
    ppermute x48 -> x41, starting transfers between devices: 45.5 us -> 40.4 us  [swap(): lax.ppermute(block, axis, [(i, i ^ bit) for i in range(lax.axis_size(axis...]
    dynamic_slice x3 -> x0, local copies, waits for them, and re-layouts: 1.96 us -> none  [own_rows(): return lax.dynamic_slice_in_dim(value, mine * size, size, 0)]
    pallas_call x11, Pallas kernels: 36.8 us -> 34.9 us  [kernel(): pl.pallas_call(run if staged else body, out_shape=out_shape, in_specs=[pl...]
    select_n x4 -> x6, other arithmetic: 1.87 us -> 3.73 us  [turned(): return jnp.where(second, jnp.concatenate([right, left], -1), value)]
    split x3 -> x4, local copies, waits for them, and re-layouts: 0.04 us -> 1.9 us  [turned(): left, right = jnp.split(value, 2, -1)]
    unnamed x90 -> x86, local copies, waits for them, and re-layouts: 2.89 us -> 3.9 us
    ppermute x48 -> x41, waiting for transfers between devices: 62.7 us -> 62.3 us  [swap(): lax.ppermute(block, axis, [(i, i ^ bit) for i in range(lax.axis_size(axis...]
  transfers between devices with their start and end apart: 48 -> 41, of which waited for: 20 -> 19; matrix products, arithmetic and copies ran while one was open for 9% -> 8% of each run, Pallas kernels for 12% -> 12%
where the time goes in v6:
time: 161 us; the launch traced here: 160 us
  waiting for transfers between devices  62.3 us (39%)
  starting transfers between devices  40.4 us (25%)
  Pallas kernels  34.9 us (22%)
  local copies, waits for them, and re-layouts  8.88 us (6%)
  other arithmetic  8.44 us (5%)
  matrix products  2.83 us (2%)
  between operations  2.3 us (1%)
    ppermute x41, waiting for transfers between devices, swap(): lax.ppermute(block, axis, [(i, i ^ bit) for i in range(lax.axis_size(axis...  62.3 us
    ppermute x41, starting transfers between devices, swap(): lax.ppermute(block, axis, [(i, i ^ bit) for i in range(lax.axis_size(axis...  40.4 us
    pallas_call x11, Pallas kernels, kernel(): pl.pallas_call(run if staged else body, out_shape=out_shape, in_specs=[pl...  34.9 us
    unnamed x86, local copies, waits for them, and re-layouts  3.9 us
    select_n x6, other arithmetic, turned(): return jnp.where(second, jnp.concatenate([right, left], -1), value)  3.73 us
  transfers between devices with their start and end apart: 41, of which 19 were waited for; matrix products, arithmetic and copies ran while one was open for 8% of the time, Pallas kernels for 12%

profile of v6, /device:TPU:0, one launch (start us, length us, event | category | flops | bytes accessed | tf_op | source)
XLA Modules:
  0.0 160.1 jit_solution(16668787760573381320)
XLA Ops:
  0.7 1.9 %dynamic-slice_bitcast_fusion = (bf16[80,1024]{1,0:T(8,128)(2,1)}, bf16[80,1024]{1,0:T(8,128)(2,1)S(1)}, bf16[80,1024]{1,0:T(8,128)(2,1)S(1)}, bf16[80,1024]{1,0:T(8,128)(2,1)}) fusion(bf16[1,160,1024]{2,1,0:T(8,128)(2,1)} %param.19, s32[]{:T(128)S(6)} %select_n.97, s32[]{:T(128)S(6)} %select_n.94, bf16[1,160,1024]{2,1,0:T(8,128)(2,1)} %param.18), kind=kLoop, calls=%fused_computation.40 | loop fusion | bytes 1310728 | tf_op jit(solution)/shard_map/dynamic_slice | solution.py:480
  2.8 2.6 %shard_map.305 = (bf16[528,768]{1,0:T(8,128)(2,1)}, f32[16,768]{1,0:T(8,128)}) custom-call(bf16[512,256]{1,0:T(8,128)(2,1)} %refs_0_.3, bf16[512,256]{1,0:T(8,128)(2,1)} %refs_1_.2, bf16[512,256]{1,0:T(8,128)(2,1)} %refs_2_.1, bf16[512]{0:T(512)(128)(2,1)} %refs_3_.1, bf16[512]{0:T(512)(128)(2,1)} %refs_4_.1, bf16[512]{0:T(512)(128)(2,1)} %refs_5_.1, ...), custom_call_target="tpu_custom_call" | custom-call | tf_op jit(solution)/shard_map/pallas_call | solution.py:96
  5.4 3.0 %collective-permute-start.1 = (bf16[528,768]{1,0:T(8,128)(2,1)}, bf16[528,768]{1,0:T(8,128)(2,1)S(1)}, u32[]{:S(2)}, u32[]{:S(2)}) collective-permute-start(bf16[528,768]{1,0:T(8,128)(2,1)} %get-tuple-element.89.refs_9_.refs_12_.refs_2_), channel_id=1, source_target_pairs={{0,16},{16,0},{1,17},{17,1},{2,18},{18,2},{3,19},{19,3},{4,20},{20... | collective-permute-start | bytes 2433032 | tf_op jit(solution)/shard_map/ppermute | solution.py:14
  8.4 1.6 collective-permute-start
  10.0 2.6 %collective-permute-start.3 = (bf16[160,1024]{1,0:T(8,128)(2,1)S(1)}, bf16[160,1024]{1,0:T(8,128)(2,1)S(1)}, u32[]{:S(2)}, u32[]{:S(2)}) collective-permute-start(bf16[160,1024]{1,0:T(8,128)(2,1)S(1)} %pad_maximum_fusion.1.refs_1_.tokens.refs_8_.cot), channel_id=1, source_target_pairs={{0,8},{4,12},{8,0},{12,4},{1,9},{5,13},{9,1},{13,5},{2,10},{6,14},... | collective-permute-start | bytes 983048 | tf_op jit(solution)/shard_map/ppermute | solution.py:14
  13.1 0.9 fusion.20
  14.1 1.0 maximum_select_fusion.5
  15.0 8.7 %collective-permute-done.refs_3_.refs_10_ = bf16[160,1024]{1,0:T(8,128)(2,1)S(1)} collective-permute-done((bf16[160,1024]{1,0:T(8,128)(2,1)S(1)}, bf16[160,1024]{1,0:T(8,128)(2,1)S(1)}, u32[]{:S(2)}, u32[]{:S(2)}) %collective-permute-start) | collective-permute-done | bytes 327712 | tf_op jit(solution)/shard_map/ppermute | solution.py:14
  23.7 3.8 %collective-permute-done.1.refs_10_.refs_13_.refs_3_ = bf16[528,768]{1,0:T(8,128)(2,1)S(1)} collective-permute-done((bf16[528,768]{1,0:T(8,128)(2,1)}, bf16[528,768]{1,0:T(8,128)(2,1)S(1)}, u32[]{:S(2)}, u32[]{:S(2)}) %collective-permute-start.1) | collective-permute-done | bytes 811040 | tf_op jit(solution)/shard_map/ppermute | solution.py:14
  27.5 0.9 fusion.19
  28.5 2.1 %collective-permute-start.12 = (bf16[512,1024]{1,0:T(8,128)(2,1)}, bf16[512,1024]{1,0:T(8,128)(2,1)S(1)}, u32[]{:S(2)}, u32[]{:S(2)}) collective-permute-start(bf16[512,1024]{1,0:T(8,128)(2,1)} %refs_17_.1), channel_id=1, source_target_pairs={{0,16},{16,0},{1,17},{17,1},{2,18},{18,2},{3,19},{19,3},{4,20},{20... | collective-permute-start | bytes 3145736 | tf_op jit(solution)/shard_map/ppermute | solution.py:14
  30.6 5.0 %collective-permute-done.3.refs_5_.refs_12_ = bf16[160,1024]{1,0:T(8,128)(2,1)S(1)} collective-permute-done((bf16[160,1024]{1,0:T(8,128)(2,1)S(1)}, bf16[160,1024]{1,0:T(8,128)(2,1)S(1)}, u32[]{:S(2)}, u32[]{:S(2)}) %collective-permute-start.3) | collective-permute-done | bytes 327712 | tf_op jit(solution)/shard_map/ppermute | solution.py:14
  36.1 1.0 maximum_select_fusion.4
  37.9 3.5 %shard_map.306 = (f32[16,1024]{1,0:T(8,128)S(1)}, bf16[640,1024]{1,0:T(8,128)(2,1)}, bf16[640,1024]{1,0:T(8,128)(2,1)}, bf16[640,768]{1,0:T(8,128)(2,1)S(1)}, bf16[160,256]{1,0:T(8,128)(2,1)S(1)}) custom-call(s32[1]{0:T(128)S(6)} %copy.35.refs_0_, bf16[160,1024]{1,0:T(8,128)(2,1)S(1)} %pad_maximum_fusion.1.refs_1_.tokens.refs_8_.cot, ...), custom_call_target="tpu_custom_call" | custom-call | flops 1000000000 | tf_op jit(solution)/shard_map/pallas_call | solution.py:96
  42.0 1.3 collective-permute-done.8
  43.3 1.6 collective-permute-start.9
  44.9 2.4 %shard_map.308.refs_16_ = bf16[480,256]{1,0:T(8,128)(2,1)S(1)} custom-call(s32[1]{0:T(128)S(6)} %copy.35.refs_0_, bf16[640,768]{1,0:T(8,128)(2,1)S(1)} %get-tuple-element.125.refs_1_.refs_11_), custom_call_target="tpu_custom_call" | custom-call | tf_op jit(solution)/shard_map/pallas_call | solution.py:96
  48.0 1.6 %collective-permute-done.9.far = bf16[80,1024]{1,0:T(8,128)(2,1)S(1)} collective-permute-done((bf16[80,1024]{1,0:T(8,128)(2,1)S(1)}, bf16[80,1024]{1,0:T(8,128)(2,1)S(1)}, u32[]{:S(2)}, u32[]{:S(2)}) %collective-permute-start.9) | collective-permute-done | bytes 163872 | tf_op jit(solution)/shard_map/ppermute | solution.py:14
  50.7 5.7 %collective-permute-start.11 = (bf16[80,1024]{1,0:T(8,128)(2,1)S(1)}, bf16[80,1024]{1,0:T(8,128)(2,1)S(1)}, u32[]{:S(2)}, u32[]{:S(2)}) collective-permute-start(bf16[80,1024]{1,0:T(8,128)(2,1)S(1)} %get-tuple-element.103.refs_0_), channel_id=1, source_target_pairs={{0,4},{4,0},{8,12},{12,8},{1,5},{5,1},{9,13},{13,9},{2,6},{6,2},{1... | collective-permute-start | bytes 491528 | tf_op jit(solution)/shard_map/ppermute | solution.py:14
  56.4 1.0 collective-permute-start.14
  57.4 1.5 collective-permute-start.16
  58.9 3.5 %collective-permute-done.11.refs_2_ = bf16[80,1024]{1,0:T(8,128)(2,1)S(1)} collective-permute-done((bf16[80,1024]{1,0:T(8,128)(2,1)S(1)}, bf16[80,1024]{1,0:T(8,128)(2,1)S(1)}, u32[]{:S(2)}, u32[]{:S(2)}) %collective-permute-start.11) | collective-permute-done | bytes 163872 | tf_op jit(solution)/shard_map/ppermute | solution.py:14
  62.5 9.0 %collective-permute-done.14.refs_4_ = bf16[80,1024]{1,0:T(8,128)(2,1)S(1)} collective-permute-done((bf16[80,1024]{1,0:T(8,128)(2,1)S(1)}, bf16[80,1024]{1,0:T(8,128)(2,1)S(1)}, u32[]{:S(2)}, u32[]{:S(2)}) %collective-permute-start.14) | collective-permute-done | bytes 163872 | tf_op jit(solution)/shard_map/ppermute | solution.py:14
  74.2 3.2 %collective-permute-done.18.refs_20_ = bf16[1024,512]{1,0:T(8,128)(2,1)} collective-permute-done((bf16[1024,512]{1,0:T(8,128)(2,1)}, bf16[1024,512]{1,0:T(8,128)(2,1)}, u32[]{:S(2)}, u32[]{:S(2)}) %collective-permute-start.18) | collective-permute-done | bytes 1048608 | tf_op jit(solution)/shard_map/ppermute | solution.py:14
  77.4 11.2 %shard_map.310 = (bf16[640,1024]{1,0:T(8,128)(2,1)}, bf16[640,1024]{1,0:T(8,128)(2,1)}, bf16[640,1024]{1,0:T(8,128)(2,1)}, bf16[640,1024]{1,0:T(8,128)(2,1)}, bf...) custom-call(bf16[80,1024]{1,0:T(8,128)(2,1)} %copy-done.25, ...), custom_call_target="tpu_custom_call" | custom-call | flops 6710886400 | bytes 7864320 | tf_op jit(solution)/shard_map/pallas_call | solution.py:96
  88.7 1.6 collective-permute-done.19
  90.3 1.0 add_convert_fusion.3.near
  91.3 1.8 %collective-permute-start.20 = (bf16[80,1024]{1,0:T(8,128)(2,1)S(1)}, bf16[80,1024]{1,0:T(8,128)(2,1)S(1)}, u32[]{:S(2)}, u32[]{:S(2)}) collective-permute-start(bf16[80,1024]{1,0:T(8,128)(2,1)S(1)} %add_convert_fusion.3.near), channel_id=1, source_target_pairs={{0,2},{1,3},{2,0},{3,1},{4,6},{5,7},{6,4},{7,5},{8,10},{9,11},{10,... | collective-permute-start | bytes 491528 | tf_op jit(solution)/shard_map/ppermute | solution.py:14
  93.1 1.6 collective-permute-start.28
  94.7 1.1 slice.29
  96.4 1.2 collective-permute-done.20.far
  97.9 1.9 %collective-permute-start.25 = (bf16[96,1024]{1,0:T(8,128)(2,1)S(1)}, bf16[96,1024]{1,0:T(8,128)(2,1)S(1)}, u32[]{:S(2)}, u32[]{:S(2)}) collective-permute-start(bf16[96,1024]{1,0:T(8,128)(2,1)S(1)} %get-tuple-element.112.refs_1_), channel_id=1, source_target_pairs={{0,4},{4,0},{8,12},{12,8},{1,5},{5,1},{9,13},{13,9},{2,6},{6,2},{1... | collective-permute-start | bytes 589832 | tf_op jit(solution)/shard_map/ppermute | solution.py:14
  99.8 2.6 %collective-permute-start.26 = (bf16[96,1024]{1,0:T(8,128)(2,1)S(1)}, bf16[96,1024]{1,0:T(8,128)(2,1)S(1)}, u32[]{:S(2)}, u32[]{:S(2)}) collective-permute-start(bf16[96,1024]{1,0:T(8,128)(2,1)S(1)} %get-tuple-element.112.refs_1_), channel_id=1, source_target_pairs={{0,8},{4,12},{8,0},{12,4},{1,9},{5,13},{9,1},{13,5},{2,10},{6,14},... | collective-permute-start | bytes 589832 | tf_op jit(solution)/shard_map/ppermute | solution.py:14
  102.5 1.0 fusion.25
  103.9 4.3 %collective-permute-done.28 = bf16[512,512]{1,0:T(8,128)(2,1)S(1)} collective-permute-done((bf16[512,512]{1,0:T(8,128)(2,1)}, bf16[512,512]{1,0:T(8,128)(2,1)S(1)}, u32[]{:S(2)}, u32[]{:S(2)}) %collective-permute-start.28) | collective-permute-done | bytes 524320 | tf_op jit(solution)/shard_map/ppermute | solution.py:14
  109.2 6.9 %collective-permute-done.26.refs_5_ = bf16[96,1024]{1,0:T(8,128)(2,1)S(1)} collective-permute-done((bf16[96,1024]{1,0:T(8,128)(2,1)S(1)}, bf16[96,1024]{1,0:T(8,128)(2,1)S(1)}, u32[]{:S(2)}, u32[]{:S(2)}) %collective-permute-start.26) | collective-permute-done | bytes 196640 | tf_op jit(solution)/shard_map/ppermute | solution.py:14
  116.6 3.8 %collective-permute-start.40 = (bf16[512,512]{1,0:T(8,128)(2,1)S(1)}, bf16[512,512]{1,0:T(8,128)(2,1)S(1)}, u32[]{:S(2)}, u32[]{:S(2)}) collective-permute-start(bf16[512,512]{1,0:T(8,128)(2,1)S(1)} %fusion), channel_id=1, source_target_pairs={{0,4},{4,0},{8,12},{12,8},{1,5},{5,1},{9,13},{13,9},{2,6},{6,2},{1... | collective-permute-start | bytes 1572872 | tf_op jit(solution)/shard_map/ppermute | solution.py:14
  120.8 11.4 %shard_map.312 = (bf16[640,1024]{1,0:T(8,128)(2,1)}, bf16[640,768]{1,0:T(8,128)(2,1)S(1)}, bf16[80,1024]{1,0:T(8,128)(2,1)S(1)}, bf16[80,1024]{1,0:T(8,128)(2,1)...) custom-call(s32[1]{0:T(128)S(6)} %copy.35.refs_0_, ...), custom_call_target="tpu_custom_call" | custom-call | flops 1048576000 | bytes 5242880 | tf_op jit(solution)/shard_map/pallas_call | solution.py:96
  132.2 1.5 collective-permute-start.36
  135.3 1.6 collective-permute-start.34
  136.9 1.6 %convert_add_fusion = f32[512,1024]{1,0:T(8,128)} fusion(f32[512,1024]{1,0:T(8,128)S(1)} %fusion.25, bf16[512,1024]{1,0:T(8,128)(2,1)S(1)} %collective-permute-done.32), kind=kLoop, calls=%fused_computation | loop fusion | flops 1048576 | bytes 5242880 | tf_op jit(solution)/shard_map/add | solution.py:679
  138.5 3.1 %collective-permute-done.34.far = bf16[80,1024]{1,0:T(8,128)(2,1)S(1)} collective-permute-done((bf16[80,1024]{1,0:T(8,128)(2,1)S(1)}, bf16[80,1024]{1,0:T(8,128)(2,1)S(1)}, u32[]{:S(2)}, u32[]{:S(2)}) %collective-permute-start.34) | collective-permute-done | bytes 163872 | tf_op jit(solution)/shard_map/ppermute | solution.py:14
  142.0 1.2 shard_map.314
  144.7 1.2 copy-done.31
  146.4 1.6 collective-permute-start.38
  148.0 1.6 %maximum_convert_fusion = f32[1024,512]{1,0:T(8,128)} fusion(bf16[512,512]{1,0:T(8,128)(2,1)S(1)} %get-tuple-element.160, bf16[512,512]{1,0:T(8,128)(2,1)S(1)} %get-tuple-element.159), kind=kLoop, calls=%fused_computation.3 | loop fusion | flops 2097152 | bytes 3145728 | tf_op jit(solution)/shard_map/convert_element_type | solution.py:632
  151.8 6.7 %collective-permute-done.39.lines = f32[10,512]{1,0:T(8,128)S(1)} collective-permute-done((f32[10,512]{1,0:T(8,128)S(1)}, f32[10,512]{1,0:T(8,128)S(1)}, u32[]{:S(2)}, u32[]{:S(2)}) %collective-permute-start.39) | collective-permute-done | bytes 20512 | tf_op jit(solution)/shard_map/ppermute | solution.py:14
  158.5 1.5 shard_map.315
  (169 shorter events, 15.5 us)
Async XLA Ops:
  2.8 46.9 %copy-start = (bf16[160,1024]{1,0:T(8,128)(2,1)}, bf16[160,1024]{1,0:T(8,128)(2,1)S(1)}, u32[]{:S(2)}) copy-start(bf16[160,1024]{1,0:T(8,128)(2,1)S(1)} %pad_maximum_fusion.1.refs_1_.tokens.refs_8_.cot) | copy-start | bytes 983044
  5.4 32.5 %copy-start.2 = (bf16[528,768]{1,0:T(8,128)(2,1)S(1)}, bf16[528,768]{1,0:T(8,128)(2,1)}, u32[]{:S(2)}) copy-start(bf16[528,768]{1,0:T(8,128)(2,1)} %get-tuple-element.89.refs_9_.refs_12_.refs_2_) | copy-start | bytes 2433028
  5.4 32.5 %copy-start.24 = (f32[16,768]{1,0:T(8,128)S(1)}, f32[16,768]{1,0:T(8,128)}, u32[]{:S(2)}) copy-start(f32[16,768]{1,0:T(8,128)} %get-tuple-element.93.refs_11_) | copy-start | bytes 147460
  5.4 22.1 %collective-permute-start.1 = (bf16[528,768]{1,0:T(8,128)(2,1)}, bf16[528,768]{1,0:T(8,128)(2,1)S(1)}, u32[]{:S(2)}, u32[]{:S(2)}) collective-permute-start(bf16[528,768]{1,0:T(8,128)(2,1)} %get-tuple-element.89.refs_9_.refs_12_.refs_2_), channel_id=1, source_target_pairs={{0,16},{16,0},{1,17},{17,1},{2,18},{18,2},{3,19},{19,3},{4,20},{20... | collective-permute-start | bytes 2433032 | tf_op jit(solution)/shard_map/ppermute | solution.py:14
  8.4 15.3 %collective-permute-start = (bf16[160,1024]{1,0:T(8,128)(2,1)S(1)}, bf16[160,1024]{1,0:T(8,128)(2,1)S(1)}, u32[]{:S(2)}, u32[]{:S(2)}) collective-permute-start(bf16[160,1024]{1,0:T(8,128)(2,1)S(1)} %pad_maximum_fusion.1.refs_1_.tokens.refs_8_.cot), channel_id=1, source_target_pairs={{0,4},{4,0},{8,12},{12,8},{1,5},{5,1},{9,13},{13,9},{2,6},{6,2},{1... | collective-permute-start | bytes 983048 | tf_op jit(solution)/shard_map/ppermute | solution.py:14
  10.0 25.6 %collective-permute-start.3 = (bf16[160,1024]{1,0:T(8,128)(2,1)S(1)}, bf16[160,1024]{1,0:T(8,128)(2,1)S(1)}, u32[]{:S(2)}, u32[]{:S(2)}) collective-permute-start(bf16[160,1024]{1,0:T(8,128)(2,1)S(1)} %pad_maximum_fusion.1.refs_1_.tokens.refs_8_.cot), channel_id=1, source_target_pairs={{0,8},{4,12},{8,0},{12,4},{1,9},{5,13},{9,1},{13,5},{2,10},{6,14},... | collective-permute-start | bytes 983048 | tf_op jit(solution)/shard_map/ppermute | solution.py:14
  12.6 23.0 %collective-permute-start.5 = (bf16[160,1024]{1,0:T(8,128)(2,1)S(1)}, bf16[160,1024]{1,0:T(8,128)(2,1)S(1)}, u32[]{:S(2)}, u32[]{:S(2)}) collective-permute-start(bf16[160,1024]{1,0:T(8,128)(2,1)S(1)} %pad_maximum_fusion.1.refs_1_.tokens.refs_8_.cot), channel_id=1, source_target_pairs={{0,12},{4,8},{8,4},{12,0},{1,13},{5,9},{9,5},{13,1},{2,14},{6,10},... | collective-permute-start | bytes 983048 | tf_op jit(solution)/shard_map/ppermute | solution.py:14
  12.8 28.7 %collective-permute-start.7 = (bf16[256,512]{1,0:T(8,128)(2,1)}, bf16[256,512]{1,0:T(8,128)(2,1)S(1)}, u32[]{:S(2)}, u32[]{:S(2)}) collective-permute-start(bf16[256,512]{1,0:T(8,128)(2,1)} %refs_9_.1), channel_id=1, source_target_pairs={{0,16},{16,0},{1,17},{17,1},{2,18},{18,2},{3,19},{19,3},{4,20},{20... | collective-permute-start | bytes 786440 | tf_op jit(solution)/shard_map/ppermute | solution.py:14
  23.7 17.7 %copy-start.16 = (bf16[160,1024]{1,0:T(8,128)(2,1)}, bf16[160,1024]{1,0:T(8,128)(2,1)S(1)}, u32[]{:S(2)}) copy-start(bf16[160,1024]{1,0:T(8,128)(2,1)S(1)} %collective-permute-done.refs_3_.refs_10_) | copy-start | bytes 983044
  27.5 10.2 %collective-permute-start.2 = (bf16[160,1024]{1,0:T(8,128)(2,1)S(1)}, bf16[160,1024]{1,0:T(8,128)(2,1)S(1)}, u32[]{:S(2)}, u32[]{:S(2)}) collective-permute-start(bf16[160,1024]{1,0:T(8,128)(2,1)S(1)} %collective-permute-done.refs_3_.refs_10_), channel_id=1, source_target_pairs={{0,1},{1,0},{2,3},{3,2},{4,5},{5,4},{6,7},{7,6},{8,9},{9,8},{10,11... | collective-permute-start | bytes 983048 | tf_op jit(solution)/shard_map/ppermute | solution.py:14
  28.5 30.4 %collective-permute-start.12 = (bf16[512,1024]{1,0:T(8,128)(2,1)}, bf16[512,1024]{1,0:T(8,128)(2,1)S(1)}, u32[]{:S(2)}, u32[]{:S(2)}) collective-permute-start(bf16[512,1024]{1,0:T(8,128)(2,1)} %refs_17_.1), channel_id=1, source_target_pairs={{0,16},{16,0},{1,17},{17,1},{2,18},{18,2},{3,19},{19,3},{4,20},{20... | collective-permute-start | bytes 3145736 | tf_op jit(solution)/shard_map/ppermute | solution.py:14
  35.6 2.3 %collective-permute-start.4 = (bf16[160,1024]{1,0:T(8,128)(2,1)S(1)}, bf16[160,1024]{1,0:T(8,128)(2,1)S(1)}, u32[]{:S(2)}, u32[]{:S(2)}) collective-permute-start(bf16[160,1024]{1,0:T(8,128)(2,1)S(1)} %collective-permute-done.3.refs_5_.refs_12_), channel_id=1, source_target_pairs={{0,1},{1,0},{2,3},{3,2},{4,5},{5,4},{6,7},{7,6},{8,9},{9,8},{10,11... | collective-permute-start | bytes 983048 | tf_op jit(solution)/shard_map/ppermute | solution.py:14
  35.6 2.3 %collective-permute-start.6 = (bf16[160,1024]{1,0:T(8,128)(2,1)S(1)}, bf16[160,1024]{1,0:T(8,128)(2,1)S(1)}, u32[]{:S(2)}, u32[]{:S(2)}) collective-permute-start(bf16[160,1024]{1,0:T(8,128)(2,1)S(1)} %collective-permute-done.5.refs_7_.refs_14_), channel_id=1, source_target_pairs={{0,1},{1,0},{2,3},{3,2},{4,5},{5,4},{6,7},{7,6},{8,9},{9,8},{10,11... | collective-permute-start | bytes 983048 | tf_op jit(solution)/shard_map/ppermute | solution.py:14
  37.7 39.6 %collective-permute-start.18 = (bf16[1024,512]{1,0:T(8,128)(2,1)}, bf16[1024,512]{1,0:T(8,128)(2,1)}, u32[]{:S(2)}, u32[]{:S(2)}) collective-permute-start(bf16[1024,512]{1,0:T(8,128)(2,1)} %refs_19_.1), channel_id=1, source_target_pairs={{0,16},{16,0},{1,17},{17,1},{2,18},{18,2},{3,19},{19,3},{4,20},{20... | collective-permute-start | bytes 3145736 | tf_op jit(solution)/shard_map/ppermute | solution.py:14
  41.8 1.5 collective-permute-start.8
  43.3 6.3 %collective-permute-start.9 = (bf16[80,1024]{1,0:T(8,128)(2,1)S(1)}, bf16[80,1024]{1,0:T(8,128)(2,1)S(1)}, u32[]{:S(2)}, u32[]{:S(2)}) collective-permute-start(bf16[80,1024]{1,0:T(8,128)(2,1)S(1)} %add_convert_fusion.4.near), channel_id=1, source_target_pairs={{0,2},{1,3},{2,0},{3,1},{4,6},{5,7},{6,4},{7,5},{8,10},{9,11},{10,... | collective-permute-start | bytes 491528 | tf_op jit(solution)/shard_map/ppermute | solution.py:14
  50.7 42.4 %copy-start.15 = (f32[16,1024]{1,0:T(8,128)S(1)}, f32[16,1024]{1,0:T(8,128)}, u32[]{:S(2)}) copy-start(f32[16,1024]{1,0:T(8,128)} %copy-done.14) | copy-start | bytes 196612
  50.7 11.8 %collective-permute-start.11 = (bf16[80,1024]{1,0:T(8,128)(2,1)S(1)}, bf16[80,1024]{1,0:T(8,128)(2,1)S(1)}, u32[]{:S(2)}, u32[]{:S(2)}) collective-permute-start(bf16[80,1024]{1,0:T(8,128)(2,1)S(1)} %get-tuple-element.103.refs_0_), channel_id=1, source_target_pairs={{0,4},{4,0},{8,12},{12,8},{1,5},{5,1},{9,13},{13,9},{2,6},{6,2},{1... | collective-permute-start | bytes 491528 | tf_op jit(solution)/shard_map/ppermute | solution.py:14
  56.4 15.1 %collective-permute-start.14 = (bf16[80,1024]{1,0:T(8,128)(2,1)S(1)}, bf16[80,1024]{1,0:T(8,128)(2,1)S(1)}, u32[]{:S(2)}, u32[]{:S(2)}) collective-permute-start(bf16[80,1024]{1,0:T(8,128)(2,1)S(1)} %get-tuple-element.103.refs_0_), channel_id=1, source_target_pairs={{0,8},{4,12},{8,0},{12,4},{1,9},{5,13},{9,1},{13,5},{2,10},{6,14},... | collective-permute-start | bytes 491528 | tf_op jit(solution)/shard_map/ppermute | solution.py:14
  57.4 14.1 %collective-permute-start.16 = (bf16[80,1024]{1,0:T(8,128)(2,1)S(1)}, bf16[80,1024]{1,0:T(8,128)(2,1)S(1)}, u32[]{:S(2)}, u32[]{:S(2)}) collective-permute-start(bf16[80,1024]{1,0:T(8,128)(2,1)S(1)} %get-tuple-element.103.refs_0_), channel_id=1, source_target_pairs={{0,12},{4,8},{8,4},{12,0},{1,13},{5,9},{9,5},{13,1},{2,14},{6,10},... | collective-permute-start | bytes 491528 | tf_op jit(solution)/shard_map/ppermute | solution.py:14
  58.9 13.1 %copy-start.32 = (bf16[512,1024]{1,0:T(8,128)(2,1)}, bf16[512,1024]{1,0:T(8,128)(2,1)S(1)}, u32[]{:S(2)}) copy-start(bf16[512,1024]{1,0:T(8,128)(2,1)S(1)} %collective-permute-done.12.refs_18_) | copy-start | bytes 3145732
  58.9 13.1 %collective-permute-start.10 = (bf16[80,1024]{1,0:T(8,128)(2,1)S(1)}, bf16[80,1024]{1,0:T(8,128)(2,1)S(1)}, u32[]{:S(2)}, u32[]{:S(2)}) collective-permute-start(bf16[80,1024]{1,0:T(8,128)(2,1)S(1)} %get-tuple-element.103.refs_0_), channel_id=1, source_target_pairs={{0,1},{1,0},{2,3},{3,2},{4,5},{5,4},{6,7},{7,6},{8,9},{9,8},{10,11... | collective-permute-start | bytes 491528 | tf_op jit(solution)/shard_map/ppermute | solution.py:14
  62.5 14.9 %copy-start.34 = (bf16[80,1024]{1,0:T(8,128)(2,1)}, bf16[80,1024]{1,0:T(8,128)(2,1)S(1)}, u32[]{:S(2)}) copy-start(bf16[80,1024]{1,0:T(8,128)(2,1)S(1)} %collective-permute-done.11.refs_2_) | copy-start | bytes 491524
  62.5 9.5 %collective-permute-start.13 = (bf16[80,1024]{1,0:T(8,128)(2,1)S(1)}, bf16[80,1024]{1,0:T(8,128)(2,1)S(1)}, u32[]{:S(2)}, u32[]{:S(2)}) collective-permute-start(bf16[80,1024]{1,0:T(8,128)(2,1)S(1)} %collective-permute-done.11.refs_2_), channel_id=1, source_target_pairs={{0,1},{1,0},{2,3},{3,2},{4,5},{5,4},{6,7},{7,6},{8,9},{9,8},{10,11... | collective-permute-start | bytes 491528 | tf_op jit(solution)/shard_map/ppermute | solution.py:14
  71.5 1.4 collective-permute-start.15
  71.5 1.6 %collective-permute-start.17 = (bf16[80,1024]{1,0:T(8,128)(2,1)S(1)}, bf16[80,1024]{1,0:T(8,128)(2,1)S(1)}, u32[]{:S(2)}, u32[]{:S(2)}) collective-permute-start(bf16[80,1024]{1,0:T(8,128)(2,1)S(1)} %collective-permute-done.16.refs_6_), channel_id=1, source_target_pairs={{0,1},{1,0},{2,3},{3,2},{4,5},{5,4},{6,7},{7,6},{8,9},{9,8},{10,11... | collective-permute-start | bytes 491528 | tf_op jit(solution)/shard_map/ppermute | solution.py:14
  88.6 1.7 %collective-permute-start.19 = (bf16[80,1024]{1,0:T(8,128)(2,1)}, bf16[80,1024]{1,0:T(8,128)(2,1)S(1)}, u32[]{:S(2)}, u32[]{:S(2)}) collective-permute-start(bf16[80,1024]{1,0:T(8,128)(2,1)} %get-tuple-element.111), channel_id=1, source_target_pairs={{0,1},{1,0},{2,3},{3,2},{4,5},{5,4},{6,7},{7,6},{8,9},{9,8},{10,11... | collective-permute-start | bytes 491528 | tf_op jit(solution)/shard_map/ppermute | solution.py:14
  91.3 6.3 %collective-permute-start.20 = (bf16[80,1024]{1,0:T(8,128)(2,1)S(1)}, bf16[80,1024]{1,0:T(8,128)(2,1)S(1)}, u32[]{:S(2)}, u32[]{:S(2)}) collective-permute-start(bf16[80,1024]{1,0:T(8,128)(2,1)S(1)} %add_convert_fusion.3.near), channel_id=1, source_target_pairs={{0,2},{1,3},{2,0},{3,1},{4,6},{5,7},{6,4},{7,5},{8,10},{9,11},{10,... | collective-permute-start | bytes 491528 | tf_op jit(solution)/shard_map/ppermute | solution.py:14
  93.1 15.1 %collective-permute-start.28 = (bf16[512,512]{1,0:T(8,128)(2,1)}, bf16[512,512]{1,0:T(8,128)(2,1)S(1)}, u32[]{:S(2)}, u32[]{:S(2)}) collective-permute-start(bf16[512,512]{1,0:T(8,128)(2,1)} %get-tuple-element.116), channel_id=1, source_target_pairs={{0,16},{16,0},{1,17},{17,1},{2,18},{18,2},{3,19},{19,3},{4,20},{20... | collective-permute-start | bytes 1572872 | tf_op jit(solution)/shard_map/ppermute | solution.py:14
  95.8 38.0 %collective-permute-start.32 = (bf16[512,1024]{1,0:T(8,128)(2,1)}, bf16[512,1024]{1,0:T(8,128)(2,1)S(1)}, u32[]{:S(2)}, u32[]{:S(2)}) collective-permute-start(bf16[512,1024]{1,0:T(8,128)(2,1)} %get-tuple-element.129), channel_id=1, source_target_pairs={{0,16},{16,0},{1,17},{17,1},{2,18},{18,2},{3,19},{19,3},{4,20},{20... | collective-permute-start | bytes 3145736 | tf_op jit(solution)/shard_map/ppermute | solution.py:14
  97.9 11.2 %collective-permute-start.25 = (bf16[96,1024]{1,0:T(8,128)(2,1)S(1)}, bf16[96,1024]{1,0:T(8,128)(2,1)S(1)}, u32[]{:S(2)}, u32[]{:S(2)}) collective-permute-start(bf16[96,1024]{1,0:T(8,128)(2,1)S(1)} %get-tuple-element.112.refs_1_), channel_id=1, source_target_pairs={{0,4},{4,0},{8,12},{12,8},{1,5},{5,1},{9,13},{13,9},{2,6},{6,2},{1... | collective-permute-start | bytes 589832 | tf_op jit(solution)/shard_map/ppermute | solution.py:14
  99.8 16.2 %collective-permute-start.26 = (bf16[96,1024]{1,0:T(8,128)(2,1)S(1)}, bf16[96,1024]{1,0:T(8,128)(2,1)S(1)}, u32[]{:S(2)}, u32[]{:S(2)}) collective-permute-start(bf16[96,1024]{1,0:T(8,128)(2,1)S(1)} %get-tuple-element.112.refs_1_), channel_id=1, source_target_pairs={{0,8},{4,12},{8,0},{12,4},{1,9},{5,13},{9,1},{13,5},{2,10},{6,14},... | collective-permute-start | bytes 589832 | tf_op jit(solution)/shard_map/ppermute | solution.py:14
  102.4 1.4 collective-permute-start.21
  103.8 12.2 %collective-permute-start.27 = (bf16[96,1024]{1,0:T(8,128)(2,1)S(1)}, bf16[96,1024]{1,0:T(8,128)(2,1)S(1)}, u32[]{:S(2)}, u32[]{:S(2)}) collective-permute-start(bf16[96,1024]{1,0:T(8,128)(2,1)S(1)} %get-tuple-element.112.refs_1_), channel_id=1, source_target_pairs={{0,12},{4,8},{8,4},{12,0},{1,13},{5,9},{9,5},{13,1},{2,14},{6,10},... | collective-permute-start | bytes 589832 | tf_op jit(solution)/shard_map/ppermute | solution.py:14
  108.2 8.4 %collective-permute-start.22 = (bf16[80,1024]{1,0:T(8,128)(2,1)S(1)}, bf16[80,1024]{1,0:T(8,128)(2,1)S(1)}, u32[]{:S(2)}, u32[]{:S(2)}) collective-permute-start(bf16[80,1024]{1,0:T(8,128)(2,1)S(1)} %add_convert_fusion.2), channel_id=1, source_target_pairs={{0,2},{1,3},{2,0},{3,1},{4,6},{5,7},{6,4},{7,5},{8,10},{9,11},{10,... | collective-permute-start | bytes 491528 | tf_op jit(solution)/shard_map/ppermute | solution.py:14
  109.1 7.5 %collective-permute-start.24 = (bf16[96,1024]{1,0:T(8,128)(2,1)S(1)}, bf16[96,1024]{1,0:T(8,128)(2,1)S(1)}, u32[]{:S(2)}, u32[]{:S(2)}) collective-permute-start(bf16[96,1024]{1,0:T(8,128)(2,1)S(1)} %get-tuple-element.112.refs_1_), channel_id=1, source_target_pairs={{0,1},{1,0},{2,3},{3,2},{4,5},{5,4},{6,7},{7,6},{8,9},{9,8},{10,11... | collective-permute-start | bytes 589832 | tf_op jit(solution)/shard_map/ppermute | solution.py:14
  116.0 4.4 %collective-permute-start.29 = (bf16[96,1024]{1,0:T(8,128)(2,1)S(1)}, bf16[96,1024]{1,0:T(8,128)(2,1)S(1)}, u32[]{:S(2)}, u32[]{:S(2)}) collective-permute-start(bf16[96,1024]{1,0:T(8,128)(2,1)S(1)} %collective-permute-done.25.refs_3_), channel_id=1, source_target_pairs={{0,1},{1,0},{2,3},{3,2},{4,5},{5,4},{6,7},{7,6},{8,9},{9,8},{10,11... | collective-permute-start | bytes 589832 | tf_op jit(solution)/shard_map/ppermute | solution.py:14
  116.1 4.7 %collective-permute-start.30 = (bf16[96,1024]{1,0:T(8,128)(2,1)S(1)}, bf16[96,1024]{1,0:T(8,128)(2,1)S(1)}, u32[]{:S(2)}, u32[]{:S(2)}) collective-permute-start(bf16[96,1024]{1,0:T(8,128)(2,1)S(1)} %collective-permute-done.26.refs_5_), channel_id=1, source_target_pairs={{0,1},{1,0},{2,3},{3,2},{4,5},{5,4},{6,7},{7,6},{8,9},{9,8},{10,11... | collective-permute-start | bytes 589832 | tf_op jit(solution)/shard_map/ppermute | solution.py:14
  116.6 4.2 %collective-permute-start.31 = (bf16[96,1024]{1,0:T(8,128)(2,1)S(1)}, bf16[96,1024]{1,0:T(8,128)(2,1)S(1)}, u32[]{:S(2)}, u32[]{:S(2)}) collective-permute-start(bf16[96,1024]{1,0:T(8,128)(2,1)S(1)} %collective-permute-done.27.refs_7_), channel_id=1, source_target_pairs={{0,1},{1,0},{2,3},{3,2},{4,5},{5,4},{6,7},{7,6},{8,9},{9,8},{10,11... | collective-permute-start | bytes 589832 | tf_op jit(solution)/shard_map/ppermute | solution.py:14
  116.6 28.0 %collective-permute-start.40 = (bf16[512,512]{1,0:T(8,128)(2,1)S(1)}, bf16[512,512]{1,0:T(8,128)(2,1)S(1)}, u32[]{:S(2)}, u32[]{:S(2)}) collective-permute-start(bf16[512,512]{1,0:T(8,128)(2,1)S(1)} %fusion), channel_id=1, source_target_pairs={{0,4},{4,0},{8,12},{12,8},{1,5},{5,1},{9,13},{13,9},{2,6},{6,2},{1... | collective-permute-start | bytes 1572872 | tf_op jit(solution)/shard_map/ppermute | solution.py:14
  120.5 13.2 %collective-permute-start.23 = (bf16[80,1024]{1,0:T(8,128)(2,1)S(1)}, bf16[80,1024]{1,0:T(8,128)(2,1)S(1)}, u32[]{:S(2)}, u32[]{:S(2)}) collective-permute-start(bf16[80,1024]{1,0:T(8,128)(2,1)S(1)} %add_convert_fusion.1), channel_id=1, source_target_pairs={{0,1},{1,0},{2,3},{3,2},{4,5},{5,4},{6,7},{7,6},{8,9},{9,8},{10,11... | collective-permute-start | bytes 491528 | tf_op jit(solution)/shard_map/ppermute | solution.py:14
  132.2 26.3 %collective-permute-start.36 = (bf16[512,1024]{1,0:T(8,128)(2,1)}, bf16[512,1024]{1,0:T(8,128)(2,1)S(1)}, u32[]{:S(2)}, u32[]{:S(2)}) collective-permute-start(bf16[512,1024]{1,0:T(8,128)(2,1)} %get-tuple-element.137), channel_id=1, source_target_pairs={{0,16},{16,0},{1,17},{17,1},{2,18},{18,2},{3,19},{19,3},{4,20},{20... | collective-permute-start | bytes 3145736 | tf_op jit(solution)/shard_map/ppermute | solution.py:14
  133.8 1.5 collective-permute-start.33
  135.3 6.3 %collective-permute-start.34 = (bf16[80,1024]{1,0:T(8,128)(2,1)S(1)}, bf16[80,1024]{1,0:T(8,128)(2,1)S(1)}, u32[]{:S(2)}, u32[]{:S(2)}) collective-permute-start(bf16[80,1024]{1,0:T(8,128)(2,1)S(1)} %add_convert_fusion.near), channel_id=1, source_target_pairs={{0,2},{1,3},{2,0},{3,1},{4,6},{5,7},{6,4},{7,5},{8,10},{9,11},{10,... | collective-permute-start | bytes 491528 | tf_op jit(solution)/shard_map/ppermute | solution.py:14
  141.9 8.8 %collective-permute-start.35 = (f32[80,1024]{1,0:T(8,128)S(1)}, f32[80,1024]{1,0:T(8,128)S(1)}, u32[]{:S(2)}, u32[]{:S(2)}) collective-permute-start(f32[80,1024]{1,0:T(8,128)S(1)} %shard_map.313), channel_id=1, source_target_pairs={{0,1},{1,0},{2,3},{3,2},{4,5},{5,4},{6,7},{7,6},{8,9},{9,8},{10,11... | collective-permute-start | bytes 983048 | tf_op jit(solution)/shard_map/ppermute | solution.py:14
  143.2 3.1 %collective-permute-start.37 = (f32[2,1024]{1,0:T(2,128)S(1)}, f32[2,1024]{1,0:T(2,128)S(1)}, u32[]{:S(2)}, u32[]{:S(2)}) collective-permute-start(f32[2,1024]{1,0:T(2,128)S(1)} %shard_map.314), channel_id=1, source_target_pairs={{0,1},{1,0},{2,3},{3,2},{4,5},{5,4},{6,7},{7,6},{8,9},{9,8},{10,11... | collective-permute-start | bytes 24584 | tf_op jit(solution)/shard_map/ppermute | solution.py:14
  146.4 3.7 %collective-permute-start.38 = (f32[2,1024]{1,0:T(2,128)S(1)}, f32[2,1024]{1,0:T(2,128)S(1)}, u32[]{:S(2)}, u32[]{:S(2)}) collective-permute-start(f32[2,1024]{1,0:T(2,128)S(1)} %add.66), channel_id=1, source_target_pairs={{0,2},{1,3},{2,0},{3,1},{4,6},{5,7},{6,4},{7,5},{8,10},{9,11},{10,... | collective-permute-start | bytes 24584 | tf_op jit(solution)/shard_map/ppermute | solution.py:14
  150.1 8.3 %collective-permute-start.39 = (f32[10,512]{1,0:T(8,128)S(1)}, f32[10,512]{1,0:T(8,128)S(1)}, u32[]{:S(2)}, u32[]{:S(2)}) collective-permute-start(f32[10,512]{1,0:T(8,128)S(1)} %pad_maximum_fusion.5), channel_id=1, source_target_pairs={{0,16},{16,0},{1,17},{17,1},{2,18},{18,2},{3,19},{19,3},{4,20},{20... | collective-permute-start | bytes 61448 | tf_op jit(solution)/shard_map/ppermute | solution.py:14
  (36 other events, 206.7 us)

commit v7 on v6

--- a/solution.py
+++ b/solution.py
@@ -259,33 +259,32 @@
 
 
 def forward_body(blocks, ways, *refs):
-    normed, cots, refs = refs[:blocks], refs[blocks : 2 * blocks], refs[2 * blocks :]
-    vec, expand, reduce = refs[0], refs[1 : 1 + ways], refs[1 + ways : 1 + 2 * ways]
-    normed_all, cot_all, act, grad, keep, send, out_keep, out_send, unit_sum, cot_sum, *aways = refs[
-        1 + 2 * ways :
-    ]
+    normed, vec, expand, refs = refs[:blocks], refs[blocks], refs[blocks + 1 :][:ways], refs[blocks + 1 + ways :]
+    cots, reduce, refs = refs[:blocks], refs[blocks : blocks + ways], refs[blocks + ways :]
+    normed_all, cot_all, act, grad, keep, send, out_keep, out_send, unit_sum, cot_sum, *aways = refs
     rows = normed[0].shape[0]
     size = normed_all.shape[1] // ways
     units = act.shape[1]
     place = lax.axis_index("context")
     for n in range(blocks):
         normed_all[n * rows : (n + 1) * rows, :] = normed[n][...]
-    for n in range(blocks):
-        cot_all[n * rows : (n + 1) * rows, :] = cots[n][rows:, :]
-    cot_sum[...] = jnp.sum(cot_all[...].astype(WIDE), 0, keepdims=True)
     step = min(256, units, size)
     back = [jnp.zeros((2 * rows, size), WIDE) for _ in range(ways)]
     out = [jnp.zeros((2 * rows, size), WIDE) for _ in range(ways)]
     for at in range(0, units, step):
         columns = slice(at, at + step)
         expands = [w[:, columns] for w in expand]
-        reduces = [w[columns, :] for w in reduce]
         sides = [slice(i * size, (i + 1) * size) for i in range(ways)]
         value = sum(dot(normed_all[:, c], w) for c, w in zip(sides, expands))
         value = value + vec[EBIAS : EBIAS + 1, columns]
         cdf = 0.5 * (1.0 + lax.erf(value * (2.0**-0.5)))
         act[:, columns] = (value * cdf).astype(LOW)
         slope = cdf + value * jnp.exp(-0.5 * value * value) * 0.3989422804014327
+        if at == 0:
+            for n in range(blocks):
+                cot_all[n * rows : (n + 1) * rows, :] = cots[n][rows:, :]
+            cot_sum[...] = jnp.sum(cot_all[...].astype(WIDE), 0, keepdims=True)
+        reduces = [w[columns, :] for w in reduce]
         part = sum(dot_rt(cot_all[:, c], w) for c, w in zip(sides, reduces))
         part = (part * slope).astype(LOW)
         grad[:, columns] = part
@@ -492,7 +491,7 @@
         message, lines = kernel(
             pack_body,
             (low(share + 16, 3 * features), wide(16, 3 * features)),
-            after(query_weight, own_piece),
+            query_weight,
             key_weight,
             value_weight,
             *vectors,
@@ -584,9 +583,9 @@
         + (wide(1, units), wide(1, width))
         + ((low(units // 2, share), low(share, units)) if pair else ()),
         *woven(mine_normed, theirs),
-        *both_pieces,
         vec,
         *expand_parts,
+        *both_pieces,
         *reduce_parts,
         flops=10 * length * width * units,
         moved=12 * length * width,
@@ -675,7 +674,7 @@
     near, far = last_terms(keep, send)
     gn_far = far
     if pair:
-        reduce_theirs = swap(reduce_half, "context", 1)
+        reduce_theirs = swap(after(reduce_half, near), "context", 1)
         grad_expand = expand_own + expand_got.astype(WIDE)
     grad_token_piece = kernel(
         first_back_body, wide(half, width), near, far, own_piece, grad_hidden, vec
@@ -707,7 +706,7 @@
         first_sums = first_sums + swap(first_sums, "tensor", bit)
         bit *= 2
     if pair:
-        grad_reduce = both_halves(reduce_half, after(reduce_theirs, gn_far), 0)
+        grad_reduce = both_halves(reduce_half, reduce_theirs, 0)
     sums = jnp.concatenate([first_sums, norm_sums, branch_sum, cot_sum], 0)
     plain = jnp.concatenate(
         [jnp.pad(head_sum, ((0, 0), (0, width - 3 * features))), unit_sum], 0
@@ -722,7 +721,7 @@
             + (wide(share),) * 6
             + (wide(heads, head_dim // 2),) * 2
             + (wide(expand_bias.shape[1], expand_bias.shape[0]),),
-            after(dot_lt(segments(after(normed_all, gn_far), 2)[0], grad_qkv), grad_tokens, output),
+            after(dot_lt(segments(after(normed_all, gn_far), 2)[0], grad_qkv), grad_tokens, output, grad_reduce),
             dot_lt(
                 jnp.concatenate([context_own, context_rest], 0),
                 segments(after(grad_branch, gn_far), 2)[0],

time: 161 us -> 155 us (0.963)
  local copies, waits for them, and re-layouts: 8.88 us -> 5.1 us
  other arithmetic: 8.44 us -> 6.76 us
    split x4, local copies, waits for them, and re-layouts: 1.9 us -> 0.05 us  [turned(): left, right = jnp.split(value, 2, -1)]
    select_n x6, other arithmetic: 3.73 us -> 1.9 us  [turned(): return jnp.where(second, jnp.concatenate([right, left], -1), value)]
    unnamed x86 -> x90, local copies, waits for them, and re-layouts: 3.9 us -> 2.72 us
  transfers between devices with their start and end apart: 41 -> 41, of which waited for: 19 -> 23; matrix products, arithmetic and copies ran while one was open for 8% -> 7% of each run, Pallas kernels for 12% -> 13%
where the time goes in v7:
time: 155 us; the launch traced here: 154 us
  waiting for transfers between devices  63.2 us (41%)
  starting transfers between devices  40 us (26%)
  Pallas kernels  34 us (22%)
  other arithmetic  6.76 us (4%)
  local copies, waits for them, and re-layouts  5.1 us (3%)
  matrix products  2.84 us (2%)
  between operations  2.28 us (1%)
    ppermute x41, waiting for transfers between devices, swap(): lax.ppermute(block, axis, [(i, i ^ bit) for i in range(lax.axis_size(axis...  63.2 us
    ppermute x41, starting transfers between devices, swap(): lax.ppermute(block, axis, [(i, i ^ bit) for i in range(lax.axis_size(axis...  40 us
    pallas_call x11, Pallas kernels, kernel(): pl.pallas_call(run if staged else body, out_shape=out_shape, in_specs=[pl...  34 us
  transfers between devices with their start and end apart: 41, of which 23 were waited for; matrix products, arithmetic and copies ran while one was open for 7% of the time, Pallas kernels for 13%

profile of v7, /device:TPU:0, one launch (start us, length us, event | category | flops | bytes accessed | tf_op | source)
XLA Modules:
  0.0 154.2 jit_solution(8657575392134316516)
XLA Ops:
  0.7 2.5 %shard_map.305 = (bf16[528,768]{1,0:T(8,128)(2,1)}, f32[16,768]{1,0:T(8,128)}) custom-call(bf16[512,256]{1,0:T(8,128)(2,1)} %refs_0_.4, bf16[512,256]{1,0:T(8,128)(2,1)} %refs_1_.2, bf16[512,256]{1,0:T(8,128)(2,1)} %refs_2_.1, bf16[512]{0:T(512)(128)(2,1)} %refs_3_.1, bf16[512]{0:T(512)(128)(2,1)} %refs_4_.1, bf16[512]{0:T(512)(128)(2,1)} %refs_5_.1, ...), custom_call_target="tpu_custom_call" | custom-call | tf_op jit(solution)/shard_map/pallas_call | solution.py:96
  3.2 3.0 %collective-permute-start.1 = (bf16[528,768]{1,0:T(8,128)(2,1)}, bf16[528,768]{1,0:T(8,128)(2,1)S(1)}, u32[]{:S(2)}, u32[]{:S(2)}) collective-permute-start(bf16[528,768]{1,0:T(8,128)(2,1)} %get-tuple-element.87.refs_9_.refs_12_.refs_2_), channel_id=1, source_target_pairs={{0,16},{16,0},{1,17},{17,1},{2,18},{18,2},{3,19},{19,3},{4,20},{20... | collective-permute-start | bytes 2433032 | tf_op jit(solution)/shard_map/ppermute | solution.py:14
  6.2 1.2 dynamic-slice_bitcast_fusion
  7.6 1.6 %collective-permute-start = (bf16[160,1024]{1,0:T(8,128)(2,1)S(1)}, bf16[160,1024]{1,0:T(8,128)(2,1)S(1)}, u32[]{:S(2)}, u32[]{:S(2)}) collective-permute-start(bf16[160,1024]{1,0:T(8,128)(2,1)S(1)} %pad_maximum_fusion.1.refs_1_.tokens.refs_11_.cot), channel_id=1, source_target_pairs={{0,4},{4,0},{8,12},{12,8},{1,5},{5,1},{9,13},{13,9},{2,6},{6,2},{1... | collective-permute-start | bytes 983048 | tf_op jit(solution)/shard_map/ppermute | solution.py:14
  9.3 2.6 %collective-permute-start.3 = (bf16[160,1024]{1,0:T(8,128)(2,1)S(1)}, bf16[160,1024]{1,0:T(8,128)(2,1)S(1)}, u32[]{:S(2)}, u32[]{:S(2)}) collective-permute-start(bf16[160,1024]{1,0:T(8,128)(2,1)S(1)} %pad_maximum_fusion.1.refs_1_.tokens.refs_11_.cot), channel_id=1, source_target_pairs={{0,8},{4,12},{8,0},{12,4},{1,9},{5,13},{9,1},{13,5},{2,10},{6,14},... | collective-permute-start | bytes 983048 | tf_op jit(solution)/shard_map/ppermute | solution.py:14
  12.4 10.5 %collective-permute-done.refs_3_.refs_13_ = bf16[160,1024]{1,0:T(8,128)(2,1)S(1)} collective-permute-done((bf16[160,1024]{1,0:T(8,128)(2,1)S(1)}, bf16[160,1024]{1,0:T(8,128)(2,1)S(1)}, u32[]{:S(2)}, u32[]{:S(2)}) %collective-permute-start) | collective-permute-done | bytes 327712 | tf_op jit(solution)/shard_map/ppermute | solution.py:14
  23.0 2.3 %collective-permute-done.1.refs_10_.refs_13_.refs_3_ = bf16[528,768]{1,0:T(8,128)(2,1)S(1)} collective-permute-done((bf16[528,768]{1,0:T(8,128)(2,1)}, bf16[528,768]{1,0:T(8,128)(2,1)S(1)}, u32[]{:S(2)}, u32[]{:S(2)}) %collective-permute-start.1) | collective-permute-done | bytes 811040 | tf_op jit(solution)/shard_map/ppermute | solution.py:14
  25.3 2.1 %collective-permute-start.12 = (bf16[512,1024]{1,0:T(8,128)(2,1)S(1)}, bf16[512,1024]{1,0:T(8,128)(2,1)S(1)}, u32[]{:S(2)}, u32[]{:S(2)}) collective-permute-start(bf16[512,1024]{1,0:T(8,128)(2,1)S(1)} %copy-done.32), channel_id=1, source_target_pairs={{0,16},{16,0},{1,17},{17,1},{2,18},{18,2},{3,19},{19,3},{4,20},{20... | collective-permute-start | bytes 3145736 | tf_op jit(solution)/shard_map/ppermute | solution.py:14
  27.4 7.4 %collective-permute-done.3.refs_5_.refs_15_ = bf16[160,1024]{1,0:T(8,128)(2,1)S(1)} collective-permute-done((bf16[160,1024]{1,0:T(8,128)(2,1)S(1)}, bf16[160,1024]{1,0:T(8,128)(2,1)S(1)}, u32[]{:S(2)}, u32[]{:S(2)}) %collective-permute-start.3) | collective-permute-done | bytes 327712 | tf_op jit(solution)/shard_map/ppermute | solution.py:14
  37.0 3.5 %shard_map.306 = (f32[16,1024]{1,0:T(8,128)S(1)}, bf16[640,1024]{1,0:T(8,128)(2,1)}, bf16[640,1024]{1,0:T(8,128)(2,1)}, bf16[640,768]{1,0:T(8,128)(2,1)S(1)}, bf16[160,256]{1,0:T(8,128)(2,1)S(1)}) custom-call(s32[1]{0:T(128)S(6)} %copy.35.refs_0_, bf16[160,1024]{1,0:T(8,128)(2,1)S(1)} %pad_maximum_fusion.1.refs_1_.tokens.refs_11_.cot, ...), custom_call_target="tpu_custom_call" | custom-call | flops 1000000000 | tf_op jit(solution)/shard_map/pallas_call | solution.py:96
  41.0 1.3 collective-permute-done.8
  42.3 1.6 %collective-permute-start.9 = (bf16[80,1024]{1,0:T(8,128)(2,1)S(1)}, bf16[80,1024]{1,0:T(8,128)(2,1)S(1)}, u32[]{:S(2)}, u32[]{:S(2)}) collective-permute-start(bf16[80,1024]{1,0:T(8,128)(2,1)S(1)} %add_convert_fusion.4.near), channel_id=1, source_target_pairs={{0,2},{1,3},{2,0},{3,1},{4,6},{5,7},{6,4},{7,5},{8,10},{9,11},{10,... | collective-permute-start | bytes 491528 | tf_op jit(solution)/shard_map/ppermute | solution.py:14
  43.9 2.4 %shard_map.308.refs_16_ = bf16[480,256]{1,0:T(8,128)(2,1)S(1)} custom-call(s32[1]{0:T(128)S(6)} %copy.35.refs_0_, bf16[640,768]{1,0:T(8,128)(2,1)S(1)} %get-tuple-element.123.refs_1_.refs_11_), custom_call_target="tpu_custom_call" | custom-call | tf_op jit(solution)/shard_map/pallas_call | solution.py:96
  47.0 1.6 %collective-permute-done.9.far = bf16[80,1024]{1,0:T(8,128)(2,1)S(1)} collective-permute-done((bf16[80,1024]{1,0:T(8,128)(2,1)S(1)}, bf16[80,1024]{1,0:T(8,128)(2,1)S(1)}, u32[]{:S(2)}, u32[]{:S(2)}) %collective-permute-start.9) | collective-permute-done | bytes 163872 | tf_op jit(solution)/shard_map/ppermute | solution.py:14
  49.7 5.4 %collective-permute-start.11 = (bf16[80,1024]{1,0:T(8,128)(2,1)S(1)}, bf16[80,1024]{1,0:T(8,128)(2,1)S(1)}, u32[]{:S(2)}, u32[]{:S(2)}) collective-permute-start(bf16[80,1024]{1,0:T(8,128)(2,1)S(1)} %get-tuple-element.101.refs_0_), channel_id=1, source_target_pairs={{0,4},{4,0},{8,12},{12,8},{1,5},{5,1},{9,13},{13,9},{2,6},{6,2},{1... | collective-permute-start | bytes 491528 | tf_op jit(solution)/shard_map/ppermute | solution.py:14
  55.1 1.0 collective-permute-start.14
  56.1 1.5 collective-permute-start.16
  57.6 3.2 %collective-permute-done.11.refs_2_ = bf16[80,1024]{1,0:T(8,128)(2,1)S(1)} collective-permute-done((bf16[80,1024]{1,0:T(8,128)(2,1)S(1)}, bf16[80,1024]{1,0:T(8,128)(2,1)S(1)}, u32[]{:S(2)}, u32[]{:S(2)}) %collective-permute-start.11) | collective-permute-done | bytes 163872 | tf_op jit(solution)/shard_map/ppermute | solution.py:14
  60.8 9.1 %collective-permute-done.14.refs_4_ = bf16[80,1024]{1,0:T(8,128)(2,1)S(1)} collective-permute-done((bf16[80,1024]{1,0:T(8,128)(2,1)S(1)}, bf16[80,1024]{1,0:T(8,128)(2,1)S(1)}, u32[]{:S(2)}, u32[]{:S(2)}) %collective-permute-start.14) | collective-permute-done | bytes 163872 | tf_op jit(solution)/shard_map/ppermute | solution.py:14
  70.5 0.9 collective-permute-done.15.refs_5_
  72.7 2.4 %collective-permute-done.18.refs_20_ = bf16[1024,512]{1,0:T(8,128)(2,1)} collective-permute-done((bf16[1024,512]{1,0:T(8,128)(2,1)S(1)}, bf16[1024,512]{1,0:T(8,128)(2,1)}, u32[]{:S(2)}, u32[]{:S(2)}) %collective-permute-start.18) | collective-permute-done | bytes 1048608 | tf_op jit(solution)/shard_map/ppermute | solution.py:14
  75.1 10.3 %shard_map.310 = (bf16[640,1024]{1,0:T(8,128)(2,1)}, bf16[640,1024]{1,0:T(8,128)(2,1)}, bf16[640,1024]{1,0:T(8,128)(2,1)}, bf16[640,1024]{1,0:T(8,128)(2,1)}, bf...) custom-call(bf16[80,1024]{1,0:T(8,128)(2,1)} %copy-done.25, ...), custom_call_target="tpu_custom_call" | custom-call | flops 6710886400 | bytes 7864320 | tf_op jit(solution)/shard_map/pallas_call | solution.py:96
  85.6 1.6 %collective-permute-done.19 = bf16[80,1024]{1,0:T(8,128)(2,1)S(1)} collective-permute-done((bf16[80,1024]{1,0:T(8,128)(2,1)}, bf16[80,1024]{1,0:T(8,128)(2,1)S(1)}, u32[]{:S(2)}, u32[]{:S(2)}) %collective-permute-start.19) | collective-permute-done | bytes 163872 | tf_op jit(solution)/shard_map/ppermute | solution.py:14
  87.1 1.0 add_convert_fusion.3.near
  88.1 1.8 %collective-permute-start.20 = (bf16[80,1024]{1,0:T(8,128)(2,1)S(1)}, bf16[80,1024]{1,0:T(8,128)(2,1)S(1)}, u32[]{:S(2)}, u32[]{:S(2)}) collective-permute-start(bf16[80,1024]{1,0:T(8,128)(2,1)S(1)} %add_convert_fusion.3.near), channel_id=1, source_target_pairs={{0,2},{1,3},{2,0},{3,1},{4,6},{5,7},{6,4},{7,5},{8,10},{9,11},{10,... | collective-permute-start | bytes 491528 | tf_op jit(solution)/shard_map/ppermute | solution.py:14
  90.0 1.6 %collective-permute-start.28 = (bf16[512,512]{1,0:T(8,128)(2,1)}, bf16[512,512]{1,0:T(8,128)(2,1)S(1)}, u32[]{:S(2)}, u32[]{:S(2)}) collective-permute-start(bf16[512,512]{1,0:T(8,128)(2,1)} %get-tuple-element.114), channel_id=1, source_target_pairs={{0,16},{16,0},{1,17},{17,1},{2,18},{18,2},{3,19},{19,3},{4,20},{20... | collective-permute-start | bytes 1572872 | tf_op jit(solution)/shard_map/ppermute | solution.py:14
  91.5 1.1 slice.29
  93.3 1.2 collective-permute-done.20.far
  94.8 1.9 %collective-permute-start.25 = (bf16[96,1024]{1,0:T(8,128)(2,1)S(1)}, bf16[96,1024]{1,0:T(8,128)(2,1)S(1)}, u32[]{:S(2)}, u32[]{:S(2)}) collective-permute-start(bf16[96,1024]{1,0:T(8,128)(2,1)S(1)} %get-tuple-element.110.refs_1_), channel_id=1, source_target_pairs={{0,4},{4,0},{8,12},{12,8},{1,5},{5,1},{9,13},{13,9},{2,6},{6,2},{1... | collective-permute-start | bytes 589832 | tf_op jit(solution)/shard_map/ppermute | solution.py:14
  96.7 2.6 %collective-permute-start.26 = (bf16[96,1024]{1,0:T(8,128)(2,1)S(1)}, bf16[96,1024]{1,0:T(8,128)(2,1)S(1)}, u32[]{:S(2)}, u32[]{:S(2)}) collective-permute-start(bf16[96,1024]{1,0:T(8,128)(2,1)S(1)} %get-tuple-element.110.refs_1_), channel_id=1, source_target_pairs={{0,8},{4,12},{8,0},{12,4},{1,9},{5,13},{9,1},{13,5},{2,10},{6,14},... | collective-permute-start | bytes 589832 | tf_op jit(solution)/shard_map/ppermute | solution.py:14
  99.3 1.0 fusion.25
  100.7 4.3 %collective-permute-done.28 = bf16[512,512]{1,0:T(8,128)(2,1)S(1)} collective-permute-done((bf16[512,512]{1,0:T(8,128)(2,1)}, bf16[512,512]{1,0:T(8,128)(2,1)S(1)}, u32[]{:S(2)}, u32[]{:S(2)}) %collective-permute-start.28) | collective-permute-done | bytes 524320 | tf_op jit(solution)/shard_map/ppermute | solution.py:14
  106.1 6.8 %collective-permute-done.26.refs_5_ = bf16[96,1024]{1,0:T(8,128)(2,1)S(1)} collective-permute-done((bf16[96,1024]{1,0:T(8,128)(2,1)S(1)}, bf16[96,1024]{1,0:T(8,128)(2,1)S(1)}, u32[]{:S(2)}, u32[]{:S(2)}) %collective-permute-start.26) | collective-permute-done | bytes 196640 | tf_op jit(solution)/shard_map/ppermute | solution.py:14
  114.9 11.5 %shard_map.312 = (bf16[640,1024]{1,0:T(8,128)(2,1)}, bf16[640,768]{1,0:T(8,128)(2,1)S(1)}, bf16[80,1024]{1,0:T(8,128)(2,1)S(1)}, bf16[80,1024]{1,0:T(8,128)(2,1)...) custom-call(s32[1]{0:T(128)S(6)} %copy.35.refs_0_, ...), custom_call_target="tpu_custom_call" | custom-call | flops 1048576000 | bytes 5242880 | tf_op jit(solution)/shard_map/pallas_call | solution.py:96
  126.4 1.5 collective-permute-start.37
  128.1 0.8 maximum_select_fusion.1
  129.5 1.6 %collective-permute-start.34 = (bf16[80,1024]{1,0:T(8,128)(2,1)S(1)}, bf16[80,1024]{1,0:T(8,128)(2,1)S(1)}, u32[]{:S(2)}, u32[]{:S(2)}) collective-permute-start(bf16[80,1024]{1,0:T(8,128)(2,1)S(1)} %add_convert_fusion.near), channel_id=1, source_target_pairs={{0,2},{1,3},{2,0},{3,1},{4,6},{5,7},{6,4},{7,5},{8,10},{9,11},{10,... | collective-permute-start | bytes 491528 | tf_op jit(solution)/shard_map/ppermute | solution.py:14
  131.0 1.8 %convert_add_fusion = f32[512,1024]{1,0:T(8,128)} fusion(f32[512,1024]{1,0:T(8,128)S(1)} %fusion.25, bf16[512,1024]{1,0:T(8,128)(2,1)S(1)} %collective-permute-done.32), kind=kLoop, calls=%fused_computation | loop fusion | flops 1048576 | bytes 5242880 | tf_op jit(solution)/shard_map/add | solution.py:678
  132.8 3.8 %collective-permute-start.36 = (bf16[512,512]{1,0:T(8,128)(2,1)S(1)}, bf16[512,512]{1,0:T(8,128)(2,1)S(1)}, u32[]{:S(2)}, u32[]{:S(2)}) collective-permute-start(bf16[512,512]{1,0:T(8,128)(2,1)S(1)} %fusion), channel_id=1, source_target_pairs={{0,4},{4,0},{8,12},{12,8},{1,5},{5,1},{9,13},{13,9},{2,6},{6,2},{1... | collective-permute-start | bytes 1572872 | tf_op jit(solution)/shard_map/ppermute | solution.py:14
  137.1 1.2 shard_map.314
  138.9 0.8 fusion.3.own
  139.7 0.7 collective-permute-start.39
  140.9 2.6 %collective-permute-done.39 = f32[2,1024]{1,0:T(2,128)S(1)} collective-permute-done((f32[2,1024]{1,0:T(2,128)S(1)}, f32[2,1024]{1,0:T(2,128)S(1)}, u32[]{:S(2)}, u32[]{:S(2)}) %collective-permute-start.39) | collective-permute-done | bytes 8224 | tf_op jit(solution)/shard_map/ppermute | solution.py:14
  144.2 0.9 maximum_select_fusion
  145.1 3.4 %collective-permute-done.36 = bf16[512,512]{1,0:T(8,128)(2,1)S(1)} collective-permute-done((bf16[512,512]{1,0:T(8,128)(2,1)S(1)}, bf16[512,512]{1,0:T(8,128)(2,1)S(1)}, u32[]{:S(2)}, u32[]{:S(2)}) %collective-permute-start.36) | collective-permute-done | bytes 524320 | tf_op jit(solution)/shard_map/ppermute | solution.py:14
  148.7 1.6 %maximum_convert_fusion = f32[1024,512]{1,0:T(8,128)} fusion(bf16[512,512]{1,0:T(8,128)(2,1)S(1)} %get-tuple-element.158, bf16[512,512]{1,0:T(8,128)(2,1)S(1)} %get-tuple-element.157), kind=kLoop, calls=%fused_computation.3 | loop fusion | flops 2097152 | bytes 3145728 | tf_op jit(solution)/shard_map/convert_element_type | solution.py:631
  150.3 2.3 %collective-permute-done.40.lines = f32[10,512]{1,0:T(8,128)S(1)} collective-permute-done((f32[10,512]{1,0:T(8,128)S(1)}, f32[10,512]{1,0:T(8,128)S(1)}, u32[]{:S(2)}, u32[]{:S(2)}) %collective-permute-start.40) | collective-permute-done | bytes 20512 | tf_op jit(solution)/shard_map/ppermute | solution.py:14
  152.6 1.5 shard_map.315
  (173 shorter events, 13.6 us)
Async XLA Ops:
  3.2 22.1 %collective-permute-start.1 = (bf16[528,768]{1,0:T(8,128)(2,1)}, bf16[528,768]{1,0:T(8,128)(2,1)S(1)}, u32[]{:S(2)}, u32[]{:S(2)}) collective-permute-start(bf16[528,768]{1,0:T(8,128)(2,1)} %get-tuple-element.87.refs_9_.refs_12_.refs_2_), channel_id=1, source_target_pairs={{0,16},{16,0},{1,17},{17,1},{2,18},{18,2},{3,19},{19,3},{4,20},{20... | collective-permute-start | bytes 2433032 | tf_op jit(solution)/shard_map/ppermute | solution.py:14
  7.4 17.9 %copy-start.32 = (bf16[512,1024]{1,0:T(8,128)(2,1)S(1)}, bf16[512,1024]{1,0:T(8,128)(2,1)}, u32[]{:S(2)}) copy-start(bf16[512,1024]{1,0:T(8,128)(2,1)} %refs_9_.2) | copy-start | bytes 3145732
  7.5 28.6 %copy-start.33 = (bf16[1024,512]{1,0:T(8,128)(2,1)S(1)}, bf16[1024,512]{1,0:T(8,128)(2,1)}, u32[]{:S(2)}) copy-start(bf16[1024,512]{1,0:T(8,128)(2,1)} %refs_19_.1) | copy-start | bytes 3145732
  7.6 41.1 %copy-start = (bf16[160,1024]{1,0:T(8,128)(2,1)}, bf16[160,1024]{1,0:T(8,128)(2,1)S(1)}, u32[]{:S(2)}) copy-start(bf16[160,1024]{1,0:T(8,128)(2,1)S(1)} %pad_maximum_fusion.1.refs_1_.tokens.refs_11_.cot) | copy-start | bytes 983044
  7.6 29.4 %copy-start.2 = (bf16[528,768]{1,0:T(8,128)(2,1)S(1)}, bf16[528,768]{1,0:T(8,128)(2,1)}, u32[]{:S(2)}) copy-start(bf16[528,768]{1,0:T(8,128)(2,1)} %get-tuple-element.87.refs_9_.refs_12_.refs_2_) | copy-start | bytes 2433028
  7.6 29.4 %copy-start.24 = (f32[16,768]{1,0:T(8,128)S(1)}, f32[16,768]{1,0:T(8,128)}, u32[]{:S(2)}) copy-start(f32[16,768]{1,0:T(8,128)} %get-tuple-element.91.refs_11_) | copy-start | bytes 147460
  7.6 15.3 %collective-permute-start = (bf16[160,1024]{1,0:T(8,128)(2,1)S(1)}, bf16[160,1024]{1,0:T(8,128)(2,1)S(1)}, u32[]{:S(2)}, u32[]{:S(2)}) collective-permute-start(bf16[160,1024]{1,0:T(8,128)(2,1)S(1)} %pad_maximum_fusion.1.refs_1_.tokens.refs_11_.cot), channel_id=1, source_target_pairs={{0,4},{4,0},{8,12},{12,8},{1,5},{5,1},{9,13},{13,9},{2,6},{6,2},{1... | collective-permute-start | bytes 983048 | tf_op jit(solution)/shard_map/ppermute | solution.py:14
  9.3 25.6 %collective-permute-start.3 = (bf16[160,1024]{1,0:T(8,128)(2,1)S(1)}, bf16[160,1024]{1,0:T(8,128)(2,1)S(1)}, u32[]{:S(2)}, u32[]{:S(2)}) collective-permute-start(bf16[160,1024]{1,0:T(8,128)(2,1)S(1)} %pad_maximum_fusion.1.refs_1_.tokens.refs_11_.cot), channel_id=1, source_target_pairs={{0,8},{4,12},{8,0},{12,4},{1,9},{5,13},{9,1},{13,5},{2,10},{6,14},... | collective-permute-start | bytes 983048 | tf_op jit(solution)/shard_map/ppermute | solution.py:14
  11.8 23.0 %collective-permute-start.5 = (bf16[160,1024]{1,0:T(8,128)(2,1)S(1)}, bf16[160,1024]{1,0:T(8,128)(2,1)S(1)}, u32[]{:S(2)}, u32[]{:S(2)}) collective-permute-start(bf16[160,1024]{1,0:T(8,128)(2,1)S(1)} %pad_maximum_fusion.1.refs_1_.tokens.refs_11_.cot), channel_id=1, source_target_pairs={{0,12},{4,8},{8,4},{12,0},{1,13},{5,9},{9,5},{13,1},{2,14},{6,10},... | collective-permute-start | bytes 983048 | tf_op jit(solution)/shard_map/ppermute | solution.py:14
  12.1 28.5 %collective-permute-start.7 = (bf16[256,512]{1,0:T(8,128)(2,1)S(1)}, bf16[256,512]{1,0:T(8,128)(2,1)S(1)}, u32[]{:S(2)}, u32[]{:S(2)}) collective-permute-start(bf16[256,512]{1,0:T(8,128)(2,1)S(1)} %copy-done.8), channel_id=1, source_target_pairs={{0,16},{16,0},{1,17},{17,1},{2,18},{18,2},{3,19},{19,3},{4,20},{20... | collective-permute-start | bytes 786440 | tf_op jit(solution)/shard_map/ppermute | solution.py:14
  23.0 17.5 %copy-start.16 = (bf16[160,1024]{1,0:T(8,128)(2,1)}, bf16[160,1024]{1,0:T(8,128)(2,1)S(1)}, u32[]{:S(2)}) copy-start(bf16[160,1024]{1,0:T(8,128)(2,1)S(1)} %collective-permute-done.refs_3_.refs_13_) | copy-start | bytes 983044
  25.3 10.8 %collective-permute-start.2 = (bf16[160,1024]{1,0:T(8,128)(2,1)S(1)}, bf16[160,1024]{1,0:T(8,128)(2,1)S(1)}, u32[]{:S(2)}, u32[]{:S(2)}) collective-permute-start(bf16[160,1024]{1,0:T(8,128)(2,1)S(1)} %collective-permute-done.refs_3_.refs_13_), channel_id=1, source_target_pairs={{0,1},{1,0},{2,3},{3,2},{4,5},{5,4},{6,7},{7,6},{8,9},{9,8},{10,11... | collective-permute-start | bytes 983048 | tf_op jit(solution)/shard_map/ppermute | solution.py:14
  25.3 32.2 %collective-permute-start.12 = (bf16[512,1024]{1,0:T(8,128)(2,1)S(1)}, bf16[512,1024]{1,0:T(8,128)(2,1)S(1)}, u32[]{:S(2)}, u32[]{:S(2)}) collective-permute-start(bf16[512,1024]{1,0:T(8,128)(2,1)S(1)} %copy-done.32), channel_id=1, source_target_pairs={{0,16},{16,0},{1,17},{17,1},{2,18},{18,2},{3,19},{19,3},{4,20},{20... | collective-permute-start | bytes 3145736 | tf_op jit(solution)/shard_map/ppermute | solution.py:14
  34.8 1.9 %collective-permute-start.4 = (bf16[160,1024]{1,0:T(8,128)(2,1)S(1)}, bf16[160,1024]{1,0:T(8,128)(2,1)S(1)}, u32[]{:S(2)}, u32[]{:S(2)}) collective-permute-start(bf16[160,1024]{1,0:T(8,128)(2,1)S(1)} %collective-permute-done.3.refs_5_.refs_15_), channel_id=1, source_target_pairs={{0,1},{1,0},{2,3},{3,2},{4,5},{5,4},{6,7},{7,6},{8,9},{9,8},{10,11... | collective-permute-start | bytes 983048 | tf_op jit(solution)/shard_map/ppermute | solution.py:14
  34.9 2.1 %collective-permute-start.6 = (bf16[160,1024]{1,0:T(8,128)(2,1)S(1)}, bf16[160,1024]{1,0:T(8,128)(2,1)S(1)}, u32[]{:S(2)}, u32[]{:S(2)}) collective-permute-start(bf16[160,1024]{1,0:T(8,128)(2,1)S(1)} %collective-permute-done.5.refs_7_.refs_17_), channel_id=1, source_target_pairs={{0,1},{1,0},{2,3},{3,2},{4,5},{5,4},{6,7},{7,6},{8,9},{9,8},{10,11... | collective-permute-start | bytes 983048 | tf_op jit(solution)/shard_map/ppermute | solution.py:14
  36.1 39.0 %collective-permute-start.18 = (bf16[1024,512]{1,0:T(8,128)(2,1)S(1)}, bf16[1024,512]{1,0:T(8,128)(2,1)}, u32[]{:S(2)}, u32[]{:S(2)}) collective-permute-start(bf16[1024,512]{1,0:T(8,128)(2,1)S(1)} %copy-done.33), channel_id=1, source_target_pairs={{0,16},{16,0},{1,17},{17,1},{2,18},{18,2},{3,19},{19,3},{4,20},{20... | collective-permute-start | bytes 3145736 | tf_op jit(solution)/shard_map/ppermute | solution.py:14
  40.8 1.5 collective-permute-start.8
  42.3 6.3 %collective-permute-start.9 = (bf16[80,1024]{1,0:T(8,128)(2,1)S(1)}, bf16[80,1024]{1,0:T(8,128)(2,1)S(1)}, u32[]{:S(2)}, u32[]{:S(2)}) collective-permute-start(bf16[80,1024]{1,0:T(8,128)(2,1)S(1)} %add_convert_fusion.4.near), channel_id=1, source_target_pairs={{0,2},{1,3},{2,0},{3,1},{4,6},{5,7},{6,4},{7,5},{8,10},{9,11},{10,... | collective-permute-start | bytes 491528 | tf_op jit(solution)/shard_map/ppermute | solution.py:14
  49.7 40.3 %copy-start.15 = (f32[16,1024]{1,0:T(8,128)S(1)}, f32[16,1024]{1,0:T(8,128)}, u32[]{:S(2)}) copy-start(f32[16,1024]{1,0:T(8,128)} %copy-done.14) | copy-start | bytes 196612
  49.7 11.1 %collective-permute-start.11 = (bf16[80,1024]{1,0:T(8,128)(2,1)S(1)}, bf16[80,1024]{1,0:T(8,128)(2,1)S(1)}, u32[]{:S(2)}, u32[]{:S(2)}) collective-permute-start(bf16[80,1024]{1,0:T(8,128)(2,1)S(1)} %get-tuple-element.101.refs_0_), channel_id=1, source_target_pairs={{0,4},{4,0},{8,12},{12,8},{1,5},{5,1},{9,13},{13,9},{2,6},{6,2},{1... | collective-permute-start | bytes 491528 | tf_op jit(solution)/shard_map/ppermute | solution.py:14
  55.1 14.9 %collective-permute-start.14 = (bf16[80,1024]{1,0:T(8,128)(2,1)S(1)}, bf16[80,1024]{1,0:T(8,128)(2,1)S(1)}, u32[]{:S(2)}, u32[]{:S(2)}) collective-permute-start(bf16[80,1024]{1,0:T(8,128)(2,1)S(1)} %get-tuple-element.101.refs_0_), channel_id=1, source_target_pairs={{0,8},{4,12},{8,0},{12,4},{1,9},{5,13},{9,1},{13,5},{2,10},{6,14},... | collective-permute-start | bytes 491528 | tf_op jit(solution)/shard_map/ppermute | solution.py:14
  56.1 13.9 %collective-permute-start.16 = (bf16[80,1024]{1,0:T(8,128)(2,1)S(1)}, bf16[80,1024]{1,0:T(8,128)(2,1)S(1)}, u32[]{:S(2)}, u32[]{:S(2)}) collective-permute-start(bf16[80,1024]{1,0:T(8,128)(2,1)S(1)} %get-tuple-element.101.refs_0_), channel_id=1, source_target_pairs={{0,12},{4,8},{8,4},{12,0},{1,13},{5,9},{9,5},{13,1},{2,14},{6,10},... | collective-permute-start | bytes 491528 | tf_op jit(solution)/shard_map/ppermute | solution.py:14
  57.6 12.9 %collective-permute-start.10 = (bf16[80,1024]{1,0:T(8,128)(2,1)S(1)}, bf16[80,1024]{1,0:T(8,128)(2,1)S(1)}, u32[]{:S(2)}, u32[]{:S(2)}) collective-permute-start(bf16[80,1024]{1,0:T(8,128)(2,1)S(1)} %get-tuple-element.101.refs_0_), channel_id=1, source_target_pairs={{0,1},{1,0},{2,3},{3,2},{4,5},{5,4},{6,7},{7,6},{8,9},{9,8},{10,11... | collective-permute-start | bytes 491528 | tf_op jit(solution)/shard_map/ppermute | solution.py:14
  60.8 9.7 %collective-permute-start.13 = (bf16[80,1024]{1,0:T(8,128)(2,1)S(1)}, bf16[80,1024]{1,0:T(8,128)(2,1)S(1)}, u32[]{:S(2)}, u32[]{:S(2)}) collective-permute-start(bf16[80,1024]{1,0:T(8,128)(2,1)S(1)} %collective-permute-done.11.refs_2_), channel_id=1, source_target_pairs={{0,1},{1,0},{2,3},{3,2},{4,5},{5,4},{6,7},{7,6},{8,9},{9,8},{10,11... | collective-permute-start | bytes 491528 | tf_op jit(solution)/shard_map/ppermute | solution.py:14
  69.9 1.4 collective-permute-start.15
  70.0 1.6 %collective-permute-start.17 = (bf16[80,1024]{1,0:T(8,128)(2,1)S(1)}, bf16[80,1024]{1,0:T(8,128)(2,1)S(1)}, u32[]{:S(2)}, u32[]{:S(2)}) collective-permute-start(bf16[80,1024]{1,0:T(8,128)(2,1)S(1)} %collective-permute-done.16.refs_6_), channel_id=1, source_target_pairs={{0,1},{1,0},{2,3},{3,2},{4,5},{5,4},{6,7},{7,6},{8,9},{9,8},{10,11... | collective-permute-start | bytes 491528 | tf_op jit(solution)/shard_map/ppermute | solution.py:14
  85.5 1.7 %collective-permute-start.19 = (bf16[80,1024]{1,0:T(8,128)(2,1)}, bf16[80,1024]{1,0:T(8,128)(2,1)S(1)}, u32[]{:S(2)}, u32[]{:S(2)}) collective-permute-start(bf16[80,1024]{1,0:T(8,128)(2,1)} %get-tuple-element.109), channel_id=1, source_target_pairs={{0,1},{1,0},{2,3},{3,2},{4,5},{5,4},{6,7},{7,6},{8,9},{9,8},{10,11... | collective-permute-start | bytes 491528 | tf_op jit(solution)/shard_map/ppermute | solution.py:14
  88.1 6.3 %collective-permute-start.20 = (bf16[80,1024]{1,0:T(8,128)(2,1)S(1)}, bf16[80,1024]{1,0:T(8,128)(2,1)S(1)}, u32[]{:S(2)}, u32[]{:S(2)}) collective-permute-start(bf16[80,1024]{1,0:T(8,128)(2,1)S(1)} %add_convert_fusion.3.near), channel_id=1, source_target_pairs={{0,2},{1,3},{2,0},{3,1},{4,6},{5,7},{6,4},{7,5},{8,10},{9,11},{10,... | collective-permute-start | bytes 491528 | tf_op jit(solution)/shard_map/ppermute | solution.py:14
  90.0 15.1 %collective-permute-start.28 = (bf16[512,512]{1,0:T(8,128)(2,1)}, bf16[512,512]{1,0:T(8,128)(2,1)S(1)}, u32[]{:S(2)}, u32[]{:S(2)}) collective-permute-start(bf16[512,512]{1,0:T(8,128)(2,1)} %get-tuple-element.114), channel_id=1, source_target_pairs={{0,16},{16,0},{1,17},{17,1},{2,18},{18,2},{3,19},{19,3},{4,20},{20... | collective-permute-start | bytes 1572872 | tf_op jit(solution)/shard_map/ppermute | solution.py:14
  92.7 35.3 %collective-permute-start.32 = (bf16[512,1024]{1,0:T(8,128)(2,1)}, bf16[512,1024]{1,0:T(8,128)(2,1)S(1)}, u32[]{:S(2)}, u32[]{:S(2)}) collective-permute-start(bf16[512,1024]{1,0:T(8,128)(2,1)} %get-tuple-element.127), channel_id=1, source_target_pairs={{0,16},{16,0},{1,17},{17,1},{2,18},{18,2},{3,19},{19,3},{4,20},{20... | collective-permute-start | bytes 3145736 | tf_op jit(solution)/shard_map/ppermute | solution.py:14
  94.8 11.1 %collective-permute-start.25 = (bf16[96,1024]{1,0:T(8,128)(2,1)S(1)}, bf16[96,1024]{1,0:T(8,128)(2,1)S(1)}, u32[]{:S(2)}, u32[]{:S(2)}) collective-permute-start(bf16[96,1024]{1,0:T(8,128)(2,1)S(1)} %get-tuple-element.110.refs_1_), channel_id=1, source_target_pairs={{0,4},{4,0},{8,12},{12,8},{1,5},{5,1},{9,13},{13,9},{2,6},{6,2},{1... | collective-permute-start | bytes 589832 | tf_op jit(solution)/shard_map/ppermute | solution.py:14
  96.7 16.2 %collective-permute-start.26 = (bf16[96,1024]{1,0:T(8,128)(2,1)S(1)}, bf16[96,1024]{1,0:T(8,128)(2,1)S(1)}, u32[]{:S(2)}, u32[]{:S(2)}) collective-permute-start(bf16[96,1024]{1,0:T(8,128)(2,1)S(1)} %get-tuple-element.110.refs_1_), channel_id=1, source_target_pairs={{0,8},{4,12},{8,0},{12,4},{1,9},{5,13},{9,1},{13,5},{2,10},{6,14},... | collective-permute-start | bytes 589832 | tf_op jit(solution)/shard_map/ppermute | solution.py:14
  99.3 1.4 collective-permute-start.21
  100.7 12.2 %collective-permute-start.27 = (bf16[96,1024]{1,0:T(8,128)(2,1)S(1)}, bf16[96,1024]{1,0:T(8,128)(2,1)S(1)}, u32[]{:S(2)}, u32[]{:S(2)}) collective-permute-start(bf16[96,1024]{1,0:T(8,128)(2,1)S(1)} %get-tuple-element.110.refs_1_), channel_id=1, source_target_pairs={{0,12},{4,8},{8,4},{12,0},{1,13},{5,9},{9,5},{13,1},{2,14},{6,10},... | collective-permute-start | bytes 589832 | tf_op jit(solution)/shard_map/ppermute | solution.py:14
  105.0 8.4 %collective-permute-start.22 = (bf16[80,1024]{1,0:T(8,128)(2,1)S(1)}, bf16[80,1024]{1,0:T(8,128)(2,1)S(1)}, u32[]{:S(2)}, u32[]{:S(2)}) collective-permute-start(bf16[80,1024]{1,0:T(8,128)(2,1)S(1)} %add_convert_fusion.2), channel_id=1, source_target_pairs={{0,2},{1,3},{2,0},{3,1},{4,6},{5,7},{6,4},{7,5},{8,10},{9,11},{10,... | collective-permute-start | bytes 491528 | tf_op jit(solution)/shard_map/ppermute | solution.py:14
  106.0 7.5 %collective-permute-start.24 = (bf16[96,1024]{1,0:T(8,128)(2,1)S(1)}, bf16[96,1024]{1,0:T(8,128)(2,1)S(1)}, u32[]{:S(2)}, u32[]{:S(2)}) collective-permute-start(bf16[96,1024]{1,0:T(8,128)(2,1)S(1)} %get-tuple-element.110.refs_1_), channel_id=1, source_target_pairs={{0,1},{1,0},{2,3},{3,2},{4,5},{5,4},{6,7},{7,6},{8,9},{9,8},{10,11... | collective-permute-start | bytes 589832 | tf_op jit(solution)/shard_map/ppermute | solution.py:14
  112.9 1.4 collective-permute-start.29
  112.9 1.7 %collective-permute-start.30 = (bf16[96,1024]{1,0:T(8,128)(2,1)S(1)}, bf16[96,1024]{1,0:T(8,128)(2,1)S(1)}, u32[]{:S(2)}, u32[]{:S(2)}) collective-permute-start(bf16[96,1024]{1,0:T(8,128)(2,1)S(1)} %collective-permute-done.26.refs_5_), channel_id=1, source_target_pairs={{0,1},{1,0},{2,3},{3,2},{4,5},{5,4},{6,7},{7,6},{8,9},{9,8},{10,11... | collective-permute-start | bytes 589832 | tf_op jit(solution)/shard_map/ppermute | solution.py:14
  113.4 1.5 collective-permute-start.31
  113.5 14.4 %collective-permute-start.23 = (bf16[80,1024]{1,0:T(8,128)(2,1)S(1)}, bf16[80,1024]{1,0:T(8,128)(2,1)S(1)}, u32[]{:S(2)}, u32[]{:S(2)}) collective-permute-start(bf16[80,1024]{1,0:T(8,128)(2,1)S(1)} %add_convert_fusion.1), channel_id=1, source_target_pairs={{0,1},{1,0},{2,3},{3,2},{4,5},{5,4},{6,7},{7,6},{8,9},{9,8},{10,11... | collective-permute-start | bytes 491528 | tf_op jit(solution)/shard_map/ppermute | solution.py:14
  126.4 26.2 %collective-permute-start.37 = (bf16[512,1024]{1,0:T(8,128)(2,1)}, bf16[512,1024]{1,0:T(8,128)(2,1)S(1)}, u32[]{:S(2)}, u32[]{:S(2)}) collective-permute-start(bf16[512,1024]{1,0:T(8,128)(2,1)} %get-tuple-element.136), channel_id=1, source_target_pairs={{0,16},{16,0},{1,17},{17,1},{2,18},{18,2},{3,19},{19,3},{4,20},{20... | collective-permute-start | bytes 3145736 | tf_op jit(solution)/shard_map/ppermute | solution.py:14
  127.9 1.5 collective-permute-start.33
  129.5 7.2 %collective-permute-start.34 = (bf16[80,1024]{1,0:T(8,128)(2,1)S(1)}, bf16[80,1024]{1,0:T(8,128)(2,1)S(1)}, u32[]{:S(2)}, u32[]{:S(2)}) collective-permute-start(bf16[80,1024]{1,0:T(8,128)(2,1)S(1)} %add_convert_fusion.near), channel_id=1, source_target_pairs={{0,2},{1,3},{2,0},{3,1},{4,6},{5,7},{6,4},{7,5},{8,10},{9,11},{10,... | collective-permute-start | bytes 491528 | tf_op jit(solution)/shard_map/ppermute | solution.py:14
  132.8 15.8 %collective-permute-start.36 = (bf16[512,512]{1,0:T(8,128)(2,1)S(1)}, bf16[512,512]{1,0:T(8,128)(2,1)S(1)}, u32[]{:S(2)}, u32[]{:S(2)}) collective-permute-start(bf16[512,512]{1,0:T(8,128)(2,1)S(1)} %fusion), channel_id=1, source_target_pairs={{0,4},{4,0},{8,12},{12,8},{1,5},{5,1},{9,13},{13,9},{2,6},{6,2},{1... | collective-permute-start | bytes 1572872 | tf_op jit(solution)/shard_map/ppermute | solution.py:14
  137.0 7.1 %collective-permute-start.35 = (f32[80,1024]{1,0:T(8,128)S(1)}, f32[80,1024]{1,0:T(8,128)S(1)}, u32[]{:S(2)}, u32[]{:S(2)}) collective-permute-start(f32[80,1024]{1,0:T(8,128)S(1)} %shard_map.313), channel_id=1, source_target_pairs={{0,1},{1,0},{2,3},{3,2},{4,5},{5,4},{6,7},{7,6},{8,9},{9,8},{10,11... | collective-permute-start | bytes 983048 | tf_op jit(solution)/shard_map/ppermute | solution.py:14
  138.3 1.4 collective-permute-start.38
  139.7 3.7 %collective-permute-start.39 = (f32[2,1024]{1,0:T(2,128)S(1)}, f32[2,1024]{1,0:T(2,128)S(1)}, u32[]{:S(2)}, u32[]{:S(2)}) collective-permute-start(f32[2,1024]{1,0:T(2,128)S(1)} %add.66), channel_id=1, source_target_pairs={{0,2},{1,3},{2,0},{3,1},{4,6},{5,7},{6,4},{7,5},{8,10},{9,11},{10,... | collective-permute-start | bytes 24584 | tf_op jit(solution)/shard_map/ppermute | solution.py:14
  143.5 9.1 %collective-permute-start.40 = (f32[10,512]{1,0:T(8,128)S(1)}, f32[10,512]{1,0:T(8,128)S(1)}, u32[]{:S(2)}, u32[]{:S(2)}) collective-permute-start(f32[10,512]{1,0:T(8,128)S(1)} %pad_maximum_fusion.5), channel_id=1, source_target_pairs={{0,16},{16,0},{1,17},{17,1},{2,18},{18,2},{3,19},{19,3},{4,20},{20... | collective-permute-start | bytes 61448 | tf_op jit(solution)/shard_map/ppermute | solution.py:14
  (38 other events, 226.2 us)
